TPU v7x, 32 devices: a whole 2x2x4 slice. The times are simulated.
32 devices in a mesh: row: 4 (over x, core), col: 8 (over z, y).
Axes of the slice: x: 2, y: 2, z: 4, core: 2. Of those that a mesh axis runs over, the one named last changes fastest.
Arguments:
- tokens: bfloat16 [1024, 2, 2560], P('col'), may hold values from -6 to 6
- segments: int32 [1024, 2], P('col'), may hold values from 0 to 3, as said below
- routes: int32 [1024, 2, 6], P('col'), may hold values from 0 to 15, all different within a row; in each aligned block of 256 rows (0 to 255, 256 to 511, ..., all dimensions but the last counted through in order) at most 128 rows name the same one
- attn_gain: bfloat16 [2560], P('col'), may hold values from 0.5 to 1.5
- query_matrix: bfloat16 [2560, 2560], P('col', 'row'), may hold values from -0.125 to 0.125
- key_matrix: bfloat16 [2560, 512], P('col', 'row'), may hold values from -0.125 to 0.125
- value_matrix: bfloat16 [2560, 512], P('col', 'row'), may hold values from -0.125 to 0.125
- attention_output_matrix: bfloat16 [2560, 2560], P('row', 'col'), may hold values from -0.5 to 0.5
- mlp_gain: bfloat16 [2560], P('col'), may hold values from 0.5 to 1.5
- w_router: bfloat16 [2560, 16], P('col'), may hold values from -0.0625 to 0.0625
- shared_gate_matrix: bfloat16 [2560, 3072], P('col', 'row'), may hold values from -0.125 to 0.125
- shared_up_matrix: bfloat16 [2560, 3072], P('col', 'row'), may hold values from -0.125 to 0.125
- shared_down_matrix: bfloat16 [3072, 2560], P('row', 'col'), may hold values from -0.109375 to 0.109375
- expert_gate: bfloat16 [16, 2560, 1536], P('col', None, 'row'), may hold values from -0.125 to 0.125
- expert_up: bfloat16 [16, 2560, 1536], P('col', None, 'row'), may hold values from -0.125 to 0.125
- expert_down: bfloat16 [16, 1536, 2560], P('col', 'row'), may hold values from -0.15625 to 0.15625
- cotangent: float32 [1024, 2, 2560], P('col', None, 'row'), may hold values from -6 to 6
Outputs:
- block_out: bfloat16 [1024, 2, 2560], P('col', None, 'row')
- d_tokens: float32 [1024, 2, 2560], P('col')
- d_attn_gain: float32 [2560], P('col')
- d_query: float32 [2560, 2560], P('col', 'row')
- d_key: float32 [2560, 512], P('col', 'row')
- d_value: float32 [2560, 512], P('col', 'row')
- d_out: float32 [2560, 2560], P('row', 'col')
- d_mlp_gain: float32 [2560], P('col')
- d_router: float32 [2560, 16], P('col')
- d_shared_gate: float32 [2560, 3072], P('col', 'row')
- d_shared_up: float32 [2560, 3072], P('col', 'row')
- d_shared_down: float32 [3072, 2560], P('row', 'col')
- d_expert_gate: float32 [16, 2560, 1536], P('col', None, 'row')
- d_expert_up: float32 [16, 2560, 1536], P('col', None, 'row')
- d_expert_down: float32 [16, 1536, 2560], P('col', 'row')
Inputs may be any that keep to these rules, and one draw needn't show every extreme that they name: `segments`: document numbers start at 0 in every sequence and never fall along it; at least one sequence is a single document. `routes`: each token names 6 different experts. Among the 256 tokens of one index of col, no expert is named more than 128 times.
All inputs are finite; a program needn't handle non-finite values.
Results may differ from a plain program's by a relative error of at most 0.015.
Values may be sent and summed in bfloat16 or wider, within the bound.
A program may use at most 384 MiB of HBM per device.

v0:
```python
import math

import jax
import jax.numpy as jnp
from jax import lax
from jax.sharding import PartitionSpec as P

HEAD_DIM = 128


norm_eps = 1e-05
rope_base = 500000.0
masked_score = -1e30


def rope_tables(start_place, local_len, head_size):
    places = (start_place + jnp.arange(local_len, dtype=jnp.int32)).astype(jnp.float32)
    frequency = jnp.power(
        rope_base, -jnp.arange(0, head_size, 2, dtype=jnp.int32).astype(jnp.float32) / head_size
    )
    angles = places[:, None] * frequency[None, :]
    return (jnp.cos(angles), jnp.sin(angles))


def apply_rotation(field_in, cosine_lookup, sine_lookup):
    half_size = field_in.shape[-1] // 2
    front_half = field_in[..., :half_size]
    back_half = field_in[..., half_size:]
    cosine_grid = cosine_lookup[:, None, None, :]
    sine_grid = sine_lookup[:, None, None, :]
    return jnp.concatenate(
        [
            front_half * cosine_grid - back_half * sine_grid,
            back_half * cosine_grid + front_half * sine_grid,
        ],
        axis=-1,
    )


def unrotate(grad_in, cosine_lookup, sine_lookup):
    half_size = grad_in.shape[-1] // 2
    front_half = grad_in[..., :half_size]
    back_half = grad_in[..., half_size:]
    cosine_grid = cosine_lookup[:, None, None, :]
    sine_grid = sine_lookup[:, None, None, :]
    return jnp.concatenate(
        [
            front_half * cosine_grid + back_half * sine_grid,
            back_half * cosine_grid - front_half * sine_grid,
        ],
        axis=-1,
    )


def to_grid(flat_rows, kv_local, query_group_width, head_size):
    local_len = flat_rows.shape[0]
    seq_count = flat_rows.shape[1]
    shaped = flat_rows.reshape(local_len, seq_count, kv_local, query_group_width, head_size)
    return shaped.transpose(1, 2, 3, 0, 4).reshape(
        seq_count, kv_local, query_group_width * local_len, head_size
    )


def from_grid(grid_rows, query_group_width, local_len):
    seq_count = grid_rows.shape[0]
    kv_local = grid_rows.shape[1]
    head_size = grid_rows.shape[3]
    shaped = grid_rows.reshape(seq_count, kv_local, query_group_width, local_len, head_size)
    return shaped.transpose(3, 0, 1, 2, 4).reshape(
        local_len, seq_count, kv_local * query_group_width * head_size
    )


def block_scores(
    query_grid, key_grid, doc_all, query_place, query_doc, start, block_len, score_scale
):
    key_block = lax.dynamic_slice_in_dim(key_grid, start, block_len, 0)
    doc_block = lax.dynamic_slice_in_dim(doc_all, start, block_len, 0)
    scores = (
        jnp.einsum("shrd,kshd->shrk", query_grid, key_block, preferred_element_type=jnp.float32)
        * score_scale
    )
    key_place = start + jnp.arange(block_len, dtype=jnp.int32)
    same_doc = query_doc[:, None, :, None] == jnp.transpose(doc_block)[:, None, None, :]
    causal = key_place[None, None, None, :] <= query_place[None, None, :, None]
    return (scores, same_doc & causal, key_block)


def rms_scale(values_in):
    return lax.rsqrt(jnp.mean(values_in * values_in, axis=-1, keepdims=True) + norm_eps)


def silu_parts(pre_gate):
    sigmoid_gate = jax.nn.sigmoid(pre_gate)
    silu_gate = pre_gate * sigmoid_gate
    slope_gate = sigmoid_gate * (1.0 + pre_gate * (1.0 - sigmoid_gate))
    return (silu_gate, slope_gate)


def on_device(
    tokens,
    segments,
    routes,
    attn_gain,
    query_matrix,
    key_matrix,
    value_matrix,
    attention_output_matrix,
    mlp_gain,
    w_router,
    shared_gate_matrix,
    shared_up_matrix,
    shared_down_matrix,
    expert_gate,
    expert_up,
    expert_down,
    cotangent,
):
    local_len = tokens.shape[0]
    seq_count = tokens.shape[1]
    model_width = tokens.shape[2]
    col_count = lax.axis_size("col")
    col_index = lax.axis_index("col")
    row_index = lax.axis_index("row")
    full_len = local_len * col_count
    head_size = HEAD_DIM
    kv_local = key_matrix.shape[1] // head_size
    query_group_width = query_matrix.shape[1] // head_size // kv_local
    rows_query = query_group_width * local_len
    row_width = cotangent.shape[2]
    tok_rows = local_len * seq_count
    top_count = routes.shape[2]
    experts = w_router.shape[1]
    exp_local = expert_gate.shape[0]
    capacity = max(2, tok_rows * top_count * 4 // (3 * experts))
    score_scale = 1.0 / math.sqrt(head_size)
    block_len = min(512, full_len)
    blocks = full_len // block_len
    (
        query_gathered,
        key_gathered,
        value_gathered,
        output_gathered,
        shared_gate_gathered,
        shared_up_gathered,
        shared_down_gathered,
        router_full,
        gain_first,
        gain_second,
    ) = (
        lax.all_gather(query_matrix, "col", axis=0, tiled=True),
        lax.all_gather(key_matrix, "col", axis=0, tiled=True),
        lax.all_gather(value_matrix, "col", axis=0, tiled=True),
        lax.all_gather(attention_output_matrix, "col", axis=1, tiled=True),
        lax.all_gather(shared_gate_matrix, "col", axis=0, tiled=True),
        lax.all_gather(shared_up_matrix, "col", axis=0, tiled=True),
        lax.all_gather(shared_down_matrix, "col", axis=1, tiled=True),
        lax.all_gather(w_router, "col", axis=0, tiled=True),
        lax.all_gather(attn_gain, "col", axis=0, tiled=True),
        lax.all_gather(mlp_gain, "col", axis=0, tiled=True),
    )
    tok_float = tokens.astype(jnp.float32)
    inv_first = rms_scale(tok_float)
    base_first = tok_float * inv_first
    gain_one = gain_first.astype(jnp.float32)
    input_normalized = (base_first * gain_one).astype(jnp.bfloat16)
    query_unrotated = jnp.einsum(
        "cjb,bk->cjk", input_normalized, query_gathered, preferred_element_type=jnp.float32
    )
    key_unrotated = jnp.einsum(
        "cjb,bk->cjk", input_normalized, key_gathered, preferred_element_type=jnp.float32
    )
    value_projected = jnp.einsum(
        "cjb,bk->cjk", input_normalized, value_gathered, preferred_element_type=jnp.float32
    )
    cosine_lookup, sine_lookup = rope_tables(col_index * local_len, local_len, head_size)
    query_rotated = apply_rotation(
        query_unrotated.reshape(local_len, seq_count, kv_local * query_group_width, head_size),
        cosine_lookup,
        sine_lookup,
    ).astype(jnp.bfloat16)
    key_rotated = apply_rotation(
        key_unrotated.reshape(local_len, seq_count, kv_local, head_size), cosine_lookup, sine_lookup
    ).astype(jnp.bfloat16)
    key_rotated = key_rotated.reshape(local_len, seq_count, kv_local * head_size)
    value_low = value_projected.astype(jnp.bfloat16)
    key_all, value_all, doc_all = (
        lax.all_gather(key_rotated, "col", axis=0, tiled=True),
        lax.all_gather(value_low, "col", axis=0, tiled=True),
        lax.all_gather(segments, "col", axis=0, tiled=True),
    )
    query_grid = to_grid(
        query_rotated.reshape(local_len, seq_count, kv_local * query_group_width * head_size),
        kv_local,
        query_group_width,
        head_size,
    )
    query_place = jnp.tile(
        col_index * local_len + jnp.arange(local_len, dtype=jnp.int32), query_group_width
    )
    query_doc = jnp.tile(jnp.transpose(segments), (1, query_group_width))
    key_grid = key_all.reshape(full_len, seq_count, kv_local, head_size)
    value_grid = value_all.reshape(full_len, seq_count, kv_local, head_size)

    def first_pass(block_index, state_pair):
        running_max, running_total = state_pair
        scores, allowed, key_block = block_scores(
            query_grid,
            key_grid,
            doc_all,
            query_place,
            query_doc,
            block_index * block_len,
            block_len,
            score_scale,
        )
        masked = jnp.where(allowed, scores, masked_score)
        new_max = jnp.maximum(running_max, jnp.max(masked, axis=-1))
        weights = jnp.where(allowed, jnp.exp(masked - new_max[..., None]), 0.0)
        return (new_max, running_total * jnp.exp(running_max - new_max) + jnp.sum(weights, axis=-1))

    start_max = jnp.full((seq_count, kv_local, rows_query), masked_score, jnp.float32)
    row_max, row_total = lax.fori_loop(
        0, blocks, first_pass, (start_max, jnp.zeros_like(start_max))
    )
    log_total = row_max + jnp.log(row_total)

    def second_pass(block_index, state_pair):
        out_sum, rest_sum = state_pair
        start = block_index * block_len
        scores, allowed, key_block = block_scores(
            query_grid, key_grid, doc_all, query_place, query_doc, start, block_len, score_scale
        )
        value_block = lax.dynamic_slice_in_dim(value_grid, start, block_len, 0)
        probs_block = jnp.where(allowed, jnp.exp(scores - log_total[..., None]), 0.0)
        probs_low = probs_block.astype(jnp.bfloat16)
        rest_low = (probs_block - probs_low.astype(jnp.float32)).astype(jnp.bfloat16)
        out_sum = out_sum + jnp.einsum(
            "shrk,kshd->shrd", probs_low, value_block, preferred_element_type=jnp.float32
        )
        rest_sum = rest_sum + jnp.einsum(
            "shrk,kshd->shrd", rest_low, value_block, preferred_element_type=jnp.float32
        )
        return (out_sum, rest_sum)

    start_out = jnp.zeros((seq_count, kv_local, rows_query, head_size), jnp.float32)
    out_sum, rest_sum = lax.fori_loop(
        0, blocks, second_pass, (start_out, jnp.zeros_like(start_out))
    )
    heads_reduced = from_grid(out_sum, query_group_width, local_len).astype(jnp.bfloat16)
    attention_slice = jnp.einsum(
        "eov,vh->eoh", heads_reduced, output_gathered, preferred_element_type=jnp.float32
    )
    attn_full = lax.psum(attention_slice, "row")
    residual_middle = tok_float + attn_full
    inv_second = rms_scale(residual_middle)
    base_second = residual_middle * inv_second
    gain_two = gain_second.astype(jnp.float32)
    middle_normalized = (base_second * gain_two).astype(jnp.bfloat16)
    logits = jnp.einsum(
        "lsd,de->lse", middle_normalized, router_full, preferred_element_type=jnp.float32
    )
    probs_router = jax.nn.softmax(logits, axis=-1)
    route_hot = (routes[..., None] == jnp.arange(experts, dtype=jnp.int32)).astype(jnp.float32)
    picked = jnp.sum(route_hot * probs_router[:, :, None, :], axis=-1)
    pick_total = jnp.sum(picked, axis=-1, keepdims=True)
    gate_weights = (picked / pick_total).reshape(tok_rows, top_count)
    flat_routes = routes.reshape(tok_rows, top_count)
    route_int = (flat_routes[..., None] == jnp.arange(experts, dtype=jnp.int32)).astype(jnp.int32)
    counts = jnp.sum(route_int, axis=1)
    before = jnp.cumsum(counts, axis=0) - counts
    slot_rank = jnp.sum(route_int * before[:, None, :], axis=2)
    places = flat_routes * capacity + slot_rank
    slot_owner = jnp.full((experts * capacity,), tok_rows * top_count, jnp.int32)
    slot_owner = slot_owner.at[places.reshape(-1)].set(
        jnp.arange(tok_rows * top_count, dtype=jnp.int32)
    )
    token_of = jnp.where(slot_owner < tok_rows * top_count, slot_owner // top_count, tok_rows)
    rows_pad = jnp.concatenate(
        [
            middle_normalized.reshape(tok_rows, model_width),
            jnp.zeros((1, model_width), jnp.bfloat16),
        ],
        axis=0,
    )
    send_rows = rows_pad[token_of].reshape(col_count, exp_local, capacity, model_width)
    received = lax.all_to_all(send_rows, "col", split_axis=0, concat_axis=0, tiled=True)
    gate_pre = jnp.einsum(
        "necd,edf->necf", received, expert_gate, preferred_element_type=jnp.float32
    )
    up_pre = jnp.einsum("necd,edf->necf", received, expert_up, preferred_element_type=jnp.float32)
    silu_gate, slope_gate = silu_parts(gate_pre)
    hidden = (silu_gate * up_pre).astype(jnp.bfloat16)
    expert_part = jnp.einsum(
        "necf,efd->necd", hidden, expert_down, preferred_element_type=jnp.float32
    )
    sgate_pre = jnp.einsum(
        "cjb,bk->cjk", middle_normalized, shared_gate_gathered, preferred_element_type=jnp.float32
    )
    shared_up_projected = jnp.einsum(
        "cjb,bk->cjk", middle_normalized, shared_up_gathered, preferred_element_type=jnp.float32
    )
    shared_silu, shared_slope = silu_parts(sgate_pre)
    shared_hidden_state = (shared_silu * shared_up_projected).astype(jnp.bfloat16)
    shared_part = jnp.einsum(
        "eov,vh->eoh", shared_hidden_state, shared_down_gathered, preferred_element_type=jnp.float32
    )
    expert_total, shared_total = (
        lax.psum_scatter(expert_part, "row", scatter_dimension=3, tiled=True),
        lax.psum_scatter(shared_part, "row", scatter_dimension=2, tiled=True),
    )
    expert_low = expert_total.astype(jnp.bfloat16)
    returned = lax.all_to_all(expert_low, "col", split_axis=0, concat_axis=0, tiled=True)
    chosen = returned.reshape(experts * capacity, row_width)[places]
    routed = jnp.sum(gate_weights[:, :, None] * chosen.astype(jnp.float32), axis=1).reshape(
        local_len, seq_count, row_width
    )
    middle_slice = lax.dynamic_slice_in_dim(residual_middle, row_index * row_width, row_width, 2)
    block_out = (middle_slice + routed + shared_total).astype(jnp.bfloat16)
    grad_full = lax.all_gather(cotangent, "row", axis=2, tiled=True)
    gradient_reduced = grad_full.astype(jnp.bfloat16)
    routed_grad = (gate_weights[:, :, None] * grad_full.reshape(tok_rows, 1, model_width)).astype(
        jnp.bfloat16
    )
    grad_pad = jnp.concatenate(
        [
            routed_grad.reshape(tok_rows * top_count, model_width),
            jnp.zeros((1, model_width), jnp.bfloat16),
        ],
        axis=0,
    )
    grad_send = grad_pad[slot_owner].reshape(col_count, exp_local, capacity, model_width)
    grad_recv = lax.all_to_all(grad_send, "col", split_axis=0, concat_axis=0, tiled=True)
    hidden_grad = jnp.einsum(
        "necd,efd->necf", grad_recv, expert_down, preferred_element_type=jnp.float32
    )
    grad_expert_down = jnp.einsum(
        "necf,necd->efd", hidden, grad_recv, preferred_element_type=jnp.float32
    )
    gate_grad = (hidden_grad * up_pre * slope_gate).astype(jnp.bfloat16)
    up_grad = (hidden_grad * silu_gate).astype(jnp.bfloat16)
    grad_expert_gate = jnp.einsum(
        "necd,necf->edf", received, gate_grad, preferred_element_type=jnp.float32
    )
    grad_expert_up = jnp.einsum(
        "necd,necf->edf", received, up_grad, preferred_element_type=jnp.float32
    )
    rows_grad = jnp.einsum(
        "necf,edf->necd", gate_grad, expert_gate, preferred_element_type=jnp.float32
    )
    rows_grad = rows_grad + jnp.einsum(
        "necf,edf->necd", up_grad, expert_up, preferred_element_type=jnp.float32
    )
    shared_hgrad = jnp.einsum(
        "tzx,bx->tzb", gradient_reduced, shared_down_gathered, preferred_element_type=jnp.float32
    )
    grad_sdown = jnp.einsum(
        "bgw,bgh->wh", shared_hidden_state, gradient_reduced, preferred_element_type=jnp.float32
    )
    shared_gate_gradient = (shared_hgrad * shared_up_projected * shared_slope).astype(jnp.bfloat16)
    shared_up_weight_gradient = (shared_hgrad * shared_silu).astype(jnp.bfloat16)
    grad_sgate = jnp.einsum(
        "tpi,tpa->ia", middle_normalized, shared_gate_gradient, preferred_element_type=jnp.float32
    )
    shared_up_gradient = jnp.einsum(
        "tpi,tpa->ia",
        middle_normalized,
        shared_up_weight_gradient,
        preferred_element_type=jnp.float32,
    )
    shared_in = jnp.einsum(
        "yme,ze->ymz",
        shared_gate_gradient,
        shared_gate_gathered,
        preferred_element_type=jnp.float32,
    )
    shared_in = shared_in + jnp.einsum(
        "yme,ze->ymz",
        shared_up_weight_gradient,
        shared_up_gathered,
        preferred_element_type=jnp.float32,
    )
    rows_back = lax.all_to_all(rows_grad, "col", split_axis=0, concat_axis=0, tiled=True)
    back_width = rows_back.shape[3]
    routed_in = jnp.sum(rows_back.reshape(experts * capacity, back_width)[places], axis=1).reshape(
        local_len, seq_count, back_width
    )
    mid_input = routed_in + shared_in
    gate_dots = jnp.sum(
        cotangent.reshape(tok_rows, 1, row_width) * chosen.astype(jnp.float32), axis=-1
    )
    gate_total, mid_grad = lax.psum((gate_dots, mid_input), "row")
    pick_grad = (
        gate_total - jnp.sum(gate_total * gate_weights, axis=-1, keepdims=True)
    ) / pick_total.reshape(tok_rows, 1)
    prob_grad = jnp.sum(
        route_hot.reshape(tok_rows, top_count, experts) * pick_grad[:, :, None], axis=1
    )
    flat_probs = probs_router.reshape(tok_rows, experts)
    logit_grad = flat_probs * (prob_grad - jnp.sum(flat_probs * prob_grad, axis=-1, keepdims=True))
    logit_low = logit_grad.astype(jnp.bfloat16).reshape(local_len, seq_count, experts)
    grad_router = jnp.einsum(
        "lsd,lse->de", middle_normalized, logit_low, preferred_element_type=jnp.float32
    )
    router_in = jnp.einsum(
        "lse,de->lsd", logit_low, router_full, preferred_element_type=jnp.float32
    )
    mid_total = mid_grad + router_in
    grad_gain_two = jnp.sum(mid_total * base_second, axis=(0, 1))
    scaled_two = mid_total * gain_two
    middle_grad = (
        inv_second
        * (scaled_two - base_second * jnp.mean(scaled_two * base_second, axis=-1, keepdims=True))
        + grad_full
    )
    attention_reduced = middle_grad.astype(jnp.bfloat16)
    output_weight_gradient = jnp.einsum(
        "bgw,bgh->wh", heads_reduced, attention_reduced, preferred_element_type=jnp.float32
    )
    heads_grad = jnp.einsum(
        "tzx,bx->tzb", attention_reduced, output_gathered, preferred_element_type=jnp.float32
    ).astype(jnp.bfloat16)
    dout_grid = to_grid(heads_grad, kv_local, query_group_width, head_size)
    delta_rows = jnp.sum(dout_grid.astype(jnp.float32) * (out_sum + rest_sum), axis=-1)

    def back_pass(query_carry, block_index):
        start = block_index * block_len
        scores, allowed, key_block = block_scores(
            query_grid, key_grid, doc_all, query_place, query_doc, start, block_len, score_scale
        )
        value_block = lax.dynamic_slice_in_dim(value_grid, start, block_len, 0)
        probs_block = jnp.where(allowed, jnp.exp(scores - log_total[..., None]), 0.0)
        probs_low = probs_block.astype(jnp.bfloat16)
        value_grad = jnp.einsum(
            "shrk,shrd->kshd", probs_low, dout_grid, preferred_element_type=jnp.float32
        )
        weight_grad = jnp.einsum(
            "shrd,kshd->shrk", dout_grid, value_block, preferred_element_type=jnp.float32
        )
        score_grad = (probs_block * (weight_grad - delta_rows[..., None])).astype(jnp.bfloat16)
        query_carry = query_carry + jnp.einsum(
            "shrk,kshd->shrd", score_grad, key_block, preferred_element_type=jnp.float32
        )
        key_grad = (
            jnp.einsum(
                "shrk,shrd->kshd", score_grad, query_grid, preferred_element_type=jnp.float32
            )
            * score_scale
        )
        return (query_carry, (key_grad, value_grad))

    query_acc, (key_blocks, value_blocks) = lax.scan(
        back_pass, jnp.zeros_like(start_out), jnp.arange(blocks, dtype=jnp.int32)
    )
    key_grads_all = key_blocks.reshape(full_len, seq_count, kv_local * head_size)
    value_grads_all = value_blocks.reshape(full_len, seq_count, kv_local * head_size)
    key_share, value_share = (
        lax.psum_scatter(key_grads_all, "col", scatter_dimension=0, tiled=True),
        lax.psum_scatter(value_grads_all, "col", scatter_dimension=0, tiled=True),
    )
    key_gradient_reduced = unrotate(
        key_share.reshape(local_len, seq_count, kv_local, head_size), cosine_lookup, sine_lookup
    )
    key_gradient_reduced = key_gradient_reduced.reshape(
        local_len, seq_count, kv_local * head_size
    ).astype(jnp.bfloat16)
    value_gradient_reduced = value_share.astype(jnp.bfloat16)
    query_flat = from_grid(query_acc * score_scale, query_group_width, local_len)
    query_gradient_reduced = unrotate(
        query_flat.reshape(local_len, seq_count, kv_local * query_group_width, head_size),
        cosine_lookup,
        sine_lookup,
    )
    query_gradient_reduced = query_gradient_reduced.reshape(
        local_len, seq_count, kv_local * query_group_width * head_size
    ).astype(jnp.bfloat16)
    grad_query = jnp.einsum(
        "tpi,tpa->ia", input_normalized, query_gradient_reduced, preferred_element_type=jnp.float32
    )
    key_gradient = jnp.einsum(
        "tpi,tpa->ia", input_normalized, key_gradient_reduced, preferred_element_type=jnp.float32
    )
    grad_value = jnp.einsum(
        "tpi,tpa->ia", input_normalized, value_gradient_reduced, preferred_element_type=jnp.float32
    )
    first_part = jnp.einsum(
        "yme,ze->ymz", query_gradient_reduced, query_gathered, preferred_element_type=jnp.float32
    )
    first_part = first_part + jnp.einsum(
        "yme,ze->ymz", key_gradient_reduced, key_gathered, preferred_element_type=jnp.float32
    )
    first_part = first_part + jnp.einsum(
        "yme,ze->ymz", value_gradient_reduced, value_gathered, preferred_element_type=jnp.float32
    )
    first_grad = lax.psum(first_part, "row")
    grad_gain_one = jnp.sum(first_grad * base_first, axis=(0, 1))
    scaled_one = first_grad * gain_one
    token_grad = (
        inv_first
        * (scaled_one - base_first * jnp.mean(scaled_one * base_first, axis=-1, keepdims=True))
        + middle_grad
    )
    (
        share_query,
        share_key,
        share_value,
        share_out,
        share_sgate,
        share_sup,
        share_sdown,
        share_router,
        share_gain_one,
        share_gain_two,
    ) = (
        lax.psum_scatter(grad_query, "col", scatter_dimension=0, tiled=True),
        lax.psum_scatter(key_gradient, "col", scatter_dimension=0, tiled=True),
        lax.psum_scatter(grad_value, "col", scatter_dimension=0, tiled=True),
        lax.psum_scatter(output_weight_gradient, "col", scatter_dimension=1, tiled=True),
        lax.psum_scatter(grad_sgate, "col", scatter_dimension=0, tiled=True),
        lax.psum_scatter(shared_up_gradient, "col", scatter_dimension=0, tiled=True),
        lax.psum_scatter(grad_sdown, "col", scatter_dimension=1, tiled=True),
        lax.psum_scatter(grad_router, "col", scatter_dimension=0, tiled=True),
        lax.psum_scatter(grad_gain_one, "col", scatter_dimension=0, tiled=True),
        lax.psum_scatter(grad_gain_two, "col", scatter_dimension=0, tiled=True),
    )
    return (
        block_out,
        token_grad,
        share_gain_one,
        share_query,
        share_key,
        share_value,
        share_out,
        share_gain_two,
        share_router,
        share_sgate,
        share_sup,
        share_sdown,
        grad_expert_gate,
        grad_expert_up,
        grad_expert_down,
    )


def solution(mesh):
    in_specs = (
        P("col", None, None),
        P("col", None),
        P("col", None, None),
        P("col"),
        P("col", "row"),
        P("col", "row"),
        P("col", "row"),
        P("row", "col"),
        P("col"),
        P("col", None),
        P("col", "row"),
        P("col", "row"),
        P("row", "col"),
        P("col", None, "row"),
        P("col", None, "row"),
        P("col", "row", None),
        P("col", None, "row"),
    )
    out_specs = (
        P("col", None, "row"),
        P("col", None, None),
        P("col"),
        P("col", "row"),
        P("col", "row"),
        P("col", "row"),
        P("row", "col"),
        P("col"),
        P("col", None),
        P("col", "row"),
        P("col", "row"),
        P("row", "col"),
        P("col", None, "row"),
        P("col", None, "row"),
        P("col", "row", None),
    )
    return jax.shard_map(
        on_device, mesh=mesh, in_specs=in_specs, out_specs=out_specs, check_vma=False
    )
```

profile of v0, /device:TPU:10, one launch (start us, length us, event | category | flops | bytes accessed | tf_op | source)
XLA Modules:
  0.0 2925.4 jit_solution(7455530494266139510)
XLA Ops:
  12.6 34.8 %all-reduce.7 = (bf16[2560]{0:T(1024)(128)(2,1)S(1)}, bf16[2560]{0:T(1024)(128)(2,1)S(1)}) all-reduce(bf16[2560]{0:T(1024)(128)(2,1)S(1)} %dynamic-update-slice, bf16[2560]{0:T(1024)(128)(2,1)S(1)} %dynamic-update-slice.1), channel_id=1, replica_groups=mesh['row'=4,'col'=8] {'col'}, use_global_device_ids=true, to_apply=%add.2 | all-reduce | flops 5120 | bytes 20480
  49.0 33.4 %all_gather.44 = bf16[2560,128]{1,0:T(8,128)(2,1)S(1)} all-gather(bf16[320,128]{1,0:T(8,128)(2,1)} %param.28), channel_id=1, replica_groups=mesh['row'=4,'col'=8] {'col'}, dimensions={0}, use_global_device_ids=true | all-gather | bytes 737280 | tf_op jit(solution)/shard_map/all_gather | solution.py:152
  84.0 31.0 %all_gather.45 = bf16[1024,2,128]{0,2,1:T(8,128)(2,1)S(1)} all-gather(bf16[128,2,128]{0,2,1:T(8,128)(2,1)S(1)} %pad_maximum_fusion.1), channel_id=1, replica_groups=mesh['row'=4,'col'=8] {'col'}, dimensions={0}, use_global_device_ids=true | all-gather | bytes 589824 | tf_op jit(solution)/shard_map/all_gather | solution.py:188
  131.1 33.1 %all_gather.47 = bf16[2560,128]{1,0:T(8,128)(2,1)S(1)} all-gather(bf16[320,128]{1,0:T(8,128)(2,1)S(1)} %copy-done.69), channel_id=1, replica_groups=mesh['row'=4,'col'=8] {'col'}, dimensions={0}, use_global_device_ids=true | all-gather | bytes 737280 | tf_op jit(solution)/shard_map/all_gather | solution.py:153
  165.7 31.4 %all_gather.48 = bf16[1024,2,128]{2,0,1:T(8,128)(2,1)S(1)} all-gather(bf16[128,2,128]{2,0,1:T(8,128)(2,1)S(1)} %convolution_convert_fusion), channel_id=1, replica_groups=mesh['row'=4,'col'=8] {'col'}, dimensions={0}, use_global_device_ids=true | all-gather | bytes 589824 | tf_op jit(solution)/shard_map/all_gather | solution.py:189
  236.8 52.4 %all-reduce.12.cloned.1.call-done = f32[128,2,2560]{2,0,1:T(8,128)} async-done(((f32[128,2,2560]{2,0,1:T(8,128)}), f32[128,2,2560]{2,0,1:T(8,128)}) %all-reduce.12.cloned.1.call-update) | async-done | bytes 2621456 | tf_op jit(solution)/shard_map/psum | solution.py:254
  315.9 244.1 %all-gather = bf16[8,320,16]{1,2,0:T(8,128)(2,1)S(1)} all-gather(bf16[1,320,16]{1,2,0:T(8,128)(2,1)S(1)} %bitcast.476), channel_id=1, replica_groups=mesh['row'=4,'col'=8] {'col'}, dimensions={0}, use_global_device_ids=true | all-gather | bytes 92160 | tf_op jit(solution)/shard_map/all_gather | solution.py:158
  579.3 18.4 mul.491
  610.6 23.8 gather_fusion.2
  663.5 199.6 %all-to-all-done.2 = bf16[8,2,128,2560]{3,2,1,0:T(8,128)(2,1)} async-done(((bf16[8,2,128,2560]{3,2,1,0:T(8,128)(2,1)}), bf16[8,2,128,2560]{3,2,1,0:T(8,128)(2,1)}, u32[]{:S(2)}, u32[]{:S(2)}) %all-to-all-start.2) | async-done | bytes 10485792 | tf_op jit(solution)/shard_map/all_to_all | solution.py:333
  903.5 22.4 add_bitcast_fusion
  925.9 17.3 copy.316
  952.8 88.0 %reduce-scatter.15.cloned.1.call-done = f32[8,2,128,640]{3,2,0,1:T(8,128)} async-done(((f32[8,2,128,2560]{3,2,0,1:T(8,128)}), f32[8,2,128,640]{3,2,0,1:T(8,128)}) %reduce-scatter.15.cloned.1.call-update) | async-done | bytes 5242896 | tf_op jit(solution)/shard_map/reduce_scatter | solution.py:309
  1045.4 419.5 %all-to-all-done.3 = f32[8,2,128,2560]{3,2,1,0:T(8,128)} async-done(((f32[8,2,128,2560]{3,2,1,0:T(8,128)}), f32[8,2,128,2560]{3,2,1,0:T(8,128)}, u32[]{:S(2)}, u32[]{:S(2)}) %all-to-all-start.3) | async-done | bytes 20971552 | tf_op jit(solution)/shard_map/all_to_all | solution.py:383
  1477.3 69.1 %all-gather.12.cloned.1.call-done = bf16[2560,768]{1,0:T(8,128)(2,1)} async-done(((bf16[320,768]{1,0:T(8,128)(2,1)}), bf16[2560,768]{1,0:T(8,128)(2,1)}) %all-gather.12.cloned.1.call-update) | async-done | bytes 3932176 | tf_op jit(solution)/shard_map/all_gather | solution.py:155
  1551.0 69.8 %all-gather.16.cloned.1.call-done = bf16[768,2560]{0,1:T(8,128)(2,1)} async-done(((bf16[768,320]{0,1:T(8,128)(2,1)}), bf16[768,2560]{0,1:T(8,128)(2,1)}) %all-gather.16.cloned.1.call-update) | async-done | bytes 3932176 | tf_op jit(solution)/shard_map/all_gather | solution.py:157
  1629.0 22.3 gather_fusion.3
  1651.3 17.7 reshape.676
  1724.8 27.3 all-reduce.14.cloned.1.call-done
  1761.1 41.7 %while.49 = (s32[]{:T(128)}, f32[2,1,640,128]{3,2,0,1:T(8,128)}, f32[2,512,2,1,128]{1,0,4,2,3:T(2,128)}, f32[2,512,2,1,128]{4,1,0,2,3:T(8,128)}, s32[2]{0:T(128)...) while((s32[]{:T(128)}, f32[2,1,640,128]{3,2,0,1:T(8,128)}, ...), condition=%wide.region_31.32_spmd.clone, body=%wide.region_30.31_spmd.clone.sunk | while | flops 845545984 | bytes 40093196 | solution.py:452
  1820.0 50.8 %reduce-scatter.19.cloned.1.call-done = f32[128,2,128]{0,2,1:T(8,128)} async-done(((f32[1024,2,128]{0,2,1:T(8,128)}), f32[128,2,128]{0,2,1:T(8,128)}) %reduce-scatter.19.cloned.1.call-update) | async-done | bytes 131088 | tf_op jit(solution)/shard_map/reduce_scatter | solution.py:458
  1875.5 61.2 %reduce-scatter.21.cloned.1.call-done = f32[128,2,128]{2,0,1:T(8,128)} async-done(((f32[1024,2,128]{2,0,1:T(8,128)}), f32[128,2,128]{2,0,1:T(8,128)}) %reduce-scatter.21.cloned.1.call-update) | async-done | bytes 131088 | tf_op jit(solution)/shard_map/reduce_scatter | solution.py:459
  2010.1 31.2 %reduce-scatter.37.cloned.1.call-done = f32[320,16]{1,0:T(8,128)} async-done(((f32[2560,16]{1,0:T(8,128)}), f32[320,16]{1,0:T(8,128)}) %reduce-scatter.37.cloned.1.call-update) | async-done | bytes 20496
  2042.9 59.0 %all-reduce.16.cloned.1.call-done = f32[128,2,2560]{2,0,1:T(8,128)} async-done(((f32[128,2,2560]{2,0,1:T(8,128)}), f32[128,2,2560]{2,0,1:T(8,128)}) %all-reduce.16.cloned.1.call-update) | async-done | bytes 2621456 | tf_op jit(solution)/shard_map/psum | solution.py:495
  2104.7 35.9 %all-reduce.6 = (f32[2560]{0:T(1024)S(1)}, f32[2560]{0:T(1024)S(1)}) all-reduce(f32[2560]{0:T(1024)S(1)} %get-tuple-element.815, f32[2560]{0:T(1024)S(1)} %copy-done.75), channel_id=6, replica_groups=mesh['row'=4,'col'=8] {'col'}, use_global_device_ids=true, to_apply=%region_37.38.clone | all-reduce | flops 5120 | bytes 40960
  2148.3 98.5 %reduce-scatter.31.cloned.1.call-done = f32[320,768]{1,0:T(8,128)} async-done(((f32[2560,768]{1,0:T(8,128)}), f32[320,768]{1,0:T(8,128)}) %reduce-scatter.31.cloned.1.call-update) | async-done | bytes 983056 | tf_op jit(solution)/shard_map/reduce_scatter | solution.py:519
  2246.8 143.2 %reduce-scatter.33.cloned.1.call-done = f32[320,768]{1,0:T(8,128)} async-done(((f32[2560,768]{1,0:T(8,128)}), f32[320,768]{1,0:T(8,128)}) %reduce-scatter.33.cloned.1.call-update) | async-done | bytes 983056 | tf_op jit(solution)/shard_map/reduce_scatter | solution.py:520
  2390.0 143.2 %reduce-scatter.35.cloned.1.call-done = f32[768,320]{0,1:T(8,128)} async-done(((f32[768,2560]{0,1:T(8,128)}), f32[768,320]{0,1:T(8,128)}) %reduce-scatter.35.cloned.1.call-update) | async-done | bytes 983056 | tf_op jit(solution)/shard_map/reduce_scatter | solution.py:521
  2533.2 68.1 %reduce-scatter.25.cloned.1.call-done = f32[320,128]{1,0:T(8,128)} async-done(((f32[2560,128]{1,0:T(8,128)}), f32[320,128]{1,0:T(8,128)}) %reduce-scatter.25.cloned.1.call-update) | async-done | bytes 163856 | tf_op jit(solution)/shard_map/reduce_scatter | solution.py:516
  2601.3 67.3 %reduce-scatter.27.cloned.1.call-done = f32[320,128]{1,0:T(8,128)} async-done(((f32[2560,128]{1,0:T(8,128)}), f32[320,128]{1,0:T(8,128)}) %reduce-scatter.27.cloned.1.call-update) | async-done | bytes 163856 | tf_op jit(solution)/shard_map/reduce_scatter | solution.py:517
  2668.6 124.2 %reduce-scatter.23.cloned.1.call-done = f32[320,640]{1,0:T(8,128)} async-done(((f32[2560,640]{1,0:T(8,128)}), f32[320,640]{1,0:T(8,128)}) %reduce-scatter.23.cloned.1.call-update) | async-done | bytes 819216 | tf_op jit(solution)/shard_map/reduce_scatter | solution.py:515
  2792.7 125.4 %reduce-scatter.29.cloned.1.call-done = f32[640,320]{0,1:T(8,128)} async-done(((f32[640,2560]{0,1:T(8,128)}), f32[640,320]{0,1:T(8,128)}) %reduce-scatter.29.cloned.1.call-update) | async-done | bytes 819216 | tf_op jit(solution)/shard_map/reduce_scatter | solution.py:518
  (468 shorter events, 462.6 us)
Async XLA Ops:
  7.2 190.1 %all-gather.8.cloned.1.call-start = ((), (), s32[]{:S(2)}) async-start(), calls=%async_computation.16 | async-start | bytes 3686400 | tf_op jit(solution)/shard_map/all_gather | solution.py:151
  7.9 215.1 %all-gather.10.cloned.1.call-start = ((), (), s32[]{:S(2)}) async-start(), calls=%async_computation.17 | async-start | bytes 3686400 | tf_op jit(solution)/shard_map/all_gather | solution.py:154
  8.7 280.5 %all-reduce.12.cloned.1.call-start = ((), (), s32[]{:S(2)}) async-start(), calls=%async_computation.18 | async-start | bytes 5242880 | tf_op jit(solution)/shard_map/psum | solution.py:254
  47.3 150.0 %copy-start.58 = (f32[2560]{0:T(1024)}, f32[2560]{0:T(1024)S(1)}, u32[]{:S(2)}) copy-start(f32[2560]{0:T(1024)S(1)} %convert_element_type.161) | copy-start | bytes 30724
  49.0 148.3 %copy-start.78 = (f32[128,2]{0,1:T(2,128)}, f32[128,2]{0,1:T(2,128)S(1)}, u32[]{:S(2)}) copy-start(f32[128,2]{0,1:T(2,128)S(1)} %add_rsqrt_fusion.1) | copy-start | bytes 3076
  83.3 117.5 %copy-start.47 = (f32[128,64]{0,1:T(8,128)}, f32[128,64]{0,1:T(8,128)S(1)}, u32[]{:S(2)}) copy-start(f32[128,64]{0,1:T(8,128)S(1)} %get-tuple-element.908) | copy-start | bytes 98308
  293.1 304.6 %copy-start.2 = (bf16[128,2,2560]{2,0,1:T(8,128)(2,1)}, bf16[128,2,2560]{2,0,1:T(8,128)(2,1)S(1)}, u32[]{:S(2)}) copy-start(bf16[128,2,2560]{2,0,1:T(8,128)(2,1)S(1)} %multiply_convert_fusion.1) | copy-start | bytes 3932164
  308.8 325.6 %all-to-all-start = ((bf16[8,2,128,2560]{3,2,1,0:T(8,128)(2,1)}), bf16[8,2,128,2560]{3,2,1,0:T(8,128)(2,1)}, u32[]{:S(2)}, u32[]{:S(2)}) async-start(bf16[8,2,128,2560]{3,2,1,0:T(8,128)(2,1)} %bitcast.447), calls=%async_computation | async-start | bytes 20971520 | tf_op jit(solution)/shard_map/all_to_all | solution.py:287
  315.0 245.2 %all-gather.18.cloned.1.call-start = ((), (), s32[]{:S(2)}) async-start(), calls=%async_computation.24 | async-start | bytes 3276800 | tf_op jit(solution)/shard_map/all_gather | solution.py:320
  634.4 228.7 %all-to-all-start.2 = ((bf16[8,2,128,2560]{3,2,1,0:T(8,128)(2,1)}), bf16[8,2,128,2560]{3,2,1,0:T(8,128)(2,1)}, u32[]{:S(2)}, u32[]{:S(2)}) async-start(bf16[8,2,128,2560]{3,2,1,0:T(8,128)(2,1)} %bitcast.448), calls=%async_computation.4 | async-start | bytes 20971520 | tf_op jit(solution)/shard_map/all_to_all | solution.py:333
  642.7 398.1 %reduce-scatter.15.cloned.1.call-start = ((), (), s32[]{:S(2)}) async-start(), calls=%async_computation.19 | async-start | bytes 26214400 | tf_op jit(solution)/shard_map/reduce_scatter | solution.py:309
  943.1 521.7 %all-to-all-start.3 = ((f32[8,2,128,2560]{3,2,1,0:T(8,128)}), f32[8,2,128,2560]{3,2,1,0:T(8,128)}, u32[]{:S(2)}, u32[]{:S(2)}) async-start(f32[8,2,128,2560]{3,2,1,0:T(8,128)} %copy.316), calls=%async_computation.5 | async-start | bytes 41943040 | tf_op jit(solution)/shard_map/all_to_all | solution.py:383
  950.7 522.0 %all-gather.14.cloned.1.call-start = ((), (), s32[]{:S(2)}) async-start(), calls=%async_computation.21 | async-start | bytes 4423680 | tf_op jit(solution)/shard_map/all_gather | solution.py:156
  951.3 595.1 %all-gather.12.cloned.1.call-start = ((), (), s32[]{:S(2)}) async-start(), calls=%async_computation.20 | async-start | bytes 4423680 | tf_op jit(solution)/shard_map/all_gather | solution.py:155
  952.0 668.7 %all-gather.16.cloned.1.call-start = ((), (), s32[]{:S(2)}) async-start(), calls=%async_computation.22 | async-start | bytes 4423680 | tf_op jit(solution)/shard_map/all_gather | solution.py:157
  1045.4 425.6 %copy-start.31 = (f32[128,2,640]{2,1,0:T(2,128)S(1)}, f32[128,2,640]{2,1,0:T(2,128)}, u32[]{:S(2)}) copy-start(f32[128,2,640]{2,1,0:T(2,128)} %param.39) | copy-start | bytes 1966084
  1045.4 426.9 %copy-start.44 = (s32[128,2,6]{2,1,0:T(2,128)S(1)}, s32[128,2,6]{2,1,0:T(2,128)}, u32[]{:S(2)}) copy-start(s32[128,2,6]{2,1,0:T(2,128)} %copy-done.43) | copy-start | bytes 18436
  1045.4 427.0 %copy-start.73 = (s32[256,6]{0,1:T(8,128)S(1)}, s32[256,6]{0,1:T(8,128)}, u32[]{:S(2)}) copy-start(s32[256,6]{0,1:T(8,128)} %copy-done.72) | copy-start | bytes 18436
  1464.9 229.1 %all-to-all-start.1 = ((bf16[8,2,128,640]{3,2,1,0:T(8,128)(2,1)}), bf16[8,2,128,640]{3,2,1,0:T(8,128)(2,1)S(1)}, u32[]{:S(2)}, u32[]{:S(2)}) async-start(bf16[8,2,128,640]{3,2,1,0:T(8,128)(2,1)} %copy.307), calls=%async_computation.2 | async-start | bytes 5242880 | tf_op jit(solution)/shard_map/all_to_all | solution.py:313
  1471.0 281.2 %all-reduce.14.cloned.1.call-start = ((), (), s32[]{:S(2)}) async-start(), calls=%async_computation.25 | async-start | bytes 5242880 | tf_op jit(solution)/shard_map/psum | solution.py:392
  1692.3 178.4 %reduce-scatter.19.cloned.1.call-start = ((), (), s32[]{:S(2)}) async-start(), calls=%async_computation.26 | async-start | bytes 1179648 | tf_op jit(solution)/shard_map/reduce_scatter | solution.py:458
  1806.0 130.7 %reduce-scatter.21.cloned.1.call-start = ((), (), s32[]{:S(2)}) async-start(), calls=%async_computation.27 | async-start | bytes 1179648 | tf_op jit(solution)/shard_map/reduce_scatter | solution.py:459
  1806.8 200.8 %reduce-scatter.17.cloned.1.call-start = ((), (), s32[]{:S(2)}) async-start(), calls=%async_computation.23 | async-start | bytes 3276800 | tf_op jit(solution)/shard_map/reduce_scatter | solution.py:310
  1811.7 229.6 %reduce-scatter.37.cloned.1.call-start = ((), (), s32[]{:S(2)}) async-start(), calls=%async_computation.36 | async-start | bytes 1474560
  1815.0 286.9 %all-reduce.16.cloned.1.call-start = ((), (), s32[]{:S(2)}) async-start(), calls=%async_computation.28 | async-start | bytes 5242880 | tf_op jit(solution)/shard_map/psum | solution.py:495
  1940.7 306.1 %reduce-scatter.31.cloned.1.call-start = ((), (), s32[]{:S(2)}) async-start(), calls=%async_computation.33 | async-start | bytes 8847360 | tf_op jit(solution)/shard_map/reduce_scatter | solution.py:519
  1946.0 443.9 %reduce-scatter.33.cloned.1.call-start = ((), (), s32[]{:S(2)}) async-start(), calls=%async_computation.34 | async-start | bytes 8847360 | tf_op jit(solution)/shard_map/reduce_scatter | solution.py:520
  1951.5 581.7 %reduce-scatter.35.cloned.1.call-start = ((), (), s32[]{:S(2)}) async-start(), calls=%async_computation.35 | async-start | bytes 8847360 | tf_op jit(solution)/shard_map/reduce_scatter | solution.py:521
  1957.5 643.8 %reduce-scatter.25.cloned.1.call-start = ((), (), s32[]{:S(2)}) async-start(), calls=%async_computation.30 | async-start | bytes 1474560 | tf_op jit(solution)/shard_map/reduce_scatter | solution.py:516
  1960.5 708.0 %reduce-scatter.27.cloned.1.call-start = ((), (), s32[]{:S(2)}) async-start(), calls=%async_computation.31 | async-start | bytes 1474560 | tf_op jit(solution)/shard_map/reduce_scatter | solution.py:517
  1962.4 830.4 %reduce-scatter.23.cloned.1.call-start = ((), (), s32[]{:S(2)}) async-start(), calls=%async_computation.29 | async-start | bytes 7372800 | tf_op jit(solution)/shard_map/reduce_scatter | solution.py:515
  1966.6 951.6 %reduce-scatter.29.cloned.1.call-start = ((), (), s32[]{:S(2)}) async-start(), calls=%async_computation.32 | async-start | bytes 7372800 | tf_op jit(solution)/shard_map/reduce_scatter | solution.py:518
  (90 other events, 1520.3 us)
Sparse Core Ops, SparseCore 0:
  10.2 73.8 all-gather.7
  86.3 75.7 all-gather.9
  228.6 60.5 all-reduce.11
  317.6 25.4 all-gather.17
  887.5 153.2 reduce-scatter.14
  1043.1 308.2 all-gather.13
  1353.8 192.4 all-gather.11
  1548.8 71.8 all-gather.15
  1692.5 59.6 all-reduce.13
  1806.1 64.6 reduce-scatter.18
  1874.2 62.5 reduce-scatter.20
  1939.9 32.8 reduce-scatter.16
  1976.2 65.0 reduce-scatter.36
  2043.5 58.3 all-reduce.15
  2105.9 140.8 reduce-scatter.30
  2250.9 139.0 reduce-scatter.32
  2394.0 139.0 reduce-scatter.34
  2537.0 64.2 reduce-scatter.24
  2605.3 63.2 reduce-scatter.26
  2672.6 120.1 reduce-scatter.22
  2797.4 120.7 reduce-scatter.28
where the time goes:
time: 2940 us; the launch traced here: 2930 us
  waiting for transfers between devices  1900 us (65%)
  blocking collectives  473 us (16%)
  matrix products  227 us (8%)
  local copies, waits for them, and re-layouts  226 us (8%)
  other arithmetic  48.8 us (2%)
    all_to_all x1, waiting for transfers between devices, on_device(): lax.all_to_all(rows_grad, 'col', split_axis=0, concat_axis=0, tiled=True)  420 us
    all_gather x1, blocking collectives, on_device(): lax.all_gather(w_router, 'col', axis=0, tiled=True)  244 us
    all_to_all x1, waiting for transfers between devices, on_device(): lax.all_to_all(grad_send, 'col', split_axis=0, concat_axis=0, tiled=True)  200 us
    reduce_scatter x1, waiting for transfers between devices, on_device(): lax.psum_scatter(grad_sdown, 'col', scatter_dimension=1, tiled=True)  143 us
    reduce_scatter x1, waiting for transfers between devices, on_device(): lax.psum_scatter(shared_up_gradient, 'col', scatter_dimension=0, tiled=True)  143 us
    reduce_scatter x1, waiting for transfers between devices, on_device(): lax.psum_scatter(output_weight_gradient, 'col', scatter_dimension=1, tile...  125 us
    reduce_scatter x1, waiting for transfers between devices, on_device(): lax.psum_scatter(grad_query, 'col', scatter_dimension=0, tiled=True)  124 us
    reduce_scatter x1, waiting for transfers between devices, on_device(): lax.psum_scatter(grad_sgate, 'col', scatter_dimension=0, tiled=True)  98.5 us
  transfers between devices with their start and end apart: 25, of which 18 were waited for; matrix products, arithmetic and copies ran while one was open for 13% of the time, Pallas kernels for 0%

commit v1 on v0

v1 whole, which is shorter than its diff:
```python
import functools
import math

import jax
import jax.numpy as jnp
from jax import lax
from jax.experimental import pallas as pl
from jax.experimental.pallas import tpu as pltpu
from jax.sharding import PartitionSpec as P

HEAD_DIM = 128
LANES = 128


norm_eps = 1e-05
rope_base = 500000.0
masked_score = -1e30

f32 = jnp.float32
bf16 = jnp.bfloat16
MESH = pl.DeviceIdType.MESH


def dot(form, left, right):
    return jnp.einsum(form, left, right, preferred_element_type=f32)


def rope_tables(start_place, local_len, head_size):
    places = (start_place + jnp.arange(local_len, dtype=jnp.int32)).astype(f32)
    frequency = jnp.power(
        rope_base, -jnp.arange(0, head_size, 2, dtype=jnp.int32).astype(f32) / head_size
    )
    angles = places[:, None] * frequency[None, :]
    return (jnp.cos(angles), jnp.sin(angles))


def rotate(field, cosine, sine):
    half = cosine.shape[1]
    parts = []
    for start in range(0, field.shape[1], 2 * half):
        front = field[:, start : start + half]
        back = field[:, start + half : start + 2 * half]
        parts.append(front * cosine - back * sine)
        parts.append(back * cosine + front * sine)
    return jnp.concatenate(parts, axis=1)


def rms_scale(values_in):
    return lax.rsqrt(jnp.mean(values_in * values_in, axis=-1, keepdims=True) + norm_eps)


def silu_parts(pre_gate):
    sigmoid_gate = jax.nn.sigmoid(pre_gate)
    silu_gate = pre_gate * sigmoid_gate
    slope_gate = sigmoid_gate * (1.0 + pre_gate * (1.0 - sigmoid_gate))
    return (silu_gate, slope_gate)


def gather_col(part):
    return lax.all_gather(part, "col", axis=0, tiled=False)


def scatter_col(blocks):
    flat = blocks.reshape(-1, blocks.shape[-1])
    return lax.psum_scatter(flat, "col", scatter_dimension=0, tiled=True)


def gather_all(part):
    got = lax.all_gather(part, ("col", "row"), axis=0, tiled=False)
    cols, rows = lax.axis_size("col"), lax.axis_size("row")
    got = got.reshape(cols, rows, *part.shape).transpose(0, 2, 1, 3)
    return got.reshape(cols, part.shape[0], rows * part.shape[1])


def scatter_all(blocks):
    flat = blocks.reshape(-1, blocks.shape[-1])
    part = lax.psum_scatter(flat, "row", scatter_dimension=1, tiled=True)
    return lax.psum_scatter(part, "col", scatter_dimension=0, tiled=True)


def swap_col(blocks):
    return lax.all_to_all(blocks, "col", split_axis=0, concat_axis=0, tiled=True)


class Net:
    def __init__(self, cols, send_sems, recv_sems):
        self.send_sems, self.recv_sems, self.used, self.sent = send_sems, recv_sems, 0, []
        self.cols, self.high_count = cols, cols // 2
        self.me = lax.axis_index("col")
        self.high, self.low = self.me // 2, self.me % 2
        self.row = lax.axis_index("row")
        self.outer, self.core = self.row // 2, self.row % 2

    def block(self, step, other=False):
        high = lax.rem(self.high + self.high_count - step, self.high_count)
        return 2 * high + (1 - self.low if other else self.low)

    def block_ahead(self, step, other=False):
        high = lax.rem(self.high + step, self.high_count)
        return 2 * high + (1 - self.low if other else self.low)

    def z_peer(self, step):
        return {"col": self.block_ahead(step)}

    def y_peer(self):
        return {"col": 2 * self.high + 1 - self.low}

    def x_peer(self):
        return {"row": 2 * (1 - self.outer) + self.core}

    def core_peer(self):
        return {"row": 2 * self.outer + 1 - self.core}

    def col_peer(self, step):
        return {"col": lax.rem(self.me + step, self.cols)}

    def greet(self, peers):
        barrier = pltpu.get_barrier_semaphore()
        for peer in peers:
            pl.semaphore_signal(barrier, inc=1, device_id=peer, device_id_type=MESH)
        pl.semaphore_wait(barrier, len(peers))

    def send(self, source, target, peer):
        copy = pltpu.make_async_remote_copy(
            src_ref=source,
            dst_ref=target,
            send_sem=self.send_sems.at[self.used],
            recv_sem=self.recv_sems.at[self.used],
            device_id=peer,
            device_id_type=MESH,
        )
        self.used += 1
        copy.start()
        self.sent.append(copy)
        return copy

    def finish(self):
        for copy in self.sent:
            copy.wait_send()


def col_peers(net):
    return [net.z_peer(step) for step in range(1, net.high_count)] + [net.y_peer()]


def row_peers(net):
    return [net.x_peer(), net.core_peer()]


def gather_kernel(cols, kinds, *refs):
    count = len(kinds)
    ins, outs = refs[:count], refs[count : 2 * count]
    send_sems, recv_sems, local_sems = refs[2 * count :]
    net = Net(cols, send_sems, recv_sems)
    swaps = "swap" in kinds
    if swaps:
        peers = [net.col_peer(step) for step in range(1, cols)]
    else:
        peers = col_peers(net)
    net.greet(peers + (row_peers(net) if "all" in kinds else []))

    def place(i, block):
        if kinds[i] == "all":
            part = ins[i].shape[1]
            return outs[i].at[block, :, pl.ds(pl.multiple_of(net.row * part, LANES), part)]
        return outs[i].at[block]

    def other_place(i, block):
        part = ins[i].shape[1]
        row = 2 * (1 - net.outer) + net.core
        return outs[i].at[block, :, pl.ds(pl.multiple_of(row * part, LANES), part)]

    locals_ = []
    steps = range(1, net.high_count)
    along_z, along_y, along_x, crossed = {}, {}, {}, []

    def spread(i, source, block, key):
        along_x[i, key] = net.send(source, place(i, block), net.x_peer())
        crossed.append(net.send(source, place(i, block), net.core_peer()))

    for i, kind in enumerate(kinds):
        own = ins[i].at[net.me] if kind == "swap" else ins[i]
        local = pltpu.make_async_copy(own, place(i, net.me), local_sems.at[i])
        local.start()
        locals_.append(local)
        if kind == "swap":
            for step in range(1, cols):
                block = lax.rem(net.me + step, cols)
                crossed.append(net.send(ins[i].at[block], outs[i].at[net.me], net.col_peer(step)))
            continue
        for step in reversed(steps):
            along_z[i, step] = net.send(ins[i], place(i, net.me), net.z_peer(step))
        along_y[i, 0] = net.send(ins[i], place(i, net.me), net.y_peer())
        if kind == "all":
            spread(i, ins[i], net.me, (0, False))
    for step in steps:
        for i, kind in enumerate(kinds):
            if kind == "swap":
                continue
            block = net.block(step)
            along_z[i, step].wait_recv()
            along_y[i, step] = net.send(place(i, block), place(i, block), net.y_peer())
            if kind == "all":
                spread(i, place(i, block), block, (step, False))
    for step in range(net.high_count):
        for i, kind in enumerate(kinds):
            if kind == "swap":
                continue
            block = net.block(step, True)
            along_y[i, step].wait_recv()
            if kind == "all":
                spread(i, place(i, block), block, (step, True))
    for other in (False, True):
        for step in range(net.high_count):
            for i, kind in enumerate(kinds):
                if kind == "all":
                    block = net.block(step, other)
                    along_x[i, (step, other)].wait_recv()
                    slot = other_place(i, block)
                    crossed.append(net.send(slot, slot, net.core_peer()))
    for copy in crossed:
        copy.wait_recv()
    for local in locals_:
        local.wait()
    net.finish()


def gather(cols, collective_id, *pairs):
    kinds = [kind for kind, _ in pairs]
    arrays = [array for _, array in pairs]
    copies = 0
    shapes = []
    for kind, array in pairs:
        if kind == "swap":
            shapes.append(jax.ShapeDtypeStruct(array.shape, array.dtype))
            copies += cols
        elif kind == "col":
            shapes.append(jax.ShapeDtypeStruct((cols, *array.shape), array.dtype))
            copies += cols
        else:
            rows = lax.axis_size("row")
            shape = (cols, array.shape[0], rows * array.shape[1])
            shapes.append(jax.ShapeDtypeStruct(shape, array.dtype))
            copies += 4 * cols
    return pl.pallas_call(
        functools.partial(gather_kernel, cols, kinds),
        out_shape=shapes,
        in_specs=[pl.BlockSpec(memory_space=pl.ANY)] * len(pairs),
        out_specs=[pl.BlockSpec(memory_space=pl.ANY)] * len(pairs),
        scratch_shapes=[
            pltpu.SemaphoreType.DMA((copies,)),
            pltpu.SemaphoreType.DMA((copies,)),
            pltpu.SemaphoreType.DMA((len(pairs),)),
        ],
        compiler_params=pltpu.CompilerParams(collective_id=collective_id, has_side_effects=True),
        name=f"gather_{collective_id}",
    )(*arrays)


def add_rows(target, terms):
    rows = target.shape[0]
    piece = 32 if rows % 32 == 0 else rows

    def body(index, carry):
        at = pl.ds(pl.multiple_of(index * piece, piece), piece)
        total = terms[0][at, :].astype(f32)
        for term in terms[1:]:
            total = total + term[at, :].astype(f32)
        target[at, :] = total.astype(target.dtype)
        return carry

    lax.fori_loop(0, rows // piece, body, 0)


def scatter_col_steps(net, part, from_y, to_y, from_z, to_z, out, ready):
    along_y, along_z = {}, {}
    order = [*range(1, net.high_count), 0]
    for step in order:
        block = net.block_ahead(step, True)
        ready(block)
        if to_y is None:
            source = part.at[block]
        else:
            source = to_y.at[step]
            add_rows(source, [part.at[block]])
        along_y[step] = net.send(source, from_y.at[step], net.y_peer())
    for step in order:
        block = net.block_ahead(step)
        ready(block)
        along_y[step].wait_recv()
        if step:
            add_rows(to_z.at[step - 1], [part.at[block], from_y.at[step]])
            along_z[step] = net.send(to_z.at[step - 1], from_z.at[step - 1], net.z_peer(step))
    for step in range(1, net.high_count):
        along_z[step].wait_recv()
    terms = [from_z.at[step - 1] for step in range(1, net.high_count)]
    add_rows(out, [part.at[net.me], from_y.at[0], *terms])


def scatter_col_kernel(cols, count, *refs):
    parts, outs, scratch = refs[:count], refs[count : 2 * count], refs[2 * count :]
    send_sems, recv_sems = scratch[-2:]
    net = Net(cols, send_sems, recv_sems)
    net.greet(col_peers(net))
    for i in range(count):
        from_y, from_z, to_z = scratch[3 * i : 3 * i + 3]
        scatter_col_steps(
            net, parts[i], from_y, None, from_z, to_z, outs[i], lambda block: None
        )
    net.finish()


def scatter_col_call(cols, collective_id, *parts):
    high_count = cols // 2
    scratch = []
    for part in parts:
        shape = part.shape[1:]
        scratch += [
            pltpu.VMEM((high_count, *shape), bf16),
            pltpu.VMEM((high_count - 1, *shape), bf16),
            pltpu.VMEM((high_count - 1, *shape), bf16),
        ]
    copies = cols * len(parts)
    return pl.pallas_call(
        functools.partial(scatter_col_kernel, cols, len(parts)),
        out_shape=[jax.ShapeDtypeStruct(part.shape[1:], f32) for part in parts],
        in_specs=[pl.BlockSpec(memory_space=pltpu.VMEM)] * len(parts),
        out_specs=[pl.BlockSpec(memory_space=pltpu.VMEM)] * len(parts),
        scratch_shapes=[
            *scratch,
            pltpu.SemaphoreType.DMA((copies,)),
            pltpu.SemaphoreType.DMA((copies,)),
        ],
        compiler_params=pltpu.CompilerParams(
            collective_id=collective_id, has_side_effects=True, vmem_limit_bytes=56 << 20
        ),
        name=f"scatter_col_{collective_id}",
    )(*parts)


def scatter_all_kernel(cols, spread_back, part, out, *scratch):
    if spread_back:
        kept, *scratch = scratch
    from_core, to_x, from_x, total, from_y, to_y, from_z, to_z, send_sems, recv_sems = scratch
    net = Net(cols, send_sems, recv_sems)
    net.greet(col_peers(net) + row_peers(net))
    width = total.shape[2]

    def features(row):
        return pl.ds(pl.multiple_of(row * width, LANES), width)

    order = [*range(1, net.high_count), 0]
    blocks = [net.block_ahead(step, True) for step in order]
    blocks += [net.block_ahead(step) for step in order]
    across, along_x = {}, {}
    for far in (1, 0):
        outer = 1 - net.outer if far else net.outer
        for j, block in enumerate(blocks):
            source = part.at[block, :, features(2 * outer + 1 - net.core)]
            across[j, far] = net.send(source, from_core.at[far, block], net.core_peer())
    for j, block in enumerate(blocks):
        across[j, 1].wait_recv()
        mine = part.at[block, :, features(2 * (1 - net.outer) + net.core)]
        add_rows(to_x.at[block], [mine, from_core.at[1, block]])
        along_x[j] = net.send(to_x.at[block], from_x.at[block], net.x_peer())
    at = iter(range(len(blocks)))

    def ready(block):
        j = next(at)
        across[j, 0].wait_recv()
        along_x[j].wait_recv()
        mine = part.at[block, :, features(net.row)]
        add_rows(total.at[block], [mine, from_core.at[0, block], from_x.at[block]])

    if not spread_back:
        scatter_col_steps(net, total, from_y, to_y, from_z, to_z, out, ready)
        net.finish()
        return
    scatter_col_steps(net, total, from_y, to_y, from_z, to_z, kept, ready)
    own, other = features(net.row), features(2 * (1 - net.outer) + net.core)
    out[:, own] = kept[...].astype(bf16)
    far = net.send(out.at[:, own], out.at[:, own], net.x_peer())
    near = net.send(out.at[:, own], out.at[:, own], net.core_peer())
    far.wait_recv()
    last = net.send(out.at[:, other], out.at[:, other], net.core_peer())
    near.wait_recv()
    last.wait_recv()
    net.finish()


def scatter_all_call(cols, collective_id, part, spread_back=False):
    high_count = cols // 2
    rows, width = part.shape[1], part.shape[2] // lax.axis_size("row")
    piece = (rows, width)
    copies = 4 * cols + 4
    out = jax.ShapeDtypeStruct(piece, f32)
    if spread_back:
        out = jax.ShapeDtypeStruct((rows, part.shape[2]), bf16)
    return pl.pallas_call(
        functools.partial(scatter_all_kernel, cols, spread_back),
        out_shape=out,
        in_specs=[pl.BlockSpec(memory_space=pltpu.VMEM)],
        out_specs=pl.BlockSpec(memory_space=pltpu.VMEM),
        scratch_shapes=[
            *([pltpu.VMEM(piece, f32)] if spread_back else []),
            pltpu.VMEM((2, cols, *piece), bf16),
            pltpu.VMEM((cols, *piece), bf16),
            pltpu.VMEM((cols, *piece), bf16),
            pltpu.VMEM((cols, *piece), f32),
            pltpu.VMEM((high_count, *piece), bf16),
            pltpu.VMEM((high_count, *piece), bf16),
            pltpu.VMEM((high_count - 1, *piece), bf16),
            pltpu.VMEM((high_count - 1, *piece), bf16),
            pltpu.SemaphoreType.DMA((copies,)),
            pltpu.SemaphoreType.DMA((copies,)),
        ],
        compiler_params=pltpu.CompilerParams(
            collective_id=collective_id, has_side_effects=True, vmem_limit_bytes=56 << 20
        ),
        name=f"scatter_all_{collective_id}",
    )(part)


def sum_row_kernel(part, out, from_core, to_x, from_x, send_sems, recv_sems):
    net = Net(2, send_sems, recv_sems)
    net.greet(row_peers(net))
    pieces = from_core.shape[0]
    rows = from_core.shape[1]

    def piece(core, i):
        start = (core * pieces + i) * rows
        return pl.ds(pl.multiple_of(start, rows), rows)

    across = [
        net.send(part.at[piece(1 - net.core, i)], from_core.at[i], net.core_peer())
        for i in range(pieces)
    ]
    along, back = [], []
    for i in range(pieces):
        across[i].wait_recv()
        add_rows(to_x.at[i], [part.at[piece(net.core, i)], from_core.at[i]])
        along.append(net.send(to_x.at[i], from_x.at[i], net.x_peer()))
    for i in range(pieces):
        along[i].wait_recv()
        mine = piece(net.core, i)
        add_rows(out.at[mine], [to_x.at[i], from_x.at[i]])
        back.append(net.send(out.at[mine], out.at[mine], net.core_peer()))
    for copy in back:
        copy.wait_recv()
    net.finish()


def sum_row_call(collective_id, part):
    pieces = 4
    rows = part.shape[0] // 2 // pieces
    piece = (pieces, rows, part.shape[1])
    return pl.pallas_call(
        sum_row_kernel,
        out_shape=jax.ShapeDtypeStruct(part.shape, bf16),
        in_specs=[pl.BlockSpec(memory_space=pltpu.VMEM)],
        out_specs=pl.BlockSpec(memory_space=pltpu.VMEM),
        scratch_shapes=[
            pltpu.VMEM(piece, bf16),
            pltpu.VMEM(piece, bf16),
            pltpu.VMEM(piece, bf16),
            pltpu.SemaphoreType.DMA((3 * pieces,)),
            pltpu.SemaphoreType.DMA((3 * pieces,)),
        ],
        compiler_params=pltpu.CompilerParams(
            collective_id=collective_id, has_side_effects=True, vmem_limit_bytes=32 << 20
        ),
        name=f"sum_row_{collective_id}",
    )(part)


def fits(cols, rows, width):
    return cols % 2 == 0 and cols * rows * width * 2 <= 12 << 20


def gather_parts(kernels, cols, collective_id, *pairs):
    if kernels:
        return gather(cols, collective_id, *pairs)
    ways = {"col": gather_col, "all": gather_all, "swap": swap_col}
    return [ways[kind](array) for kind, array in pairs]


def scatter_col_parts(kernels, cols, collective_id, *parts):
    if kernels:
        return scatter_col_call(cols, collective_id, *parts)
    return [scatter_col(part).astype(f32) for part in parts]


def scatter_all_part(kernels, cols, collective_id, part):
    if kernels:
        return scatter_all_call(cols, collective_id, part)
    return scatter_all(part).astype(f32)


def scatter_all_back(kernels, cols, collective_id, part):
    if kernels:
        return scatter_all_call(cols, collective_id, part, True)
    return lax.all_gather(scatter_all(part), "row", axis=1, tiled=True)


def sum_row(kernels, collective_id, part):
    if kernels:
        return sum_row_call(collective_id, part)
    return lax.psum(part, "row")


def on_device(
    tokens,
    segments,
    routes,
    attn_gain,
    query_matrix,
    key_matrix,
    value_matrix,
    attention_output_matrix,
    mlp_gain,
    w_router,
    shared_gate_matrix,
    shared_up_matrix,
    shared_down_matrix,
    expert_gate,
    expert_up,
    expert_down,
    cotangent,
):
    local_len, seqs, width = tokens.shape
    cols = lax.axis_size("col")
    col_index = lax.axis_index("col")
    rows_w = query_matrix.shape[0]
    full_len = local_len * cols
    size = HEAD_DIM
    q_width = query_matrix.shape[1]
    kv_width = key_matrix.shape[1]
    kv_local = kv_width // size
    group = q_width // kv_width
    row_width = cotangent.shape[2]
    toks = local_len * seqs
    top = routes.shape[2]
    experts = w_router.shape[1]
    exp_local = expert_gate.shape[0]
    hidden_local = expert_gate.shape[2]
    capacity = max(2, toks * top * 4 // (3 * experts))
    shared_part = shared_gate_matrix.shape[1] // cols
    scale = 1.0 / math.sqrt(size)
    kernels = fits(cols, toks, width)

    def seq_major(a):
        return jnp.swapaxes(a, 0, 1).reshape(toks, a.shape[2])

    misc = jnp.concatenate(
        [
            w_router,
            attn_gain[:, None],
            mlp_gain[:, None],
            jnp.zeros((rows_w, LANES - experts - 2), bf16),
        ],
        axis=1,
    )
    first_weights = jnp.concatenate([query_matrix, key_matrix, value_matrix, misc], axis=1)
    shared_weights = jnp.concatenate(
        [
            shared_gate_matrix.reshape(rows_w, cols, shared_part),
            shared_up_matrix.reshape(rows_w, cols, shared_part),
            shared_down_matrix.T.reshape(rows_w, cols, shared_part),
        ],
        axis=2,
    )
    first_weights, out_weights, shared_weights, grad_all = gather_parts(
        kernels,
        cols,
        0,
        ("col", first_weights),
        ("col", attention_output_matrix.T),
        ("swap", jnp.swapaxes(shared_weights, 0, 1)),
        ("all", seq_major(cotangent).astype(bf16)),
    )
    first_weights = first_weights.reshape(width, -1)
    out_weights = out_weights.reshape(width, q_width)
    shared_weights = shared_weights.reshape(width, 3 * shared_part)
    qkv_width = q_width + 2 * kv_width
    qkv_weights = first_weights[:, :qkv_width]
    router = first_weights[:, qkv_width : qkv_width + experts]
    gain_one = first_weights[:, qkv_width + experts].astype(f32)
    gain_two = first_weights[:, qkv_width + experts + 1].astype(f32)
    shared_in_weights = shared_weights[:, : 2 * shared_part]
    shared_down = shared_weights[:, 2 * shared_part :]


    x = seq_major(tokens).astype(f32)
    inv_first = rms_scale(x)
    base_first = x * inv_first
    h1 = (base_first * gain_one).astype(bf16)
    qkv = dot("tb,bk->tk", h1, qkv_weights)
    cosine, sine = rope_tables(col_index * local_len, local_len, size)
    cosine, sine = jnp.tile(cosine, (seqs, 1)), jnp.tile(sine, (seqs, 1))
    qk = rotate(qkv[:, : q_width + kv_width], cosine, sine).astype(bf16)
    value_low = qkv[:, q_width + kv_width :].astype(bf16)

    flat_routes = seq_major(routes)
    named = flat_routes[:, :, None] == jnp.arange(experts, dtype=jnp.int32)
    mask = jnp.any(named, axis=1)
    order = jnp.arange(toks, dtype=jnp.int32)
    upto = (order[None, :] <= order[:, None]).astype(bf16)
    rank = jnp.where(mask, dot("ij,je->ie", upto, mask.astype(bf16)), 0.0)

    doc = jnp.transpose(segments)
    side = jnp.concatenate(
        [
            rank.astype(bf16),
            doc.reshape(toks, 1).astype(bf16),
            jnp.zeros((toks, LANES - experts - 1), bf16),
        ],
        axis=1,
    )
    (kv_all,) = gather_parts(
        kernels, cols, 1, ("col", jnp.concatenate([qk[:, q_width:], value_low, side], axis=1))
    )
    rank_all = kv_all[:, :, 2 * kv_width : 2 * kv_width + experts]
    kv_seq = jnp.swapaxes(kv_all.reshape(cols, seqs, local_len, -1), 0, 1)
    kv_seq = kv_seq.reshape(seqs, full_len, -1)
    key_all = kv_seq[:, :, :kv_width].reshape(seqs, full_len, kv_local, size)
    value_all = kv_seq[:, :, kv_width : 2 * kv_width].reshape(seqs, full_len, kv_local, size)
    doc_all = kv_seq[:, :, 2 * kv_width + experts]

    def to_grid(flat):
        shaped = flat.reshape(seqs, local_len, kv_local, group, size)
        return shaped.transpose(0, 2, 3, 1, 4).reshape(seqs, kv_local, group * local_len, size)

    def from_grid(grid):
        shaped = grid.reshape(seqs, kv_local, group, local_len, size)
        return shaped.transpose(0, 3, 1, 2, 4).reshape(toks, q_width)

    query_grid = to_grid(qk[:, :q_width])
    place = col_index * local_len + jnp.arange(local_len, dtype=jnp.int32)
    same = doc.astype(bf16)[:, :, None] == doc_all[:, None, :]
    causal = jnp.arange(full_len, dtype=jnp.int32)[None, :] <= place[:, None]
    allowed = jnp.tile(same & causal[None], (1, group, 1))[:, None]
    scores = dot("shrd,skhd->shrk", query_grid, key_all) * scale
    scores = jnp.where(allowed, scores, masked_score)
    weights = jnp.exp(scores - jnp.max(scores, axis=-1, keepdims=True))
    weights = jnp.where(allowed, weights, 0.0)
    probs = (weights / jnp.sum(weights, axis=-1, keepdims=True)).astype(bf16)
    heads = from_grid(dot("shrk,skhd->shrd", probs, value_all)).astype(bf16)
    attn = sum_row(kernels, 2, dot("tk,bk->tb", heads, out_weights).astype(bf16))
    middle = x + attn.astype(f32)

    inv_second = rms_scale(middle)
    base_second = middle * inv_second
    h2 = (base_second * gain_two).astype(bf16)
    row_index = lax.axis_index("row")
    h2_slice = lax.dynamic_slice_in_dim(h2, row_index * row_width, row_width, 1)
    (h2_all,) = gather_parts(kernels, cols, 3, ("all", h2_slice))

    all_mask = (rank_all > 0).astype(f32)
    all_probs = jax.nn.softmax(dot("ctd,de->cte", h2_all, router), axis=-1)
    all_picked = all_probs * all_mask
    all_gate = all_picked / jnp.sum(all_picked, axis=-1, keepdims=True)
    own = col_index * exp_local
    own_gate = lax.dynamic_slice_in_dim(all_gate, own, exp_local, 2)
    own_rank = lax.dynamic_slice_in_dim(rank_all, own, exp_local, 2).astype(jnp.int32)
    slots = jnp.arange(1, capacity + 1, dtype=jnp.int32)
    pick = jnp.swapaxes(own_rank, 1, 2)[:, :, None, :] == slots[:, None]
    slot_gate = jnp.sum(
        jnp.where(pick, jnp.swapaxes(own_gate, 1, 2)[:, :, None, :], 0.0), axis=3
    )[..., None]
    pick_low = pick.astype(bf16).reshape(cols, exp_local * capacity, toks)
    slot_shape = (cols, exp_local, capacity, width)
    slot_rows = dot("cut,ctd->cud", pick_low, h2_all).astype(bf16).reshape(slot_shape)
    slot_grad = dot("cut,ctd->cud", pick_low, grad_all).astype(bf16).reshape(slot_shape)
    gate_pre = dot("necd,edf->necf", slot_rows, expert_gate)
    up_pre = dot("necd,edf->necf", slot_rows, expert_up)
    silu_gate, slope_gate = silu_parts(gate_pre)
    hidden = silu_gate * up_pre
    gated = (hidden * slot_gate).astype(bf16)
    slot_out = dot("necf,efd->necd", gated, expert_down).astype(bf16)
    hidden_grad = dot("necd,efd->necf", slot_grad, expert_down)
    slot_dots = jnp.sum(hidden * hidden_grad, axis=-1)
    hidden_grad = hidden_grad * slot_gate
    gate_grad = (hidden_grad * up_pre * slope_gate).astype(bf16)
    up_grad = (hidden_grad * silu_gate).astype(bf16)
    slot_back = dot("necf,edf->necd", gate_grad, expert_gate)
    slot_back = (slot_back + dot("necf,edf->necd", up_grad, expert_up)).astype(bf16)
    grad_expert_down = dot("necf,necd->efd", gated, slot_grad)
    grad_expert_gate = dot("necd,necf->edf", slot_rows, gate_grad)
    grad_expert_up = dot("necd,necf->edf", slot_rows, up_grad)
    pick_flat = pick_low.reshape(cols, exp_local * capacity, toks)
    slot_out = slot_out.reshape(cols, exp_local * capacity, width)
    slot_back = slot_back.reshape(cols, exp_local * capacity, width)

    shared_pre = dot("ctd,dk->ctk", h2_all, shared_in_weights)
    sgate_pre, sup_pre = shared_pre[:, :, :shared_part], shared_pre[:, :, shared_part:]
    shared_silu, shared_slope = silu_parts(sgate_pre)
    shared_hidden = (shared_silu * sup_pre).astype(bf16)
    part_out = dot("cut,cud->ctd", pick_flat, slot_out) + dot(
        "ctk,dk->ctd", shared_hidden, shared_down
    )
    shared_hgrad = dot("ctd,dk->ctk", grad_all, shared_down)
    shared_grads = jnp.concatenate(
        [shared_hgrad * sup_pre * shared_slope, shared_hgrad * shared_silu], axis=2
    ).astype(bf16)
    part_back = dot("cut,cud->ctd", pick_flat, slot_back) + dot(
        "ctk,dk->ctd", shared_grads, shared_in_weights
    )
    token_dots = jnp.einsum(
        "ceu,ceut->cte", slot_dots, pick.astype(f32), precision=lax.Precision.HIGHEST
    )
    gate_dots = lax.psum(swap_col(token_dots), "row")
    gate_dots = jnp.swapaxes(gate_dots, 0, 1).reshape(toks, experts)

    back_full = scatter_all_back(kernels, cols, 4, part_back.astype(bf16)).astype(f32)
    out_slice = scatter_all_part(kernels, cols, 5, part_out.astype(bf16))
    middle_slice = lax.dynamic_slice_in_dim(middle, row_index * row_width, row_width, 1)
    block_out = (middle_slice + out_slice).astype(bf16)

    shared_share = jnp.concatenate(
        [dot("ctd,ctk->dk", h2_all, shared_grads), dot("ctd,ctk->dk", grad_all, shared_hidden)],
        axis=1,
    ).astype(bf16)
    shared_share = swap_col(shared_share.reshape(cols, rows_w, 3 * shared_part))
    shared_share = jnp.swapaxes(shared_share, 0, 1).astype(f32)
    share_sgate, share_sup, share_sdown = (
        shared_share[:, :, i * shared_part : (i + 1) * shared_part].reshape(rows_w, -1)
        for i in range(3)
    )

    logits = dot("td,de->te", h2, router)
    probs_router = jax.nn.softmax(logits, axis=-1)
    picked = jnp.where(mask, probs_router, 0.0)
    pick_total = jnp.sum(picked, axis=-1, keepdims=True)
    gate = picked / pick_total
    pick_grad = gate_dots - jnp.sum(gate * gate_dots, axis=-1, keepdims=True)
    prob_grad = jnp.where(mask, pick_grad / pick_total, 0.0)
    logit_grad = probs_router * (
        prob_grad - jnp.sum(probs_router * prob_grad, axis=-1, keepdims=True)
    )
    logit_low = logit_grad.astype(bf16)
    grad_router = dot("td,te->de", h2, logit_low)

    back_full = back_full + dot("te,de->td", logit_low, router)
    grad_own = lax.dynamic_slice_in_dim(grad_all, col_index, 1, 0)[0].astype(f32)
    grad_gain_two = jnp.sum(back_full * base_second, axis=0)
    scaled_two = back_full * gain_two
    middle_grad = (
        inv_second
        * (scaled_two - base_second * jnp.mean(scaled_two * base_second, axis=-1, keepdims=True))
        + grad_own
    )
    attn_grad = middle_grad.astype(bf16)
    grad_out = dot("td,tk->dk", attn_grad, heads).astype(bf16)

    heads_grad = to_grid(dot("td,dk->tk", attn_grad, out_weights).astype(bf16))
    value_grad = dot("shrk,shrd->skhd", probs, heads_grad)
    weight_grad = dot("shrd,skhd->shrk", heads_grad, value_all)
    probs_wide = probs.astype(f32)
    delta = jnp.sum(probs_wide * weight_grad, axis=-1, keepdims=True)
    score_grad = (probs_wide * (weight_grad - delta)).astype(bf16)
    query_grad = from_grid(dot("shrk,skhd->shrd", score_grad, key_all)) * scale
    key_grad = dot("shrk,shrd->skhd", score_grad, query_grid) * scale
    kv_grad = jnp.concatenate(
        [key_grad.reshape(seqs, full_len, kv_width), value_grad.reshape(seqs, full_len, kv_width)],
        axis=2,
    ).astype(bf16)
    kv_grad = jnp.swapaxes(kv_grad.reshape(seqs, cols, local_len, 2 * kv_width), 0, 1)
    (kv_share,) = scatter_col_parts(kernels, cols, 6, kv_grad.reshape(cols, toks, 2 * kv_width))
    qk_grad = rotate(
        jnp.concatenate([query_grad, kv_share[:, :kv_width]], axis=1), cosine, -sine
    )
    qkv_grad = jnp.concatenate([qk_grad, kv_share[:, kv_width:]], axis=1).astype(bf16)
    first_grad = dot("tk,bk->tb", qkv_grad, qkv_weights).astype(bf16)
    first_grad = sum_row(kernels, 7, first_grad).astype(f32)
    grad_gain_one = jnp.sum(first_grad * base_first, axis=0)
    scaled_one = first_grad * gain_one
    token_grad = (
        inv_first
        * (scaled_one - base_first * jnp.mean(scaled_one * base_first, axis=-1, keepdims=True))
        + middle_grad
    )
    grad_first = jnp.concatenate(
        [
            dot("tb,tk->bk", h1, qkv_grad),
            grad_router,
            grad_gain_one[:, None],
            grad_gain_two[:, None],
            jnp.zeros((width, LANES - experts - 2), f32),
        ],
        axis=1,
    ).astype(bf16)
    share_out, share_first = scatter_col_parts(
        kernels,
        cols,
        8,
        grad_out.reshape(cols, rows_w, q_width),
        grad_first.reshape(cols, rows_w, -1),
    )

    def tokens_first(a):
        return jnp.swapaxes(a.reshape(seqs, local_len, a.shape[1]), 0, 1)

    return (
        tokens_first(block_out),
        tokens_first(token_grad),
        share_first[:, qkv_width + experts],
        share_first[:, :q_width],
        share_first[:, q_width : q_width + kv_width],
        share_first[:, q_width + kv_width : qkv_width],
        share_out.T,
        share_first[:, qkv_width + experts + 1],
        share_first[:, qkv_width : qkv_width + experts],
        share_sgate,
        share_sup,
        share_sdown.T,
        grad_expert_gate,
        grad_expert_up,
        grad_expert_down,
    )


def solution(mesh):
    in_specs = (
        P("col", None, None),
        P("col", None),
        P("col", None, None),
        P("col"),
        P("col", "row"),
        P("col", "row"),
        P("col", "row"),
        P("row", "col"),
        P("col"),
        P("col", None),
        P("col", "row"),
        P("col", "row"),
        P("row", "col"),
        P("col", None, "row"),
        P("col", None, "row"),
        P("col", "row", None),
        P("col", None, "row"),
    )
    out_specs = (
        P("col", None, "row"),
        P("col", None, None),
        P("col"),
        P("col", "row"),
        P("col", "row"),
        P("col", "row"),
        P("row", "col"),
        P("col"),
        P("col", None),
        P("col", "row"),
        P("col", "row"),
        P("row", "col"),
        P("col", None, "row"),
        P("col", None, "row"),
        P("col", "row", None),
    )
    return jax.shard_map(
        on_device, mesh=mesh, in_specs=in_specs, out_specs=out_specs, check_vma=False
    )
```

time: 2940 us -> 1130 us (0.38)
  waiting for transfers between devices: 1900 us -> 0.01 us
  Pallas kernels: 0 us -> 711 us
  blocking collectives: 473 us -> 12.4 us
  local copies, waits for them, and re-layouts: 226 us -> 101 us
    reduce_scatter x11 -> x0, waiting for transfers between devices: 970 us -> none  [the longest x1 143 us: on_device(): lax.psum_scatter(grad_sdown, 'col', scatter_dimension=1, tiled=True)]
    pallas_call x0 -> x9, Pallas kernels: none -> 711 us  [the longest x3 357 us: gather(): pl.pallas_call(functools.partial(gather_kernel, cols, kinds), out_shape=s...]
    all_to_all x4 -> x2, waiting for transfers between devices: 619 us -> 0.01 us  [swap_col(): lax.all_to_all(blocks, 'col', split_axis=0, concat_axis=0, tiled=True)]
    all_gather x6 -> x0, blocking collectives: 388 us -> none  [the longest x1 244 us: on_device(): lax.all_gather(w_router, 'col', axis=0, tiled=True)]
    all_gather x6 -> x0, waiting for transfers between devices: 139 us -> none  [the longest x1 69.8 us: on_device(): lax.all_gather(shared_down_matrix, 'col', axis=1, tiled=True)]
    psum x3 -> x0, waiting for transfers between devices: 139 us -> none  [the longest x1 59 us: on_device(): first_grad = lax.psum(first_part, 'row')]
    gather x5 -> x0, local copies, waits for them, and re-layouts: 80.8 us -> none  [the longest x2 40 us: on_device(): rows_back.reshape(experts * capacity, back_width)[places]]
    unnamed x2 -> x0, blocking collectives: 70.6 us -> none
  transfers between devices with their start and end apart: 25 -> 2, of which waited for: 18 -> 0; matrix products, arithmetic and copies ran while one was open for 13% -> 21% of each run, Pallas kernels for 0% -> 30%
where the time goes in v1:
time: 1130 us; the launch traced here: 1120 us
  Pallas kernels  711 us (63%)
  matrix products  227 us (20%)
  local copies, waits for them, and re-layouts  101 us (9%)
  other arithmetic  52.7 us (5%)
  starting transfers between devices  15.4 us (1%)
  blocking collectives  12.4 us (1%)
    pallas_call x3, Pallas kernels, gather(): pl.pallas_call(functools.partial(gather_kernel, cols, kinds), out_shape=s...  357 us
    dot_general x36, matrix products, dot(): return jnp.einsum(form, left, right, preferred_element_type=f32)  226 us
    pallas_call x2, Pallas kernels, scatter_all_call(): pl.pallas_call(functools.partial(scatter_all_kernel, cols, spread_back),...  166 us
    pallas_call x2, Pallas kernels, scatter_col_call(): pl.pallas_call(functools.partial(scatter_col_kernel, cols, len(parts)), o...  149 us
    pallas_call x2, Pallas kernels, sum_row_call(): pl.pallas_call(sum_row_kernel, out_shape=jax.ShapeDtypeStruct(part.shape,...  39.2 us
  transfers between devices with their start and end apart: 2, of which 0 were waited for; matrix products, arithmetic and copies ran while one was open for 21% of the time, Pallas kernels for 30%

profile of v1, /device:TPU:10, one launch (start us, length us, event | category | flops | bytes accessed | tf_op | source)
XLA Modules:
  0.0 1122.8 jit_solution(131095088916860675)
XLA Ops:
  14.0 209.6 %gather_0.1 = (bf16[8,320,1024]{2,1,0:T(8,128)(2,1)}, bf16[8,320,640]{2,1,0:T(8,128)(2,1)}, bf16[8,320,288]{2,1,0:T(8,128)(2,1)}, bf16[8,256,2560]{2,1,0:T(8,128)(2,1)}) custom-call(bf16[320,1024]{1,0:T(8,128)(2,1)} %concatenate.53.refs_0_, bf16[320,640]{1,0:T(8,128)(2,1)} %bitcast.576, bf16[8,320,288]{2,1,0:T(8,128)(2,1)} %maximum_bitcast_fusion.refs_2_, ...), custom_call_target="tpu_custom_call" | custom-call | tf_op jit(solution)/shard_map/gather_0/pallas_call | solution.py:245
  242.2 66.5 %gather_1.1 = bf16[8,256,384]{2,1,0:T(8,128)(2,1)} custom-call(bf16[256,384]{1,0:T(8,128)(2,1)} %concatenate.55.refs_0_), custom_call_target="tpu_custom_call" | custom-call | tf_op jit(solution)/shard_map/gather_1/pallas_call | solution.py:245
  323.9 19.7 %sum_row_2.1 = bf16[256,2560]{1,0:T(8,128)(2,1)S(1)} custom-call(bf16[256,2560]{1,0:T(8,128)(2,1)S(1)} %convolution_convert_fusion.3.part), custom_call_target="tpu_custom_call" | custom-call | tf_op jit(solution)/shard_map/sum_row_2/pallas_call | solution.py:457
  349.6 80.7 %gather_3.1 = bf16[8,256,2560]{2,1,0:T(8,128)(2,1)} custom-call(bf16[256,640]{1,0:T(8,128)(2,1)} %constant_dynamic-slice_fusion.refs_0_), custom_call_target="tpu_custom_call" | custom-call | tf_op jit(solution)/shard_map/gather_3/pallas_call | solution.py:245
  430.3 7.0 fusion.153
  437.7 12.8 %fusion.154 = (f32[8,256]{1,0:T(8,128)S(1)}, f32[8,256,16]{2,1,0:T(8,128)S(1)}) fusion(f32[8,256,16]{2,1,0:T(8,128)S(1)} %copy.300, f32[8,256]{1,0:T(8,128)S(1)} %get-tuple-element.176, bf16[8,256,384]{2,1,0:T(8,128)(2,1)} %gather_1.1), kind=kOutput, calls=%fused_computation.290 | output fusion | flops 262159 | bytes 2318336 | tf_op jit(solution)/shard_map/div | solution.py:659
  465.5 9.8 convolution_convert_fusion.1
  475.3 10.4 fusion.6
  485.8 7.2 fusion.8
  493.0 9.8 convolution_convert_fusion
  502.8 12.2 %fusion.31 = (f32[8,2,128]{2,0,1:T(8,128)S(1)}, bf16[8,2,128,384]{3,2,0,1:T(8,128)(2,1)}, bf16[8,2,128,384]{3,2,0,1:T(8,128)(2,1)}, bf16[8,2,128,384]{3,2,0,1:T(8,128)(2,1)}) fusion(f32[2,8,128,384]{3,2,1,0:T(8,128)} %fusion.6, f32[2,8,128,384]{3,2,1,0:T(8,128)} %fusion.8, f32[8,2,128]{2,0,1:T(8,128)S(1)} %copy.301, ...), kind=kOutput, calls=%fused_computation.53 | convolution fusion | flops 4041472000 | bytes 25444352 | tf_op jit(solution)/shard_map/necd,efd->necf/dot_general | solution.py:25
  516.5 10.5 all-to-all-start
  528.6 8.0 fusion.54
  536.7 7.7 multiply_convert_fusion.5
  547.5 10.6 fusion.53
  558.1 11.5 %fusion.21 = f32[2,8,128,2560]{3,2,1,0:T(8,128)} fusion(bf16[8,2,128,384]{3,2,0,1:T(8,128)(2,1)} %get-tuple-element.113, bf16[2,2560,384]{2,1,0:T(8,128)(2,1)S(1)} %copy-done.18), kind=kOutput, calls=%fused_computation.34 | convolution fusion | flops 4026531840 | bytes 26476544 | tf_op jit(solution)/shard_map/necf,edf->necd/dot_general | solution.py:25
  569.7 9.6 convolution_bitcast_fusion.1
  586.1 10.5 convert_bitcast_fusion
  598.3 10.1 fusion.75
  613.1 12.5 %convolution_bitcast_fusion = f32[2,2560,384]{2,1,0:T(8,128)} fusion(bf16[8,2,128,2560]{3,2,1,0:T(8,128)(2,1)} %bitcast.518, bf16[8,2,128,384]{3,2,0,1:T(8,128)(2,1)} %get-tuple-element.115), kind=kOutput, calls=%fused_computation.21 | convolution fusion | flops 4026531840 | bytes 19922944 | tf_op jit(solution)/shard_map/necd,necf->edf/dot_general | solution.py:25
  625.6 13.4 %fusion.1 = bf16[8,2,128,2560]{3,2,0,1:T(8,128)(2,1)} fusion(f32[2,8,128,2560]{3,2,1,0:T(8,128)} %fusion.21, bf16[8,2,128,384]{3,2,0,1:T(8,128)(2,1)S(1)} %copy-done.29, bf16[2,2560,384]{2,1,0:T(8,128)(2,1)} %param.31), kind=kOutput, calls=%fused_computation.4 | convolution fusion | flops 4037017600 | bytes 36962304 | tf_op jit(solution)/shard_map/necf,edf->necd/dot_general | solution.py:25
  638.9 8.9 copy.308
  647.8 8.8 copy.302
  656.6 14.8 %add_convert_fusion.2.part = bf16[8,256,2560]{2,1,0:T(8,128)(2,1)} fusion(f32[8,256,2560]{2,1,0:T(8,128)} %fusion.75, pred[8,256,256]{1,2,0:T(32,128)(4,1)S(1)} %broadcast_compare_fusion.1, bf16[8,256,2560]{2,1,0:T(8,128)(2,1)} %bitcast.514), kind=kOutput, calls=%fused_computation.3 | convolution fusion | flops 2694840320 | bytes 42467328 | tf_op jit(solution)/shard_map/cut,cud->ctd/dot_general | solution.py:25
  671.4 78.9 %scatter_all_5.1 = f32[256,640]{1,0:T(8,128)} custom-call(bf16[8,256,2560]{2,1,0:T(8,128)(2,1)} %add_convert_fusion.2.part), custom_call_target="tpu_custom_call" | custom-call | tf_op jit(solution)/shard_map/scatter_all_5/pallas_call | solution.py:399
  753.9 14.6 %add_convert_fusion.part = bf16[8,256,2560]{2,1,0:T(8,128)(2,1)} fusion(f32[8,256,2560]{2,1,0:T(8,128)} %fusion.53, pred[8,256,256]{1,2,0:T(32,128)(4,1)S(1)} %broadcast_compare_fusion.1, bf16[8,256,2560]{2,1,0:T(8,128)(2,1)} %bitcast.513), kind=kOutput, calls=%fused_computation.1 | convolution fusion | flops 2694840320 | bytes 42467328 | tf_op jit(solution)/shard_map/cut,cud->ctd/dot_general | solution.py:25
  768.7 87.2 %scatter_all_4.1 = bf16[256,2560]{1,0:T(8,128)(2,1)} custom-call(bf16[8,256,2560]{2,1,0:T(8,128)(2,1)} %add_convert_fusion.part), custom_call_target="tpu_custom_call" | custom-call | tf_op jit(solution)/shard_map/scatter_all_4/pallas_call | solution.py:399
  864.5 12.4 %psum.7 = f32[256,16]{1,0:T(8,128)S(1)} all-reduce(f32[256,16]{1,0:T(8,128)S(1)} %copy.310), channel_id=1, replica_groups=mesh['row'=4,'col'=8] {'row'}, use_global_device_ids=true, to_apply=%region_12.13 | all-reduce | flops 4096 | bytes 32768 | tf_op jit(solution)/shard_map/psum | solution.py:711
  902.6 22.4 %scatter_col_6.1 = f32[256,256]{1,0:T(8,128)} custom-call(bf16[8,256,256]{2,1,0:T(8,128)(2,1)} %bitcast.540), custom_call_target="tpu_custom_call" | custom-call | tf_op jit(solution)/shard_map/scatter_col_6/pallas_call | solution.py:324
  932.6 19.5 %sum_row_7.1 = bf16[256,2560]{1,0:T(8,128)(2,1)S(1)} custom-call(bf16[256,2560]{1,0:T(8,128)(2,1)S(1)} %fusion.26.part), custom_call_target="tpu_custom_call" | custom-call | tf_op jit(solution)/shard_map/sum_row_7/pallas_call | solution.py:457
  962.1 9.9 concatenate.65.refs_1_
  976.8 127.0 %scatter_col_8.1 = (f32[320,640]{1,0:T(8,128)}, f32[320,1024]{1,0:T(8,128)}) custom-call(bf16[8,320,640]{2,1,0:T(8,128)(2,1)} %bitcast.527, bf16[8,320,1024]{2,1,0:T(8,128)(2,1)} %concatenate.65.refs_1_), custom_call_target="tpu_custom_call" | custom-call | tf_op jit(solution)/shard_map/scatter_col_8/pallas_call | solution.py:324
  (323 shorter events, 166.1 us)
Async XLA Ops:
  228.7 114.9 %copy-start = (f32[2,128,2560]{2,1,0:T(8,128)}, f32[2,128,2560]{2,1,0:T(8,128)S(1)}, u32[]{:S(2)}) copy-start(f32[2,128,2560]{2,1,0:T(8,128)S(1)} %copy.275) | copy-start | bytes 7864324
  240.2 72.8 %copy-start.21 = (bf16[2,1,5,128,128]{4,3,2,0,1:T(8,128)(2,1)}, bf16[2,1,5,128,128]{4,3,2,0,1:T(8,128)(2,1)S(1)}, u32[]{:S(2)}) copy-start(bf16[2,1,5,128,128]{4,3,2,0,1:T(8,128)(2,1)S(1)} %copy.293) | copy-start | bytes 983044
  437.7 12.8 %copy-start.25 = (bf16[8,256,16]{2,1,0:T(8,128)(2,1)S(1)}, bf16[8,256,16]{2,1,0:T(8,128)(2,1)}, u32[]{:S(2)}) copy-start(bf16[8,256,16]{2,1,0:T(8,128)(2,1)} %slice.181) | copy-start | bytes 196612
  502.8 12.2 %copy-start.33 = (pred[8,2,128,256]{2,1,3,0:T(4,128)(4,1)S(1)}, pred[8,2,128,256]{2,1,3,0:T(4,128)(4,1)}, u32[]{:S(2)}) copy-start(pred[8,2,128,256]{2,1,3,0:T(4,128)(4,1)} %get-tuple-element.109) | copy-start | bytes 1572868
  502.8 24.2 %copy-start.9 = (bf16[256,2560]{1,0:T(8,128)(2,1)S(1)}, bf16[256,2560]{1,0:T(8,128)(2,1)}, u32[]{:S(2)}) copy-start(bf16[256,2560]{1,0:T(8,128)(2,1)} %copy-done.8) | copy-start | bytes 3932164
  516.5 343.0 %all-to-all-start = ((f32[8,256,2]{1,2,0:T(2,128)}), f32[8,256,2]{1,2,0:T(2,128)S(1)}, u32[]{:S(2)}, u32[]{:S(2)}) async-start(f32[8,256,2]{1,2,0:T(2,128)} %bitcast.506), calls=%async_computation | async-start | bytes 32768 | tf_op jit(solution)/shard_map/all_to_all | solution.py:82
  528.6 15.7 %slice-start = ((s8[10485760]{0:T(1024)(128)(4,1)}), s8[4194304]{0:T(1024)(128)(4,1)S(1)}, s32[]{:S(2)}) async-start(s8[10485760]{0:T(1024)(128)(4,1)} %bitcast.509), calls=%async_computation.2 | async-start | bytes 8388608
  528.6 15.7 %slice-start.1 = ((s8[10485760]{0:T(1024)(128)(4,1)}), s8[4194304]{0:T(1024)(128)(4,1)S(1)}, s32[]{:S(2)}) async-start(s8[10485760]{0:T(1024)(128)(4,1)} %bitcast.509), calls=%async_computation.3 | async-start | bytes 8388608
  547.5 10.6 copy-start.18
  547.5 22.2 %slice-start.8 = ((s8[10485760]{0:T(1024)(128)(4,1)}), s8[4194304]{0:T(1024)(128)(4,1)S(1)}, s32[]{:S(2)}) async-start(s8[10485760]{0:T(1024)(128)(4,1)} %bitcast.520), calls=%async_computation.10 | async-start | bytes 8388608
  547.5 22.2 %slice-start.9 = ((s8[10485760]{0:T(1024)(128)(4,1)}), s8[4194304]{0:T(1024)(128)(4,1)S(1)}, s32[]{:S(2)}) async-start(s8[10485760]{0:T(1024)(128)(4,1)} %bitcast.520), calls=%async_computation.11 | async-start | bytes 8388608
  558.1 11.6 %slice-start.10 = ((s8[10485760]{0:T(1024)(128)(4,1)}), s8[2097152]{0:T(1024)(128)(4,1)S(1)}, s32[]{:S(2)}) async-start(s8[10485760]{0:T(1024)(128)(4,1)} %bitcast.520), calls=%async_computation.12 | async-start | bytes 4194304
  558.1 21.2 %slice-start.11 = ((s8[10485760]{0:T(1024)(128)(4,1)}), s8[4194304]{0:T(1024)(128)(4,1)S(1)}, s32[]{:S(2)}) async-start(s8[10485760]{0:T(1024)(128)(4,1)} %bitcast.524), calls=%async_computation.13 | async-start | bytes 8388608
  558.1 21.2 %slice-start.12 = ((s8[10485760]{0:T(1024)(128)(4,1)}), s8[4194304]{0:T(1024)(128)(4,1)S(1)}, s32[]{:S(2)}) async-start(s8[10485760]{0:T(1024)(128)(4,1)} %bitcast.524), calls=%async_computation.14 | async-start | bytes 8388608
  579.4 17.2 %slice-start.3 = ((s8[10485760]{0:T(1024)(128)(4,1)}), s8[2097152]{0:T(1024)(128)(4,1)S(1)}, s32[]{:S(2)}) async-start(s8[10485760]{0:T(1024)(128)(4,1)} %bitcast.511), calls=%async_computation.5 | async-start | bytes 4194304
  579.4 17.2 %slice-start.4 = ((s8[10485760]{0:T(1024)(128)(4,1)}), s8[4194304]{0:T(1024)(128)(4,1)S(1)}, s32[]{:S(2)}) async-start(s8[10485760]{0:T(1024)(128)(4,1)} %bitcast.511), calls=%async_computation.6 | async-start | bytes 8388608
  586.0 10.5 slice-start.5
  613.1 12.5 %copy-start.29 = (bf16[8,2,128,384]{3,2,0,1:T(8,128)(2,1)S(1)}, bf16[8,2,128,384]{3,2,0,1:T(8,128)(2,1)}, u32[]{:S(2)}) copy-start(bf16[8,2,128,384]{3,2,0,1:T(8,128)(2,1)} %get-tuple-element.115) | copy-start | bytes 4718596
  671.4 78.9 %copy-start.2 = (f32[256,2560]{1,0:T(8,128)S(1)}, f32[256,2560]{1,0:T(8,128)}, u32[]{:S(2)}) copy-start(f32[256,2560]{1,0:T(8,128)} %get-tuple-element.111) | copy-start | bytes 7864324
  671.4 80.8 %copy-start.16 = (bf16[8,320,192]{1,2,0:T(8,128)(2,1)S(1)}, bf16[8,320,192]{1,2,0:T(8,128)(2,1)}, u32[]{:S(2)}) copy-start(bf16[8,320,192]{1,2,0:T(8,128)(2,1)} %copy.335) | copy-start | bytes 2949124
  671.4 80.8 %copy-start.24 = (bf16[8,320,96]{1,2,0:T(8,128)(2,1)S(1)}, bf16[8,320,96]{1,2,0:T(8,128)(2,1)}, u32[]{:S(2)}) copy-start(bf16[8,320,96]{1,2,0:T(8,128)(2,1)} %copy.336) | copy-start | bytes 1474564
  753.9 14.6 %copy-start.39 = (pred[256,16]{1,0:T(32,128)(4,1)S(1)}, pred[256,16]{1,0:T(32,128)(4,1)}, u32[]{:S(2)}) copy-start(pred[256,16]{1,0:T(32,128)(4,1)} %copy-done.38) | copy-start | bytes 12292
  859.5 19.9 %copy-start.52 = (f32[2560]{0:T(1024)S(1)}, f32[2560]{0:T(1024)}, u32[]{:S(2)}) copy-start(f32[2560]{0:T(1024)} %copy-done.51) | copy-start | bytes 30724
  859.5 19.9 %copy-start.60 = (f32[256]{0:T(256)S(1)}, f32[256]{0:T(256)}, u32[]{:S(2)}) copy-start(f32[256]{0:T(256)} %copy-done.59) | copy-start | bytes 3076
  859.5 256.4 %all-to-all-start.1 = ((bf16[8,320,288]{1,2,0:T(8,128)(2,1)}), bf16[8,320,288]{1,2,0:T(8,128)(2,1)}, u32[]{:S(2)}, u32[]{:S(2)}) async-start(bf16[8,320,288]{1,2,0:T(8,128)(2,1)} %pad_maximum_fusion), calls=%async_computation.1 | async-start | bytes 3538944 | tf_op jit(solution)/shard_map/all_to_all | solution.py:82
  901.0 25.0 %copy-start.35 = (f32[128,64]{1,0:T(8,128)S(1)}, f32[128,64]{1,0:T(8,128)}, u32[]{:S(2)}) copy-start(f32[128,64]{1,0:T(8,128)} %copy-done.34) | copy-start | bytes 98308
  901.0 25.0 %copy-start.37 = (f32[128,64]{1,0:T(8,128)S(1)}, f32[128,64]{1,0:T(8,128)}, u32[]{:S(2)}) copy-start(f32[128,64]{1,0:T(8,128)} %copy-done.36) | copy-start | bytes 98308
  901.1 24.9 %copy-start.43 = (f32[256,64]{1,0:T(8,128)S(1)}, f32[256,64]{1,0:T(8,128)}, u32[]{:S(2)}) copy-start(f32[256,64]{1,0:T(8,128)} %copy.375) | copy-start | bytes 196612
  901.5 24.5 %copy-start.44 = (f32[256,64]{1,0:T(8,128)S(1)}, f32[256,64]{1,0:T(8,128)}, u32[]{:S(2)}) copy-start(f32[256,64]{1,0:T(8,128)} %copy.376) | copy-start | bytes 196612
  928.7 23.4 %copy-start.54 = (f32[2560]{0:T(1024)S(1)}, f32[2560]{0:T(1024)}, u32[]{:S(2)}) copy-start(f32[2560]{0:T(1024)} %copy-done.53) | copy-start | bytes 30724
  928.7 23.4 %copy-start.62 = (f32[128,2]{0,1:T(2,128)S(1)}, f32[128,2]{0,1:T(2,128)}, u32[]{:S(2)}) copy-start(f32[128,2]{0,1:T(2,128)} %copy-done.61) | copy-start | bytes 3076
  932.6 19.5 %copy-start.1 = (f32[2,128,2560]{2,1,0:T(8,128)S(1)}, f32[2,128,2560]{2,1,0:T(8,128)}, u32[]{:S(2)}) copy-start(f32[2,128,2560]{2,1,0:T(8,128)} %copy-done) | copy-start | bytes 7864324
  (54 other events, 216.5 us)

commit v2 on v1

v2 whole, which is shorter than its diff:
```python
import functools
import math

import jax
import jax.numpy as jnp
from jax import lax
from jax.experimental import pallas as pl
from jax.experimental.pallas import tpu as pltpu
from jax.sharding import PartitionSpec as P

HEAD_DIM = 128
LANES = 128


norm_eps = 1e-05
rope_base = 500000.0
masked_score = -1e30

f32 = jnp.float32
bf16 = jnp.bfloat16
MESH = pl.DeviceIdType.MESH


def dot(form, left, right):
    return jnp.einsum(form, left, right, preferred_element_type=f32)


def rope_tables(start_place, local_len, head_size):
    places = (start_place + jnp.arange(local_len, dtype=jnp.int32)).astype(f32)
    frequency = jnp.power(
        rope_base, -jnp.arange(0, head_size, 2, dtype=jnp.int32).astype(f32) / head_size
    )
    angles = places[:, None] * frequency[None, :]
    return (jnp.cos(angles), jnp.sin(angles))


def rotate(field, cosine, sine):
    half = cosine.shape[1]
    parts = []
    for start in range(0, field.shape[1], 2 * half):
        front = field[:, start : start + half]
        back = field[:, start + half : start + 2 * half]
        parts.append(front * cosine - back * sine)
        parts.append(back * cosine + front * sine)
    return jnp.concatenate(parts, axis=1)


def rms_scale(values_in):
    return lax.rsqrt(jnp.mean(values_in * values_in, axis=-1, keepdims=True) + norm_eps)


def silu_parts(pre_gate):
    sigmoid_gate = jax.nn.sigmoid(pre_gate)
    silu_gate = pre_gate * sigmoid_gate
    slope_gate = sigmoid_gate * (1.0 + pre_gate * (1.0 - sigmoid_gate))
    return (silu_gate, slope_gate)


def gather_col(part):
    return lax.all_gather(part, "col", axis=0, tiled=False)


def scatter_col(blocks):
    flat = blocks.reshape(-1, blocks.shape[-1])
    return lax.psum_scatter(flat, "col", scatter_dimension=0, tiled=True)


def gather_all(part):
    got = lax.all_gather(part, ("col", "row"), axis=0, tiled=False)
    cols, rows = lax.axis_size("col"), lax.axis_size("row")
    got = got.reshape(cols, rows, *part.shape).transpose(0, 2, 1, 3)
    return got.reshape(cols, part.shape[0], rows * part.shape[1])


def scatter_all(blocks):
    flat = blocks.reshape(-1, blocks.shape[-1])
    part = lax.psum_scatter(flat, "row", scatter_dimension=1, tiled=True)
    return lax.psum_scatter(part, "col", scatter_dimension=0, tiled=True)


def swap_col(blocks):
    return lax.all_to_all(blocks, "col", split_axis=0, concat_axis=0, tiled=True)


class Net:
    def __init__(self, cols, send_sems, recv_sems):
        self.send_sems, self.recv_sems, self.used, self.sent = send_sems, recv_sems, 0, []
        self.cols, self.high_count = cols, cols // 2
        self.me = lax.axis_index("col")
        self.high, self.low = self.me // 2, self.me % 2
        self.row = lax.axis_index("row")
        self.outer, self.core = self.row // 2, self.row % 2

    def block(self, step, other=False):
        high = lax.rem(self.high + self.high_count - step, self.high_count)
        return 2 * high + (1 - self.low if other else self.low)

    def block_ahead(self, step, other=False):
        high = lax.rem(self.high + step, self.high_count)
        return 2 * high + (1 - self.low if other else self.low)

    def z_peer(self, step):
        return {"col": self.block_ahead(step)}

    def y_peer(self):
        return {"col": 2 * self.high + 1 - self.low}

    def x_peer(self):
        return {"row": 2 * (1 - self.outer) + self.core}

    def core_peer(self):
        return {"row": 2 * self.outer + 1 - self.core}

    def col_peer(self, step):
        return {"col": lax.rem(self.me + step, self.cols)}

    def greet(self, peers):
        barrier = pltpu.get_barrier_semaphore()
        for peer in peers:
            pl.semaphore_signal(barrier, inc=1, device_id=peer, device_id_type=MESH)
        pl.semaphore_wait(barrier, len(peers))

    def send(self, source, target, peer):
        copy = pltpu.make_async_remote_copy(
            src_ref=source,
            dst_ref=target,
            send_sem=self.send_sems.at[self.used],
            recv_sem=self.recv_sems.at[self.used],
            device_id=peer,
            device_id_type=MESH,
        )
        self.used += 1
        copy.start()
        self.sent.append(copy)
        return copy

    def left(self, copy):
        copy.wait_send()
        self.sent = [other for other in self.sent if other is not copy]

    def finish(self):
        for copy in self.sent:
            copy.wait_send()


def col_peers(net):
    return [net.z_peer(step) for step in range(1, net.high_count)] + [net.y_peer()]


def row_peers(net):
    return [net.x_peer(), net.core_peer()]


def gather_kernel(cols, kinds, pieces, *refs):
    count = len(kinds)
    ins, outs = refs[:count], refs[count : 2 * count]
    send_sems, recv_sems, local_sems = refs[2 * count :]
    net = Net(cols, send_sems, recv_sems)
    swaps = [i for i, kind in enumerate(kinds) if kind == "swap"]
    peers = [net.col_peer(step) for step in range(1, cols)] if swaps else col_peers(net)
    net.greet(peers + (row_peers(net) if "all" in kinds else []))
    other_row = 2 * (1 - net.outer) + net.core

    def place(i, block, rows, row):
        if kinds[i] == "all":
            part = ins[i].shape[1]
            return outs[i].at[block, rows, pl.ds(pl.multiple_of(row * part, LANES), part)]
        return outs[i].at[block, rows]

    order = []
    for i in sorted(range(count), key=lambda i: kinds[i] != "all"):
        if kinds[i] != "swap":
            rows = ins[i].shape[0] // pieces[i]
            order += [(i, pl.ds(q * rows, rows)) for q in range(pieces[i])]
    swap_sends = [(i, step) for i in swaps for step in range(1, cols)]
    steps = range(net.high_count)
    along_z, along_y, along_x, to_core, moved = {}, {}, {}, {}, []
    locals_ = []
    for i, kind in enumerate(kinds):
        own = ins[i].at[net.me] if kind == "swap" else ins[i]
        slot = outs[i].at[net.me] if kind == "swap" else place(
            i, net.me, pl.ds(0, ins[i].shape[0]), net.row
        )
        local = pltpu.make_async_copy(own, slot, local_sems.at[i])
        local.start()
        locals_.append(local)

    def swap_next():
        if swap_sends:
            i, step = swap_sends.pop(0)
            block = lax.rem(net.me + step, cols)
            moved.append(net.send(ins[i].at[block], outs[i].at[net.me], net.col_peer(step)))

    def in_chip(q, step, other, source, slot):
        if kinds[order[q][0]] == "all":
            along_x[q, step, other] = net.send(source, slot, net.x_peer())
            to_core[q, step, other] = net.send(source, slot, net.core_peer())

    def start(q):
        i, rows = order[q]
        source, slot = ins[i].at[rows], place(i, net.me, rows, net.row)
        for step in reversed(range(1, net.high_count)):
            along_z[q, step] = net.send(source, slot, net.z_peer(step))
        along_y[q, 0] = net.send(source, slot, net.y_peer())
        in_chip(q, 0, False, source, slot)

    def after_z(q):
        i, rows = order[q]
        for step in reversed(range(1, net.high_count)):
            along_z[q, step].wait_recv()
            slot = place(i, net.block(step), rows, net.row)
            along_y[q, step] = net.send(slot, slot, net.y_peer())
            in_chip(q, step, False, slot, slot)

    def after_y(q):
        i, rows = order[q]
        for step in steps:
            along_y[q, step].wait_recv()
            slot = place(i, net.block(step, True), rows, net.row)
            in_chip(q, step, True, slot, slot)

    def after_x(q):
        i, rows = order[q]
        if kinds[i] == "all":
            for other in (False, True):
                for step in steps:
                    along_x[q, step, other].wait_recv()
                    slot = place(i, net.block(step, other), rows, other_row)
                    moved.append(net.send(slot, slot, net.core_peer()))

    for tick in range(len(order) + 3):
        if tick < len(order):
            if tick >= 2:
                for step in range(1, net.high_count):
                    net.left(along_z[tick - 2, step])
            start(tick)
        if tick % 2:
            swap_next()
        for stage, lag in ((after_z, 1), (after_y, 2), (after_x, 3)):
            if 0 <= tick - lag < len(order):
                stage(tick - lag)
    while swap_sends:
        swap_next()
    for copy in [*moved, *to_core.values()]:
        copy.wait_recv()
    for local in locals_:
        local.wait()
    net.finish()


def gather(cols, collective_id, *triples):
    kinds = [kind for kind, _, _ in triples]
    pieces = [piece for _, piece, _ in triples]
    arrays = [array for _, _, array in triples]
    copies = 0
    shapes = []
    for kind, piece, array in triples:
        if kind == "swap":
            shapes.append(jax.ShapeDtypeStruct(array.shape, array.dtype))
            copies += cols
        elif kind == "col":
            shapes.append(jax.ShapeDtypeStruct((cols, *array.shape), array.dtype))
            copies += cols * piece
        else:
            rows = lax.axis_size("row")
            shape = (cols, array.shape[0], rows * array.shape[1])
            shapes.append(jax.ShapeDtypeStruct(shape, array.dtype))
            copies += 4 * cols * piece
    return pl.pallas_call(
        functools.partial(gather_kernel, cols, kinds, pieces),
        out_shape=shapes,
        in_specs=[pl.BlockSpec(memory_space=pl.ANY)] * len(triples),
        out_specs=[pl.BlockSpec(memory_space=pl.ANY)] * len(triples),
        scratch_shapes=[
            pltpu.SemaphoreType.DMA((copies,)),
            pltpu.SemaphoreType.DMA((copies,)),
            pltpu.SemaphoreType.DMA((len(triples),)),
        ],
        compiler_params=pltpu.CompilerParams(collective_id=collective_id, has_side_effects=True),
        name=f"gather_{collective_id}",
    )(*arrays)


def add_rows(target, terms):
    rows = target.shape[0]
    piece = 32 if rows % 32 == 0 else 16

    def body(index, carry):
        at = pl.ds(pl.multiple_of(index * piece, piece), piece)
        total = terms[0][at, :].astype(f32)
        for term in terms[1:]:
            total = total + term[at, :].astype(f32)
        target[at, :] = total.astype(target.dtype)
        return carry

    lax.fori_loop(0, rows // piece, body, 0)


class ScatterCol:
    def __init__(self, net, part, rows, from_y, from_z, out):
        self.net, self.part, self.rows = net, part, rows
        self.from_y, self.from_z, self.out = from_y, from_z, out
        self.order = [*range(1, net.high_count), 0]
        self.along_y, self.along_z = {}, {}
        self.stages = [self.send_y, self.send_z, self.last]

    def send_y(self):
        for step in self.order:
            source = self.part.at[self.net.block_ahead(step, True), self.rows]
            self.along_y[step] = self.net.send(
                source, self.from_y.at[step, self.rows], self.net.y_peer()
            )

    def send_z(self):
        for step in self.order:
            self.along_y[step].wait_recv()
            mine = self.part.at[self.net.block_ahead(step), self.rows]
            slot = self.from_y.at[step, self.rows]
            if step:
                add_rows(slot, [mine, slot])
                self.along_z[step] = self.net.send(
                    slot, self.from_z.at[step - 1, self.rows], self.net.z_peer(step)
                )

    def last(self):
        for step in range(1, self.net.high_count):
            self.along_z[step].wait_recv()
        terms = [
            self.from_z.at[step - 1, self.rows] for step in range(1, self.net.high_count)
        ]
        mine = self.part.at[self.net.me, self.rows]
        add_rows(self.out.at[self.rows], [mine, self.from_y.at[0, self.rows], *terms])

    def clear_y(self):
        for step in self.order:
            self.net.left(self.along_y[step])


class ScatterAll:
    def __init__(self, net, part, rows, from_core, from_x, from_y, from_z, out):
        self.net, self.part, self.rows, self.out = net, part, rows, out
        self.from_core, self.from_x, self.from_y, self.from_z = from_core, from_x, from_y, from_z
        self.order = [*range(1, net.high_count), 0]
        self.blocks = [(step, True) for step in self.order]
        self.blocks += [(step, False) for step in self.order]
        self.across, self.onward, self.along_y, self.along_z = {}, {}, {}, {}
        self.other_row = 2 * (1 - net.outer) + net.core
        self.stages = [self.send_core, self.send_x, self.send_y, self.send_z, self.last]

    def features(self, row):
        width = self.out.shape[1]
        return pl.ds(pl.multiple_of(row * width, LANES), width)

    def block(self, key):
        return self.net.block_ahead(*key)

    def send_core(self):
        net = self.net
        for far in (1, 0):
            outer = 1 - net.outer if far else net.outer
            for key in self.blocks:
                block = self.block(key)
                features = self.features(2 * outer + 1 - net.core)
                self.across[far, key] = net.send(
                    self.part.at[block, self.rows, features],
                    self.from_core.at[far, block, self.rows],
                    net.core_peer(),
                )

    def send_x(self):
        for key in self.blocks:
            self.across[1, key].wait_recv()
            block = self.block(key)
            slot = self.from_core.at[1, block, self.rows]
            mine = self.part.at[block, self.rows, self.features(self.other_row)]
            add_rows(slot, [mine, slot])
            self.onward[key] = self.net.send(
                slot, self.from_x.at[block, self.rows], self.net.x_peer()
            )

    def send_y(self):
        for key in self.blocks:
            self.across[0, key].wait_recv()
            self.onward[key].wait_recv()
            block = self.block(key)
            slot = self.from_core.at[0, block, self.rows]
            mine = self.part.at[block, self.rows, self.features(self.net.row)]
            add_rows(slot, [mine, slot, self.from_x.at[block, self.rows]])
            step, other = key
            if other:
                self.along_y[step] = self.net.send(
                    slot, self.from_y.at[step, self.rows], self.net.y_peer()
                )

    def send_z(self):
        for step in self.order:
            self.along_y[step].wait_recv()
            slot = self.from_core.at[0, self.block((step, False)), self.rows]
            add_rows(slot, [slot, self.from_y.at[step, self.rows]])
            if step:
                self.along_z[step] = self.net.send(
                    slot, self.from_z.at[step - 1, self.rows], self.net.z_peer(step)
                )

    def last(self):
        for step in range(1, self.net.high_count):
            self.along_z[step].wait_recv()
        terms = [
            self.from_z.at[step - 1, self.rows] for step in range(1, self.net.high_count)
        ]
        mine = self.from_core.at[0, self.net.me, self.rows]
        add_rows(self.out.at[self.rows], [mine, *terms])


def scatter_kernel(cols, kinds, pieces, *refs):
    count = len(kinds)
    parts, outs, scratch = refs[:count], refs[count : 2 * count], list(refs[2 * count :])
    send_sems, recv_sems = scratch[-2:]
    net = Net(cols, send_sems, recv_sems)
    net.greet(col_peers(net) + (row_peers(net) if "all" in kinds else []))
    lines = {"all": [], "col": []}
    for i, kind in enumerate(kinds):
        buffers = [scratch.pop(0) for _ in range(4 if kind == "all" else 2)]
        rows = outs[i].shape[0] // pieces[i]
        make = ScatterAll if kind == "all" else ScatterCol
        lines[kind] += [
            make(net, parts[i], pl.ds(q * rows, rows), *buffers, outs[i])
            for q in range(pieces[i])
        ]
    ticks = max(len(lines["all"]) + 4, len(lines["col"]) + 2)
    for tick in range(ticks):
        for kind in ("col", "all"):
            line = lines[kind]
            if kind == "col" and 2 <= tick < len(line):
                line[tick - 2].clear_y()
            depth = 5 if kind == "all" else 3
            for stage in range(depth):
                if 0 <= tick - stage < len(line):
                    line[tick - stage].stages[stage]()
    net.finish()


def scatter(cols, collective_id, *triples):
    high = cols // 2
    scratch, outs, copies = [], [], 0
    for kind, piece, array in triples:
        rows, width = array.shape[1:]
        if kind == "all":
            width = width // lax.axis_size("row")
            scratch += [
                pltpu.VMEM((2, cols, rows, width), bf16),
                pltpu.VMEM((cols, rows, width), bf16),
            ]
            copies += 3 * cols * piece
        copies += cols * piece
        scratch += [pltpu.VMEM((high, rows, width), bf16), pltpu.VMEM((high - 1, rows, width), bf16)]
        outs.append(jax.ShapeDtypeStruct((rows, width), f32))
    vmem = pl.BlockSpec(memory_space=pltpu.VMEM)
    return pl.pallas_call(
        functools.partial(
            scatter_kernel, cols, [kind for kind, _, _ in triples], [p for _, p, _ in triples]
        ),
        out_shape=outs,
        in_specs=[vmem] * len(triples),
        out_specs=[vmem] * len(triples),
        scratch_shapes=[
            *scratch,
            pltpu.SemaphoreType.DMA((copies,)),
            pltpu.SemaphoreType.DMA((copies,)),
        ],
        compiler_params=pltpu.CompilerParams(
            collective_id=collective_id, has_side_effects=True, vmem_limit_bytes=60 << 20
        ),
        name=f"scatter_{collective_id}",
    )(*[array for _, _, array in triples])


def sum_row_kernel(part, out, from_core, to_x, from_x, send_sems, recv_sems):
    net = Net(2, send_sems, recv_sems)
    net.greet(row_peers(net))
    pieces = from_core.shape[0]
    rows = from_core.shape[1]

    def piece(core, i):
        start = (core * pieces + i) * rows
        return pl.ds(pl.multiple_of(start, rows), rows)

    across = [
        net.send(part.at[piece(1 - net.core, i)], from_core.at[i], net.core_peer())
        for i in range(pieces)
    ]
    along, back = [], []
    for i in range(pieces):
        across[i].wait_recv()
        add_rows(to_x.at[i], [part.at[piece(net.core, i)], from_core.at[i]])
        along.append(net.send(to_x.at[i], from_x.at[i], net.x_peer()))
    for i in range(pieces):
        along[i].wait_recv()
        mine = piece(net.core, i)
        add_rows(out.at[mine], [to_x.at[i], from_x.at[i]])
        back.append(net.send(out.at[mine], out.at[mine], net.core_peer()))
    for copy in back:
        copy.wait_recv()
    net.finish()


def sum_row_call(collective_id, part):
    pieces = 4
    rows = part.shape[0] // 2 // pieces
    piece = (pieces, rows, part.shape[1])
    return pl.pallas_call(
        sum_row_kernel,
        out_shape=jax.ShapeDtypeStruct(part.shape, bf16),
        in_specs=[pl.BlockSpec(memory_space=pltpu.VMEM)],
        out_specs=pl.BlockSpec(memory_space=pltpu.VMEM),
        scratch_shapes=[
            pltpu.VMEM(piece, bf16),
            pltpu.VMEM(piece, bf16),
            pltpu.VMEM(piece, bf16),
            pltpu.SemaphoreType.DMA((3 * pieces,)),
            pltpu.SemaphoreType.DMA((3 * pieces,)),
        ],
        compiler_params=pltpu.CompilerParams(
            collective_id=collective_id, has_side_effects=True, vmem_limit_bytes=32 << 20
        ),
        name=f"sum_row_{collective_id}",
    )(part)


def dot_nn(left, right):
    return lax.dot_general(left, right, (((1,), (0,)), ((), ())), preferred_element_type=f32)


def dot_nt(left, right):
    return lax.dot_general(left, right, (((1,), (1,)), ((), ())), preferred_element_type=f32)


def dot_tn(left, right):
    return lax.dot_general(left, right, (((0,), (0,)), ((), ())), preferred_element_type=f32)


def each_tile(count, body):
    def step(index, carry):
        body(index)
        return carry

    lax.fori_loop(0, count, step, 0)


TILE = 512


def tile_at(index, tile=TILE):
    if isinstance(index, int):
        return pl.ds(index * tile, tile)
    return pl.ds(pl.multiple_of(index * tile, tile), tile)


def experts_kernel(
    cols,
    capacity,
    h2,
    grads,
    w_gate,
    w_up,
    w_down,
    w_shared,
    rank_row,
    rank_col,
    gate_own,
    out_part,
    back,
    g_gate,
    g_up,
    g_down,
    g_shared,
    gate_dots,
    h2_all,
    xs_all,
    cs_all,
    wgu,
    wd,
    ws,
    gates,
    hb,
    xbuf,
    ybuf,
    obuf,
    part,
    pre,
    gcol,
    dcol,
    dz_all,
    zg_all,
    dgu_all,
    sdz_all,
    sz_all,
    sgu_all,
    from_core,
    from_x,
    from_y,
    from_z,
    kept,
    dots,
    dots_core,
    dots_x,
    tiles,
    tiles_all,
    stage,
    stage_low,
    send_sems,
    recv_sems,
    local_sems,
):
    net = Net(cols, send_sems, recv_sems)
    toks, width = h2.shape
    exp_local, _, hidden = w_gate.shape
    high = net.high_count
    pad = ws.shape[1] // 3
    slots = exp_local * capacity
    pair = 2 * capacity
    piece = width // lax.axis_size("row")
    share = width // LANES // 5 * LANES
    rest = (width - 4 * share) // 2
    wide = width // TILE
    net.greet([net.col_peer(step) for step in range(1, cols)] + row_peers(net))

    def local_copy(source, target, index):
        copy = pltpu.make_async_copy(source, target, local_sems.at[index])
        copy.start()
        return copy

    gate_copies = [
        net.send(gate_own, gates.at[net.me], net.col_peer(step)) for step in range(1, cols)
    ]
    gates[net.me] = gate_own[...]

    def feature_e(row):
        return pl.ds(pl.multiple_of(row * share, LANES), share)

    def feature_r(core):
        return pl.ds(pl.multiple_of(4 * share + core * rest, LANES), rest)

    own_e, own_r = feature_e(net.row), feature_r(net.core)
    far_e = feature_e(2 * (1 - net.outer) + net.core)

    def pass_on(source, block, features, peer):
        return net.send(source.at[..., features], h2_all.at[block, :, features], peer)

    along_z, along_y, along_x, to_core = {}, {}, {}, {}
    for step in range(high - 1, 0, -1):
        along_z[high - step] = [
            pass_on(h2, net.me, own_e, net.z_peer(step)),
            pass_on(h2, net.me, own_r, net.z_peer(step)),
        ]
    along_y[0] = [
        pass_on(h2, net.me, own_e, net.y_peer()),
        pass_on(h2, net.me, own_r, net.y_peer()),
    ]

    def block_of(step, other):
        return net.block_ahead(step, other)

    def share_in_chip(step, other):
        block = block_of(step, other)
        source = h2_all.at[block]
        along_x[step, other] = pass_on(source, block, own_e, net.x_peer())
        to_core[step, other] = [
            pass_on(source, block, own_e, net.core_peer()),
            pass_on(source, block, own_r, net.core_peer()),
        ]

    def arrived_y(step):
        for copy in along_y[step]:
            copy.wait_recv()
        share_in_chip(step, True)

    def arrived_z(step):
        for copy in along_z[step]:
            copy.wait_recv()
        block = block_of(step, False)
        along_y[step] = [
            pass_on(h2_all.at[block], block, own_e, net.y_peer()),
            pass_on(h2_all.at[block], block, own_r, net.y_peer()),
        ]
        share_in_chip(step, False)

    def arrived_x(step, other):
        along_x[step, other].wait_recv()
        block = block_of(step, other)
        to_core[step, other].append(pass_on(h2_all.at[block], block, far_e, net.core_peer()))

    def whole(step, other):
        for copy in to_core[step, other]:
            copy.wait_recv()

    events = [functools.partial(arrived_y, 0)]
    for step in range(1, high):
        events.append(functools.partial(arrived_z, step))
        events.append(functools.partial(arrived_x, step - 1, True))
        events.append(functools.partial(arrived_y, step))
        events.append(functools.partial(arrived_x, step, False))
    events.append(functools.partial(arrived_x, high - 1, True))
    events = iter(events)

    def pump(count=1):
        for _ in range(count):
            event = next(events, None)
            if event is not None:
                event()

    loads = []
    for e in range(exp_local):
        loads.append(local_copy(w_down.at[e], wd.at[e], 3 * e))
        loads.append(local_copy(w_gate.at[e], wgu.at[e, :, pl.ds(0, hidden)], 3 * e + 1))
        loads.append(local_copy(w_up.at[e], wgu.at[e, :, pl.ds(hidden, hidden)], 3 * e + 2))
    base = 3 * exp_local
    loads.append(local_copy(w_shared, ws, base))
    keep_own = local_copy(h2, h2_all.at[net.me], base + 1)
    base += 2

    def load_pair(source, step):
        first = local_copy(source.at[block_of(step, False)], hb.at[0], base)
        second = local_copy(source.at[block_of(step, True)], hb.at[1], base + 1)
        first.wait()
        second.wait()

    slot_row = lax.broadcasted_iota(jnp.int32, (capacity, toks), 0).astype(f32) + 1.0
    slot_lane = lax.broadcasted_iota(jnp.int32, (toks, capacity), 1).astype(f32) + 1.0

    def chosen(block, e):
        return rank_row[block, e : e + 1, :] == slot_row

    def picks(block):
        rows = [
            jnp.where(chosen(block, e), 1.0, 0.0).astype(bf16) for e in range(exp_local)
        ]
        return jnp.concatenate(rows, axis=0)

    def picks_back(block):
        lanes = [
            jnp.where(rank_col[block, :, e : e + 1] == slot_lane, 1.0, 0.0).astype(bf16)
            for e in range(exp_local)
        ]
        return jnp.concatenate(lanes, axis=1)

    def dispatch(step):
        for b in (0, 1):
            table = picks(block_of(step, b == 1))

            def tile(index, b=b, table=table):
                at = tile_at(index)
                rows = dot_nn(table, hb[b, :, at]).astype(bf16)
                for e in range(exp_local):
                    xbuf[e, pl.ds(b * capacity, capacity), at] = rows[
                        e * capacity : (e + 1) * capacity
                    ]

            each_tile(wide, tile)

    def save_rows(target, step):
        return [
            local_copy(
                xbuf.at[e], target.at[e, pl.ds(step * pair, pair)], base + 2 + e
            )
            for e in range(exp_local)
        ]

    saved = []
    for step in range(high):
        load_pair(grads, step)
        if step == 0:
            for copy in loads:
                copy.wait()
        for copy in saved:
            copy.wait()
        dispatch(step)
        saved = save_rows(cs_all, step)
        for e in range(exp_local):
            dz_all[e, pl.ds(step * pair, pair), :] = dot_nt(xbuf[e], wd[e]).astype(bf16)
        for b in (0, 1):
            sdz_all[block_of(step, b == 1)] = dot_nn(hb[b], ws[:, 2 * pad :]).astype(bf16)
        pump()
    for copy in gate_copies:
        copy.wait_recv()
    keep_own.wait()

    across, onward, upward, far_z = {}, {}, {}, {}

    def features(row):
        return pl.ds(pl.multiple_of(row * piece, LANES), piece)

    other_row = 2 * (1 - net.outer) + net.core

    def hand_over(step):
        for b in (1, 0):
            for far in (1, 0):
                outer = 1 - net.outer if far else net.outer
                source = part.at[b, :, features(2 * outer + 1 - net.core)]
                across[step, b, far] = net.send(
                    source, from_core.at[far, step, b], net.core_peer()
                )

    def sum_cores(step):
        for b in (1, 0):
            for far, row in ((1, other_row), (0, net.row)):
                across[step, b, far].wait_recv()
                slot = from_core.at[far, step, b]
                add_rows(slot, [part.at[b, :, features(row)], slot])
                if far:
                    onward[step, b] = net.send(slot, from_x.at[step, b], net.x_peer())
        for b in (1, 0):
            for far in (1, 0):
                net.left(across[step, b, far])

    def sum_chips(step):
        for b in (1, 0):
            onward[step, b].wait_recv()
            slot = from_core.at[0, step, b]
            add_rows(slot, [slot, from_x.at[step, b]])
            if b:
                upward[step] = net.send(slot, from_y.at[step], net.y_peer())

    def sum_plane(step):
        upward[step].wait_recv()
        slot = from_core.at[0, step, 0]
        add_rows(slot, [slot, from_y.at[step]])
        if step:
            far_z[step] = net.send(slot, from_z.at[step - 1], net.z_peer(step))

    own_expert = lax.rem(net.me, cols) * exp_local
    gate_rows = gates.shape[1]
    gate_row = lax.broadcasted_iota(jnp.int32, (gate_rows, toks), 0)
    dots[...] = jnp.zeros_like(dots)
    for step in range(high):
        if step:
            whole(step, False)
        whole(step, True)
        load_pair(h2_all, step)
        for copy in saved:
            copy.wait()
        dispatch(step)
        saved = save_rows(xs_all, step)
        pump()
        for b in (0, 1):
            block = block_of(step, b == 1)
            inner = dot_nn(hb[b], ws[:, : 2 * pad])
            sa, su = inner[:, :pad], inner[:, pad:]
            sig = 1.0 / (1.0 + jnp.exp(-sa))
            silu = sa * sig
            slope = sig * (1.0 + sa * (1.0 - sig))
            sz_all[block] = (silu * su).astype(bf16)
            sdz = sdz_all[block].astype(f32)
            sgu_all[block, :, :pad] = (sdz * su * slope).astype(bf16)
            sgu_all[block, :, pad:] = (sdz * silu).astype(bf16)
        if step:
            sum_cores(step - 1)
        rows = pl.ds(step * pair, pair)
        for e in range(exp_local):

            def inner_tile(index, e=e):
                at = tile_at(index, 256)
                pre[:, at] = dot_nn(xbuf[e], wgu[e, :, at])

            each_tile(2 * hidden // 256, inner_tile)
            for b in (0, 1):
                block = block_of(step, b == 1)
                gate = jnp.sum(
                    jnp.where(gate_row == own_expert + e, gates[block], 0.0), axis=0, keepdims=True
                )
                gate = jnp.sum(jnp.where(chosen(block, e), gate, 0.0), axis=1, keepdims=True)
                gcol[pl.ds(b * capacity, capacity), :] = jnp.broadcast_to(gate, (capacity, LANES))

            def gating(index, e=e, step=step):
                at = pl.ds(pl.multiple_of(index * 32, 32), 32)
                saved_at = pl.ds(pl.multiple_of(step * pair + index * 32, 32), 32)
                a, u = pre[at, :hidden], pre[at, hidden:]
                gate = jnp.concatenate([gcol[at, :]] * (hidden // LANES), axis=1)
                dz = dz_all[e, saved_at, :].astype(f32)
                sig = 1.0 / (1.0 + jnp.exp(-a))
                silu = a * sig
                slope = sig * (1.0 + a * (1.0 - sig))
                z = silu * u
                dcol[at, :] = jnp.broadcast_to(
                    jnp.sum(z * dz, axis=1, keepdims=True), (32, LANES)
                )
                zg_all[e, saved_at, :] = (z * gate).astype(bf16)
                dz = dz * gate
                dgu_all[e, saved_at, :hidden] = (dz * u * slope).astype(bf16)
                dgu_all[e, saved_at, hidden:] = (dz * silu).astype(bf16)

            each_tile(pair // 32, gating)
            for b in (0, 1):
                block = block_of(step, b == 1)
                col = dcol[pl.ds(b * capacity, capacity), :]
                col = jnp.concatenate([col] * (toks // LANES), axis=1)
                dots[block, e : e + 1, :] = jnp.sum(
                    jnp.where(chosen(block, e), col, 0.0), axis=0, keepdims=True
                )

            def out_tile(index, e=e):
                at = tile_at(index)
                y = dot_nn(zg_all[e, rows, :], wd[e, :, at]).astype(bf16)
                for b in (0, 1):
                    ybuf[b, pl.ds(e * capacity, capacity), at] = y[b * capacity : (b + 1) * capacity]

            each_tile(wide, out_tile)
            pump()
        if step:
            for copy in out_copies:
                copy.wait()
        out_copies = []
        for b in (0, 1):
            block = block_of(step, b == 1)
            table = picks_back(block)

            def join_tile(index, b=b, table=table, block=block):
                at = tile_at(index)
                total = dot_nn(table, ybuf[b, :, at])
                total = total + dot_nt(sz_all[block], ws[at, 2 * pad :])
                obuf[b, :, at] = total.astype(bf16)

            each_tile(wide, join_tile)
            out_copies.append(
                local_copy(obuf.at[b], out_part.at[block], base + 2 + exp_local + b)
            )
        pump()
        if step:
            sum_chips(step - 1)
        for e in range(exp_local):

            def back_tile(index, e=e):
                at = tile_at(index)
                y = dot_nt(dgu_all[e, rows, :], wgu[e, at, :]).astype(bf16)
                for b in (0, 1):
                    ybuf[b, pl.ds(e * capacity, capacity), at] = y[b * capacity : (b + 1) * capacity]

            each_tile(wide, back_tile)
        pump()
        for b in (1, 0):
            block = block_of(step, b == 1)
            table = picks_back(block)

            def back_join(index, b=b, table=table, block=block):
                at = tile_at(index)
                total = dot_nn(table, ybuf[b, :, at])
                total = total + dot_nt(sgu_all[block], ws[at, : 2 * pad])
                part[b, :, at] = total.astype(bf16)

            each_tile(wide, back_join)
        hand_over(step)
        if step:
            sum_plane(step - 1)
    pump(64)
    last = high - 1
    for copy in saved + out_copies:
        copy.wait()

    load_sem, store_sem = base + 4 + exp_local, base + 6 + exp_local

    def passes(count, load, work, stores):
        def load_copy(j, slot):
            source, target = load(j, slot)
            return pltpu.make_async_copy(source, target, local_sems.at[load_sem + slot])

        def store_copies(j, slot):
            return [
                pltpu.make_async_copy(
                    source, target, local_sems.at[store_sem + 2 * slot + i]
                )
                for i, (source, target) in enumerate(stores(j, slot))
            ]

        load_copy(0, 0).start()

        def body(j):
            slot = lax.rem(j, 2)

            @pl.when(j + 1 < count)
            def _():
                load_copy(j + 1, 1 - slot).start()

            load_copy(j, slot).wait()

            @pl.when(j >= 2)
            def _():
                for copy in store_copies(j - 2, slot):
                    copy.wait()

            work(j, slot)
            for copy in store_copies(j, slot):
                copy.start()

        each_tile(count, body)
        for j in range(max(0, count - 2), count):
            for copy in store_copies(j, j % 2):
                copy.wait()

    def inner_grads(e):
        passes(
            wide,
            lambda j, slot: (
                xs_all.at[e, :, tile_at(j)],
                tiles.at[slot],
            ),
            lambda j, slot: put(stage.at[slot], dot_tn(tiles[slot], dgu_all[e])),
            lambda j, slot: [
                (stage.at[slot, :, pl.ds(0, hidden)], g_gate.at[e, tile_at(j)]),
                (stage.at[slot, :, pl.ds(hidden, hidden)], g_up.at[e, tile_at(j)]),
            ],
        )

    def put(target, value):
        target[...] = value

    def down_grads(e):
        passes(
            wide,
            lambda j, slot: (
                cs_all.at[e, :, tile_at(j)],
                tiles.at[slot],
            ),
            lambda j, slot: put(
                stage.at[slot, pl.ds(0, hidden), pl.ds(0, TILE)],
                dot_tn(zg_all[e], tiles[slot]),
            ),
            lambda j, slot: [
                (
                    stage.at[slot, pl.ds(0, hidden), pl.ds(0, TILE)],
                    g_down.at[e, :, tile_at(j)],
                ),
            ],
        )

    def shared_grads(source, others, start, size):
        def work(j, slot):
            total = dot_tn(tiles_all[slot, 0], others[0])
            for c in range(1, cols):
                total = total + dot_tn(tiles_all[slot, c], others[c])
            stage_low[slot, :, :size] = total.astype(bf16)

        def load(j, slot):
            return (source.at[:, :, tile_at(j)], tiles_all.at[slot])

        passes(
            wide,
            lambda j, slot: load(j, slot),
            work,
            lambda j, slot: [
                (
                    stage_low.at[slot, :, pl.ds(0, size)],
                    g_shared.at[tile_at(j), pl.ds(start, size)],
                ),
            ],
        )

    first_dots = net.send(dots, dots_core, net.core_peer())
    inner_grads(0)
    sum_cores(last)
    first_dots.wait_recv()
    net.left(first_dots)
    dots[...] = dots[...] + dots_core[...]
    second_dots = net.send(dots, dots_x, net.x_peer())
    inner_grads(1)
    sum_chips(last)
    second_dots.wait_recv()
    dots_core[...] = dots[...] + dots_x[...]
    third_dots = []
    for step in range(1, cols):
        block = lax.rem(net.me + step, cols)
        third_dots.append(
            net.send(dots_core.at[block], gate_dots.at[net.me], net.col_peer(step))
        )
    gate_dots[net.me] = dots_core[net.me]
    down_grads(0)
    sum_plane(last)
    down_grads(1)
    for step in range(1, high):
        far_z[step].wait_recv()
    add_rows(kept, [from_core.at[0, 0, 0], *[from_z.at[step - 1] for step in range(1, high)]])
    own, other = features(net.row), features(other_row)
    back[:, own] = kept[...].astype(bf16)
    far = net.send(back.at[:, own], back.at[:, own], net.x_peer())
    near = net.send(back.at[:, own], back.at[:, own], net.core_peer())
    shared_grads(h2_all, sgu_all, 0, 2 * pad)
    far.wait_recv()
    crossed = net.send(back.at[:, other], back.at[:, other], net.core_peer())
    shared_grads(grads, sz_all, 2 * pad, pad)
    near.wait_recv()
    crossed.wait_recv()
    for copy in third_dots:
        copy.wait_recv()
    net.finish()


def experts_call(
    cols, collective_id, capacity, h2, grads, w_gate, w_up, w_down, w_shared, rank_row, rank_col, gate
):
    toks, width = h2.shape
    exp_local, _, hidden = w_gate.shape
    high = cols // 2
    pad = w_shared.shape[1] // 3
    piece = width // lax.axis_size("row")
    pair = 2 * capacity
    any_space = pl.BlockSpec(memory_space=pl.ANY)
    vmem = pl.BlockSpec(memory_space=pltpu.VMEM)
    copies = 160

    def shape(*dims, dtype=bf16):
        return jax.ShapeDtypeStruct(dims, dtype)

    return pl.pallas_call(
        functools.partial(experts_kernel, cols, capacity),
        out_shape=[
            shape(cols, toks, width),
            shape(toks, width),
            shape(exp_local, width, hidden, dtype=f32),
            shape(exp_local, width, hidden, dtype=f32),
            shape(exp_local, hidden, width, dtype=f32),
            shape(width, 3 * pad),
            shape(cols, 8, toks, dtype=f32),
            shape(cols, toks, width),
            shape(exp_local, cols * capacity, width),
            shape(exp_local, cols * capacity, width),
        ],
        in_specs=[any_space] * 6 + [vmem] * 3,
        out_specs=[
            any_space,
            vmem,
            any_space,
            any_space,
            any_space,
            any_space,
            vmem,
            any_space,
            any_space,
            any_space,
        ],
        scratch_shapes=[
            pltpu.VMEM((exp_local, width, 2 * hidden), bf16),
            pltpu.VMEM((exp_local, hidden, width), bf16),
            pltpu.VMEM((width, 3 * pad), bf16),
            pltpu.VMEM((cols, *gate.shape), f32),
            pltpu.VMEM((2, toks, width), bf16),
            pltpu.VMEM((exp_local, pair, width), bf16),
            pltpu.VMEM((2, exp_local * capacity, width), bf16),
            pltpu.VMEM((2, toks, width), bf16),
            pltpu.VMEM((2, toks, width), bf16),
            pltpu.VMEM((pair, 2 * hidden), f32),
            pltpu.VMEM((pair, LANES), f32),
            pltpu.VMEM((pair, LANES), f32),
            pltpu.VMEM((exp_local, cols * capacity, hidden), bf16),
            pltpu.VMEM((exp_local, cols * capacity, hidden), bf16),
            pltpu.VMEM((exp_local, cols * capacity, 2 * hidden), bf16),
            pltpu.VMEM((cols, toks, pad), bf16),
            pltpu.VMEM((cols, toks, pad), bf16),
            pltpu.VMEM((cols, toks, 2 * pad), bf16),
            pltpu.VMEM((2, high, 2, toks, piece), bf16),
            pltpu.VMEM((high, 2, toks, piece), bf16),
            pltpu.VMEM((high, toks, piece), bf16),
            pltpu.VMEM((high - 1, toks, piece), bf16),
            pltpu.VMEM((toks, piece), f32),
            pltpu.VMEM((cols, 8, toks), f32),
            pltpu.VMEM((cols, 8, toks), f32),
            pltpu.VMEM((cols, 8, toks), f32),
            pltpu.VMEM((2, cols * capacity, TILE), bf16),
            pltpu.VMEM((2, cols, toks, TILE), bf16),
            pltpu.VMEM((2, TILE, 2 * hidden), f32),
            pltpu.VMEM((2, TILE, 2 * pad), bf16),
            pltpu.SemaphoreType.DMA((copies,)),
            pltpu.SemaphoreType.DMA((copies,)),
            pltpu.SemaphoreType.DMA((24,)),
        ],
        compiler_params=pltpu.CompilerParams(
            collective_id=collective_id, has_side_effects=True, vmem_limit_bytes=62 << 20
        ),
        name=f"experts_{collective_id}",
    )(h2, grads, w_gate, w_up, w_down, w_shared, rank_row, rank_col, gate)


def experts_kernels(
    cols, collective_id, capacity, h2, grad_all, w_gate, w_up, w_down, shared_weights, *tables
):
    width, shared_part = shared_weights.shape[0], shared_weights.shape[1] // 3
    pad = -shared_part % LANES
    padded = jnp.pad(shared_weights.reshape(width, 3, shared_part), ((0, 0), (0, 0), (0, pad)))
    padded = padded.reshape(width, -1)
    out_part, back, g_gate, g_up, g_down, g_shared, gate_dots, *_ = experts_call(
        cols, collective_id, capacity, h2, grad_all, w_gate, w_up, w_down, padded, *tables
    )
    gate_dots = gate_dots[:, : w_gate.shape[0]].reshape(-1, h2.shape[0]).T
    g_shared = g_shared.reshape(width, 3, -1)[:, :, :shared_part].reshape(width, -1)
    return (out_part, back, gate_dots, g_shared, g_gate, g_up, g_down)


def fits(cols, rows, width):
    return cols % 2 == 0 and cols * rows * width * 2 <= 12 << 20


def gather_parts(kernels, cols, collective_id, *triples):
    if kernels:
        return gather(cols, collective_id, *triples)
    ways = {"col": gather_col, "all": gather_all, "swap": swap_col}
    return [ways[kind](array) for kind, _, array in triples]


def scatter_parts(kernels, cols, collective_id, *triples):
    if kernels:
        return scatter(cols, collective_id, *triples)
    ways = {"col": scatter_col, "all": scatter_all}
    return [ways[kind](array).astype(f32) for kind, _, array in triples]


def sum_row(kernels, collective_id, part):
    if kernels:
        return sum_row_call(collective_id, part)
    return lax.psum(part, "row")


def experts_plain(
    h2, grad_all, w_gate, w_up, w_down, shared_weights, router, rank_all, capacity, row_width
):
    cols = lax.axis_size("col")
    col_index, row_index = lax.axis_index("col"), lax.axis_index("row")
    toks, width = h2.shape
    exp_local = w_gate.shape[0]
    experts = rank_all.shape[2]
    shared_part = shared_weights.shape[1] // 3
    shared_in_weights = shared_weights[:, : 2 * shared_part]
    shared_down = shared_weights[:, 2 * shared_part :]
    h2_slice = lax.dynamic_slice_in_dim(h2, row_index * row_width, row_width, 1)
    h2_all = gather_all(h2_slice)

    all_mask = (rank_all > 0).astype(f32)
    all_probs = jax.nn.softmax(dot("ctd,de->cte", h2_all, router), axis=-1)
    all_picked = all_probs * all_mask
    all_gate = all_picked / jnp.sum(all_picked, axis=-1, keepdims=True)
    own = col_index * exp_local
    own_gate = lax.dynamic_slice_in_dim(all_gate, own, exp_local, 2)
    own_rank = lax.dynamic_slice_in_dim(rank_all, own, exp_local, 2).astype(jnp.int32)
    slots = jnp.arange(1, capacity + 1, dtype=jnp.int32)
    pick = jnp.swapaxes(own_rank, 1, 2)[:, :, None, :] == slots[:, None]
    slot_gate = jnp.sum(
        jnp.where(pick, jnp.swapaxes(own_gate, 1, 2)[:, :, None, :], 0.0), axis=3
    )[..., None]
    pick_low = pick.astype(bf16).reshape(cols, exp_local * capacity, toks)
    slot_shape = (cols, exp_local, capacity, width)
    slot_rows = dot("cut,ctd->cud", pick_low, h2_all).astype(bf16).reshape(slot_shape)
    slot_grad = dot("cut,ctd->cud", pick_low, grad_all).astype(bf16).reshape(slot_shape)
    gate_pre = dot("necd,edf->necf", slot_rows, w_gate)
    up_pre = dot("necd,edf->necf", slot_rows, w_up)
    silu_gate, slope_gate = silu_parts(gate_pre)
    hidden = silu_gate * up_pre
    gated = (hidden * slot_gate).astype(bf16)
    slot_out = dot("necf,efd->necd", gated, w_down).astype(bf16)
    hidden_grad = dot("necd,efd->necf", slot_grad, w_down)
    slot_dots = jnp.sum(hidden * hidden_grad, axis=-1)
    hidden_grad = hidden_grad * slot_gate
    gate_grad = (hidden_grad * up_pre * slope_gate).astype(bf16)
    up_grad = (hidden_grad * silu_gate).astype(bf16)
    slot_back = dot("necf,edf->necd", gate_grad, w_gate)
    slot_back = (slot_back + dot("necf,edf->necd", up_grad, w_up)).astype(bf16)
    grad_expert_down = dot("necf,necd->efd", gated, slot_grad)
    grad_expert_gate = dot("necd,necf->edf", slot_rows, gate_grad)
    grad_expert_up = dot("necd,necf->edf", slot_rows, up_grad)
    pick_flat = pick_low.reshape(cols, exp_local * capacity, toks)
    slot_out = slot_out.reshape(cols, exp_local * capacity, width)
    slot_back = slot_back.reshape(cols, exp_local * capacity, width)

    shared_pre = dot("ctd,dk->ctk", h2_all, shared_in_weights)
    sgate_pre, sup_pre = shared_pre[:, :, :shared_part], shared_pre[:, :, shared_part:]
    shared_silu, shared_slope = silu_parts(sgate_pre)
    shared_hidden = (shared_silu * sup_pre).astype(bf16)
    part_out = dot("cut,cud->ctd", pick_flat, slot_out) + dot(
        "ctk,dk->ctd", shared_hidden, shared_down
    )
    shared_hgrad = dot("ctd,dk->ctk", grad_all, shared_down)
    shared_grads = jnp.concatenate(
        [shared_hgrad * sup_pre * shared_slope, shared_hgrad * shared_silu], axis=2
    ).astype(bf16)
    part_back = dot("cut,cud->ctd", pick_flat, slot_back) + dot(
        "ctk,dk->ctd", shared_grads, shared_in_weights
    )
    token_dots = jnp.einsum(
        "ceu,ceut->cte", slot_dots, pick.astype(f32), precision=lax.Precision.HIGHEST
    )
    gate_dots = lax.psum(swap_col(token_dots), "row")
    gate_dots = jnp.swapaxes(gate_dots, 0, 1).reshape(toks, experts)

    shared_share = jnp.concatenate(
        [dot("ctd,ctk->dk", h2_all, shared_grads), dot("ctd,ctk->dk", grad_all, shared_hidden)],
        axis=1,
    ).astype(bf16)
    back_full = lax.all_gather(scatter_all(part_back.astype(bf16)), "row", axis=1, tiled=True)
    return (
        part_out.astype(bf16),
        back_full,
        gate_dots,
        shared_share,
        grad_expert_gate,
        grad_expert_up,
        grad_expert_down,
    )


def on_device(
    tokens,
    segments,
    routes,
    attn_gain,
    query_matrix,
    key_matrix,
    value_matrix,
    attention_output_matrix,
    mlp_gain,
    w_router,
    shared_gate_matrix,
    shared_up_matrix,
    shared_down_matrix,
    expert_gate,
    expert_up,
    expert_down,
    cotangent,
):
    local_len, seqs, width = tokens.shape
    cols = lax.axis_size("col")
    col_index = lax.axis_index("col")
    rows_w = query_matrix.shape[0]
    full_len = local_len * cols
    size = HEAD_DIM
    q_width = query_matrix.shape[1]
    kv_width = key_matrix.shape[1]
    kv_local = kv_width // size
    group = q_width // kv_width
    row_width = cotangent.shape[2]
    toks = local_len * seqs
    top = routes.shape[2]
    experts = w_router.shape[1]
    exp_local = expert_gate.shape[0]
    hidden_local = expert_gate.shape[2]
    capacity = max(2, toks * top * 4 // (3 * experts))
    shared_part = shared_gate_matrix.shape[1] // cols
    scale = 1.0 / math.sqrt(size)
    kernels = fits(cols, toks, width)

    def seq_major(a):
        return jnp.swapaxes(a, 0, 1).reshape(toks, a.shape[2])

    misc = jnp.concatenate(
        [
            w_router,
            attn_gain[:, None],
            mlp_gain[:, None],
            jnp.zeros((rows_w, LANES - experts - 2), bf16),
        ],
        axis=1,
    )
    first_weights = jnp.concatenate([query_matrix, key_matrix, value_matrix, misc], axis=1)
    shared_weights = jnp.concatenate(
        [
            shared_gate_matrix.reshape(rows_w, cols, shared_part),
            shared_up_matrix.reshape(rows_w, cols, shared_part),
            shared_down_matrix.T.reshape(rows_w, cols, shared_part),
        ],
        axis=2,
    )
    first_weights, out_weights, shared_weights, grad_all = gather_parts(
        kernels,
        cols,
        0,
        ("col", 5, first_weights),
        ("col", 4, attention_output_matrix.T),
        ("swap", 1, jnp.swapaxes(shared_weights, 0, 1)),
        ("all", 4, seq_major(cotangent).astype(bf16)),
    )
    first_weights = first_weights.reshape(width, -1)
    out_weights = out_weights.reshape(width, q_width)
    shared_weights = shared_weights.reshape(width, 3 * shared_part)
    qkv_width = q_width + 2 * kv_width
    qkv_weights = first_weights[:, :qkv_width]
    router = first_weights[:, qkv_width : qkv_width + experts]
    gain_one = first_weights[:, qkv_width + experts].astype(f32)
    gain_two = first_weights[:, qkv_width + experts + 1].astype(f32)


    x = seq_major(tokens).astype(f32)
    inv_first = rms_scale(x)
    base_first = x * inv_first
    h1 = (base_first * gain_one).astype(bf16)
    qkv = dot("tb,bk->tk", h1, qkv_weights)
    cosine, sine = rope_tables(col_index * local_len, local_len, size)
    cosine, sine = jnp.tile(cosine, (seqs, 1)), jnp.tile(sine, (seqs, 1))
    qk = rotate(qkv[:, : q_width + kv_width], cosine, sine).astype(bf16)
    value_low = qkv[:, q_width + kv_width :].astype(bf16)

    flat_routes = seq_major(routes)
    named = flat_routes[:, :, None] == jnp.arange(experts, dtype=jnp.int32)
    mask = jnp.any(named, axis=1)
    order = jnp.arange(toks, dtype=jnp.int32)
    upto = (order[None, :] <= order[:, None]).astype(bf16)
    rank = jnp.where(mask, dot("ij,je->ie", upto, mask.astype(bf16)), 0.0)

    doc = jnp.transpose(segments)
    side = jnp.concatenate(
        [
            rank.astype(bf16),
            doc.reshape(toks, 1).astype(bf16),
            jnp.zeros((toks, LANES - experts - 1), bf16),
        ],
        axis=1,
    )
    (kv_all,) = gather_parts(
        kernels, cols, 1, ("col", 4, jnp.concatenate([qk[:, q_width:], value_low, side], axis=1))
    )
    rank_all = kv_all[:, :, 2 * kv_width : 2 * kv_width + experts]
    kv_seq = jnp.swapaxes(kv_all.reshape(cols, seqs, local_len, -1), 0, 1)
    kv_seq = kv_seq.reshape(seqs, full_len, -1)
    key_all = kv_seq[:, :, :kv_width].reshape(seqs, full_len, kv_local, size)
    value_all = kv_seq[:, :, kv_width : 2 * kv_width].reshape(seqs, full_len, kv_local, size)
    doc_all = kv_seq[:, :, 2 * kv_width + experts]

    def to_grid(flat):
        shaped = flat.reshape(seqs, local_len, kv_local, group, size)
        return shaped.transpose(0, 2, 3, 1, 4).reshape(seqs, kv_local, group * local_len, size)

    def from_grid(grid):
        shaped = grid.reshape(seqs, kv_local, group, local_len, size)
        return shaped.transpose(0, 3, 1, 2, 4).reshape(toks, q_width)

    query_grid = to_grid(qk[:, :q_width])
    place = col_index * local_len + jnp.arange(local_len, dtype=jnp.int32)
    same = doc.astype(bf16)[:, :, None] == doc_all[:, None, :]
    causal = jnp.arange(full_len, dtype=jnp.int32)[None, :] <= place[:, None]
    allowed = jnp.tile(same & causal[None], (1, group, 1))[:, None]
    scores = dot("shrd,skhd->shrk", query_grid, key_all) * scale
    scores = jnp.where(allowed, scores, masked_score)
    weights = jnp.exp(scores - jnp.max(scores, axis=-1, keepdims=True))
    weights = jnp.where(allowed, weights, 0.0)
    probs = (weights / jnp.sum(weights, axis=-1, keepdims=True)).astype(bf16)
    heads = from_grid(dot("shrk,skhd->shrd", probs, value_all)).astype(bf16)
    attn = sum_row(kernels, 2, dot("tk,bk->tb", heads, out_weights).astype(bf16))
    middle = x + attn.astype(f32)

    inv_second = rms_scale(middle)
    base_second = middle * inv_second
    h2 = (base_second * gain_two).astype(bf16)
    row_index = lax.axis_index("row")
    probs_router = jax.nn.softmax(dot("td,de->te", h2, router), axis=-1)
    picked = jnp.where(mask, probs_router, 0.0)
    pick_total = jnp.sum(picked, axis=-1, keepdims=True)
    gate = picked / pick_total
    if kernels:
        rank_own = lax.dynamic_slice_in_dim(rank_all, col_index * exp_local, exp_local, 2)
        rank_own = rank_own.astype(f32)
        part_out, back_full, gate_dots, shared_share, *expert_grads = experts_kernels(
            cols,
            3,
            capacity,
            h2,
            grad_all,
            expert_gate,
            expert_up,
            expert_down,
            shared_weights,
            jnp.swapaxes(rank_own, 1, 2),
            rank_own,
            gate.T,
        )
    else:
        part_out, back_full, gate_dots, shared_share, *expert_grads = experts_plain(
            h2,
            grad_all,
            expert_gate,
            expert_up,
            expert_down,
            shared_weights,
            router,
            rank_all,
            capacity,
            row_width,
        )
    back_full = back_full.astype(f32)
    shared_share = swap_col(shared_share.reshape(cols, rows_w, 3 * shared_part))
    shared_share = jnp.swapaxes(shared_share, 0, 1).astype(f32)
    share_sgate, share_sup, share_sdown = (
        shared_share[:, :, i * shared_part : (i + 1) * shared_part].reshape(rows_w, -1)
        for i in range(3)
    )

    pick_grad = gate_dots - jnp.sum(gate * gate_dots, axis=-1, keepdims=True)
    prob_grad = jnp.where(mask, pick_grad / pick_total, 0.0)
    logit_grad = probs_router * (
        prob_grad - jnp.sum(probs_router * prob_grad, axis=-1, keepdims=True)
    )
    logit_low = logit_grad.astype(bf16)
    grad_router = dot("td,te->de", h2, logit_low)

    back_full = back_full + dot("te,de->td", logit_low, router)
    grad_own = lax.dynamic_slice_in_dim(grad_all, col_index, 1, 0)[0].astype(f32)
    grad_gain_two = jnp.sum(back_full * base_second, axis=0)
    scaled_two = back_full * gain_two
    middle_grad = (
        inv_second
        * (scaled_two - base_second * jnp.mean(scaled_two * base_second, axis=-1, keepdims=True))
        + grad_own
    )
    attn_grad = middle_grad.astype(bf16)
    grad_out = dot("td,tk->dk", attn_grad, heads).astype(bf16)

    heads_grad = to_grid(dot("td,dk->tk", attn_grad, out_weights).astype(bf16))
    value_grad = dot("shrk,shrd->skhd", probs, heads_grad)
    weight_grad = dot("shrd,skhd->shrk", heads_grad, value_all)
    probs_wide = probs.astype(f32)
    delta = jnp.sum(probs_wide * weight_grad, axis=-1, keepdims=True)
    score_grad = (probs_wide * (weight_grad - delta)).astype(bf16)
    query_grad = from_grid(dot("shrk,skhd->shrd", score_grad, key_all)) * scale
    key_grad = dot("shrk,shrd->skhd", score_grad, query_grid) * scale
    kv_grad = jnp.concatenate(
        [key_grad.reshape(seqs, full_len, kv_width), value_grad.reshape(seqs, full_len, kv_width)],
        axis=2,
    ).astype(bf16)
    kv_grad = jnp.swapaxes(kv_grad.reshape(seqs, cols, local_len, 2 * kv_width), 0, 1)
    (kv_share,) = scatter_parts(
        kernels, cols, 6, ("col", 4, kv_grad.reshape(cols, toks, 2 * kv_width))
    )
    qk_grad = rotate(
        jnp.concatenate([query_grad, kv_share[:, :kv_width]], axis=1), cosine, -sine
    )
    qkv_grad = jnp.concatenate([qk_grad, kv_share[:, kv_width:]], axis=1).astype(bf16)
    first_grad = dot("tk,bk->tb", qkv_grad, qkv_weights).astype(bf16)
    first_grad = sum_row(kernels, 7, first_grad).astype(f32)
    grad_gain_one = jnp.sum(first_grad * base_first, axis=0)
    scaled_one = first_grad * gain_one
    token_grad = (
        inv_first
        * (scaled_one - base_first * jnp.mean(scaled_one * base_first, axis=-1, keepdims=True))
        + middle_grad
    )
    grad_first = jnp.concatenate(
        [
            dot("tb,tk->bk", h1, qkv_grad),
            grad_router,
            grad_gain_one[:, None],
            grad_gain_two[:, None],
            jnp.zeros((width, LANES - experts - 2), f32),
        ],
        axis=1,
    ).astype(bf16)
    out_slice, share_out, share_first = scatter_parts(
        kernels,
        cols,
        8,
        ("all", 4, part_out),
        ("col", 4, grad_out.reshape(cols, rows_w, q_width)),
        ("col", 5, grad_first.reshape(cols, rows_w, -1)),
    )
    middle_slice = lax.dynamic_slice_in_dim(middle, row_index * row_width, row_width, 1)
    block_out = (middle_slice + out_slice).astype(bf16)

    def tokens_first(a):
        return jnp.swapaxes(a.reshape(seqs, local_len, a.shape[1]), 0, 1)

    return (
        tokens_first(block_out),
        tokens_first(token_grad),
        share_first[:, qkv_width + experts],
        share_first[:, :q_width],
        share_first[:, q_width : q_width + kv_width],
        share_first[:, q_width + kv_width : qkv_width],
        share_out.T,
        share_first[:, qkv_width + experts + 1],
        share_first[:, qkv_width : qkv_width + experts],
        share_sgate,
        share_sup,
        share_sdown.T,
        *expert_grads,
    )


def solution(mesh):
    in_specs = (
        P("col", None, None),
        P("col", None),
        P("col", None, None),
        P("col"),
        P("col", "row"),
        P("col", "row"),
        P("col", "row"),
        P("row", "col"),
        P("col"),
        P("col", None),
        P("col", "row"),
        P("col", "row"),
        P("row", "col"),
        P("col", None, "row"),
        P("col", None, "row"),
        P("col", "row", None),
        P("col", None, "row"),
    )
    out_specs = (
        P("col", None, "row"),
        P("col", None, None),
        P("col"),
        P("col", "row"),
        P("col", "row"),
        P("col", "row"),
        P("row", "col"),
        P("col"),
        P("col", None),
        P("col", "row"),
        P("col", "row"),
        P("row", "col"),
        P("col", None, "row"),
        P("col", None, "row"),
        P("col", "row", None),
    )
    return jax.shard_map(
        on_device, mesh=mesh, in_specs=in_specs, out_specs=out_specs, check_vma=False
    )
```

time: 1130 us -> 831 us (0.74)
  matrix products: 227 us -> 36 us
  Pallas kernels: 711 us -> 644 us
  other arithmetic: 52.7 us -> 34.5 us
  blocking collectives: 12.4 us -> 0 us
    dot_general x36 -> x16, matrix products: 226 us -> 36 us  [dot(): return jnp.einsum(form, left, right, preferred_element_type=f32)]
    pallas_call x7 -> x5, Pallas kernels: 672 us -> 605 us  [the longest x1 219 us: experts_call(): pl.pallas_call(functools.partial(experts_kernel, cols, capacity), out_sha...]
    convert_element_type x2 -> x1, local copies, waits for them, and re-layouts: 17.7 us -> 0.15 us  [on_device(): rank.astype(bf16)]
    unnamed x196 -> x125, local copies, waits for them, and re-layouts: 20.4 us -> 35.4 us
    psum x1 -> x0, blocking collectives: 12.4 us -> none  [on_device(): gate_dots = lax.psum(swap_col(token_dots), 'row')]
    div x1, other arithmetic: 12.8 us -> 0.63 us  [on_device(): gate = picked / pick_total]
  transfers between devices with their start and end apart: 2 -> 1, of which waited for: 0 -> 0; matrix products, arithmetic and copies ran while one was open for 21% -> 9% of each run, Pallas kernels for 30% -> 24%
where the time goes in v2:
time: 831 us; the launch traced here: 821 us
  Pallas kernels  644 us (77%)
  local copies, waits for them, and re-layouts  98.2 us (12%)
  matrix products  36 us (4%)
  other arithmetic  34.5 us (4%)
    pallas_call x1, Pallas kernels, experts_call(): pl.pallas_call(functools.partial(experts_kernel, cols, capacity), out_sha...  219 us
    pallas_call x2, Pallas kernels, gather(): pl.pallas_call(functools.partial(gather_kernel, cols, kinds, pieces), out...  213 us
    pallas_call x2, Pallas kernels, scatter(): pl.pallas_call(functools.partial(scatter_kernel, cols, [kind for kind, _,...  173 us
    pallas_call x2, Pallas kernels, sum_row_call(): pl.pallas_call(sum_row_kernel, out_shape=jax.ShapeDtypeStruct(part.shape,...  39 us
    dot_general x16, matrix products, dot(): return jnp.einsum(form, left, right, preferred_element_type=f32)  36 us
    unnamed x125, local copies, waits for them, and re-layouts  35.4 us
  transfers between devices with their start and end apart: 1, of which 0 were waited for; matrix products, arithmetic and copies ran while one was open for 9% of the time, Pallas kernels for 24%

profile of v2, /device:TPU:10, one launch (start us, length us, event | category | flops | bytes accessed | tf_op | source)
XLA Modules:
  0.0 821.3 jit_solution(17285198325121880233)
XLA Ops:
  0.7 3.8 convert_bitcast_fusion.1
  10.9 2.2 maximum_bitcast_fusion.refs_2_
  14.5 183.5 %gather_0.1 = (bf16[8,320,1024]{2,1,0:T(8,128)(2,1)}, bf16[8,320,640]{2,1,0:T(8,128)(2,1)}, bf16[8,320,288]{2,1,0:T(8,128)(2,1)}, bf16[8,256,2560]{2,1,0:T(8,128)(2,1)}) custom-call(bf16[320,1024]{1,0:T(8,128)(2,1)} %concatenate.40.refs_0_, bf16[320,640]{1,0:T(8,128)(2,1)} %bitcast.429, bf16[8,320,288]{2,1,0:T(8,128)(2,1)} %maximum_bitcast_fusion.refs_2_, ...), custom_call_target="tpu_custom_call" | custom-call | tf_op jit(solution)/shard_map/gather_0/pallas_call | solution.py:269
  197.9 2.6 fusion.104
  200.8 2.2 copy.211
  204.8 3.8 fusion.5
  218.1 29.1 %gather_1.1 = bf16[8,256,384]{2,1,0:T(8,128)(2,1)} custom-call(bf16[256,384]{1,0:T(8,128)(2,1)} %concatenate.42.refs_0_), custom_call_target="tpu_custom_call" | custom-call | tf_op jit(solution)/shard_map/gather_1/pallas_call | solution.py:269
  259.1 3.3 convolution_convert_fusion.1.part
  262.4 18.7 %sum_row_2.1 = bf16[256,2560]{1,0:T(8,128)(2,1)S(1)} custom-call(bf16[256,2560]{1,0:T(8,128)(2,1)S(1)} %convolution_convert_fusion.1.part), custom_call_target="tpu_custom_call" | custom-call | tf_op jit(solution)/shard_map/sum_row_2/pallas_call | solution.py:511
  283.2 2.1 multiply_convert_fusion.h2
  285.3 2.0 fusion.109
  290.3 3.5 copy.231
  295.1 2.3 copy.232.w_shared
  297.4 219.0 %experts_3.1 = (bf16[8,256,2560]{2,1,0:T(8,128)(2,1)}, bf16[256,2560]{1,0:T(8,128)(2,1)}, f32[2,2560,384]{2,1,0:T(8,128)}, f32[2,2560,384]{2,1,0:T(8,128)}, f32[...) custom-call(bf16[256,2560]{1,0:T(8,128)(2,1)} %copy-done.7, ...), custom_call_target="tpu_custom_call" | custom-call | tf_op jit(solution)/shard_map/experts_3/pallas_call | solution.py:1112
  516.4 2.7 copy.257
  522.0 6.8 all-to-all-start
  529.8 4.0 multiply_reduce_fusion
  533.8 3.0 convert_add_fusion
  541.9 2.8 fusion.1
  553.9 25.5 %scatter_6.1 = f32[256,256]{1,0:T(8,128)} custom-call(bf16[8,256,256]{2,1,0:T(8,128)(2,1)} %bitcast.398), custom_call_target="tpu_custom_call" | custom-call | tf_op jit(solution)/shard_map/scatter_6/pallas_call | solution.py:459
  583.2 3.8 fusion.7.part
  587.1 20.3 %sum_row_7.1 = bf16[256,2560]{1,0:T(8,128)(2,1)S(1)} custom-call(bf16[256,2560]{1,0:T(8,128)(2,1)S(1)} %fusion.7.part), custom_call_target="tpu_custom_call" | custom-call | tf_op jit(solution)/shard_map/sum_row_7/pallas_call | solution.py:511
  614.1 5.2 convolution_convert_fusion.3
  620.2 9.8 %concatenate.51.refs_2_ = bf16[8,320,1024]{2,1,0:T(8,128)(2,1)} concatenate(bf16[8,320,896]{2,1,0:T(8,128)(2,1)} %convolution_convert_fusion.3, bf16[8,320,16]{2,1,0:T(8,128)(2,1)S(1)} %bitcast.405, bf16[8,320,1]{2,1,0:T(8,128)(2,1)S(1)} %concatenate.52, bf16[8,320,1]{2,1,0:T(8,128)(2,1)S(1)} %concatenate.53, bf16[8,320,110]{2,1,0:T(8,128)(2,1)} %broadcast_in_dim.30), dimensions={2} | concatenate | bytes 10485760 | tf_op jit(solution)/shard_map/concatenate | solution.py:1539
  630.0 4.7 convolution_convert_fusion
  634.7 147.8 %scatter_8.1 = (f32[256,640]{1,0:T(8,128)}, f32[320,640]{1,0:T(8,128)}, f32[320,1024]{1,0:T(8,128)}) custom-call(bf16[8,256,2560]{2,1,0:T(8,128)(2,1)} %get-tuple-element.33.refs_0_, bf16[8,320,640]{2,1,0:T(8,128)(2,1)} %bitcast.381, bf16[8,320,1024]{2,1,0:T(8,128)(2,1)} %concatenate.51.refs_2_), custom_call_target="tpu_custom_call" | custom-call | tf_op jit(solution)/shard_map/scatter_8/pallas_call | solution.py:459
  782.5 2.1 slice.193
  785.6 3.2 fusion.14
  788.8 3.5 copy.298
  803.6 7.1 copy.308
  810.7 7.1 copy.309
  817.9 3.2 copy.310
  (214 shorter events, 78.6 us)
Async XLA Ops:
  0.6 3.9 copy-start.13
  0.7 5.8 copy-start.31
  7.1 2.6 copy-start.39
  7.2 2.7 copy-start.30
  9.9 3.3 copy-start.33
  9.9 3.3 copy-start.37
  9.9 3.3 copy-start.38
  203.1 78.0 %copy-start = (f32[2,128,2560]{2,1,0:T(8,128)}, f32[2,128,2560]{2,1,0:T(8,128)S(1)}, u32[]{:S(2)}) copy-start(f32[2,128,2560]{2,1,0:T(8,128)S(1)} %copy.211) | copy-start | bytes 7864324
  212.6 4.6 copy-start.34
  212.7 4.6 copy-start.35
  212.7 4.6 copy-start.36
  215.3 36.2 %copy-start.15 = (bf16[2,1,5,128,128]{4,3,2,0,1:T(8,128)(2,1)}, bf16[2,1,5,128,128]{4,3,2,0,1:T(8,128)(2,1)S(1)}, u32[]{:S(2)}) copy-start(bf16[2,1,5,128,128]{4,3,2,0,1:T(8,128)(2,1)S(1)} %copy.228) | copy-start | bytes 983044
  247.1 3.9 copy-start.42
  250.6 4.1 copy-start.9
  259.1 3.3 copy-start.22
  283.2 4.8 copy-start.19
  285.3 5.0 copy-start.7
  522.0 7.8 copy-start.2
  522.0 274.9 %all-to-all-start = ((bf16[8,320,288]{1,2,0:T(8,128)(2,1)}), bf16[8,320,288]{1,2,0:T(8,128)(2,1)}, u32[]{:S(2)}, u32[]{:S(2)}) async-start(bf16[8,320,288]{1,2,0:T(8,128)(2,1)} %copy.258), calls=%async_computation | async-start | bytes 3538944 | tf_op jit(solution)/shard_map/all_to_all | solution.py:82
  533.8 4.5 copy-start.14
  538.3 3.6 copy-start.10
  539.4 5.3 slice-start
  541.9 3.0 slice-start.1
  552.2 28.1 %copy-start.24 = (f32[128,64]{1,0:T(8,128)S(1)}, f32[128,64]{1,0:T(8,128)}, u32[]{:S(2)}) copy-start(f32[128,64]{1,0:T(8,128)} %copy-done.23) | copy-start | bytes 98308
  552.2 28.1 %copy-start.26 = (f32[128,64]{1,0:T(8,128)S(1)}, f32[128,64]{1,0:T(8,128)}, u32[]{:S(2)}) copy-start(f32[128,64]{1,0:T(8,128)} %copy-done.25) | copy-start | bytes 98308
  587.1 20.3 %copy-start.1 = (f32[2,128,2560]{2,1,0:T(8,128)S(1)}, f32[2,128,2560]{2,1,0:T(8,128)}, u32[]{:S(2)}) copy-start(f32[2,128,2560]{2,1,0:T(8,128)} %copy-done) | copy-start | bytes 7864324
  607.4 4.0 copy-start.12
  614.1 6.1 copy-start.17
  788.8 3.5 copy-start.28
  788.8 6.5 copy-start.20
  803.6 14.2 %slice-start.2 = ((s8[7864320]{0:T(1024)(128)(4,1)}), s8[4194304]{0:T(1024)(128)(4,1)S(1)}, s32[]{:S(2)}) async-start(s8[7864320]{0:T(1024)(128)(4,1)} %bitcast.384), calls=%async_computation.3 | async-start | bytes 8388608
  810.7 7.1 slice-start.3
  (16 other events, 31.6 us)

commit v3 on v2

--- a/solution.py
+++ b/solution.py
@@ -554,6 +554,404 @@
     if isinstance(index, int):
         return pl.ds(index * tile, tile)
     return pl.ds(pl.multiple_of(index * tile, tile), tile)
+
+
+class Line:
+    def __init__(self, net, items, direct=(), direct_from=0):
+        self.net, self.items, self.direct, self.direct_from = net, items, list(direct), direct_from
+        self.other_row = 2 * (1 - net.outer) + net.core
+        self.along_z, self.along_y, self.along_x, self.to_core = {}, {}, {}, {}
+        self.moved = []
+        self.now = 0
+
+    def in_chip(self, q, step, other, source, slot):
+        if self.items[q][2]:
+            self.along_x[q, step, other] = self.net.send(source, slot, self.net.x_peer())
+            self.to_core[q, step, other] = self.net.send(source, slot, self.net.core_peer())
+
+    def start(self, q):
+        net = self.net
+        source, slot_of, _ = self.items[q]
+        slot = slot_of(net.me, net.row)
+        for step in reversed(range(1, net.high_count)):
+            self.along_z[q, step] = net.send(source, slot, net.z_peer(step))
+        self.along_y[q, 0] = net.send(source, slot, net.y_peer())
+        self.in_chip(q, 0, False, source, slot)
+
+    def after_z(self, q):
+        net = self.net
+        for step in reversed(range(1, net.high_count)):
+            self.along_z[q, step].wait_recv()
+            slot = self.items[q][1](net.block(step), net.row)
+            self.along_y[q, step] = net.send(slot, slot, net.y_peer())
+            self.in_chip(q, step, False, slot, slot)
+
+    def after_y(self, q):
+        net = self.net
+        for step in range(net.high_count):
+            self.along_y[q, step].wait_recv()
+            slot = self.items[q][1](net.block(step, True), net.row)
+            self.in_chip(q, step, True, slot, slot)
+
+    def after_x(self, q):
+        net = self.net
+        if self.items[q][2]:
+            for other in (False, True):
+                for step in range(net.high_count):
+                    self.along_x[q, step, other].wait_recv()
+                    slot = self.items[q][1](net.block(step, other), self.other_row)
+                    self.moved.append(net.send(slot, slot, net.core_peer()))
+
+    def tick(self, count=1):
+        net = self.net
+        for _ in range(count):
+            now, self.now = self.now, self.now + 1
+            if now < len(self.items):
+                if now >= 2:
+                    for step in range(1, net.high_count):
+                        net.left(self.along_z[now - 2, step])
+                self.start(now)
+            if now >= self.direct_from and self.direct:
+                self.moved.append(net.send(*self.direct.pop(0)))
+            for stage, lag in ((self.after_z, 1), (self.after_y, 2), (self.after_x, 3)):
+                if 0 <= now - lag < len(self.items):
+                    stage(now - lag)
+
+    def drain(self):
+        while self.now < len(self.items) + 3 or self.direct:
+            self.tick()
+        for copy in [*self.moved, *self.to_core.values()]:
+            copy.wait_recv()
+
+
+def front_kernel(
+    cols,
+    experts,
+    tokens,
+    query,
+    key,
+    value,
+    misc,
+    out_own,
+    shared_own,
+    grad_own,
+    table_row,
+    table_col,
+    doc_col,
+    cosine,
+    sine,
+    weights,
+    out_weights,
+    shared_all,
+    grad_all,
+    rows_all,
+    cols_all,
+    h1,
+    q_low,
+    kv_all,
+    probs,
+    heads,
+    attn,
+    h2,
+    gate,
+    router_probs,
+    gains,
+    inverse,
+    kv_low,
+    keys,
+    values,
+    bias,
+    partial,
+    from_core,
+    to_x,
+    from_x,
+    send_sems,
+    recv_sems,
+    local_sems,
+):
+    net = Net(cols, send_sems, recv_sems)
+    toks, width = tokens.shape
+    size = HEAD_DIM
+    q_width = q_low.shape[1]
+    group = q_width // size
+    rows_w = query.shape[0]
+    seqs = probs.shape[0]
+    local_len = toks // seqs
+    full_len = local_len * cols
+    scale = 1.0 / math.sqrt(size)
+    mine = pl.ds(pl.multiple_of(net.me * rows_w, 16), rows_w)
+
+    copies = []
+
+    def local_copy(source, target):
+        copy = pltpu.make_async_copy(source, target, local_sems.at[len(copies)])
+        copy.start()
+        copies.append(copy)
+
+    local_copy(query, weights.at[mine, pl.ds(0, q_width)])
+    local_copy(key, weights.at[mine, pl.ds(q_width, size)])
+    local_copy(value, weights.at[mine, pl.ds(q_width + size, size)])
+    local_copy(misc, weights.at[mine, pl.ds(q_width + 2 * size, LANES)])
+    first = len(copies)
+    local_copy(out_own, out_weights.at[mine])
+    local_copy(shared_own.at[net.me], shared_all.at[net.me])
+    part = grad_own.shape[1]
+    local_copy(
+        grad_own, grad_all.at[net.me, :, pl.ds(pl.multiple_of(net.row * part, LANES), part)]
+    )
+    local_copy(table_row, rows_all.at[net.me])
+    local_copy(table_col, cols_all.at[net.me])
+    net.greet([net.col_peer(step) for step in range(1, cols)] + row_peers(net))
+    for copy in copies[:first]:
+        copy.wait()
+
+    def weight_slot(target, start, count):
+        def slot(block, row):
+            return target.at[pl.ds(pl.multiple_of(block * rows_w + start, 16), count)]
+
+        return slot
+
+    def grad_slot(start, count):
+        def slot(block, row):
+            return grad_all.at[
+                block, pl.ds(start, count), pl.ds(pl.multiple_of(row * part, LANES), part)
+            ]
+
+        return slot
+
+    items = [(table_row, lambda block, row: rows_all.at[block], False)]
+    pieces, out_pieces, grad_pieces = 5, 4, 4
+    count = rows_w // pieces
+    for q in range(pieces):
+        slot = weight_slot(weights, q * count, count)
+        items.append((slot(net.me, net.row), slot, False))
+    ready_weights = len(items) + 2
+    out_items, grad_items = [], []
+    count = rows_w // out_pieces
+    for q in range(out_pieces):
+        slot = weight_slot(out_weights, q * count, count)
+        out_items.append((out_own.at[pl.ds(q * count, count)], slot, False))
+    count = toks // grad_pieces
+    for q in range(grad_pieces):
+        grad_items.append((grad_own.at[pl.ds(q * count, count)], grad_slot(q * count, count), True))
+    items += out_items[:2]
+    for q in range(2, out_pieces):
+        items += [grad_items[q - 2], out_items[q]]
+    ready_out = len(items) + 2
+    items += grad_items[out_pieces - 2 :]
+    items.append((table_col, lambda block, row: cols_all.at[block], False))
+    direct = []
+    for step in range(1, cols):
+        block = lax.rem(net.me + step, cols)
+        direct.append((shared_own.at[block], shared_all.at[net.me], net.col_peer(step)))
+    line = Line(net, items, direct, ready_weights - 2)
+
+    line.tick(2)
+    copies[first + 3].wait()
+
+    def chunks(body, rows=32):
+        def step(index, carry):
+            body(pl.ds(pl.multiple_of(index * rows, rows), rows))
+            return carry
+
+        lax.fori_loop(0, toks // rows, step, 0)
+
+    def measure_first(at):
+        x = tokens[at, :].astype(f32)
+        total = jnp.sum(x * x, axis=1, keepdims=True)
+        inverse[at, :] = jnp.broadcast_to(lax.rsqrt(total / width + norm_eps), (32, LANES))
+
+    chunks(measure_first)
+    line.tick(ready_weights - line.now)
+
+    start = q_width + 2 * size
+    for tile in range(width // TILE):
+        at = pl.ds(tile * TILE, TILE)
+        turned = jnp.transpose(weights[at, start : start + LANES].astype(f32))
+        gains[:, at] = turned[experts : experts + 8]
+
+    def norm_first(at):
+        x = tokens[at, :].astype(f32) * inverse[at, 0:1]
+        h1[at, :] = (x * gains[0:1, :]).astype(bf16)
+
+    chunks(norm_first)
+    line.tick()
+    heads_all = group + 2
+    for head in range(heads_all - 1, -1, -1):
+        raw = dot_nn(h1[...], weights[:, head * size : (head + 1) * size])
+        if head <= group:
+            raw = raw * cosine[...] + pltpu.roll(raw, size // 2, 1) * sine[...]
+        if head < group:
+            q_low[:, head * size : (head + 1) * size] = raw.astype(bf16)
+        else:
+            kv_low[:, (head - group) * size : (head - group + 1) * size] = raw.astype(bf16)
+        if head == group:
+            kv_all[net.me] = kv_low[...]
+
+            def kv_slot(s):
+                rows = pl.ds(s * local_len, local_len)
+                return lambda block, row: kv_all.at[block, rows]
+
+            kv_line = Line(
+                net,
+                [
+                    (kv_low.at[pl.ds(s * local_len, local_len)], kv_slot(s), False)
+                    for s in range(seqs)
+                ],
+            )
+            kv_line.tick()
+        if head == group // 2:
+            kv_line.tick()
+    line.tick()
+    kv_line.tick()
+
+    for s in range(seqs):
+        if s:
+            kv_line.tick()
+        rows = pl.ds(s * local_len, local_len)
+        place = lax.broadcasted_iota(jnp.int32, (local_len, local_len), 0)
+        lane = lax.broadcasted_iota(jnp.int32, (local_len, local_len), 1)
+        for c in range(cols):
+            at = pl.ds(c * local_len, local_len)
+            keys[at, :] = kv_all[c, rows, :size]
+            values[at, :] = kv_all[c, rows, size:]
+            same = doc_col[rows, :] == rows_all[c, experts : experts + 1, rows]
+            ahead = (c - net.me) * local_len
+            allowed = same & (lane + ahead <= place)
+            bias[:, at] = jnp.where(allowed, 0.0, masked_score)
+
+        def attend(g, carry, s=s, rows=rows):
+            at = pl.ds(pl.multiple_of(g * size, size), size)
+            scores = dot_nt(q_low[rows, at], keys[...]) * scale + bias[...]
+            weight = jnp.exp(scores - jnp.max(scores, axis=1, keepdims=True))
+            p = (weight / jnp.sum(weight, axis=1, keepdims=True)).astype(bf16)
+            probs[s, g] = p
+            heads[rows, at] = dot_nn(p, values[...]).astype(bf16)
+            return carry
+
+        lax.fori_loop(0, group, attend, 0)
+        if line.now < ready_out:
+            line.tick()
+    line.tick(max(0, ready_out - line.now))
+    copies[first].wait()
+
+    pieces = from_core.shape[0]
+    piece_rows = from_core.shape[1]
+
+    def row_piece(core, i):
+        return pl.ds(
+            pl.multiple_of((core * pieces + i) * piece_rows, piece_rows), piece_rows
+        )
+
+    half = pieces * piece_rows
+    across = []
+    for core in (1 - net.core, net.core):
+        at_rows = pl.ds(pl.multiple_of(core * half, half), half)
+        for tile in range(width // TILE):
+            at = pl.ds(tile * TILE, TILE)
+            partial[at_rows, at] = dot_nt(heads[at_rows, :], out_weights[at, :]).astype(bf16)
+        if not across:
+            across = [
+                net.send(partial.at[row_piece(1 - net.core, i)], from_core.at[i], net.core_peer())
+                for i in range(pieces)
+            ]
+    along, back = [], []
+    for i in range(pieces):
+        across[i].wait_recv()
+        add_rows(to_x.at[i], [partial.at[row_piece(net.core, i)], from_core.at[i]])
+        along.append(net.send(to_x.at[i], from_x.at[i], net.x_peer()))
+    line.tick()
+    for i in range(pieces):
+        along[i].wait_recv()
+        at = row_piece(net.core, i)
+        add_rows(attn.at[at], [to_x.at[i], from_x.at[i]])
+        back.append(net.send(attn.at[at], attn.at[at], net.core_peer()))
+    line.tick()
+    for copy in back:
+        copy.wait_recv()
+
+    def norm_second(at):
+        x = tokens[at, :].astype(f32) + attn[at, :].astype(f32)
+        total = jnp.sum(x * x, axis=1, keepdims=True)
+        h2[at, :] = (x * lax.rsqrt(total / width + norm_eps) * gains[1:2, :]).astype(bf16)
+
+    chunks(norm_second)
+    line.tick()
+    logits = dot_nn(h2[...], weights[:, start : start + LANES])
+    lane = lax.broadcasted_iota(jnp.int32, (toks, LANES), 1)
+    logits = jnp.where(lane < experts, logits, masked_score)
+    weight = jnp.exp(logits - jnp.max(logits, axis=1, keepdims=True))
+    chance = weight / jnp.sum(weight, axis=1, keepdims=True)
+    router_probs[...] = chance
+    picked = jnp.where((table_col[...] > 0) & (lane < experts), chance, 0.0)
+    gate[...] = picked / jnp.sum(picked, axis=1, keepdims=True)
+    line.drain()
+    kv_line.drain()
+    for copy in [*copies[first + 1 : first + 3], copies[first + 4]]:
+        copy.wait()
+    net.finish()
+
+
+def front_call(
+    cols, collective_id, experts, tokens, query, key, value, misc, out_own, shared_own, grad_own,
+    table_row, table_col, doc_col, cosine, sine, seqs,
+):
+    toks, width = tokens.shape
+    q_width = query.shape[1]
+    size = HEAD_DIM
+    local_len = toks // seqs
+    vmem, any_space = pl.BlockSpec(memory_space=pltpu.VMEM), pl.BlockSpec(memory_space=pl.ANY)
+
+    def shape(*dims, dtype=bf16):
+        return jax.ShapeDtypeStruct(dims, dtype)
+
+    pieces = 4
+    piece = (pieces, toks // 2 // pieces, width)
+    copies = 320
+    return pl.pallas_call(
+        functools.partial(front_kernel, cols, experts),
+        out_shape=[
+            shape(width, q_width + 2 * size + LANES),
+            shape(width, q_width),
+            shape(*shared_own.shape),
+            shape(cols, toks, width),
+            shape(cols, *table_row.shape, dtype=f32),
+            shape(cols, *table_col.shape),
+            shape(toks, width),
+            shape(toks, q_width),
+            shape(cols, toks, 2 * size),
+            shape(seqs, q_width // size, local_len, cols * local_len),
+            shape(toks, q_width),
+            shape(toks, width),
+            shape(toks, width),
+            shape(toks, LANES, dtype=f32),
+            shape(toks, LANES, dtype=f32),
+        ],
+        in_specs=[vmem] + [any_space] * 7 + [vmem] * 5,
+        out_specs=[vmem, vmem, any_space, any_space] + [vmem] * 11,
+        scratch_shapes=[
+            pltpu.VMEM((8, width), f32),
+            pltpu.VMEM((toks, LANES), f32),
+            pltpu.VMEM((toks, 2 * size), bf16),
+            pltpu.VMEM((cols * local_len, size), bf16),
+            pltpu.VMEM((cols * local_len, size), bf16),
+            pltpu.VMEM((local_len, cols * local_len), f32),
+            pltpu.VMEM((toks, width), bf16),
+            pltpu.VMEM(piece, bf16),
+            pltpu.VMEM(piece, bf16),
+            pltpu.VMEM(piece, bf16),
+            pltpu.SemaphoreType.DMA((copies,)),
+            pltpu.SemaphoreType.DMA((copies,)),
+            pltpu.SemaphoreType.DMA((16,)),
+        ],
+        compiler_params=pltpu.CompilerParams(
+            collective_id=collective_id, has_side_effects=True, vmem_limit_bytes=48 << 20
+        ),
+        name=f"front_{collective_id}",
+    )(
+        tokens, query, key, value, misc, out_own, shared_own, grad_own,
+        table_row, table_col, doc_col, cosine, sine,
+    )
 
 
 def experts_kernel(
@@ -1341,7 +1739,7 @@
     capacity = max(2, toks * top * 4 // (3 * experts))
     shared_part = shared_gate_matrix.shape[1] // cols
     scale = 1.0 / math.sqrt(size)
-    kernels = fits(cols, toks, width)
+    kernels = fits(cols, toks, width) and kv_local == 1 and exp_local == 2
 
     def seq_major(a):
         return jnp.swapaxes(a, 0, 1).reshape(toks, a.shape[2])
@@ -1355,7 +1753,6 @@
         ],
         axis=1,
     )
-    first_weights = jnp.concatenate([query_matrix, key_matrix, value_matrix, misc], axis=1)
     shared_weights = jnp.concatenate(
         [
             shared_gate_matrix.reshape(rows_w, cols, shared_part),
@@ -1364,35 +1761,11 @@
         ],
         axis=2,
     )
-    first_weights, out_weights, shared_weights, grad_all = gather_parts(
-        kernels,
-        cols,
-        0,
-        ("col", 5, first_weights),
-        ("col", 4, attention_output_matrix.T),
-        ("swap", 1, jnp.swapaxes(shared_weights, 0, 1)),
-        ("all", 4, seq_major(cotangent).astype(bf16)),
-    )
-    first_weights = first_weights.reshape(width, -1)
-    out_weights = out_weights.reshape(width, q_width)
-    shared_weights = shared_weights.reshape(width, 3 * shared_part)
-    qkv_width = q_width + 2 * kv_width
-    qkv_weights = first_weights[:, :qkv_width]
-    router = first_weights[:, qkv_width : qkv_width + experts]
-    gain_one = first_weights[:, qkv_width + experts].astype(f32)
-    gain_two = first_weights[:, qkv_width + experts + 1].astype(f32)
-
-
-    x = seq_major(tokens).astype(f32)
-    inv_first = rms_scale(x)
-    base_first = x * inv_first
-    h1 = (base_first * gain_one).astype(bf16)
-    qkv = dot("tb,bk->tk", h1, qkv_weights)
+    shared_own = jnp.swapaxes(shared_weights, 0, 1)
+    grad_own = seq_major(cotangent).astype(bf16)
     cosine, sine = rope_tables(col_index * local_len, local_len, size)
     cosine, sine = jnp.tile(cosine, (seqs, 1)), jnp.tile(sine, (seqs, 1))
-    qk = rotate(qkv[:, : q_width + kv_width], cosine, sine).astype(bf16)
-    value_low = qkv[:, q_width + kv_width :].astype(bf16)
-
+    qkv_width = q_width + 2 * kv_width
     flat_routes = seq_major(routes)
     named = flat_routes[:, :, None] == jnp.arange(experts, dtype=jnp.int32)
     mask = jnp.any(named, axis=1)
@@ -1401,54 +1774,116 @@
     rank = jnp.where(mask, dot("ij,je->ie", upto, mask.astype(bf16)), 0.0)
 
     doc = jnp.transpose(segments)
-    side = jnp.concatenate(
-        [
-            rank.astype(bf16),
-            doc.reshape(toks, 1).astype(bf16),
-            jnp.zeros((toks, LANES - experts - 1), bf16),
-        ],
-        axis=1,
-    )
-    (kv_all,) = gather_parts(
-        kernels, cols, 1, ("col", 4, jnp.concatenate([qk[:, q_width:], value_low, side], axis=1))
-    )
-    rank_all = kv_all[:, :, 2 * kv_width : 2 * kv_width + experts]
+    def to_grid(flat):
+        shaped = flat.reshape(seqs, local_len, kv_local, group, size)
+        return shaped.transpose(0, 2, 3, 1, 4).reshape(seqs, kv_local, group * local_len, size)
+
+    def from_grid(grid):
+        shaped = grid.reshape(seqs, kv_local, group, local_len, size)
+        return shaped.transpose(0, 3, 1, 2, 4).reshape(toks, q_width)
+
+    token_rows = seq_major(tokens)
+    x = token_rows.astype(f32)
+    inv_first = rms_scale(x)
+    base_first = x * inv_first
+    if kernels:
+        table_row = jnp.concatenate([rank.T, doc.reshape(1, toks).astype(f32)], axis=0)
+        table_row = jnp.pad(table_row, ((0, -(experts + 1) % 8), (0, 0)))
+        table_col = jnp.pad(rank, ((0, 0), (0, LANES - experts))).astype(bf16)
+        (
+            first_weights,
+            out_weights,
+            shared_weights,
+            grad_all,
+            rows_all,
+            rank_all,
+            h1,
+            q_low,
+            kv_all,
+            probs,
+            heads,
+            attn,
+            h2,
+            gate,
+            probs_router,
+        ) = front_call(
+            cols,
+            0,
+            experts,
+            token_rows,
+            query_matrix,
+            key_matrix,
+            value_matrix,
+            misc,
+            attention_output_matrix.T,
+            shared_own,
+            grad_own,
+            table_row,
+            table_col,
+            doc.reshape(toks, 1).astype(f32),
+            jnp.concatenate([cosine, cosine], axis=1),
+            jnp.concatenate([-sine, sine], axis=1),
+            seqs,
+        )
+        gate, probs_router = gate[:, :experts], probs_router[:, :experts]
+    else:
+        first_weights = jnp.concatenate([query_matrix, key_matrix, value_matrix, misc], axis=1)
+        first_weights = gather_col(first_weights).reshape(width, -1)
+        out_weights = gather_col(attention_output_matrix.T).reshape(width, q_width)
+        shared_weights, grad_all = swap_col(shared_own), gather_all(grad_own)
+        gain_one = first_weights[:, qkv_width + experts].astype(f32)
+        h1 = (base_first * gain_one).astype(bf16)
+        qkv = dot("tb,bk->tk", h1, first_weights[:, :qkv_width])
+        qk = rotate(qkv[:, : q_width + kv_width], cosine, sine).astype(bf16)
+        q_low = qk[:, :q_width]
+        value_low = qkv[:, q_width + kv_width :].astype(bf16)
+        side = jnp.concatenate(
+            [
+                rank.astype(bf16),
+                doc.reshape(toks, 1).astype(bf16),
+                jnp.zeros((toks, LANES - experts - 1), bf16),
+            ],
+            axis=1,
+        )
+        kv_all = gather_col(jnp.concatenate([qk[:, q_width:], value_low, side], axis=1))
+        rank_all = kv_all[:, :, 2 * kv_width : 2 * kv_width + experts]
+    shared_weights = shared_weights.reshape(width, 3 * shared_part)
+    qkv_weights = first_weights[:, :qkv_width]
+    router = first_weights[:, qkv_width : qkv_width + experts]
+    gain_one = first_weights[:, qkv_width + experts].astype(f32)
+    gain_two = first_weights[:, qkv_width + experts + 1].astype(f32)
     kv_seq = jnp.swapaxes(kv_all.reshape(cols, seqs, local_len, -1), 0, 1)
     kv_seq = kv_seq.reshape(seqs, full_len, -1)
     key_all = kv_seq[:, :, :kv_width].reshape(seqs, full_len, kv_local, size)
     value_all = kv_seq[:, :, kv_width : 2 * kv_width].reshape(seqs, full_len, kv_local, size)
-    doc_all = kv_seq[:, :, 2 * kv_width + experts]
-
-    def to_grid(flat):
-        shaped = flat.reshape(seqs, local_len, kv_local, group, size)
-        return shaped.transpose(0, 2, 3, 1, 4).reshape(seqs, kv_local, group * local_len, size)
-
-    def from_grid(grid):
-        shaped = grid.reshape(seqs, kv_local, group, local_len, size)
-        return shaped.transpose(0, 3, 1, 2, 4).reshape(toks, q_width)
-
-    query_grid = to_grid(qk[:, :q_width])
-    place = col_index * local_len + jnp.arange(local_len, dtype=jnp.int32)
-    same = doc.astype(bf16)[:, :, None] == doc_all[:, None, :]
-    causal = jnp.arange(full_len, dtype=jnp.int32)[None, :] <= place[:, None]
-    allowed = jnp.tile(same & causal[None], (1, group, 1))[:, None]
-    scores = dot("shrd,skhd->shrk", query_grid, key_all) * scale
-    scores = jnp.where(allowed, scores, masked_score)
-    weights = jnp.exp(scores - jnp.max(scores, axis=-1, keepdims=True))
-    weights = jnp.where(allowed, weights, 0.0)
-    probs = (weights / jnp.sum(weights, axis=-1, keepdims=True)).astype(bf16)
-    heads = from_grid(dot("shrk,skhd->shrd", probs, value_all)).astype(bf16)
-    attn = sum_row(kernels, 2, dot("tk,bk->tb", heads, out_weights).astype(bf16))
+    query_grid = to_grid(q_low)
+    if kernels:
+        probs = probs.reshape(seqs, kv_local, group * local_len, full_len)
+    else:
+        doc_all = kv_seq[:, :, 2 * kv_width + experts]
+        place = col_index * local_len + jnp.arange(local_len, dtype=jnp.int32)
+        same = doc.astype(bf16)[:, :, None] == doc_all[:, None, :]
+        causal = jnp.arange(full_len, dtype=jnp.int32)[None, :] <= place[:, None]
+        allowed = jnp.tile(same & causal[None], (1, group, 1))[:, None]
+        scores = dot("shrd,skhd->shrk", query_grid, key_all) * scale
+        scores = jnp.where(allowed, scores, masked_score)
+        weights = jnp.exp(scores - jnp.max(scores, axis=-1, keepdims=True))
+        weights = jnp.where(allowed, weights, 0.0)
+        probs = (weights / jnp.sum(weights, axis=-1, keepdims=True)).astype(bf16)
+        heads = from_grid(dot("shrk,skhd->shrd", probs, value_all)).astype(bf16)
+        attn = lax.psum(dot("tk,bk->tb", heads, out_weights).astype(bf16), "row")
     middle = x + attn.astype(f32)
 
     inv_second = rms_scale(middle)
     base_second = middle * inv_second
-    h2 = (base_second * gain_two).astype(bf16)
     row_index = lax.axis_index("row")
-    probs_router = jax.nn.softmax(dot("td,de->te", h2, router), axis=-1)
+    if not kernels:
+        h2 = (base_second * gain_two).astype(bf16)
+        probs_router = jax.nn.softmax(dot("td,de->te", h2, router), axis=-1)
     picked = jnp.where(mask, probs_router, 0.0)
     pick_total = jnp.sum(picked, axis=-1, keepdims=True)
-    gate = picked / pick_total
+    if not kernels:
+        gate = picked / pick_total
     if kernels:
         rank_own = lax.dynamic_slice_in_dim(rank_all, col_index * exp_local, exp_local, 2)
         rank_own = rank_own.astype(f32)
@@ -1462,7 +1897,7 @@
             expert_up,
             expert_down,
             shared_weights,
-            jnp.swapaxes(rank_own, 1, 2),
+            lax.dynamic_slice_in_dim(rows_all, col_index * exp_local, exp_local, 1),
             rank_own,
             gate.T,
         )

time: 831 us -> 850 us (1.023)
  Pallas kernels: 644 us -> 659 us
  local copies, waits for them, and re-layouts: 98.2 us -> 108 us
    pallas_call x2 -> x1, Pallas kernels: 213 us -> 240 us  [front_call(): pl.pallas_call(functools.partial(front_kernel, cols, experts), out_shape=...]
    pallas_call x2 -> x1, Pallas kernels: 39 us -> 18.7 us  [sum_row_call(): pl.pallas_call(sum_row_kernel, out_shape=jax.ShapeDtypeStruct(part.shape,...]
    pallas_call x1, Pallas kernels: 219 us -> 231 us  [experts_call(): pl.pallas_call(functools.partial(experts_kernel, cols, capacity), out_sha...]
    dot_general x16 -> x11, matrix products: 36 us -> 31.7 us  [dot(): return jnp.einsum(form, left, right, preferred_element_type=f32)]
    unnamed x125 -> x142, local copies, waits for them, and re-layouts: 35.4 us -> 36.8 us
  transfers between devices with their start and end apart: 1 -> 1, of which waited for: 0 -> 0; matrix products, arithmetic and copies ran while one was open for 9% -> 12% of each run, Pallas kernels for 24% -> 22%
where the time goes in v3:
time: 850 us; the launch traced here: 843 us
  Pallas kernels  659 us (78%)
  local copies, waits for them, and re-layouts  108 us (13%)
  other arithmetic  37.3 us (4%)
  matrix products  31.7 us (4%)
    pallas_call x1, Pallas kernels, front_call(): pl.pallas_call(functools.partial(front_kernel, cols, experts), out_shape=...  240 us
    pallas_call x1, Pallas kernels, experts_call(): pl.pallas_call(functools.partial(experts_kernel, cols, capacity), out_sha...  231 us
    pallas_call x2, Pallas kernels, scatter(): pl.pallas_call(functools.partial(scatter_kernel, cols, [kind for kind, _,...  169 us
    unnamed x142, local copies, waits for them, and re-layouts  36.8 us
    dot_general x11, matrix products, dot(): return jnp.einsum(form, left, right, preferred_element_type=f32)  31.7 us
    pallas_call x1, Pallas kernels, sum_row_call(): pl.pallas_call(sum_row_kernel, out_shape=jax.ShapeDtypeStruct(part.shape,...  18.7 us
  transfers between devices with their start and end apart: 1, of which 0 were waited for; matrix products, arithmetic and copies ran while one was open for 12% of the time, Pallas kernels for 22%

profile of v3, /device:TPU:10, one launch (start us, length us, event | category | flops | bytes accessed | tf_op | source)
XLA Modules:
  0.0 843.0 jit_solution(2876008491051884439)
XLA Ops:
  3.9 2.5 copy.250
  14.2 240.3 %front_0.1 = (bf16[2560,1024]{1,0:T(8,128)(2,1)}, bf16[2560,640]{1,0:T(8,128)(2,1)}, bf16[8,320,288]{2,1,0:T(8,128)(2,1)}, bf16[8,256,2560]{2,1,0:T(8,128)(2,1)}...) custom-call(bf16[256,2560]{1,0:T(8,128)(2,1)} %bitcast.235, ...), custom_call_target="tpu_custom_call" | custom-call | tf_op jit(solution)/shard_map/front_0/pallas_call | solution.py:911
  258.5 3.9 copy.263
  262.5 3.9 reshape_reshape.6
  266.4 2.8 pad.15
  269.2 4.1 copy.265.w_shared
  275.9 230.6 %experts_3.1 = (bf16[8,256,2560]{2,1,0:T(8,128)(2,1)}, bf16[256,2560]{1,0:T(8,128)(2,1)}, f32[2,2560,384]{2,1,0:T(8,128)}, f32[2,2560,384]{2,1,0:T(8,128)}, f32[...) custom-call(bf16[256,2560]{1,0:T(8,128)(2,1)} %get-tuple-element.41., ...), custom_call_target="tpu_custom_call" | custom-call | tf_op jit(solution)/shard_map/experts_3/pallas_call | solution.py:1510
  506.6 4.0 copy.293
  512.0 2.5 reshape_reshape.7
  514.6 2.9 copy.294
  517.5 5.8 all-to-all-start
  523.3 3.4 multiply_reduce_fusion.1
  529.9 3.4 convert_add_fusion
  533.3 2.8 convert_reduce_fusion
  536.9 4.4 multiply_reduce_fusion
  541.3 5.1 convert_add_fusion.1
  546.4 3.0 convolution_convert_fusion.4
  553.6 2.8 fusion
  570.7 2.4 fusion.14
  579.5 20.6 %scatter_6.1 = f32[256,256]{1,0:T(8,128)} custom-call(bf16[8,256,256]{2,1,0:T(8,128)(2,1)} %bitcast.248), custom_call_target="tpu_custom_call" | custom-call | tf_op jit(solution)/shard_map/scatter_6/pallas_call | solution.py:459
  605.6 3.8 fusion.4.part
  609.5 18.7 %sum_row_7.1 = bf16[256,2560]{1,0:T(8,128)(2,1)S(1)} custom-call(bf16[256,2560]{1,0:T(8,128)(2,1)S(1)} %fusion.4.part), custom_call_target="tpu_custom_call" | custom-call | tf_op jit(solution)/shard_map/sum_row_7/pallas_call | solution.py:511
  628.3 2.4 fusion.12
  637.1 4.7 convolution_convert_fusion
  641.9 9.9 %concatenate.54.refs_2_ = bf16[8,320,1024]{2,1,0:T(8,128)(2,1)} concatenate(bf16[8,320,896]{2,1,0:T(8,128)(2,1)} %bitcast.236, bf16[8,320,16]{2,1,0:T(8,128)(2,1)} %bitcast.251, bf16[8,320,1]{2,1,0:T(8,128)(2,1)} %concatenate.55, bf16[8,320,1]{2,1,0:T(8,128)(2,1)} %concatenate.56, bf16[8,320,110]{2,1,0:T(8,128)(2,1)S(1)} %broadcast_in_dim.18), dimensions={2} | concatenate | bytes 10485760 | tf_op jit(solution)/shard_map/concatenate | solution.py:1974
  651.8 4.7 convolution_convert_fusion.1
  656.4 148.4 %scatter_8.1 = (f32[256,640]{1,0:T(8,128)}, f32[320,640]{1,0:T(8,128)}, f32[320,1024]{1,0:T(8,128)}) custom-call(bf16[8,256,2560]{2,1,0:T(8,128)(2,1)} %get-tuple-element.47.refs_0_, bf16[8,320,640]{2,1,0:T(8,128)(2,1)} %bitcast.237, bf16[8,320,1024]{2,1,0:T(8,128)(2,1)} %concatenate.54.refs_2_), custom_call_target="tpu_custom_call" | custom-call | tf_op jit(solution)/shard_map/scatter_8/pallas_call | solution.py:459
  808.0 2.5 fusion.11
  810.6 3.5 copy.321
  825.4 7.1 copy.330
  832.5 7.1 copy.331
  839.6 3.2 copy.332
  (211 shorter events, 73.7 us)
Async XLA Ops:
  1.0 9.7 %copy-start.21 = (f32[128,64]{1,0:T(8,128)}, f32[128,64]{1,0:T(8,128)S(1)}, u32[]{:S(2)}) copy-start(f32[128,64]{1,0:T(8,128)S(1)} %get-tuple-element.203) | copy-start | bytes 98308
  256.8 9.6 %copy-start.4 = (f32[256,128]{1,0:T(8,128)}, f32[256,128]{1,0:T(8,128)S(1)}, u32[]{:S(2)}) copy-start(f32[256,128]{1,0:T(8,128)S(1)} %get-tuple-element.49) | copy-start | bytes 393220
  257.9 8.5 %copy-start.36 = (f32[256,128]{0,1:T(8,128)}, f32[256,128]{0,1:T(8,128)S(1)}, u32[]{:S(2)}) copy-start(f32[256,128]{0,1:T(8,128)S(1)} %copy.264) | copy-start | bytes 393220
  517.5 10.9 %copy-start.5 = (f32[256,128]{1,0:T(8,128)S(1)}, f32[256,128]{1,0:T(8,128)}, u32[]{:S(2)}) copy-start(f32[256,128]{1,0:T(8,128)} %copy-done.4) | copy-start | bytes 393220
  517.5 11.6 %copy-start.39 = (pred[256,16]{0,1:T(8,128)(4,1)S(1)}, pred[256,16]{0,1:T(8,128)(4,1)}, u32[]{:S(2)}) copy-start(pred[256,16]{0,1:T(8,128)(4,1)} %copy-done.38) | copy-start | bytes 12292
  517.5 12.4 %copy-start.10 = (bf16[2,128,2560]{2,1,0:T(8,128)(2,1)S(1)}, bf16[2,128,2560]{2,1,0:T(8,128)(2,1)}, u32[]{:S(2)}) copy-start(bf16[2,128,2560]{2,1,0:T(8,128)(2,1)} %copy.250) | copy-start | bytes 3932164
  517.5 301.2 %all-to-all-start = ((bf16[8,320,288]{1,2,0:T(8,128)(2,1)}), bf16[8,320,288]{1,2,0:T(8,128)(2,1)}, u32[]{:S(2)}, u32[]{:S(2)}) async-start(bf16[8,320,288]{1,2,0:T(8,128)(2,1)} %copy.294), calls=%async_computation | async-start | bytes 3538944 | tf_op jit(solution)/shard_map/all_to_all | solution.py:82
  528.3 8.5 %copy-start.43 = (f32[256]{0:T(256)}, f32[256]{0:T(256)S(1)}, u32[]{:S(2)}) copy-start(f32[256]{0:T(256)S(1)} %fusion.46) | copy-start | bytes 3076
  529.8 7.0 copy-start.45
  529.9 7.0 copy-start.15
  529.9 7.0 copy-start.54
  546.4 7.1 copy-start.1
  575.9 25.7 %copy-start.22 = (f32[128,64]{1,0:T(8,128)S(1)}, f32[128,64]{1,0:T(8,128)}, u32[]{:S(2)}) copy-start(f32[128,64]{1,0:T(8,128)} %copy-done.21) | copy-start | bytes 98308
  576.0 25.7 %copy-start.23 = (f32[256,64]{1,0:T(8,128)S(1)}, f32[256,64]{1,0:T(8,128)}, u32[]{:S(2)}) copy-start(f32[256,64]{1,0:T(8,128)} %copy.302) | copy-start | bytes 196612
  576.0 25.7 %copy-start.24 = (f32[256,64]{1,0:T(8,128)S(1)}, f32[256,64]{1,0:T(8,128)}, u32[]{:S(2)}) copy-start(f32[256,64]{1,0:T(8,128)} %copy.303) | copy-start | bytes 196612
  576.0 25.7 %copy-start.25 = (f32[256,64]{1,0:T(8,128)S(1)}, f32[256,64]{1,0:T(8,128)}, u32[]{:S(2)}) copy-start(f32[256,64]{1,0:T(8,128)} %copy.304) | copy-start | bytes 196612
  576.0 25.7 %copy-start.26 = (f32[256,64]{1,0:T(8,128)S(1)}, f32[256,64]{1,0:T(8,128)}, u32[]{:S(2)}) copy-start(f32[256,64]{1,0:T(8,128)} %copy.305) | copy-start | bytes 196612
  577.2 24.4 %copy-start.27 = (f32[256,64]{1,0:T(8,128)S(1)}, f32[256,64]{1,0:T(8,128)}, u32[]{:S(2)}) copy-start(f32[256,64]{1,0:T(8,128)} %copy.306) | copy-start | bytes 196612
  577.2 24.5 %copy-start.28 = (f32[256,64]{1,0:T(8,128)S(1)}, f32[256,64]{1,0:T(8,128)}, u32[]{:S(2)}) copy-start(f32[256,64]{1,0:T(8,128)} %copy.307) | copy-start | bytes 196612
  577.2 24.5 %copy-start.29 = (f32[256,64]{1,0:T(8,128)S(1)}, f32[256,64]{1,0:T(8,128)}, u32[]{:S(2)}) copy-start(f32[256,64]{1,0:T(8,128)} %copy.308) | copy-start | bytes 196612
  577.2 24.5 %copy-start.30 = (f32[256,64]{1,0:T(8,128)S(1)}, f32[256,64]{1,0:T(8,128)}, u32[]{:S(2)}) copy-start(f32[256,64]{1,0:T(8,128)} %copy.309) | copy-start | bytes 196612
  577.2 24.5 %copy-start.31 = (f32[256,64]{1,0:T(8,128)S(1)}, f32[256,64]{1,0:T(8,128)}, u32[]{:S(2)}) copy-start(f32[256,64]{1,0:T(8,128)} %copy.310) | copy-start | bytes 196612
  609.4 18.7 %copy-start.35 = (f32[2,128]{0,1:T(8,128)S(1)}, f32[2,128]{0,1:T(8,128)}, u32[]{:S(2)}) copy-start(f32[2,128]{0,1:T(8,128)} %multiply_reduce_fusion.1) | copy-start | bytes 3076
  609.4 18.8 %copy-start.37 = (f32[2560]{0:T(1024)S(1)}, f32[2560]{0:T(1024)}, u32[]{:S(2)}) copy-start(f32[2560]{0:T(1024)} %get-tuple-element.157) | copy-start | bytes 30724
  609.4 21.2 %copy-start.40 = (pred[256,16]{0,1:T(8,128)(4,1)S(1)}, pred[256,16]{0,1:T(8,128)(4,1)}, u32[]{:S(2)}) copy-start(pred[256,16]{0,1:T(8,128)(4,1)} %copy-done.38) | copy-start | bytes 12292
  609.4 21.2 %copy-start.44 = (f32[256]{0:T(256)S(1)}, f32[256]{0:T(256)}, u32[]{:S(2)}) copy-start(f32[256]{0:T(256)} %copy-done.43) | copy-start | bytes 3076
  609.5 21.2 %copy-start.46 = (f32[256]{0:T(256)S(1)}, f32[256]{0:T(256)}, u32[]{:S(2)}) copy-start(f32[256]{0:T(256)} %copy-done.45) | copy-start | bytes 3076
  609.5 21.2 %copy-start.51 = (f32[256]{0:T(256)S(1)}, f32[256]{0:T(256)}, u32[]{:S(2)}) copy-start(f32[256]{0:T(256)} %copy-done.50) | copy-start | bytes 3076
  628.3 6.7 copy-start.49
  810.6 6.5 copy-start.17
  825.4 14.2 %slice-start = ((s8[7864320]{0:T(1024)(128)(4,1)}), s8[4194304]{0:T(1024)(128)(4,1)S(1)}, s32[]{:S(2)}) async-start(s8[7864320]{0:T(1024)(128)(4,1)} %bitcast.240), calls=%async_computation.1 | async-start | bytes 8388608
  832.5 7.1 slice-start.1
  (26 other events, 76.5 us)

commit v4 on v3

--- a/solution.py
+++ b/solution.py
@@ -151,136 +151,6 @@
     return [net.x_peer(), net.core_peer()]
 
 
-def gather_kernel(cols, kinds, pieces, *refs):
-    count = len(kinds)
-    ins, outs = refs[:count], refs[count : 2 * count]
-    send_sems, recv_sems, local_sems = refs[2 * count :]
-    net = Net(cols, send_sems, recv_sems)
-    swaps = [i for i, kind in enumerate(kinds) if kind == "swap"]
-    peers = [net.col_peer(step) for step in range(1, cols)] if swaps else col_peers(net)
-    net.greet(peers + (row_peers(net) if "all" in kinds else []))
-    other_row = 2 * (1 - net.outer) + net.core
-
-    def place(i, block, rows, row):
-        if kinds[i] == "all":
-            part = ins[i].shape[1]
-            return outs[i].at[block, rows, pl.ds(pl.multiple_of(row * part, LANES), part)]
-        return outs[i].at[block, rows]
-
-    order = []
-    for i in sorted(range(count), key=lambda i: kinds[i] != "all"):
-        if kinds[i] != "swap":
-            rows = ins[i].shape[0] // pieces[i]
-            order += [(i, pl.ds(q * rows, rows)) for q in range(pieces[i])]
-    swap_sends = [(i, step) for i in swaps for step in range(1, cols)]
-    steps = range(net.high_count)
-    along_z, along_y, along_x, to_core, moved = {}, {}, {}, {}, []
-    locals_ = []
-    for i, kind in enumerate(kinds):
-        own = ins[i].at[net.me] if kind == "swap" else ins[i]
-        slot = outs[i].at[net.me] if kind == "swap" else place(
-            i, net.me, pl.ds(0, ins[i].shape[0]), net.row
-        )
-        local = pltpu.make_async_copy(own, slot, local_sems.at[i])
-        local.start()
-        locals_.append(local)
-
-    def swap_next():
-        if swap_sends:
-            i, step = swap_sends.pop(0)
-            block = lax.rem(net.me + step, cols)
-            moved.append(net.send(ins[i].at[block], outs[i].at[net.me], net.col_peer(step)))
-
-    def in_chip(q, step, other, source, slot):
-        if kinds[order[q][0]] == "all":
-            along_x[q, step, other] = net.send(source, slot, net.x_peer())
-            to_core[q, step, other] = net.send(source, slot, net.core_peer())
-
-    def start(q):
-        i, rows = order[q]
-        source, slot = ins[i].at[rows], place(i, net.me, rows, net.row)
-        for step in reversed(range(1, net.high_count)):
-            along_z[q, step] = net.send(source, slot, net.z_peer(step))
-        along_y[q, 0] = net.send(source, slot, net.y_peer())
-        in_chip(q, 0, False, source, slot)
-
-    def after_z(q):
-        i, rows = order[q]
-        for step in reversed(range(1, net.high_count)):
-            along_z[q, step].wait_recv()
-            slot = place(i, net.block(step), rows, net.row)
-            along_y[q, step] = net.send(slot, slot, net.y_peer())
-            in_chip(q, step, False, slot, slot)
-
-    def after_y(q):
-        i, rows = order[q]
-        for step in steps:
-            along_y[q, step].wait_recv()
-            slot = place(i, net.block(step, True), rows, net.row)
-            in_chip(q, step, True, slot, slot)
-
-    def after_x(q):
-        i, rows = order[q]
-        if kinds[i] == "all":
-            for other in (False, True):
-                for step in steps:
-                    along_x[q, step, other].wait_recv()
-                    slot = place(i, net.block(step, other), rows, other_row)
-                    moved.append(net.send(slot, slot, net.core_peer()))
-
-    for tick in range(len(order) + 3):
-        if tick < len(order):
-            if tick >= 2:
-                for step in range(1, net.high_count):
-                    net.left(along_z[tick - 2, step])
-            start(tick)
-        if tick % 2:
-            swap_next()
-        for stage, lag in ((after_z, 1), (after_y, 2), (after_x, 3)):
-            if 0 <= tick - lag < len(order):
-                stage(tick - lag)
-    while swap_sends:
-        swap_next()
-    for copy in [*moved, *to_core.values()]:
-        copy.wait_recv()
-    for local in locals_:
-        local.wait()
-    net.finish()
-
-
-def gather(cols, collective_id, *triples):
-    kinds = [kind for kind, _, _ in triples]
-    pieces = [piece for _, piece, _ in triples]
-    arrays = [array for _, _, array in triples]
-    copies = 0
-    shapes = []
-    for kind, piece, array in triples:
-        if kind == "swap":
-            shapes.append(jax.ShapeDtypeStruct(array.shape, array.dtype))
-            copies += cols
-        elif kind == "col":
-            shapes.append(jax.ShapeDtypeStruct((cols, *array.shape), array.dtype))
-            copies += cols * piece
-        else:
-            rows = lax.axis_size("row")
-            shape = (cols, array.shape[0], rows * array.shape[1])
-            shapes.append(jax.ShapeDtypeStruct(shape, array.dtype))
-            copies += 4 * cols * piece
-    return pl.pallas_call(
-        functools.partial(gather_kernel, cols, kinds, pieces),
-        out_shape=shapes,
-        in_specs=[pl.BlockSpec(memory_space=pl.ANY)] * len(triples),
-        out_specs=[pl.BlockSpec(memory_space=pl.ANY)] * len(triples),
-        scratch_shapes=[
-            pltpu.SemaphoreType.DMA((copies,)),
-            pltpu.SemaphoreType.DMA((copies,)),
-            pltpu.SemaphoreType.DMA((len(triples),)),
-        ],
-        compiler_params=pltpu.CompilerParams(collective_id=collective_id, has_side_effects=True),
-        name=f"gather_{collective_id}",
-    )(*arrays)
-
-
 def add_rows(target, terms):
     rows = target.shape[0]
     piece = 32 if rows % 32 == 0 else 16
@@ -294,237 +164,6 @@
         return carry
 
     lax.fori_loop(0, rows // piece, body, 0)
-
-
-class ScatterCol:
-    def __init__(self, net, part, rows, from_y, from_z, out):
-        self.net, self.part, self.rows = net, part, rows
-        self.from_y, self.from_z, self.out = from_y, from_z, out
-        self.order = [*range(1, net.high_count), 0]
-        self.along_y, self.along_z = {}, {}
-        self.stages = [self.send_y, self.send_z, self.last]
-
-    def send_y(self):
-        for step in self.order:
-            source = self.part.at[self.net.block_ahead(step, True), self.rows]
-            self.along_y[step] = self.net.send(
-                source, self.from_y.at[step, self.rows], self.net.y_peer()
-            )
-
-    def send_z(self):
-        for step in self.order:
-            self.along_y[step].wait_recv()
-            mine = self.part.at[self.net.block_ahead(step), self.rows]
-            slot = self.from_y.at[step, self.rows]
-            if step:
-                add_rows(slot, [mine, slot])
-                self.along_z[step] = self.net.send(
-                    slot, self.from_z.at[step - 1, self.rows], self.net.z_peer(step)
-                )
-
-    def last(self):
-        for step in range(1, self.net.high_count):
-            self.along_z[step].wait_recv()
-        terms = [
-            self.from_z.at[step - 1, self.rows] for step in range(1, self.net.high_count)
-        ]
-        mine = self.part.at[self.net.me, self.rows]
-        add_rows(self.out.at[self.rows], [mine, self.from_y.at[0, self.rows], *terms])
-
-    def clear_y(self):
-        for step in self.order:
-            self.net.left(self.along_y[step])
-
-
-class ScatterAll:
-    def __init__(self, net, part, rows, from_core, from_x, from_y, from_z, out):
-        self.net, self.part, self.rows, self.out = net, part, rows, out
-        self.from_core, self.from_x, self.from_y, self.from_z = from_core, from_x, from_y, from_z
-        self.order = [*range(1, net.high_count), 0]
-        self.blocks = [(step, True) for step in self.order]
-        self.blocks += [(step, False) for step in self.order]
-        self.across, self.onward, self.along_y, self.along_z = {}, {}, {}, {}
-        self.other_row = 2 * (1 - net.outer) + net.core
-        self.stages = [self.send_core, self.send_x, self.send_y, self.send_z, self.last]
-
-    def features(self, row):
-        width = self.out.shape[1]
-        return pl.ds(pl.multiple_of(row * width, LANES), width)
-
-    def block(self, key):
-        return self.net.block_ahead(*key)
-
-    def send_core(self):
-        net = self.net
-        for far in (1, 0):
-            outer = 1 - net.outer if far else net.outer
-            for key in self.blocks:
-                block = self.block(key)
-                features = self.features(2 * outer + 1 - net.core)
-                self.across[far, key] = net.send(
-                    self.part.at[block, self.rows, features],
-                    self.from_core.at[far, block, self.rows],
-                    net.core_peer(),
-                )
-
-    def send_x(self):
-        for key in self.blocks:
-            self.across[1, key].wait_recv()
-            block = self.block(key)
-            slot = self.from_core.at[1, block, self.rows]
-            mine = self.part.at[block, self.rows, self.features(self.other_row)]
-            add_rows(slot, [mine, slot])
-            self.onward[key] = self.net.send(
-                slot, self.from_x.at[block, self.rows], self.net.x_peer()
-            )
-
-    def send_y(self):
-        for key in self.blocks:
-            self.across[0, key].wait_recv()
-            self.onward[key].wait_recv()
-            block = self.block(key)
-            slot = self.from_core.at[0, block, self.rows]
-            mine = self.part.at[block, self.rows, self.features(self.net.row)]
-            add_rows(slot, [mine, slot, self.from_x.at[block, self.rows]])
-            step, other = key
-            if other:
-                self.along_y[step] = self.net.send(
-                    slot, self.from_y.at[step, self.rows], self.net.y_peer()
-                )
-
-    def send_z(self):
-        for step in self.order:
-            self.along_y[step].wait_recv()
-            slot = self.from_core.at[0, self.block((step, False)), self.rows]
-            add_rows(slot, [slot, self.from_y.at[step, self.rows]])
-            if step:
-                self.along_z[step] = self.net.send(
-                    slot, self.from_z.at[step - 1, self.rows], self.net.z_peer(step)
-                )
-
-    def last(self):
-        for step in range(1, self.net.high_count):
-            self.along_z[step].wait_recv()
-        terms = [
-            self.from_z.at[step - 1, self.rows] for step in range(1, self.net.high_count)
-        ]
-        mine = self.from_core.at[0, self.net.me, self.rows]
-        add_rows(self.out.at[self.rows], [mine, *terms])
-
-
-def scatter_kernel(cols, kinds, pieces, *refs):
-    count = len(kinds)
-    parts, outs, scratch = refs[:count], refs[count : 2 * count], list(refs[2 * count :])
-    send_sems, recv_sems = scratch[-2:]
-    net = Net(cols, send_sems, recv_sems)
-    net.greet(col_peers(net) + (row_peers(net) if "all" in kinds else []))
-    lines = {"all": [], "col": []}
-    for i, kind in enumerate(kinds):
-        buffers = [scratch.pop(0) for _ in range(4 if kind == "all" else 2)]
-        rows = outs[i].shape[0] // pieces[i]
-        make = ScatterAll if kind == "all" else ScatterCol
-        lines[kind] += [
-            make(net, parts[i], pl.ds(q * rows, rows), *buffers, outs[i])
-            for q in range(pieces[i])
-        ]
-    ticks = max(len(lines["all"]) + 4, len(lines["col"]) + 2)
-    for tick in range(ticks):
-        for kind in ("col", "all"):
-            line = lines[kind]
-            if kind == "col" and 2 <= tick < len(line):
-                line[tick - 2].clear_y()
-            depth = 5 if kind == "all" else 3
-            for stage in range(depth):
-                if 0 <= tick - stage < len(line):
-                    line[tick - stage].stages[stage]()
-    net.finish()
-
-
-def scatter(cols, collective_id, *triples):
-    high = cols // 2
-    scratch, outs, copies = [], [], 0
-    for kind, piece, array in triples:
-        rows, width = array.shape[1:]
-        if kind == "all":
-            width = width // lax.axis_size("row")
-            scratch += [
-                pltpu.VMEM((2, cols, rows, width), bf16),
-                pltpu.VMEM((cols, rows, width), bf16),
-            ]
-            copies += 3 * cols * piece
-        copies += cols * piece
-        scratch += [pltpu.VMEM((high, rows, width), bf16), pltpu.VMEM((high - 1, rows, width), bf16)]
-        outs.append(jax.ShapeDtypeStruct((rows, width), f32))
-    vmem = pl.BlockSpec(memory_space=pltpu.VMEM)
-    return pl.pallas_call(
-        functools.partial(
-            scatter_kernel, cols, [kind for kind, _, _ in triples], [p for _, p, _ in triples]
-        ),
-        out_shape=outs,
-        in_specs=[vmem] * len(triples),
-        out_specs=[vmem] * len(triples),
-        scratch_shapes=[
-            *scratch,
-            pltpu.SemaphoreType.DMA((copies,)),
-            pltpu.SemaphoreType.DMA((copies,)),
-        ],
-        compiler_params=pltpu.CompilerParams(
-            collective_id=collective_id, has_side_effects=True, vmem_limit_bytes=60 << 20
-        ),
-        name=f"scatter_{collective_id}",
-    )(*[array for _, _, array in triples])
-
-
-def sum_row_kernel(part, out, from_core, to_x, from_x, send_sems, recv_sems):
-    net = Net(2, send_sems, recv_sems)
-    net.greet(row_peers(net))
-    pieces = from_core.shape[0]
-    rows = from_core.shape[1]
-
-    def piece(core, i):
-        start = (core * pieces + i) * rows
-        return pl.ds(pl.multiple_of(start, rows), rows)
-
-    across = [
-        net.send(part.at[piece(1 - net.core, i)], from_core.at[i], net.core_peer())
-        for i in range(pieces)
-    ]
-    along, back = [], []
-    for i in range(pieces):
-        across[i].wait_recv()
-        add_rows(to_x.at[i], [part.at[piece(net.core, i)], from_core.at[i]])
-        along.append(net.send(to_x.at[i], from_x.at[i], net.x_peer()))
-    for i in range(pieces):
-        along[i].wait_recv()
-        mine = piece(net.core, i)
-        add_rows(out.at[mine], [to_x.at[i], from_x.at[i]])
-        back.append(net.send(out.at[mine], out.at[mine], net.core_peer()))
-    for copy in back:
-        copy.wait_recv()
-    net.finish()
-
-
-def sum_row_call(collective_id, part):
-    pieces = 4
-    rows = part.shape[0] // 2 // pieces
-    piece = (pieces, rows, part.shape[1])
-    return pl.pallas_call(
-        sum_row_kernel,
-        out_shape=jax.ShapeDtypeStruct(part.shape, bf16),
-        in_specs=[pl.BlockSpec(memory_space=pltpu.VMEM)],
-        out_specs=pl.BlockSpec(memory_space=pltpu.VMEM),
-        scratch_shapes=[
-            pltpu.VMEM(piece, bf16),
-            pltpu.VMEM(piece, bf16),
-            pltpu.VMEM(piece, bf16),
-            pltpu.SemaphoreType.DMA((3 * pieces,)),
-            pltpu.SemaphoreType.DMA((3 * pieces,)),
-        ],
-        compiler_params=pltpu.CompilerParams(
-            collective_id=collective_id, has_side_effects=True, vmem_limit_bytes=32 << 20
-        ),
-        name=f"sum_row_{collective_id}",
-    )(part)
 
 
 def dot_nn(left, right):
@@ -1586,7 +1225,6 @@
     out_part, back, g_gate, g_up, g_down, g_shared, gate_dots, *_ = experts_call(
         cols, collective_id, capacity, h2, grad_all, w_gate, w_up, w_down, padded, *tables
     )
-    gate_dots = gate_dots[:, : w_gate.shape[0]].reshape(-1, h2.shape[0]).T
     g_shared = g_shared.reshape(width, 3, -1)[:, :, :shared_part].reshape(width, -1)
     return (out_part, back, gate_dots, g_shared, g_gate, g_up, g_down)
 
@@ -1595,24 +1233,519 @@
     return cols % 2 == 0 and cols * rows * width * 2 <= 12 << 20
 
 
-def gather_parts(kernels, cols, collective_id, *triples):
-    if kernels:
-        return gather(cols, collective_id, *triples)
-    ways = {"col": gather_col, "all": gather_all, "swap": swap_col}
-    return [ways[kind](array) for kind, _, array in triples]
-
-
-def scatter_parts(kernels, cols, collective_id, *triples):
-    if kernels:
-        return scatter(cols, collective_id, *triples)
-    ways = {"col": scatter_col, "all": scatter_all}
-    return [ways[kind](array).astype(f32) for kind, _, array in triples]
-
-
-def sum_row(kernels, collective_id, part):
-    if kernels:
-        return sum_row_call(collective_id, part)
-    return lax.psum(part, "row")
+class Sum2D:
+    def __init__(self, net, source, start, count, from_y, from_z, out):
+        self.net, self.source, self.start, self.count = net, source, start, count
+        self.from_y, self.from_z, self.out = from_y, from_z, out
+        self.rows = pl.ds(start, count)
+        self.order = [*range(1, net.high_count), 0]
+        self.along_y, self.along_z = {}, {}
+
+    def mine(self, block):
+        return self.source(block, self.start, self.count)
+
+    def send_y(self):
+        for step in self.order:
+            source = self.mine(self.net.block_ahead(step, True))
+            self.along_y[step] = self.net.send(
+                source, self.from_y.at[step, self.rows], self.net.y_peer()
+            )
+
+    def send_z(self):
+        for step in self.order:
+            self.along_y[step].wait_recv()
+            slot = self.from_y.at[step, self.rows]
+            if step:
+                add_rows(slot, [self.mine(self.net.block_ahead(step)), slot])
+                self.along_z[step] = self.net.send(
+                    slot, self.from_z.at[step - 1, self.rows], self.net.z_peer(step)
+                )
+
+    def last(self):
+        for step in range(1, self.net.high_count):
+            self.along_z[step].wait_recv()
+        terms = [
+            self.from_z.at[step - 1, self.rows] for step in range(1, self.net.high_count)
+        ]
+        mine = self.mine(self.net.me)
+        add_rows(self.out.at[self.rows], [mine, self.from_y.at[0, self.rows], *terms])
+
+
+def rear_kernel(
+    cols,
+    experts,
+    out_part,
+    back,
+    gate_dots,
+    gate,
+    router_probs,
+    table_col,
+    h1,
+    h2,
+    tokens,
+    attn,
+    weights_in,
+    out_weights_in,
+    grads,
+    heads,
+    q_low,
+    kv_all,
+    probs,
+    cosine,
+    sine,
+    out_slice,
+    d_tokens,
+    share_qkv,
+    share_misc,
+    share_out,
+    weights,
+    out_weights,
+    misc,
+    misc_low,
+    grad_own,
+    gains,
+    dots,
+    logit_low,
+    low,
+    dob,
+    keys,
+    values,
+    stacked,
+    ds_all,
+    kv_grad,
+    kv_share,
+    dqkv,
+    gain_sums,
+    own,
+    from_core,
+    from_x,
+    from_y,
+    from_z,
+    kv_y,
+    kv_z,
+    out_y,
+    out_z,
+    qkv_y,
+    qkv_z,
+    misc_y,
+    misc_z,
+    row_core,
+    row_to,
+    row_from,
+    send_sems,
+    recv_sems,
+    local_sems,
+):
+    net = Net(cols, send_sems, recv_sems)
+    toks, width = back.shape
+    size = HEAD_DIM
+    q_width = q_low.shape[1]
+    group = q_width // size
+    qkv_width = q_width + 2 * size
+    seqs = probs.shape[0]
+    local_len = toks // seqs
+    rows_w = width // cols
+    piece = width // lax.axis_size("row")
+    scale = 1.0 / math.sqrt(size)
+    other_row = 2 * (1 - net.outer) + net.core
+
+    def local_copy(source, target, index):
+        copy = pltpu.make_async_copy(source, target, local_sems.at[index])
+        copy.start()
+        return copy
+
+    def features(row):
+        return pl.ds(pl.multiple_of(row * piece, LANES), piece)
+
+    loads = [
+        local_copy(weights_in, weights, 0),
+        local_copy(out_weights_in, out_weights, 1),
+        local_copy(grads.at[net.me], grad_own, 2),
+    ]
+    near_load = local_copy(out_part.at[:, :, features(net.row)], own.at[0], 3)
+    far_load = local_copy(out_part.at[:, :, features(other_row)], own.at[1], 4)
+    net.greet(col_peers(net) + row_peers(net))
+
+    pieces = 4
+    count = toks // pieces
+    order = [*range(1, net.high_count), 0]
+    keys_of = [(step, True) for step in order] + [(step, False) for step in order]
+    across, onward, along_y, along_z = {}, {}, {}, {}
+
+    def rows_of(q):
+        return pl.ds(q * count, count)
+
+    def out_core(q):
+        for far in (1, 0):
+            outer = 1 - net.outer if far else net.outer
+            for key in keys_of:
+                block = net.block_ahead(*key)
+                across[q, far, key] = net.send(
+                    out_part.at[block, rows_of(q), features(2 * outer + 1 - net.core)],
+                    from_core.at[far, block, rows_of(q)],
+                    net.core_peer(),
+                )
+
+    def out_x(q):
+        for key in keys_of:
+            across[q, 1, key].wait_recv()
+            block = net.block_ahead(*key)
+            slot = from_core.at[1, block, rows_of(q)]
+            add_rows(slot, [own.at[1, block, rows_of(q)], slot])
+            onward[q, key] = net.send(slot, from_x.at[block, rows_of(q)], net.x_peer())
+
+    def out_y_stage(q):
+        for key in keys_of:
+            across[q, 0, key].wait_recv()
+            onward[q, key].wait_recv()
+            block = net.block_ahead(*key)
+            slot = from_core.at[0, block, rows_of(q)]
+            add_rows(slot, [own.at[0, block, rows_of(q)], slot, from_x.at[block, rows_of(q)]])
+            if key[1]:
+                along_y[q, key[0]] = net.send(
+                    slot, from_y.at[key[0], rows_of(q)], net.y_peer()
+                )
+
+    def out_z_stage(q):
+        for step in order:
+            along_y[q, step].wait_recv()
+            slot = from_core.at[0, net.block_ahead(step), rows_of(q)]
+            add_rows(slot, [slot, from_y.at[step, rows_of(q)]])
+            if step:
+                along_z[q, step] = net.send(
+                    slot, from_z.at[step - 1, rows_of(q)], net.z_peer(step)
+                )
+
+    def out_last(q):
+        for step in range(1, net.high_count):
+            along_z[q, step].wait_recv()
+        terms = [from_z.at[step - 1, rows_of(q)] for step in range(1, net.high_count)]
+        add_rows(out_slice.at[rows_of(q)], [from_core.at[0, net.me, rows_of(q)], *terms])
+
+    state = {"tick": 0}
+
+    def pump(ticks=1):
+        for _ in range(ticks):
+            tick = state["tick"]
+            state["tick"] += 1
+            for lag, stage in enumerate((out_core, out_x, out_y_stage, out_z_stage, out_last)):
+                if 0 <= tick - lag < pieces:
+                    stage(tick - lag)
+
+    pump()
+    for copy in loads:
+        copy.wait()
+
+    def chunks(body, rows=32):
+        def step(index, carry):
+            body(pl.ds(pl.multiple_of(index * rows, rows), rows))
+            return carry
+
+        lax.fori_loop(0, toks // rows, step, 0)
+
+    for tile in range(width // TILE):
+        at = pl.ds(tile * TILE, TILE)
+        turned = jnp.transpose(weights[at, qkv_width : qkv_width + LANES].astype(f32))
+        gains[:, at] = turned[experts : experts + 8]
+    dots[...] = jnp.zeros_like(dots)
+    for c in range(cols):
+        dots[2 * c : 2 * c + 2, :] = gate_dots[c, 0:2, :]
+    gate_grad = jnp.transpose(dots[...])
+    lane = lax.broadcasted_iota(jnp.int32, (toks, LANES), 1)
+    mask = (table_col[...] > 0) & (lane < experts)
+    chance, gates = router_probs[...], gate[...]
+    total = jnp.sum(jnp.where(mask, chance, 0.0), axis=1, keepdims=True)
+    gate_grad = jnp.where(mask, gate_grad, 0.0)
+    pick_grad = gate_grad - jnp.sum(gates * gate_grad, axis=1, keepdims=True)
+    chance_grad = jnp.where(mask, pick_grad / total, 0.0)
+    logit_grad = chance * (chance_grad - jnp.sum(chance * chance_grad, axis=1, keepdims=True))
+    logit_low[...] = logit_grad.astype(bf16)
+    near_load.wait()
+    far_load.wait()
+    pump()
+
+    for tile in range(width // TILE):
+        at = pl.ds(tile * TILE, TILE)
+        d_tokens[:, at] = back[:, at].astype(f32) + dot_nt(
+            logit_low[...], weights[at, qkv_width : qkv_width + LANES]
+        )
+    gain_sums[...] = jnp.zeros_like(gain_sums)
+
+    def fold(values, start):
+        total = values[0:8]
+        for r in range(8, values.shape[0], 8):
+            total = total + values[r : r + 8]
+        gain_sums[start : start + 8, :] = gain_sums[start : start + 8, :] + total
+
+    def norm_second(at):
+        x = tokens[at, :].astype(f32) + attn[at, :].astype(f32)
+        inverse = lax.rsqrt(jnp.sum(x * x, axis=1, keepdims=True) / width + norm_eps)
+        base = x * inverse
+        dh = d_tokens[at, :]
+        fold(dh * base, 8)
+        scaled = dh * gains[1:2, :]
+        mean = jnp.sum(scaled * base, axis=1, keepdims=True) / width
+        middle = inverse * (scaled - base * mean) + grad_own[at, :].astype(f32)
+        d_tokens[at, :] = middle
+        low[at, :] = middle.astype(bf16)
+
+    chunks(norm_second, 16)
+    dob[...] = dot_nn(low[...], out_weights[...]).astype(bf16)
+    pump()
+    for tile in range(width // TILE):
+        at = pl.ds(tile * TILE, TILE)
+        out_weights[at, :] = dot_tn(low[:, at], heads[...]).astype(bf16)
+
+    def blocks_of(array):
+        def source(block, start, count):
+            return array.at[pl.ds(pl.multiple_of(block * rows_w + start, 16), count)]
+
+        return source
+
+    out_pieces = 4
+    out_count = rows_w // out_pieces
+    out_line = [
+        Sum2D(net, blocks_of(out_weights), q * out_count, out_count, out_y, out_z, share_out)
+        for q in range(out_pieces)
+    ]
+    out_line[0].send_y()
+    out_line[1].send_y()
+
+    kv_line = [
+        Sum2D(
+            net,
+            lambda block, start, count: kv_grad.at[block, pl.ds(start, count)],
+            s * local_len,
+            local_len,
+            kv_y,
+            kv_z,
+            kv_share,
+        )
+        for s in range(seqs)
+    ]
+    for s in range(seqs):
+        rows = pl.ds(s * local_len, local_len)
+        for c in range(cols):
+            at = pl.ds(c * local_len, local_len)
+            keys[at, :] = kv_all[c, rows, :size]
+            values[at, :] = kv_all[c, rows, size:]
+
+        def attend(g, carry, s=s, rows=rows):
+            at = pl.ds(pl.multiple_of(g * size, size), size)
+            grow = pl.ds(pl.multiple_of(g * local_len, local_len), local_len)
+            dout = dob[rows, at]
+            stacked[0, grow, :] = q_low[rows, at]
+            stacked[1, grow, :] = dout
+            p = probs[s, g]
+            p = p.astype(f32)
+            dp = dot_nt(dout, values[...])
+            delta = jnp.sum(p * dp, axis=1, keepdims=True)
+            ds = (p * (dp - delta)).astype(bf16)
+            ds_all[grow, :] = ds
+            raw = dot_nn(ds, keys[...]) * scale
+            dqkv[rows, at] = (
+                raw * cosine[rows, :] - pltpu.roll(raw, size // 2, 1) * sine[rows, :]
+            ).astype(bf16)
+            return carry
+
+        lax.fori_loop(0, group, attend, 0)
+        dk = (dot_tn(ds_all[...], stacked[0]) * scale).astype(bf16)
+        dv = dot_tn(probs[s].reshape(group * local_len, -1), stacked[1]).astype(bf16)
+        for c in range(cols):
+            kv_grad[c, rows, :size] = dk[c * local_len : (c + 1) * local_len]
+            kv_grad[c, rows, size:] = dv[c * local_len : (c + 1) * local_len]
+        kv_line[s].send_y()
+        if s == 0:
+            out_line[0].send_z()
+            pump()
+        else:
+            kv_line[s - 1].send_z()
+    kv_line[seqs - 1].send_z()
+    out_line[1].send_z()
+    out_line[2].send_y()
+    for s in range(seqs):
+        kv_line[s].last()
+    raw = kv_share[:, :size]
+    dqkv[:, q_width : q_width + size] = (
+        raw * cosine[...] - pltpu.roll(raw, size // 2, 1) * sine[...]
+    ).astype(bf16)
+    dqkv[:, q_width + size : qkv_width] = kv_share[:, size:].astype(bf16)
+
+    row_pieces, piece_rows = row_core.shape[0], row_core.shape[1]
+    half = row_pieces * piece_rows
+
+    def row_piece(core, i):
+        return pl.ds(pl.multiple_of((core * row_pieces + i) * piece_rows, piece_rows), piece_rows)
+
+    over = []
+    for core in (1 - net.core, net.core):
+        at_rows = pl.ds(pl.multiple_of(core * half, half), half)
+        for tile in range(width // TILE):
+            at = pl.ds(tile * TILE, TILE)
+            low[at_rows, at] = dot_nt(dqkv[at_rows, :], weights[at, :qkv_width]).astype(bf16)
+        if not over:
+            over = [
+                net.send(low.at[row_piece(1 - net.core, i)], row_core.at[i], net.core_peer())
+                for i in range(row_pieces)
+            ]
+
+    qkv_pieces = 5
+    qkv_count = rows_w // qkv_pieces
+    for tile in range(width // TILE):
+        at = pl.ds(tile * TILE, TILE)
+        misc[at, :] = dot_tn(h2[:, at], logit_low[...])
+        weights[at, :qkv_width] = dot_tn(h1[:, at], dqkv[...]).astype(bf16)
+    qkv_line = [
+        Sum2D(
+            net,
+            lambda block, start, count: weights.at[
+                pl.ds(pl.multiple_of(block * rows_w + start, 16), count), pl.ds(0, qkv_width)
+            ],
+            q * qkv_count,
+            qkv_count,
+            qkv_y,
+            qkv_z,
+            share_qkv,
+        )
+        for q in range(qkv_pieces)
+    ]
+    qkv_line[0].send_y()
+    along, returned = [], []
+    for i in range(row_pieces):
+        over[i].wait_recv()
+        add_rows(row_to.at[i], [low.at[row_piece(net.core, i)], row_core.at[i]])
+        along.append(net.send(row_to.at[i], row_from.at[i], net.x_peer()))
+    qkv_line[1].send_y()
+    for i in range(row_pieces):
+        along[i].wait_recv()
+        at = row_piece(net.core, i)
+        add_rows(grad_own.at[at], [row_to.at[i], row_from.at[i]])
+        returned.append(net.send(grad_own.at[at], grad_own.at[at], net.core_peer()))
+    qkv_line[0].send_z()
+    pump()
+    for copy in returned:
+        copy.wait_recv()
+
+    def norm_first(at):
+        x = tokens[at, :].astype(f32)
+        inverse = lax.rsqrt(jnp.sum(x * x, axis=1, keepdims=True) / width + norm_eps)
+        base = x * inverse
+        dh = grad_own[at, :].astype(f32)
+        fold(dh * base, 0)
+        scaled = dh * gains[0:1, :]
+        mean = jnp.sum(scaled * base, axis=1, keepdims=True) / width
+        d_tokens[at, :] = d_tokens[at, :] + inverse * (scaled - base * mean)
+
+    chunks(norm_first, 16)
+    total = [jnp.sum(gain_sums[8 * i : 8 * i + 8, :], axis=0, keepdims=True) for i in (0, 1)]
+    row_at = lax.broadcasted_iota(jnp.int32, (LANES, TILE), 0)
+    for tile in range(width // TILE):
+        at = pl.ds(tile * TILE, TILE)
+        part = slice(tile * TILE, (tile + 1) * TILE)
+        placed = jnp.where(row_at == experts, total[0][:, part], 0.0)
+        placed = jnp.where(row_at == experts + 1, total[1][:, part], placed)
+        lanes = lax.broadcasted_iota(jnp.int32, (TILE, LANES), 1)
+        misc_low[at, :] = jnp.where(lanes < experts, misc[at, :], jnp.transpose(placed)).astype(bf16)
+    misc_line = Sum2D(net, blocks_of(misc_low), 0, rows_w, misc_y, misc_z, share_misc)
+    misc_line.send_y()
+    qkv_line[2].send_y()
+    qkv_line[1].send_z()
+    out_line[2].send_z()
+    out_line[3].send_y()
+    pump()
+    misc_line.send_z()
+    qkv_line[3].send_y()
+    qkv_line[2].send_z()
+    out_line[3].send_z()
+    pump()
+    qkv_line[4].send_y()
+    qkv_line[3].send_z()
+    pump()
+    qkv_line[4].send_z()
+    pump(8)
+    for piece_sum in (*out_line, misc_line, *qkv_line):
+        piece_sum.last()
+    net.finish()
+
+
+def rear_call(
+    cols, collective_id, experts, out_part, back, gate_dots, gate, router_probs, table_col, h1, h2,
+    tokens, attn, weights, out_weights, grads, heads, q_low, kv_all, probs, cosine, sine,
+):
+    toks, width = back.shape
+    q_width = q_low.shape[1]
+    size = HEAD_DIM
+    qkv_width = q_width + 2 * size
+    seqs, group, local_len, full_len = probs.shape
+    rows_w, high = width // cols, cols // 2
+    piece = width // lax.axis_size("row")
+    row_pieces = 4
+    row_piece = (row_pieces, toks // 2 // row_pieces, width)
+    vmem, any_space = pl.BlockSpec(memory_space=pltpu.VMEM), pl.BlockSpec(memory_space=pl.ANY)
+
+    def shape(*dims, dtype=f32):
+        return jax.ShapeDtypeStruct(dims, dtype)
+
+    def sums(rows, columns):
+        return [
+            pltpu.VMEM((high, rows, columns), bf16),
+            pltpu.VMEM((high - 1, rows, columns), bf16),
+        ]
+
+    copies = 420
+    return pl.pallas_call(
+        functools.partial(rear_kernel, cols, experts),
+        out_shape=[
+            shape(toks, piece),
+            shape(toks, width),
+            shape(rows_w, qkv_width),
+            shape(rows_w, LANES),
+            shape(rows_w, q_width),
+        ],
+        in_specs=[any_space] + [vmem] * 9 + [any_space] * 3 + [vmem] * 6,
+        out_specs=[vmem] * 5,
+        scratch_shapes=[
+            pltpu.VMEM((width, qkv_width + LANES), bf16),
+            pltpu.VMEM((width, q_width), bf16),
+            pltpu.VMEM((width, LANES), f32),
+            pltpu.VMEM((width, LANES), bf16),
+            pltpu.VMEM((toks, width), bf16),
+            pltpu.VMEM((8, width), f32),
+            pltpu.VMEM((LANES, toks), f32),
+            pltpu.VMEM((toks, LANES), bf16),
+            pltpu.VMEM((toks, width), bf16),
+            pltpu.VMEM((toks, q_width), bf16),
+            pltpu.VMEM((full_len, size), bf16),
+            pltpu.VMEM((full_len, size), bf16),
+            pltpu.VMEM((2, group * local_len, size), bf16),
+            pltpu.VMEM((group * local_len, full_len), bf16),
+            pltpu.VMEM((cols, toks, 2 * size), bf16),
+            pltpu.VMEM((toks, 2 * size), f32),
+            pltpu.VMEM((toks, qkv_width), bf16),
+            pltpu.VMEM((16, width), f32),
+            pltpu.VMEM((2, cols, toks, piece), bf16),
+            pltpu.VMEM((2, cols, toks, piece), bf16),
+            pltpu.VMEM((cols, toks, piece), bf16),
+            *sums(toks, piece),
+            *sums(toks, 2 * size),
+            *sums(rows_w, q_width),
+            *sums(rows_w, qkv_width),
+            *sums(rows_w, LANES),
+            pltpu.VMEM(row_piece, bf16),
+            pltpu.VMEM(row_piece, bf16),
+            pltpu.VMEM(row_piece, bf16),
+            pltpu.SemaphoreType.DMA((copies,)),
+            pltpu.SemaphoreType.DMA((copies,)),
+            pltpu.SemaphoreType.DMA((8,)),
+        ],
+        compiler_params=pltpu.CompilerParams(
+            collective_id=collective_id, has_side_effects=True, vmem_limit_bytes=62 << 20
+        ),
+        name=f"rear_{collective_id}",
+    )(
+        out_part, back, gate_dots, gate, router_probs, table_col, h1, h2, tokens, attn, weights,
+        out_weights, grads, heads, q_low, kv_all, probs, cosine, sine,
+    )
 
 
 def experts_plain(
@@ -1825,7 +1958,6 @@
             jnp.concatenate([-sine, sine], axis=1),
             seqs,
         )
-        gate, probs_router = gate[:, :experts], probs_router[:, :experts]
     else:
         first_weights = jnp.concatenate([query_matrix, key_matrix, value_matrix, misc], axis=1)
         first_weights = gather_col(first_weights).reshape(width, -1)
@@ -1857,9 +1989,7 @@
     key_all = kv_seq[:, :, :kv_width].reshape(seqs, full_len, kv_local, size)
     value_all = kv_seq[:, :, kv_width : 2 * kv_width].reshape(seqs, full_len, kv_local, size)
     query_grid = to_grid(q_low)
-    if kernels:
-        probs = probs.reshape(seqs, kv_local, group * local_len, full_len)
-    else:
+    if not kernels:
         doc_all = kv_seq[:, :, 2 * kv_width + experts]
         place = col_index * local_len + jnp.arange(local_len, dtype=jnp.int32)
         same = doc.astype(bf16)[:, :, None] == doc_all[:, None, :]
@@ -1880,9 +2010,8 @@
     if not kernels:
         h2 = (base_second * gain_two).astype(bf16)
         probs_router = jax.nn.softmax(dot("td,de->te", h2, router), axis=-1)
-    picked = jnp.where(mask, probs_router, 0.0)
-    pick_total = jnp.sum(picked, axis=-1, keepdims=True)
-    if not kernels:
+        picked = jnp.where(mask, probs_router, 0.0)
+        pick_total = jnp.sum(picked, axis=-1, keepdims=True)
         gate = picked / pick_total
     if kernels:
         rank_own = lax.dynamic_slice_in_dim(rank_all, col_index * exp_local, exp_local, 2)
@@ -1899,7 +2028,7 @@
             shared_weights,
             lax.dynamic_slice_in_dim(rows_all, col_index * exp_local, exp_local, 1),
             rank_own,
-            gate.T,
+            gate[:, :experts].T,
         )
     else:
         part_out, back_full, gate_dots, shared_share, *expert_grads = experts_plain(
@@ -1914,7 +2043,8 @@
             capacity,
             row_width,
         )
-    back_full = back_full.astype(f32)
+    if not kernels:
+        back_full = back_full.astype(f32)
     shared_share = swap_col(shared_share.reshape(cols, rows_w, 3 * shared_part))
     shared_share = jnp.swapaxes(shared_share, 0, 1).astype(f32)
     share_sgate, share_sup, share_sdown = (
@@ -1922,73 +2052,93 @@
         for i in range(3)
     )
 
-    pick_grad = gate_dots - jnp.sum(gate * gate_dots, axis=-1, keepdims=True)
-    prob_grad = jnp.where(mask, pick_grad / pick_total, 0.0)
-    logit_grad = probs_router * (
-        prob_grad - jnp.sum(probs_router * prob_grad, axis=-1, keepdims=True)
-    )
-    logit_low = logit_grad.astype(bf16)
-    grad_router = dot("td,te->de", h2, logit_low)
-
-    back_full = back_full + dot("te,de->td", logit_low, router)
-    grad_own = lax.dynamic_slice_in_dim(grad_all, col_index, 1, 0)[0].astype(f32)
-    grad_gain_two = jnp.sum(back_full * base_second, axis=0)
-    scaled_two = back_full * gain_two
-    middle_grad = (
-        inv_second
-        * (scaled_two - base_second * jnp.mean(scaled_two * base_second, axis=-1, keepdims=True))
-        + grad_own
-    )
-    attn_grad = middle_grad.astype(bf16)
-    grad_out = dot("td,tk->dk", attn_grad, heads).astype(bf16)
-
-    heads_grad = to_grid(dot("td,dk->tk", attn_grad, out_weights).astype(bf16))
-    value_grad = dot("shrk,shrd->skhd", probs, heads_grad)
-    weight_grad = dot("shrd,skhd->shrk", heads_grad, value_all)
-    probs_wide = probs.astype(f32)
-    delta = jnp.sum(probs_wide * weight_grad, axis=-1, keepdims=True)
-    score_grad = (probs_wide * (weight_grad - delta)).astype(bf16)
-    query_grad = from_grid(dot("shrk,skhd->shrd", score_grad, key_all)) * scale
-    key_grad = dot("shrk,shrd->skhd", score_grad, query_grid) * scale
-    kv_grad = jnp.concatenate(
-        [key_grad.reshape(seqs, full_len, kv_width), value_grad.reshape(seqs, full_len, kv_width)],
-        axis=2,
-    ).astype(bf16)
-    kv_grad = jnp.swapaxes(kv_grad.reshape(seqs, cols, local_len, 2 * kv_width), 0, 1)
-    (kv_share,) = scatter_parts(
-        kernels, cols, 6, ("col", 4, kv_grad.reshape(cols, toks, 2 * kv_width))
-    )
-    qk_grad = rotate(
-        jnp.concatenate([query_grad, kv_share[:, :kv_width]], axis=1), cosine, -sine
-    )
-    qkv_grad = jnp.concatenate([qk_grad, kv_share[:, kv_width:]], axis=1).astype(bf16)
-    first_grad = dot("tk,bk->tb", qkv_grad, qkv_weights).astype(bf16)
-    first_grad = sum_row(kernels, 7, first_grad).astype(f32)
-    grad_gain_one = jnp.sum(first_grad * base_first, axis=0)
-    scaled_one = first_grad * gain_one
-    token_grad = (
-        inv_first
-        * (scaled_one - base_first * jnp.mean(scaled_one * base_first, axis=-1, keepdims=True))
-        + middle_grad
-    )
-    grad_first = jnp.concatenate(
-        [
-            dot("tb,tk->bk", h1, qkv_grad),
-            grad_router,
-            grad_gain_one[:, None],
-            grad_gain_two[:, None],
-            jnp.zeros((width, LANES - experts - 2), f32),
-        ],
-        axis=1,
-    ).astype(bf16)
-    out_slice, share_out, share_first = scatter_parts(
-        kernels,
-        cols,
-        8,
-        ("all", 4, part_out),
-        ("col", 4, grad_out.reshape(cols, rows_w, q_width)),
-        ("col", 5, grad_first.reshape(cols, rows_w, -1)),
-    )
+    if kernels:
+        out_slice, token_grad, share_qkv, share_misc, share_out = rear_call(
+            cols,
+            5,
+            experts,
+            part_out,
+            back_full,
+            gate_dots,
+            gate,
+            probs_router,
+            table_col,
+            h1,
+            h2,
+            token_rows,
+            attn,
+            first_weights,
+            out_weights,
+            grad_all,
+            heads,
+            q_low,
+            kv_all,
+            probs,
+            jnp.concatenate([cosine, cosine], axis=1),
+            jnp.concatenate([-sine, sine], axis=1),
+        )
+    else:
+        pick_grad = gate_dots - jnp.sum(gate * gate_dots, axis=-1, keepdims=True)
+        prob_grad = jnp.where(mask, pick_grad / pick_total, 0.0)
+        logit_grad = probs_router * (
+            prob_grad - jnp.sum(probs_router * prob_grad, axis=-1, keepdims=True)
+        )
+        logit_low = logit_grad.astype(bf16)
+        grad_router = dot("td,te->de", h2, logit_low)
+
+        back_full = back_full + dot("te,de->td", logit_low, router)
+        grad_own = lax.dynamic_slice_in_dim(grad_all, col_index, 1, 0)[0].astype(f32)
+        grad_gain_two = jnp.sum(back_full * base_second, axis=0)
+        scaled_two = back_full * gain_two
+        middle_grad = (
+            inv_second
+            * (scaled_two - base_second * jnp.mean(scaled_two * base_second, axis=-1, keepdims=True))
+            + grad_own
+        )
+        attn_grad = middle_grad.astype(bf16)
+        grad_out = dot("td,tk->dk", attn_grad, heads).astype(bf16)
+
+        heads_grad = to_grid(dot("td,dk->tk", attn_grad, out_weights).astype(bf16))
+        value_grad = dot("shrk,shrd->skhd", probs, heads_grad)
+        weight_grad = dot("shrd,skhd->shrk", heads_grad, value_all)
+        probs_wide = probs.astype(f32)
+        delta = jnp.sum(probs_wide * weight_grad, axis=-1, keepdims=True)
+        score_grad = (probs_wide * (weight_grad - delta)).astype(bf16)
+        query_grad = from_grid(dot("shrk,skhd->shrd", score_grad, key_all)) * scale
+        key_grad = dot("shrk,shrd->skhd", score_grad, query_grid) * scale
+        kv_grad = jnp.concatenate(
+            [key_grad.reshape(seqs, full_len, kv_width), value_grad.reshape(seqs, full_len, kv_width)],
+            axis=2,
+        ).astype(bf16)
+        kv_grad = jnp.swapaxes(kv_grad.reshape(seqs, cols, local_len, 2 * kv_width), 0, 1)
+        kv_share = scatter_col(kv_grad.reshape(cols, toks, 2 * kv_width)).astype(f32)
+        qk_grad = rotate(
+            jnp.concatenate([query_grad, kv_share[:, :kv_width]], axis=1), cosine, -sine
+        )
+        qkv_grad = jnp.concatenate([qk_grad, kv_share[:, kv_width:]], axis=1).astype(bf16)
+        first_grad = dot("tk,bk->tb", qkv_grad, qkv_weights).astype(bf16)
+        first_grad = lax.psum(first_grad, "row").astype(f32)
+        grad_gain_one = jnp.sum(first_grad * base_first, axis=0)
+        scaled_one = first_grad * gain_one
+        token_grad = (
+            inv_first
+            * (scaled_one - base_first * jnp.mean(scaled_one * base_first, axis=-1, keepdims=True))
+            + middle_grad
+        )
+        grad_first = jnp.concatenate(
+            [
+                dot("tb,tk->bk", h1, qkv_grad),
+                grad_router,
+                grad_gain_one[:, None],
+                grad_gain_two[:, None],
+                jnp.zeros((width, LANES - experts - 2), f32),
+            ],
+            axis=1,
+        ).astype(bf16)
+        out_slice = scatter_all(part_out).astype(f32)
+        share_out = scatter_col(grad_out.reshape(cols, rows_w, q_width)).astype(f32)
+        share_first = scatter_col(grad_first.reshape(cols, rows_w, -1)).astype(f32)
+        share_qkv, share_misc = share_first[:, :qkv_width], share_first[:, qkv_width:]
     middle_slice = lax.dynamic_slice_in_dim(middle, row_index * row_width, row_width, 1)
     block_out = (middle_slice + out_slice).astype(bf16)
 
@@ -1998,13 +2148,13 @@
     return (
         tokens_first(block_out),
         tokens_first(token_grad),
-        share_first[:, qkv_width + experts],
-        share_first[:, :q_width],
-        share_first[:, q_width : q_width + kv_width],
-        share_first[:, q_width + kv_width : qkv_width],
+        share_misc[:, experts],
+        share_qkv[:, :q_width],
+        share_qkv[:, q_width : q_width + kv_width],
+        share_qkv[:, q_width + kv_width :],
         share_out.T,
-        share_first[:, qkv_width + experts + 1],
-        share_first[:, qkv_width : qkv_width + experts],
+        share_misc[:, experts + 1],
+        share_misc[:, :experts],
         share_sgate,
         share_sup,
         share_sdown.T,

time: 850 us -> 751 us (0.88)
  local copies, waits for them, and re-layouts: 108 us -> 62.4 us
  matrix products: 31.7 us -> 0.8 us
  other arithmetic: 37.3 us -> 7.73 us
  Pallas kernels: 659 us -> 668 us
    dot_general x11 -> x1, matrix products: 31.7 us -> 0.8 us  [dot(): return jnp.einsum(form, left, right, preferred_element_type=f32)]
    concatenate x6 -> x0, local copies, waits for them, and re-layouts: 16.8 us -> none  [the longest x3 14.2 us: on_device(): jnp.concatenate([dot('tb,tk->bk', h1, qkv_grad), grad_router, grad_gain_o...]
    add x3 -> x0, other arithmetic: 11 us -> none  [the longest x1 5.11 us: on_device(): inv_second * (scaled_two - base_second * jnp.mean(scaled_two * base_secon...]
    pallas_call x3 -> x1, Pallas kernels: 188 us -> 198 us  [rear_call(): pl.pallas_call(functools.partial(rear_kernel, cols, experts), out_shape=[...]
    unnamed x142 -> x55, local copies, waits for them, and re-layouts: 36.8 us -> 30.6 us
  transfers between devices with their start and end apart: 1 -> 1, of which waited for: 0 -> 0; matrix products, arithmetic and copies ran while one was open for 12% -> 1% of each run, Pallas kernels for 22% -> 27%
where the time goes in v4:
time: 751 us; the launch traced here: 746 us
  Pallas kernels  668 us (89%)
  local copies, waits for them, and re-layouts  62.4 us (8%)
  other arithmetic  7.73 us (1%)
    pallas_call x1, Pallas kernels, front_call(): pl.pallas_call(functools.partial(front_kernel, cols, experts), out_shape=...  240 us
    pallas_call x1, Pallas kernels, experts_call(): pl.pallas_call(functools.partial(experts_kernel, cols, capacity), out_sha...  230 us
    pallas_call x1, Pallas kernels, rear_call(): pl.pallas_call(functools.partial(rear_kernel, cols, experts), out_shape=[...  198 us
    unnamed x55, local copies, waits for them, and re-layouts  30.6 us
  transfers between devices with their start and end apart: 1, of which 0 were waited for; matrix products, arithmetic and copies ran while one was open for 1% of the time, Pallas kernels for 27%

profile of v4, /device:TPU:10, one launch (start us, length us, event | category | flops | bytes accessed | tf_op | source)
XLA Modules:
  0.0 745.6 jit_solution(12906295977625189867)
XLA Ops:
  3.8 0.8 copy.99
  5.1 0.8 fusion.3
  6.0 1.4 convert_bitcast_fusion.1
  8.8 1.3 copy.104
  10.5 2.5 copy.98
  13.4 2.2 maximum_bitcast_fusion.shared_own
  15.8 240.0 %front_0.1 = (bf16[2560,1024]{1,0:T(8,128)(2,1)}, bf16[2560,640]{1,0:T(8,128)(2,1)}, bf16[8,320,288]{2,1,0:T(8,128)(2,1)}, bf16[8,256,2560]{2,1,0:T(8,128)(2,1)}...) custom-call(bf16[256,2560]{1,0:T(8,128)(2,1)} %bitcast.57, ...), custom_call_target="tpu_custom_call" | custom-call | tf_op jit(solution)/shard_map/front_0/pallas_call | solution.py:550
  255.8 1.0 copy-done
  256.9 1.0 copy-done.3
  260.0 3.6 copy.113
  263.5 2.3 reshape_reshape.6
  266.6 1.5 pad.15
  268.1 2.7 copy.115.w_shared
  271.4 1.2 dynamic-slice_convert_fusion.rank_col
  272.6 230.2 %experts_3.1 = (bf16[8,256,2560]{2,1,0:T(8,128)(2,1)}, bf16[256,2560]{1,0:T(8,128)(2,1)}, f32[2,2560,384]{2,1,0:T(8,128)}, f32[2,2560,384]{2,1,0:T(8,128)}, f32[...) custom-call(bf16[256,2560]{1,0:T(8,128)(2,1)} %get-tuple-element.43., ...), custom_call_target="tpu_custom_call" | custom-call | tf_op jit(solution)/shard_map/experts_3/pallas_call | solution.py:1149
  502.7 2.7 copy.118
  505.5 1.4 reshape_reshape.7
  506.9 1.4 copy.119
  508.3 5.5 all-to-all-start
  513.9 197.7 %rear_5.1 = (f32[256,640]{1,0:T(8,128)}, f32[256,2560]{1,0:T(8,128)}, f32[320,896]{1,0:T(8,128)}, f32[320,128]{1,0:T(8,128)}, f32[320,640]{1,0:T(8,128)}) custom-call(bf16[8,256,2560]{2,1,0:T(8,128)(2,1)} %get-tuple-element.49.out_part, bf16[256,2560]{1,0:T(8,128)(2,1)} %get-tuple-element.50.back, f32[8,8,256]{2,1,0:T(8,128)} %get-tuple-element.51.gate_dots, ...), custom_call_target="tpu_custom_call" | custom-call | tf_op jit(solution)/shard_map/rear_5/pallas_call | solution.py:1696
  711.7 1.4 add_convert_fusion
  713.0 1.1 copy.130
  714.1 5.4 copy.129
  720.2 0.9 slice.35
  721.1 0.9 slice_reduce_fusion
  723.2 1.3 copy.123
  724.5 1.3 copy.122
  725.8 1.3 copy.121
  727.1 0.9 copy.137
  728.0 7.1 copy.138
  735.1 7.1 copy.139
  742.2 3.2 copy.140
  (76 shorter events, 11.2 us)
Async XLA Ops:
  0.6 6.8 copy-start.16
  6.0 2.1 copy-start.17
  10.5 2.5 copy-start.18
  13.0 2.7 copy-start.4
  13.3 2.4 copy-start.1
  13.3 2.4 copy-start.2
  13.3 2.4 copy-start.6
  13.3 2.4 copy-start.7
  13.4 2.4 copy-start.11
  13.4 2.4 copy-start.12
  255.8 1.1 copy-start
  256.9 1.0 copy-start.3
  257.8 0.7 copy-start.8
  258.6 0.7 copy-start.9
  259.3 0.7 copy-start.10
  259.9 5.9 copy-start.5
  508.3 214.4 %all-to-all-start = ((bf16[8,320,288]{1,2,0:T(8,128)(2,1)}), bf16[8,320,288]{1,2,0:T(8,128)(2,1)S(1)}, u32[]{:S(2)}, u32[]{:S(2)}) async-start(bf16[8,320,288]{1,2,0:T(8,128)(2,1)} %copy.119), calls=%async_computation | async-start | bytes 3538944 | tf_op jit(solution)/shard_map/all_to_all | solution.py:82
  714.1 5.4 copy-start.13
  714.1 6.1 copy-start.14
  724.5 2.6 copy-start.15
  728.0 14.2 %slice-start = ((s8[7864320]{0:T(1024)(128)(4,1)}), s8[4194304]{0:T(1024)(128)(4,1)S(1)}, s32[]{:S(2)}) async-start(s8[7864320]{0:T(1024)(128)(4,1)} %bitcast.60), calls=%async_computation.1 | async-start | bytes 8388608
  735.1 7.1 slice-start.1

commit v5 on v4

--- a/solution.py
+++ b/solution.py
@@ -292,6 +292,7 @@
     heads,
     attn,
     h2,
+    h2_turned,
     gate,
     router_probs,
     gains,
@@ -334,9 +335,9 @@
     first = len(copies)
     local_copy(out_own, out_weights.at[mine])
     local_copy(shared_own.at[net.me], shared_all.at[net.me])
-    part = grad_own.shape[1]
+    part = grad_own.shape[0]
     local_copy(
-        grad_own, grad_all.at[net.me, :, pl.ds(pl.multiple_of(net.row * part, LANES), part)]
+        grad_own, grad_all.at[net.me, pl.ds(pl.multiple_of(net.row * part, LANES), part)]
     )
     local_copy(table_row, rows_all.at[net.me])
     local_copy(table_col, cols_all.at[net.me])
@@ -352,9 +353,7 @@
 
     def grad_slot(start, count):
         def slot(block, row):
-            return grad_all.at[
-                block, pl.ds(start, count), pl.ds(pl.multiple_of(row * part, LANES), part)
-            ]
+            return grad_all.at[block, pl.ds(pl.multiple_of(row * part + start, 16), count)]
 
         return slot
 
@@ -370,7 +369,7 @@
     for q in range(out_pieces):
         slot = weight_slot(out_weights, q * count, count)
         out_items.append((out_own.at[pl.ds(q * count, count)], slot, False))
-    count = toks // grad_pieces
+    count = part // grad_pieces
     for q in range(grad_pieces):
         grad_items.append((grad_own.at[pl.ds(q * count, count)], grad_slot(q * count, count), True))
     items += out_items[:2]
@@ -516,6 +515,9 @@
 
     chunks(norm_second)
     line.tick()
+    for tile in range(width // 256):
+        at = slice(tile * 256, (tile + 1) * 256)
+        h2_turned[at, :] = turn(h2[:, at])
     logits = dot_nn(h2[...], weights[:, start : start + LANES])
     lane = lax.broadcasted_iota(jnp.int32, (toks, LANES), 1)
     logits = jnp.where(lane < experts, logits, masked_score)
@@ -553,7 +555,7 @@
             shape(width, q_width + 2 * size + LANES),
             shape(width, q_width),
             shape(*shared_own.shape),
-            shape(cols, toks, width),
+            shape(cols, width, toks),
             shape(cols, *table_row.shape, dtype=f32),
             shape(cols, *table_col.shape),
             shape(toks, width),
@@ -563,11 +565,12 @@
             shape(toks, q_width),
             shape(toks, width),
             shape(toks, width),
+            shape(width, toks),
             shape(toks, LANES, dtype=f32),
             shape(toks, LANES, dtype=f32),
         ],
         in_specs=[vmem] + [any_space] * 7 + [vmem] * 5,
-        out_specs=[vmem, vmem, any_space, any_space] + [vmem] * 11,
+        out_specs=[vmem, vmem, any_space, any_space] + [vmem] * 12,
         scratch_shapes=[
             pltpu.VMEM((8, width), f32),
             pltpu.VMEM((toks, LANES), f32),
@@ -593,6 +596,19 @@
     )
 
 
+def one_hot_square(size):
+    row = lax.broadcasted_iota(jnp.int32, (size, size), 0)
+    lane = lax.broadcasted_iota(jnp.int32, (size, size), 1)
+    return jnp.where(row == lane, 1.0, 0.0).astype(bf16)
+
+
+def turn(values):
+    return dot_nt(one_hot_square(values.shape[1]), values).astype(bf16)
+
+
+WIDE = 1280
+
+
 def experts_kernel(
     cols,
     capacity,
@@ -616,23 +632,24 @@
     xs_all,
     cs_all,
     wgu,
+    wgu_t,
     wd,
+    wd_t,
     ws,
+    ws_t,
     gates,
     hb,
     xbuf,
     ybuf,
-    obuf,
     part,
     pre,
-    gcol,
-    dcol,
     dz_all,
     zg_all,
     dgu_all,
     sdz_all,
-    sz_all,
-    sgu_all,
+    s_all,
+    z_all,
+    stage_low,
     from_core,
     from_x,
     from_y,
@@ -641,19 +658,16 @@
     dots,
     dots_core,
     dots_x,
-    tiles,
-    tiles_all,
-    stage,
-    stage_low,
     send_sems,
     recv_sems,
     local_sems,
 ):
     net = Net(cols, send_sems, recv_sems)
-    toks, width = h2.shape
+    width, toks = h2.shape
     exp_local, _, hidden = w_gate.shape
     high = net.high_count
-    pad = ws.shape[1] // 3
+    rows_w, packed = w_shared.shape[1:]
+    third = packed // 3
     slots = exp_local * capacity
     pair = 2 * capacity
     piece = width // lax.axis_size("row")
@@ -682,14 +696,21 @@
     far_e = feature_e(2 * (1 - net.outer) + net.core)
 
     def pass_on(source, block, features, peer):
-        return net.send(source.at[..., features], h2_all.at[block, :, features], peer)
+        return net.send(source.at[features], h2_all.at[block, features], peer)
 
     along_z, along_y, along_x, to_core = {}, {}, {}, {}
-    for step in range(high - 1, 0, -1):
-        along_z[high - step] = [
-            pass_on(h2, net.me, own_e, net.z_peer(step)),
-            pass_on(h2, net.me, own_r, net.z_peer(step)),
+
+    def start_z(step):
+        along_z[step] = [
+            pass_on(h2, net.me, own_e, net.z_peer(high - step)),
+            pass_on(h2, net.me, own_r, net.z_peer(high - step)),
         ]
+
+    def left_z(step):
+        for copy in along_z[step]:
+            net.left(copy)
+
+    start_z(1)
     along_y[0] = [
         pass_on(h2, net.me, own_e, net.y_peer()),
         pass_on(h2, net.me, own_r, net.y_peer()),
@@ -752,9 +773,11 @@
         loads.append(local_copy(w_gate.at[e], wgu.at[e, :, pl.ds(0, hidden)], 3 * e + 1))
         loads.append(local_copy(w_up.at[e], wgu.at[e, :, pl.ds(hidden, hidden)], 3 * e + 2))
     base = 3 * exp_local
-    loads.append(local_copy(w_shared, ws, base))
-    keep_own = local_copy(h2, h2_all.at[net.me], base + 1)
-    base += 2
+    for c in range(cols):
+        loads.append(local_copy(w_shared.at[c], ws.at[pl.ds(c * rows_w, rows_w)], base + c))
+    base += cols
+    keep_own = local_copy(h2, h2_all.at[net.me], base)
+    base += 1
 
     def load_pair(source, step):
         first = local_copy(source.at[block_of(step, False)], hb.at[0], base)
@@ -765,12 +788,10 @@
     slot_row = lax.broadcasted_iota(jnp.int32, (capacity, toks), 0).astype(f32) + 1.0
     slot_lane = lax.broadcasted_iota(jnp.int32, (toks, capacity), 1).astype(f32) + 1.0
 
-    def chosen(block, e):
-        return rank_row[block, e : e + 1, :] == slot_row
-
     def picks(block):
         rows = [
-            jnp.where(chosen(block, e), 1.0, 0.0).astype(bf16) for e in range(exp_local)
+            jnp.where(rank_row[block, e : e + 1, :] == slot_row, 1.0, 0.0).astype(bf16)
+            for e in range(exp_local)
         ]
         return jnp.concatenate(rows, axis=0)
 
@@ -783,22 +804,22 @@
 
     def dispatch(step):
         for b in (0, 1):
-            table = picks(block_of(step, b == 1))
+            table = picks_back(block_of(step, b == 1))
 
             def tile(index, b=b, table=table):
-                at = tile_at(index)
-                rows = dot_nn(table, hb[b, :, at]).astype(bf16)
+                at = tile_at(index, WIDE)
+                rows = dot_nn(hb[b, at, :], table).astype(bf16)
                 for e in range(exp_local):
-                    xbuf[e, pl.ds(b * capacity, capacity), at] = rows[
-                        e * capacity : (e + 1) * capacity
+                    xbuf[e, at, pl.ds(b * capacity, capacity)] = rows[
+                        :, e * capacity : (e + 1) * capacity
                     ]
 
-            each_tile(wide, tile)
+            each_tile(width // WIDE, tile)
 
     def save_rows(target, step):
         return [
             local_copy(
-                xbuf.at[e], target.at[e, pl.ds(step * pair, pair)], base + 2 + e
+                xbuf.at[e], target.at[e, :, pl.ds(step * pair, pair)], base + 2 + e
             )
             for e in range(exp_local)
         ]
@@ -809,15 +830,34 @@
         if step == 0:
             for copy in loads:
                 copy.wait()
+
+            def turn_tile(index):
+                at = tile_at(index, 256)
+                for e in range(exp_local):
+                    wd_t[e, at, :] = turn(wd[e, :, at])
+                    for k in range(2 * hidden // 256):
+                        wgu_t[e, k * 256 : (k + 1) * 256, at] = turn(
+                            wgu[e, at, k * 256 : (k + 1) * 256]
+                        )
+                ws_t[:, at] = turn(ws[at, :])
+
+            each_tile(width // 256, turn_tile)
         for copy in saved:
             copy.wait()
         dispatch(step)
         saved = save_rows(cs_all, step)
+        cols_at = pl.ds(step * pair, pair)
         for e in range(exp_local):
-            dz_all[e, pl.ds(step * pair, pair), :] = dot_nt(xbuf[e], wd[e]).astype(bf16)
+            dz_all[e, :, cols_at] = dot_nn(wd[e], xbuf[e]).astype(bf16)
         for b in (0, 1):
-            sdz_all[block_of(step, b == 1)] = dot_nn(hb[b], ws[:, 2 * pad :]).astype(bf16)
+            sdz_all[block_of(step, b == 1)] = dot_nn(ws_t[2 * third :, :], hb[b]).astype(bf16)
+        if step + 2 < high:
+            left_z(step + 1)
+        if step + 2 <= high - 1:
+            start_z(step + 2)
         pump()
+    for copy in saved:
+        copy.wait()
     for copy in gate_copies:
         copy.wait_recv()
     keep_own.wait()
@@ -833,7 +873,7 @@
         for b in (1, 0):
             for far in (1, 0):
                 outer = 1 - net.outer if far else net.outer
-                source = part.at[b, :, features(2 * outer + 1 - net.core)]
+                source = part.at[b, features(2 * outer + 1 - net.core)]
                 across[step, b, far] = net.send(
                     source, from_core.at[far, step, b], net.core_peer()
                 )
@@ -843,7 +883,7 @@
             for far, row in ((1, other_row), (0, net.row)):
                 across[step, b, far].wait_recv()
                 slot = from_core.at[far, step, b]
-                add_rows(slot, [part.at[b, :, features(row)], slot])
+                add_rows(slot, [part.at[b, features(row)], slot])
                 if far:
                     onward[step, b] = net.send(slot, from_x.at[step, b], net.x_peer())
         for b in (1, 0):
@@ -865,126 +905,141 @@
         if step:
             far_z[step] = net.send(slot, from_z.at[step - 1], net.z_peer(step))
 
-    own_expert = lax.rem(net.me, cols) * exp_local
+    own_expert = net.me * exp_local
     gate_rows = gates.shape[1]
-    gate_row = lax.broadcasted_iota(jnp.int32, (gate_rows, toks), 0)
+    gate_at = lax.broadcasted_iota(jnp.int32, (gate_rows, slots), 0)
+    gate_of = own_expert + lax.broadcasted_iota(jnp.int32, (gate_rows, slots), 1) // capacity
+    dot_at = lax.broadcasted_iota(jnp.int32, (16, slots), 0)
+    dot_of = lax.broadcasted_iota(jnp.int32, (16, slots), 1) // capacity
     dots[...] = jnp.zeros_like(dots)
+    s_all[2 * third :, :] = jnp.zeros((third, cols * toks), bf16)
+    z_all[: 2 * third, :] = jnp.zeros((2 * third, cols * toks), bf16)
+
+    def split(values):
+        high_part = values.astype(bf16)
+        return high_part, (values - high_part.astype(f32)).astype(bf16)
+
+    saved, out_copies = [], []
     for step in range(high):
         if step:
             whole(step, False)
         whole(step, True)
+        for copy in out_copies:
+            copy.wait()
         load_pair(h2_all, step)
         for copy in saved:
             copy.wait()
         dispatch(step)
         saved = save_rows(xs_all, step)
         pump()
+        slot_gates = []
         for b in (0, 1):
             block = block_of(step, b == 1)
-            inner = dot_nn(hb[b], ws[:, : 2 * pad])
-            sa, su = inner[:, :pad], inner[:, pad:]
+            at = pl.ds(pl.multiple_of(block * toks, toks), toks)
+            inner = dot_nn(ws_t[: 2 * third, :], hb[b])
+            sa, su = inner[:third], inner[third:]
             sig = 1.0 / (1.0 + jnp.exp(-sa))
             silu = sa * sig
             slope = sig * (1.0 + sa * (1.0 - sig))
-            sz_all[block] = (silu * su).astype(bf16)
             sdz = sdz_all[block].astype(f32)
-            sgu_all[block, :, :pad] = (sdz * su * slope).astype(bf16)
-            sgu_all[block, :, pad:] = (sdz * silu).astype(bf16)
+            s_all[:third, at] = (sdz * su * slope).astype(bf16)
+            s_all[third : 2 * third, at] = (sdz * silu).astype(bf16)
+            z_all[2 * third :, at] = (silu * su).astype(bf16)
+            table = picks_back(block)
+            first, second = split(gates[block])
+            found = dot_nn(first, table) + dot_nn(second, table)
+            slot_gates.append(
+                jnp.sum(jnp.where(gate_at == gate_of, found, 0.0), axis=0, keepdims=True)
+            )
         if step:
             sum_cores(step - 1)
-        rows = pl.ds(step * pair, pair)
+        cols_at = pl.ds(step * pair, pair)
+        slot_dots = []
         for e in range(exp_local):
-
-            def inner_tile(index, e=e):
-                at = tile_at(index, 256)
-                pre[:, at] = dot_nn(xbuf[e], wgu[e, :, at])
-
-            each_tile(2 * hidden // 256, inner_tile)
-            for b in (0, 1):
-                block = block_of(step, b == 1)
-                gate = jnp.sum(
-                    jnp.where(gate_row == own_expert + e, gates[block], 0.0), axis=0, keepdims=True
-                )
-                gate = jnp.sum(jnp.where(chosen(block, e), gate, 0.0), axis=1, keepdims=True)
-                gcol[pl.ds(b * capacity, capacity), :] = jnp.broadcast_to(gate, (capacity, LANES))
-
-            def gating(index, e=e, step=step):
+            pre[...] = dot_nn(wgu_t[e], xbuf[e])
+            gate = jnp.concatenate(
+                [row[:, e * capacity : (e + 1) * capacity] for row in slot_gates], axis=1
+            )
+
+            def gating(index, total, e=e, cols_at=cols_at, gate=gate):
                 at = pl.ds(pl.multiple_of(index * 32, 32), 32)
-                saved_at = pl.ds(pl.multiple_of(step * pair + index * 32, 32), 32)
-                a, u = pre[at, :hidden], pre[at, hidden:]
-                gate = jnp.concatenate([gcol[at, :]] * (hidden // LANES), axis=1)
-                dz = dz_all[e, saved_at, :].astype(f32)
+                up_at = pl.ds(pl.multiple_of(hidden + index * 32, 32), 32)
+                a, u = pre[at, :], pre[up_at, :]
+                dz = dz_all[e, at, cols_at].astype(f32)
                 sig = 1.0 / (1.0 + jnp.exp(-a))
                 silu = a * sig
                 slope = sig * (1.0 + a * (1.0 - sig))
                 z = silu * u
-                dcol[at, :] = jnp.broadcast_to(
-                    jnp.sum(z * dz, axis=1, keepdims=True), (32, LANES)
-                )
-                zg_all[e, saved_at, :] = (z * gate).astype(bf16)
+                total = total + jnp.sum(z * dz, axis=0, keepdims=True)
+                zg_all[e, at, cols_at] = (z * gate).astype(bf16)
                 dz = dz * gate
-                dgu_all[e, saved_at, :hidden] = (dz * u * slope).astype(bf16)
-                dgu_all[e, saved_at, hidden:] = (dz * silu).astype(bf16)
-
-            each_tile(pair // 32, gating)
-            for b in (0, 1):
-                block = block_of(step, b == 1)
-                col = dcol[pl.ds(b * capacity, capacity), :]
-                col = jnp.concatenate([col] * (toks // LANES), axis=1)
-                dots[block, e : e + 1, :] = jnp.sum(
-                    jnp.where(chosen(block, e), col, 0.0), axis=0, keepdims=True
-                )
-
-            def out_tile(index, e=e):
-                at = tile_at(index)
-                y = dot_nn(zg_all[e, rows, :], wd[e, :, at]).astype(bf16)
+                dgu_all[e, at, cols_at] = (dz * u * slope).astype(bf16)
+                dgu_all[e, up_at, cols_at] = (dz * silu).astype(bf16)
+                return total
+
+            slot_dots.append(
+                lax.fori_loop(0, hidden // 32, gating, jnp.zeros((1, pair), f32))
+            )
+
+            def out_tile(index, e=e, cols_at=cols_at):
+                at = tile_at(index, WIDE)
+                y = dot_nn(wd_t[e, at, :], zg_all[e, :, cols_at]).astype(bf16)
                 for b in (0, 1):
-                    ybuf[b, pl.ds(e * capacity, capacity), at] = y[b * capacity : (b + 1) * capacity]
-
-            each_tile(wide, out_tile)
+                    ybuf[b, at, pl.ds(e * capacity, capacity)] = y[
+                        :, b * capacity : (b + 1) * capacity
+                    ]
+
+            each_tile(width // WIDE, out_tile)
             pump()
-        if step:
-            for copy in out_copies:
-                copy.wait()
         out_copies = []
         for b in (0, 1):
             block = block_of(step, b == 1)
-            table = picks_back(block)
-
-            def join_tile(index, b=b, table=table, block=block):
-                at = tile_at(index)
-                total = dot_nn(table, ybuf[b, :, at])
-                total = total + dot_nt(sz_all[block], ws[at, 2 * pad :])
-                obuf[b, :, at] = total.astype(bf16)
-
-            each_tile(wide, join_tile)
+            at_toks = pl.ds(pl.multiple_of(block * toks, toks), toks)
+            table = picks(block)
+            row = jnp.concatenate(
+                [part_dots[:, b * capacity : (b + 1) * capacity] for part_dots in slot_dots], axis=1
+            )
+            first, second = split(row)
+            both = jnp.where(dot_at == dot_of, first.astype(f32), 0.0)
+            both = both + jnp.where(dot_at == dot_of + 8, second.astype(f32), 0.0)
+            found = dot_nn(both.astype(bf16), table)
+            dots[block] = found[:8] + found[8:]
+
+            def join_tile(index, b=b, table=table, at_toks=at_toks):
+                at = tile_at(index, WIDE)
+                total = dot_nn(ybuf[b, at, :], table) + dot_nn(ws[at, :], z_all[:, at_toks])
+                hb[b, at, :] = total.astype(bf16)
+
+            each_tile(width // WIDE, join_tile)
             out_copies.append(
-                local_copy(obuf.at[b], out_part.at[block], base + 2 + exp_local + b)
+                local_copy(hb.at[b], out_part.at[block], base + 2 + exp_local + b)
             )
         pump()
         if step:
             sum_chips(step - 1)
         for e in range(exp_local):
 
-            def back_tile(index, e=e):
-                at = tile_at(index)
-                y = dot_nt(dgu_all[e, rows, :], wgu[e, at, :]).astype(bf16)
+            def back_tile(index, e=e, cols_at=cols_at):
+                at = tile_at(index, WIDE)
+                y = dot_nn(wgu[e, at, :], dgu_all[e, :, cols_at]).astype(bf16)
                 for b in (0, 1):
-                    ybuf[b, pl.ds(e * capacity, capacity), at] = y[b * capacity : (b + 1) * capacity]
-
-            each_tile(wide, back_tile)
+                    ybuf[b, at, pl.ds(e * capacity, capacity)] = y[
+                        :, b * capacity : (b + 1) * capacity
+                    ]
+
+            each_tile(width // WIDE, back_tile)
         pump()
         for b in (1, 0):
             block = block_of(step, b == 1)
-            table = picks_back(block)
-
-            def back_join(index, b=b, table=table, block=block):
-                at = tile_at(index)
-                total = dot_nn(table, ybuf[b, :, at])
-                total = total + dot_nt(sgu_all[block], ws[at, : 2 * pad])
-                part[b, :, at] = total.astype(bf16)
-
-            each_tile(wide, back_join)
+            at_toks = pl.ds(pl.multiple_of(block * toks, toks), toks)
+            table = picks(block)
+
+            def back_join(index, b=b, table=table, at_toks=at_toks):
+                at = tile_at(index, WIDE)
+                total = dot_nn(ybuf[b, at, :], table) + dot_nn(ws[at, :], s_all[:, at_toks])
+                part[b, at, :] = total.astype(bf16)
+
+            each_tile(width // WIDE, back_join)
         hand_over(step)
         if step:
             sum_plane(step - 1)
@@ -1033,63 +1088,70 @@
             for copy in store_copies(j, j % 2):
                 copy.wait()
 
+    depth = cols * capacity
+    total_toks = cols * toks
+    top, next_top = pl.ds(0, TILE), pl.ds(TILE, TILE)
+
     def inner_grads(e):
+        def work(j, slot):
+            found = dot_nt(wgu_t[slot, :TILE, :depth], dgu_all[e]).astype(bf16)
+            wd_t[slot, :TILE, :] = found[:, :hidden]
+            wd_t[slot, TILE : 2 * TILE, :] = found[:, hidden:]
+
         passes(
             wide,
             lambda j, slot: (
-                xs_all.at[e, :, tile_at(j)],
-                tiles.at[slot],
+                xs_all.at[e, tile_at(j)],
+                wgu_t.at[slot, top, pl.ds(0, depth)],
             ),
-            lambda j, slot: put(stage.at[slot], dot_tn(tiles[slot], dgu_all[e])),
+            work,
             lambda j, slot: [
-                (stage.at[slot, :, pl.ds(0, hidden)], g_gate.at[e, tile_at(j)]),
-                (stage.at[slot, :, pl.ds(hidden, hidden)], g_up.at[e, tile_at(j)]),
+                (wd_t.at[slot, top], g_gate.at[e, tile_at(j)]),
+                (wd_t.at[slot, next_top], g_up.at[e, tile_at(j)]),
             ],
         )
 
-    def put(target, value):
-        target[...] = value
-
     def down_grads(e):
+        def work(j, slot):
+            found = dot_nt(zg_all[e], wgu_t[slot, :TILE, :depth])
+            wd[slot, :, :TILE] = found.astype(bf16)
+
         passes(
             wide,
             lambda j, slot: (
-                cs_all.at[e, :, tile_at(j)],
-                tiles.at[slot],
+                cs_all.at[e, tile_at(j)],
+                wgu_t.at[slot, top, pl.ds(0, depth)],
             ),
-            lambda j, slot: put(
-                stage.at[slot, pl.ds(0, hidden), pl.ds(0, TILE)],
-                dot_tn(zg_all[e], tiles[slot]),
-            ),
+            work,
             lambda j, slot: [
-                (
-                    stage.at[slot, pl.ds(0, hidden), pl.ds(0, TILE)],
-                    g_down.at[e, :, tile_at(j)],
-                ),
+                (wd.at[slot, :, top], g_down.at[e, :, tile_at(j)]),
             ],
         )
 
-    def shared_grads(source, others, start, size):
-        def work(j, slot):
-            total = dot_tn(tiles_all[slot, 0], others[0])
-            for c in range(1, cols):
-                total = total + dot_tn(tiles_all[slot, c], others[c])
-            stage_low[slot, :, :size] = total.astype(bf16)
-
-        def load(j, slot):
-            return (source.at[:, :, tile_at(j)], tiles_all.at[slot])
-
-        passes(
-            wide,
-            lambda j, slot: load(j, slot),
-            work,
-            lambda j, slot: [
-                (
-                    stage_low.at[slot, :, pl.ds(0, size)],
-                    g_shared.at[tile_at(j), pl.ds(start, size)],
-                ),
-            ],
-        )
+    def shared_grads():
+        def tile(index):
+            at = tile_at(index)
+            copies = [
+                pltpu.make_async_copy(
+                    source.at[c, at],
+                    wgu_t.at[slot, top, pl.ds(c * toks, toks)],
+                    local_sems.at[slot * cols + c],
+                )
+                for slot, source in enumerate((h2_all, grads))
+                for c in range(cols)
+            ]
+            for copy in copies:
+                copy.start()
+            for copy in copies:
+                copy.wait()
+            found = dot_nt(wgu_t[0, :TILE, :total_toks], s_all[...])
+            found = found + dot_nt(wgu_t[1, :TILE, :total_toks], z_all[...])
+            stage_low[...] = found.astype(bf16)
+            copy = pltpu.make_async_copy(stage_low, g_shared.at[at], local_sems.at[store_sem])
+            copy.start()
+            copy.wait()
+
+        each_tile(wide, tile)
 
     first_dots = net.send(dots, dots_core, net.core_peer())
     inner_grads(0)
@@ -1116,13 +1178,12 @@
         far_z[step].wait_recv()
     add_rows(kept, [from_core.at[0, 0, 0], *[from_z.at[step - 1] for step in range(1, high)]])
     own, other = features(net.row), features(other_row)
-    back[:, own] = kept[...].astype(bf16)
-    far = net.send(back.at[:, own], back.at[:, own], net.x_peer())
-    near = net.send(back.at[:, own], back.at[:, own], net.core_peer())
-    shared_grads(h2_all, sgu_all, 0, 2 * pad)
+    back[own, :] = kept[...].astype(bf16)
+    far = net.send(back.at[own], back.at[own], net.x_peer())
+    near = net.send(back.at[own], back.at[own], net.core_peer())
+    shared_grads()
     far.wait_recv()
-    crossed = net.send(back.at[:, other], back.at[:, other], net.core_peer())
-    shared_grads(grads, sz_all, 2 * pad, pad)
+    crossed = net.send(back.at[other], back.at[other], net.core_peer())
     near.wait_recv()
     crossed.wait_recv()
     for copy in third_dots:
@@ -1133,12 +1194,12 @@
 def experts_call(
     cols, collective_id, capacity, h2, grads, w_gate, w_up, w_down, w_shared, rank_row, rank_col, gate
 ):
-    toks, width = h2.shape
+    width, toks = h2.shape
     exp_local, _, hidden = w_gate.shape
     high = cols // 2
-    pad = w_shared.shape[1] // 3
+    packed = w_shared.shape[2]
     piece = width // lax.axis_size("row")
-    pair = 2 * capacity
+    pair, depth = 2 * capacity, cols * capacity
     any_space = pl.BlockSpec(memory_space=pl.ANY)
     vmem = pl.BlockSpec(memory_space=pltpu.VMEM)
     copies = 160
@@ -1149,16 +1210,16 @@
     return pl.pallas_call(
         functools.partial(experts_kernel, cols, capacity),
         out_shape=[
-            shape(cols, toks, width),
-            shape(toks, width),
-            shape(exp_local, width, hidden, dtype=f32),
-            shape(exp_local, width, hidden, dtype=f32),
-            shape(exp_local, hidden, width, dtype=f32),
-            shape(width, 3 * pad),
+            shape(cols, width, toks),
+            shape(width, toks),
+            shape(exp_local, width, hidden),
+            shape(exp_local, width, hidden),
+            shape(exp_local, hidden, width),
+            shape(width, packed),
             shape(cols, 8, toks, dtype=f32),
-            shape(cols, toks, width),
-            shape(exp_local, cols * capacity, width),
-            shape(exp_local, cols * capacity, width),
+            shape(cols, width, toks),
+            shape(exp_local, width, depth),
+            shape(exp_local, width, depth),
         ],
         in_specs=[any_space] * 6 + [vmem] * 3,
         out_specs=[
@@ -1175,41 +1236,38 @@
         ],
         scratch_shapes=[
             pltpu.VMEM((exp_local, width, 2 * hidden), bf16),
+            pltpu.VMEM((exp_local, 2 * hidden, width), bf16),
             pltpu.VMEM((exp_local, hidden, width), bf16),
-            pltpu.VMEM((width, 3 * pad), bf16),
+            pltpu.VMEM((exp_local, width, hidden), bf16),
+            pltpu.VMEM((width, packed), bf16),
+            pltpu.VMEM((packed, width), bf16),
             pltpu.VMEM((cols, *gate.shape), f32),
-            pltpu.VMEM((2, toks, width), bf16),
-            pltpu.VMEM((exp_local, pair, width), bf16),
-            pltpu.VMEM((2, exp_local * capacity, width), bf16),
-            pltpu.VMEM((2, toks, width), bf16),
-            pltpu.VMEM((2, toks, width), bf16),
-            pltpu.VMEM((pair, 2 * hidden), f32),
-            pltpu.VMEM((pair, LANES), f32),
-            pltpu.VMEM((pair, LANES), f32),
-            pltpu.VMEM((exp_local, cols * capacity, hidden), bf16),
-            pltpu.VMEM((exp_local, cols * capacity, hidden), bf16),
-            pltpu.VMEM((exp_local, cols * capacity, 2 * hidden), bf16),
-            pltpu.VMEM((cols, toks, pad), bf16),
-            pltpu.VMEM((cols, toks, pad), bf16),
-            pltpu.VMEM((cols, toks, 2 * pad), bf16),
-            pltpu.VMEM((2, high, 2, toks, piece), bf16),
-            pltpu.VMEM((high, 2, toks, piece), bf16),
-            pltpu.VMEM((high, toks, piece), bf16),
-            pltpu.VMEM((high - 1, toks, piece), bf16),
-            pltpu.VMEM((toks, piece), f32),
+            pltpu.VMEM((2, width, toks), bf16),
+            pltpu.VMEM((exp_local, width, pair), bf16),
+            pltpu.VMEM((2, width, exp_local * capacity), bf16),
+            pltpu.VMEM((2, width, toks), bf16),
+            pltpu.VMEM((2 * hidden, pair), f32),
+            pltpu.VMEM((exp_local, hidden, depth), bf16),
+            pltpu.VMEM((exp_local, hidden, depth), bf16),
+            pltpu.VMEM((exp_local, 2 * hidden, depth), bf16),
+            pltpu.VMEM((cols, packed // 3, toks), bf16),
+            pltpu.VMEM((packed, cols * toks), bf16),
+            pltpu.VMEM((packed, cols * toks), bf16),
+            pltpu.VMEM((TILE, packed), bf16),
+            pltpu.VMEM((2, high, 2, piece, toks), bf16),
+            pltpu.VMEM((high, 2, piece, toks), bf16),
+            pltpu.VMEM((high, piece, toks), bf16),
+            pltpu.VMEM((high - 1, piece, toks), bf16),
+            pltpu.VMEM((piece, toks), f32),
             pltpu.VMEM((cols, 8, toks), f32),
             pltpu.VMEM((cols, 8, toks), f32),
             pltpu.VMEM((cols, 8, toks), f32),
-            pltpu.VMEM((2, cols * capacity, TILE), bf16),
-            pltpu.VMEM((2, cols, toks, TILE), bf16),
-            pltpu.VMEM((2, TILE, 2 * hidden), f32),
-            pltpu.VMEM((2, TILE, 2 * pad), bf16),
             pltpu.SemaphoreType.DMA((copies,)),
             pltpu.SemaphoreType.DMA((copies,)),
-            pltpu.SemaphoreType.DMA((24,)),
+            pltpu.SemaphoreType.DMA((40,)),
         ],
         compiler_params=pltpu.CompilerParams(
-            collective_id=collective_id, has_side_effects=True, vmem_limit_bytes=62 << 20
+            collective_id=collective_id, has_side_effects=True, vmem_limit_bytes=63 << 20
         ),
         name=f"experts_{collective_id}",
     )(h2, grads, w_gate, w_up, w_down, w_shared, rank_row, rank_col, gate)
@@ -1218,15 +1276,11 @@
 def experts_kernels(
     cols, collective_id, capacity, h2, grad_all, w_gate, w_up, w_down, shared_weights, *tables
 ):
-    width, shared_part = shared_weights.shape[0], shared_weights.shape[1] // 3
-    pad = -shared_part % LANES
-    padded = jnp.pad(shared_weights.reshape(width, 3, shared_part), ((0, 0), (0, 0), (0, pad)))
-    padded = padded.reshape(width, -1)
     out_part, back, g_gate, g_up, g_down, g_shared, gate_dots, *_ = experts_call(
-        cols, collective_id, capacity, h2, grad_all, w_gate, w_up, w_down, padded, *tables
+        cols, collective_id, capacity, h2, grad_all, w_gate, w_up, w_down, shared_weights, *tables
     )
-    g_shared = g_shared.reshape(width, 3, -1)[:, :, :shared_part].reshape(width, -1)
-    return (out_part, back, gate_dots, g_shared, g_gate, g_up, g_down)
+    wide = (grad.astype(f32) for grad in (g_gate, g_up, g_down))
+    return (out_part, back, gate_dots, g_shared, *wide)
 
 
 def fits(cols, rows, width):
@@ -1302,6 +1356,7 @@
     out_weights,
     misc,
     misc_low,
+    grad_turned,
     grad_own,
     gains,
     dots,
@@ -1337,7 +1392,7 @@
     local_sems,
 ):
     net = Net(cols, send_sems, recv_sems)
-    toks, width = back.shape
+    width, toks = back.shape
     size = HEAD_DIM
     q_width = q_low.shape[1]
     group = q_width // size
@@ -1360,14 +1415,14 @@
     loads = [
         local_copy(weights_in, weights, 0),
         local_copy(out_weights_in, out_weights, 1),
-        local_copy(grads.at[net.me], grad_own, 2),
+        local_copy(grads.at[net.me], grad_turned, 2),
     ]
-    near_load = local_copy(out_part.at[:, :, features(net.row)], own.at[0], 3)
-    far_load = local_copy(out_part.at[:, :, features(other_row)], own.at[1], 4)
+    near_load = local_copy(out_part.at[:, features(net.row)], own.at[0], 3)
+    far_load = local_copy(out_part.at[:, features(other_row)], own.at[1], 4)
     net.greet(col_peers(net) + row_peers(net))
 
     pieces = 4
-    count = toks // pieces
+    count = piece // pieces
     order = [*range(1, net.high_count), 0]
     keys_of = [(step, True) for step in order] + [(step, False) for step in order]
     across, onward, along_y, along_z = {}, {}, {}, {}
@@ -1381,7 +1436,15 @@
             for key in keys_of:
                 block = net.block_ahead(*key)
                 across[q, far, key] = net.send(
-                    out_part.at[block, rows_of(q), features(2 * outer + 1 - net.core)],
+                    out_part.at[
+                        block,
+                        pl.ds(
+                            pl.multiple_of(
+                                (2 * outer + 1 - net.core) * piece + q * count, 16
+                            ),
+                            count,
+                        ),
+                    ],
                     from_core.at[far, block, rows_of(q)],
                     net.core_peer(),
                 )
@@ -1466,9 +1529,10 @@
 
     for tile in range(width // TILE):
         at = pl.ds(tile * TILE, TILE)
-        d_tokens[:, at] = back[:, at].astype(f32) + dot_nt(
+        d_tokens[:, at] = dot_nt(one_hot_square(toks), back[at, :]) + dot_nt(
             logit_low[...], weights[at, qkv_width : qkv_width + LANES]
         )
+        grad_own[:, at] = dot_nt(one_hot_square(toks), grad_turned[at, :]).astype(bf16)
     gain_sums[...] = jnp.zeros_like(gain_sums)
 
     def fold(values, start):
@@ -1672,7 +1736,7 @@
     cols, collective_id, experts, out_part, back, gate_dots, gate, router_probs, table_col, h1, h2,
     tokens, attn, weights, out_weights, grads, heads, q_low, kv_all, probs, cosine, sine,
 ):
-    toks, width = back.shape
+    width, toks = back.shape
     q_width = q_low.shape[1]
     size = HEAD_DIM
     qkv_width = q_width + 2 * size
@@ -1696,7 +1760,7 @@
     return pl.pallas_call(
         functools.partial(rear_kernel, cols, experts),
         out_shape=[
-            shape(toks, piece),
+            shape(piece, toks),
             shape(toks, width),
             shape(rows_w, qkv_width),
             shape(rows_w, LANES),
@@ -1709,6 +1773,7 @@
             pltpu.VMEM((width, q_width), bf16),
             pltpu.VMEM((width, LANES), f32),
             pltpu.VMEM((width, LANES), bf16),
+            pltpu.VMEM((width, toks), bf16),
             pltpu.VMEM((toks, width), bf16),
             pltpu.VMEM((8, width), f32),
             pltpu.VMEM((LANES, toks), f32),
@@ -1723,10 +1788,10 @@
             pltpu.VMEM((toks, 2 * size), f32),
             pltpu.VMEM((toks, qkv_width), bf16),
             pltpu.VMEM((16, width), f32),
-            pltpu.VMEM((2, cols, toks, piece), bf16),
-            pltpu.VMEM((2, cols, toks, piece), bf16),
-            pltpu.VMEM((cols, toks, piece), bf16),
-            *sums(toks, piece),
+            pltpu.VMEM((2, cols, piece, toks), bf16),
+            pltpu.VMEM((2, cols, piece, toks), bf16),
+            pltpu.VMEM((cols, piece, toks), bf16),
+            *sums(piece, toks),
             *sums(toks, 2 * size),
             *sums(rows_w, q_width),
             *sums(rows_w, qkv_width),
@@ -1937,6 +2002,7 @@
             heads,
             attn,
             h2,
+            h2_turned,
             gate,
             probs_router,
         ) = front_call(
@@ -1950,7 +2016,7 @@
             misc,
             attention_output_matrix.T,
             shared_own,
-            grad_own,
+            grad_own.T,
             table_row,
             table_col,
             doc.reshape(toks, 1).astype(f32),
@@ -1979,7 +2045,8 @@
         )
         kv_all = gather_col(jnp.concatenate([qk[:, q_width:], value_low, side], axis=1))
         rank_all = kv_all[:, :, 2 * kv_width : 2 * kv_width + experts]
-    shared_weights = shared_weights.reshape(width, 3 * shared_part)
+    if not kernels:
+        shared_weights = shared_weights.reshape(width, 3 * shared_part)
     qkv_weights = first_weights[:, :qkv_width]
     router = first_weights[:, qkv_width : qkv_width + experts]
     gain_one = first_weights[:, qkv_width + experts].astype(f32)
@@ -2020,7 +2087,7 @@
             cols,
             3,
             capacity,
-            h2,
+            h2_turned,
             grad_all,
             expert_gate,
             expert_up,
@@ -2139,6 +2206,8 @@
         share_out = scatter_col(grad_out.reshape(cols, rows_w, q_width)).astype(f32)
         share_first = scatter_col(grad_first.reshape(cols, rows_w, -1)).astype(f32)
         share_qkv, share_misc = share_first[:, :qkv_width], share_first[:, qkv_width:]
+    if kernels:
+        out_slice = out_slice.T
     middle_slice = lax.dynamic_slice_in_dim(middle, row_index * row_width, row_width, 1)
     block_out = (middle_slice + out_slice).astype(bf16)
 

time: 751 us -> 755 us (level)
  local copies, waits for them, and re-layouts: 62.4 us -> 35.5 us
  other arithmetic: 7.73 us -> 21.7 us
  Pallas kernels: 668 us -> 681 us
    unnamed x55 -> x53, local copies, waits for them, and re-layouts: 30.6 us -> 13.2 us
    convert_element_type x0 -> x3, other arithmetic: none -> 14.2 us  [experts_kernels(): wide = (grad.astype(f32) for grad in (g_gate, g_up, g_down))]
    pallas_call x1, Pallas kernels: 198 us -> 207 us  [rear_call(): pl.pallas_call(functools.partial(rear_kernel, cols, experts), out_shape=[...]
  transfers between devices with their start and end apart: 1 -> 1, of which waited for: 0 -> 0; matrix products, arithmetic and copies ran while one was open for 1% -> 4% of each run, Pallas kernels for 27% -> 28%
where the time goes in v5:
time: 755 us; the launch traced here: 745 us
  Pallas kernels  681 us (90%)
  local copies, waits for them, and re-layouts  35.5 us (5%)
  other arithmetic  21.7 us (3%)
    pallas_call x1, Pallas kernels, front_call(): pl.pallas_call(functools.partial(front_kernel, cols, experts), out_shape=...  241 us
    pallas_call x1, Pallas kernels, experts_call(): pl.pallas_call(functools.partial(experts_kernel, cols, capacity), out_sha...  233 us
    pallas_call x1, Pallas kernels, rear_call(): pl.pallas_call(functools.partial(rear_kernel, cols, experts), out_shape=[...  207 us
  transfers between devices with their start and end apart: 1, of which 0 were waited for; matrix products, arithmetic and copies ran while one was open for 4% of the time, Pallas kernels for 28%

profile of v5, /device:TPU:10, one launch (start us, length us, event | category | flops | bytes accessed | tf_op | source)
XLA Modules:
  0.0 745.0 jit_solution(7111448055268251946)
XLA Ops:
  0.7 0.7 convert_element_type.81
  2.2 0.8 broadcast_in_dim.22
  3.0 0.8 broadcast_in_dim.23
  3.8 0.8 copy.96
  5.2 0.8 fusion.4
  6.0 1.4 convert_bitcast_fusion.1
  7.4 1.0 copy.105
  9.8 1.3 copy.101
  11.5 2.5 copy.95
  14.4 2.2 maximum_bitcast_fusion.shared_own
  16.8 240.7 %front_0.1 = (bf16[2560,1024]{1,0:T(8,128)(2,1)}, bf16[2560,640]{1,0:T(8,128)(2,1)}, bf16[8,320,288]{2,1,0:T(8,128)(2,1)}, bf16[8,2560,256]{2,1,0:T(8,128)(2,1)}...) custom-call(bf16[256,2560]{1,0:T(8,128)(2,1)} %bitcast.64, ...), custom_call_target="tpu_custom_call" | custom-call | tf_op jit(solution)/shard_map/front_0/pallas_call | solution.py:552
  257.5 1.0 copy-done
  258.6 1.0 copy-done.3
  263.0 1.2 dynamic-slice_convert_fusion.rank_col
  264.2 233.4 %experts_3.1 = (bf16[8,2560,256]{2,1,0:T(8,128)(2,1)}, bf16[2560,256]{1,0:T(8,128)(2,1)}, bf16[2,2560,384]{2,1,0:T(8,128)(2,1)}, bf16[2,2560,384]{2,1,0:T(8,128)...) custom-call(bf16[2560,256]{1,0:T(8,128)(2,1)} %get-tuple-element.44., ...), custom_call_target="tpu_custom_call" | custom-call | tf_op jit(solution)/shard_map/experts_3/pallas_call | solution.py:1210
  497.6 3.8 copy.114
  501.4 4.5 all-to-all-start
  505.9 207.2 %rear_5.1 = (f32[640,256]{1,0:T(8,128)}, f32[256,2560]{1,0:T(8,128)}, f32[320,896]{1,0:T(8,128)}, f32[320,128]{1,0:T(8,128)}, f32[320,640]{1,0:T(8,128)}) custom-call(bf16[8,2560,256]{2,1,0:T(8,128)(2,1)} %get-tuple-element.50.out_part, bf16[2560,256]{1,0:T(8,128)(2,1)} %get-tuple-element.51.back, f32[8,8,256]{2,1,0:T(8,128)} %get-tuple-element.52.gate_dots, ...), custom_call_target="tpu_custom_call" | custom-call | tf_op jit(solution)/shard_map/rear_5/pallas_call | solution.py:1760
  713.1 1.3 copy.111
  714.4 1.2 fusion
  715.6 1.1 copy.128
  716.7 5.4 copy.126
  722.8 0.9 slice.32
  723.7 6.0 convert_element_type.92
  729.7 3.9 convert_element_type.93
  733.6 4.3 convert_element_type.94
  737.9 0.9 slice_reduce_fusion
  738.8 0.7 fusion.3
  740.0 1.3 copy.118
  741.3 1.3 copy.117
  742.6 1.3 copy.116
  743.9 0.9 copy.132
  (70 shorter events, 8.1 us)
Async XLA Ops:
  0.6 7.8 %copy-start.18 = (bf16[320,768]{1,0:T(8,128)(2,1)S(1)}, bf16[320,768]{1,0:T(8,128)(2,1)}, u32[]{:S(2)}) copy-start(bf16[320,768]{1,0:T(8,128)(2,1)} %param.27) | copy-start | bytes 1474564
  5.0 4.2 copy-start.19
  11.5 2.5 copy-start.20
  14.1 2.7 copy-start.4
  14.2 2.6 copy-start.6
  14.2 2.6 copy-start.7
  14.2 2.6 copy-start.11
  14.2 2.6 copy-start.12
  14.4 243.1 %copy-start.1 = (f32[256,128]{1,0:T(8,128)}, f32[256,128]{1,0:T(8,128)S(1)}, u32[]{:S(2)}) copy-start(f32[256,128]{1,0:T(8,128)S(1)} %get-tuple-element.142.cosine) | copy-start | bytes 393220
  14.4 243.1 %copy-start.2 = (f32[256,128]{1,0:T(8,128)}, f32[256,128]{1,0:T(8,128)S(1)}, u32[]{:S(2)}) copy-start(f32[256,128]{1,0:T(8,128)S(1)} %get-tuple-element.143.sine) | copy-start | bytes 393220
  257.5 1.1 copy-start
  258.6 1.0 copy-start.3
  259.6 0.7 copy-start.8
  260.3 0.7 copy-start.9
  261.0 0.7 copy-start.10
  261.7 235.9 %copy-start.5 = (f32[256,128]{1,0:T(8,128)}, f32[256,128]{1,0:T(8,128)S(1)}, u32[]{:S(2)}) copy-start(f32[256,128]{1,0:T(8,128)S(1)} %get-tuple-element.49.gate) | copy-start | bytes 393220
  501.4 238.1 %all-to-all-start = ((bf16[8,320,288]{1,2,0:T(8,128)(2,1)}), bf16[8,320,288]{1,2,0:T(8,128)(2,1)S(1)}, u32[]{:S(2)}, u32[]{:S(2)}) async-start(bf16[8,320,288]{1,2,0:T(8,128)(2,1)} %copy.114), calls=%async_computation | async-start | bytes 3538944 | tf_op jit(solution)/shard_map/all_to_all | solution.py:82
  716.7 5.4 copy-start.15
  716.7 6.1 copy-start.16
  723.7 6.0 copy-start.14
  729.7 3.9 copy-start.13
  741.3 2.6 copy-start.17

commit v6 on v4

--- a/solution.py
+++ b/solution.py
@@ -187,6 +187,7 @@
 
 
 TILE = 512
+WIDE = 1280
 
 
 def tile_at(index, tile=TILE):
@@ -685,11 +686,14 @@
         return net.send(source.at[..., features], h2_all.at[block, :, features], peer)
 
     along_z, along_y, along_x, to_core = {}, {}, {}, {}
-    for step in range(high - 1, 0, -1):
-        along_z[high - step] = [
-            pass_on(h2, net.me, own_e, net.z_peer(step)),
-            pass_on(h2, net.me, own_r, net.z_peer(step)),
+
+    def start_z(step):
+        along_z[step] = [
+            pass_on(h2, net.me, own_e, net.z_peer(high - step)),
+            pass_on(h2, net.me, own_r, net.z_peer(high - step)),
         ]
+
+    start_z(1)
     along_y[0] = [
         pass_on(h2, net.me, own_e, net.y_peer()),
         pass_on(h2, net.me, own_r, net.y_peer()),
@@ -786,14 +790,14 @@
             table = picks(block_of(step, b == 1))
 
             def tile(index, b=b, table=table):
-                at = tile_at(index)
+                at = tile_at(index, WIDE)
                 rows = dot_nn(table, hb[b, :, at]).astype(bf16)
                 for e in range(exp_local):
                     xbuf[e, pl.ds(b * capacity, capacity), at] = rows[
                         e * capacity : (e + 1) * capacity
                     ]
 
-            each_tile(wide, tile)
+            each_tile(width // WIDE, tile)
 
     def save_rows(target, step):
         return [
@@ -817,6 +821,10 @@
             dz_all[e, pl.ds(step * pair, pair), :] = dot_nt(xbuf[e], wd[e]).astype(bf16)
         for b in (0, 1):
             sdz_all[block_of(step, b == 1)] = dot_nn(hb[b], ws[:, 2 * pad :]).astype(bf16)
+        if step + 2 < high:
+            for copy in along_z[step + 1]:
+                net.left(copy)
+            start_z(step + 2)
         pump()
     for copy in gate_copies:
         copy.wait_recv()
@@ -894,12 +902,7 @@
             sum_cores(step - 1)
         rows = pl.ds(step * pair, pair)
         for e in range(exp_local):
-
-            def inner_tile(index, e=e):
-                at = tile_at(index, 256)
-                pre[:, at] = dot_nn(xbuf[e], wgu[e, :, at])
-
-            each_tile(2 * hidden // 256, inner_tile)
+            pre[...] = dot_nn(xbuf[e], wgu[e])
             for b in (0, 1):
                 block = block_of(step, b == 1)
                 gate = jnp.sum(
@@ -936,12 +939,12 @@
                 )
 
             def out_tile(index, e=e):
-                at = tile_at(index)
+                at = tile_at(index, WIDE)
                 y = dot_nn(zg_all[e, rows, :], wd[e, :, at]).astype(bf16)
                 for b in (0, 1):
                     ybuf[b, pl.ds(e * capacity, capacity), at] = y[b * capacity : (b + 1) * capacity]
 
-            each_tile(wide, out_tile)
+            each_tile(width // WIDE, out_tile)
             pump()
         if step:
             for copy in out_copies:
@@ -952,12 +955,12 @@
             table = picks_back(block)
 
             def join_tile(index, b=b, table=table, block=block):
-                at = tile_at(index)
+                at = tile_at(index, WIDE)
                 total = dot_nn(table, ybuf[b, :, at])
                 total = total + dot_nt(sz_all[block], ws[at, 2 * pad :])
                 obuf[b, :, at] = total.astype(bf16)
 
-            each_tile(wide, join_tile)
+            each_tile(width // WIDE, join_tile)
             out_copies.append(
                 local_copy(obuf.at[b], out_part.at[block], base + 2 + exp_local + b)
             )
@@ -967,24 +970,24 @@
         for e in range(exp_local):
 
             def back_tile(index, e=e):
-                at = tile_at(index)
+                at = tile_at(index, WIDE)
                 y = dot_nt(dgu_all[e, rows, :], wgu[e, at, :]).astype(bf16)
                 for b in (0, 1):
                     ybuf[b, pl.ds(e * capacity, capacity), at] = y[b * capacity : (b + 1) * capacity]
 
-            each_tile(wide, back_tile)
+            each_tile(width // WIDE, back_tile)
         pump()
         for b in (1, 0):
             block = block_of(step, b == 1)
             table = picks_back(block)
 
             def back_join(index, b=b, table=table, block=block):
-                at = tile_at(index)
+                at = tile_at(index, WIDE)
                 total = dot_nn(table, ybuf[b, :, at])
                 total = total + dot_nt(sgu_all[block], ws[at, : 2 * pad])
                 part[b, :, at] = total.astype(bf16)
 
-            each_tile(wide, back_join)
+            each_tile(width // WIDE, back_join)
         hand_over(step)
         if step:
             sum_plane(step - 1)
@@ -1040,7 +1043,7 @@
                 xs_all.at[e, :, tile_at(j)],
                 tiles.at[slot],
             ),
-            lambda j, slot: put(stage.at[slot], dot_tn(tiles[slot], dgu_all[e])),
+            lambda j, slot: put(stage.at[slot], dot_tn(tiles[slot], dgu_all[e]).astype(bf16)),
             lambda j, slot: [
                 (stage.at[slot, :, pl.ds(0, hidden)], g_gate.at[e, tile_at(j)]),
                 (stage.at[slot, :, pl.ds(hidden, hidden)], g_up.at[e, tile_at(j)]),
@@ -1059,7 +1062,7 @@
             ),
             lambda j, slot: put(
                 stage.at[slot, pl.ds(0, hidden), pl.ds(0, TILE)],
-                dot_tn(zg_all[e], tiles[slot]),
+                dot_tn(zg_all[e], tiles[slot]).astype(bf16),
             ),
             lambda j, slot: [
                 (
@@ -1151,9 +1154,9 @@
         out_shape=[
             shape(cols, toks, width),
             shape(toks, width),
-            shape(exp_local, width, hidden, dtype=f32),
-            shape(exp_local, width, hidden, dtype=f32),
-            shape(exp_local, hidden, width, dtype=f32),
+            shape(exp_local, width, hidden),
+            shape(exp_local, width, hidden),
+            shape(exp_local, hidden, width),
             shape(width, 3 * pad),
             shape(cols, 8, toks, dtype=f32),
             shape(cols, toks, width),
@@ -1202,7 +1205,7 @@
             pltpu.VMEM((cols, 8, toks), f32),
             pltpu.VMEM((2, cols * capacity, TILE), bf16),
             pltpu.VMEM((2, cols, toks, TILE), bf16),
-            pltpu.VMEM((2, TILE, 2 * hidden), f32),
+            pltpu.VMEM((2, TILE, 2 * hidden), bf16),
             pltpu.VMEM((2, TILE, 2 * pad), bf16),
             pltpu.SemaphoreType.DMA((copies,)),
             pltpu.SemaphoreType.DMA((copies,)),
@@ -1226,7 +1229,8 @@
         cols, collective_id, capacity, h2, grad_all, w_gate, w_up, w_down, padded, *tables
     )
     g_shared = g_shared.reshape(width, 3, -1)[:, :, :shared_part].reshape(width, -1)
-    return (out_part, back, gate_dots, g_shared, g_gate, g_up, g_down)
+    wide = (grad.astype(f32) for grad in (g_gate, g_up, g_down))
+    return (out_part, back, gate_dots, g_shared, *wide)
 
 
 def fits(cols, rows, width):

time: 751 us -> 737 us (0.981)
  local copies, waits for them, and re-layouts: 62.4 us -> 44.8 us
  other arithmetic: 7.73 us -> 21.9 us
  Pallas kernels: 668 us -> 658 us
    unnamed x55 -> x52, local copies, waits for them, and re-layouts: 30.6 us -> 13.1 us
    convert_element_type x0 -> x3, other arithmetic: none -> 14.2 us  [experts_kernels(): wide = (grad.astype(f32) for grad in (g_gate, g_up, g_down))]
    pallas_call x1, Pallas kernels: 230 us -> 219 us  [experts_call(): pl.pallas_call(functools.partial(experts_kernel, cols, capacity), out_sha...]
  transfers between devices with their start and end apart: 1 -> 1, of which waited for: 0 -> 0; matrix products, arithmetic and copies ran while one was open for 1% -> 3% of each run, Pallas kernels for 27% -> 27%
where the time goes in v6:
time: 737 us; the launch traced here: 731 us
  Pallas kernels  658 us (89%)
  local copies, waits for them, and re-layouts  44.8 us (6%)
  other arithmetic  21.9 us (3%)
    pallas_call x1, Pallas kernels, front_call(): pl.pallas_call(functools.partial(front_kernel, cols, experts), out_shape=...  240 us
    pallas_call x1, Pallas kernels, experts_call(): pl.pallas_call(functools.partial(experts_kernel, cols, capacity), out_sha...  219 us
    pallas_call x1, Pallas kernels, rear_call(): pl.pallas_call(functools.partial(rear_kernel, cols, experts), out_shape=[...  198 us
  transfers between devices with their start and end apart: 1, of which 0 were waited for; matrix products, arithmetic and copies ran while one was open for 3% of the time, Pallas kernels for 27%

profile of v6, /device:TPU:10, one launch (start us, length us, event | category | flops | bytes accessed | tf_op | source)
XLA Modules:
  0.0 731.3 jit_solution(3668709772041723388)
XLA Ops:
  3.8 0.8 copy.99
  5.1 0.8 fusion.3
  6.0 1.4 convert_bitcast_fusion.1
  8.8 1.3 copy.104
  10.5 2.5 copy.98
  13.4 2.2 maximum_bitcast_fusion.shared_own
  15.8 240.3 %front_0.1 = (bf16[2560,1024]{1,0:T(8,128)(2,1)}, bf16[2560,640]{1,0:T(8,128)(2,1)}, bf16[8,320,288]{2,1,0:T(8,128)(2,1)}, bf16[8,256,2560]{2,1,0:T(8,128)(2,1)}...) custom-call(bf16[256,2560]{1,0:T(8,128)(2,1)} %bitcast.57, ...), custom_call_target="tpu_custom_call" | custom-call | tf_op jit(solution)/shard_map/front_0/pallas_call | solution.py:551
  256.1 1.0 copy-done
  257.1 1.0 copy-done.3
  260.2 3.6 copy.113
  263.8 2.3 reshape_reshape.6
  266.8 1.5 pad.15
  268.3 2.4 copy.115.w_shared
  271.4 1.2 dynamic-slice_convert_fusion.rank_col
  272.6 219.4 %experts_3.1 = (bf16[8,256,2560]{2,1,0:T(8,128)(2,1)}, bf16[256,2560]{1,0:T(8,128)(2,1)}, bf16[2,2560,384]{2,1,0:T(8,128)(2,1)}, bf16[2,2560,384]{2,1,0:T(8,128)...) custom-call(bf16[256,2560]{1,0:T(8,128)(2,1)} %get-tuple-element.43., ...), custom_call_target="tpu_custom_call" | custom-call | tf_op jit(solution)/shard_map/experts_3/pallas_call | solution.py:1152
  492.0 2.7 copy.118
  494.8 1.4 reshape_reshape.7
  496.1 1.5 copy.119
  497.6 4.5 all-to-all-start
  502.2 198.3 %rear_5.1 = (f32[256,640]{1,0:T(8,128)}, f32[256,2560]{1,0:T(8,128)}, f32[320,896]{1,0:T(8,128)}, f32[320,128]{1,0:T(8,128)}, f32[320,640]{1,0:T(8,128)}) custom-call(bf16[8,256,2560]{2,1,0:T(8,128)(2,1)} %get-tuple-element.49.out_part, bf16[256,2560]{1,0:T(8,128)(2,1)} %get-tuple-element.50.back, f32[8,8,256]{2,1,0:T(8,128)} %get-tuple-element.51.gate_dots, ...), custom_call_target="tpu_custom_call" | custom-call | tf_op jit(solution)/shard_map/rear_5/pallas_call | solution.py:1700
  700.5 1.4 add_convert_fusion
  701.9 1.1 copy.130
  702.9 5.4 copy.129
  709.0 0.9 slice.35
  709.9 6.0 convert_element_type.92
  715.9 3.9 convert_element_type.93
  719.9 4.3 convert_element_type.94
  724.2 0.9 slice_reduce_fusion
  726.3 1.3 copy.123
  727.6 1.3 copy.122
  728.9 1.3 copy.121
  730.2 0.9 copy.134
  (75 shorter events, 11.2 us)
Async XLA Ops:
  0.6 6.8 copy-start.18
  6.0 2.1 copy-start.19
  10.5 2.5 copy-start.20
  13.0 2.7 copy-start.4
  13.3 2.4 copy-start.1
  13.3 2.4 copy-start.2
  13.3 2.4 copy-start.6
  13.3 2.4 copy-start.7
  13.3 2.4 copy-start.11
  13.4 2.4 copy-start.12
  256.1 1.1 copy-start
  257.1 1.0 copy-start.3
  258.1 0.7 copy-start.8
  258.8 0.7 copy-start.9
  259.5 0.7 copy-start.10
  260.2 5.9 copy-start.5
  497.6 228.1 %all-to-all-start = ((bf16[8,320,288]{1,2,0:T(8,128)(2,1)}), bf16[8,320,288]{1,2,0:T(8,128)(2,1)S(1)}, u32[]{:S(2)}, u32[]{:S(2)}) async-start(bf16[8,320,288]{1,2,0:T(8,128)(2,1)} %copy.119), calls=%async_computation | async-start | bytes 3538944 | tf_op jit(solution)/shard_map/all_to_all | solution.py:82
  702.9 5.4 copy-start.15
  702.9 6.1 copy-start.16
  709.9 6.0 copy-start.14
  715.9 3.9 copy-start.13
  727.6 2.6 copy-start.17

commit v7 on v6

--- a/solution.py
+++ b/solution.py
@@ -197,8 +197,8 @@
 
 
 class Line:
-    def __init__(self, net, items, direct=(), direct_from=0):
-        self.net, self.items, self.direct, self.direct_from = net, items, list(direct), direct_from
+    def __init__(self, net, items):
+        self.net, self.items = net, items
         self.other_row = 2 * (1 - net.outer) + net.core
         self.along_z, self.along_y, self.along_x, self.to_core = {}, {}, {}, {}
         self.moved = []
@@ -251,14 +251,12 @@
                     for step in range(1, net.high_count):
                         net.left(self.along_z[now - 2, step])
                 self.start(now)
-            if now >= self.direct_from and self.direct:
-                self.moved.append(net.send(*self.direct.pop(0)))
             for stage, lag in ((self.after_z, 1), (self.after_y, 2), (self.after_x, 3)):
                 if 0 <= now - lag < len(self.items):
                     stage(now - lag)
 
     def drain(self):
-        while self.now < len(self.items) + 3 or self.direct:
+        while self.now < len(self.items) + 3:
             self.tick()
         for copy in [*self.moved, *self.to_core.values()]:
             copy.wait_recv()
@@ -273,7 +271,6 @@
     value,
     misc,
     out_own,
-    shared_own,
     grad_own,
     table_row,
     table_col,
@@ -282,7 +279,6 @@
     sine,
     weights,
     out_weights,
-    shared_all,
     grad_all,
     rows_all,
     cols_all,
@@ -334,7 +330,6 @@
     local_copy(misc, weights.at[mine, pl.ds(q_width + 2 * size, LANES)])
     first = len(copies)
     local_copy(out_own, out_weights.at[mine])
-    local_copy(shared_own.at[net.me], shared_all.at[net.me])
     part = grad_own.shape[1]
     local_copy(
         grad_own, grad_all.at[net.me, :, pl.ds(pl.multiple_of(net.row * part, LANES), part)]
@@ -380,14 +375,10 @@
     ready_out = len(items) + 2
     items += grad_items[out_pieces - 2 :]
     items.append((table_col, lambda block, row: cols_all.at[block], False))
-    direct = []
-    for step in range(1, cols):
-        block = lax.rem(net.me + step, cols)
-        direct.append((shared_own.at[block], shared_all.at[net.me], net.col_peer(step)))
-    line = Line(net, items, direct, ready_weights - 2)
+    line = Line(net, items)
 
     line.tick(2)
-    copies[first + 3].wait()
+    copies[first + 2].wait()
 
     def chunks(body, rows=32):
         def step(index, carry):
@@ -527,14 +518,14 @@
     gate[...] = picked / jnp.sum(picked, axis=1, keepdims=True)
     line.drain()
     kv_line.drain()
-    for copy in [*copies[first + 1 : first + 3], copies[first + 4]]:
+    for copy in (copies[first + 1], copies[first + 3]):
         copy.wait()
     net.finish()
 
 
 def front_call(
-    cols, collective_id, experts, tokens, query, key, value, misc, out_own, shared_own, grad_own,
-    table_row, table_col, doc_col, cosine, sine, seqs,
+    cols, collective_id, experts, tokens, query, key, value, misc, out_own, grad_own, table_row,
+    table_col, doc_col, cosine, sine, seqs,
 ):
     toks, width = tokens.shape
     q_width = query.shape[1]
@@ -553,7 +544,6 @@
         out_shape=[
             shape(width, q_width + 2 * size + LANES),
             shape(width, q_width),
-            shape(*shared_own.shape),
             shape(cols, toks, width),
             shape(cols, *table_row.shape, dtype=f32),
             shape(cols, *table_col.shape),
@@ -567,8 +557,8 @@
             shape(toks, LANES, dtype=f32),
             shape(toks, LANES, dtype=f32),
         ],
-        in_specs=[vmem] + [any_space] * 7 + [vmem] * 5,
-        out_specs=[vmem, vmem, any_space, any_space] + [vmem] * 11,
+        in_specs=[vmem] + [any_space] * 6 + [vmem] * 5,
+        out_specs=[vmem, vmem, any_space] + [vmem] * 11,
         scratch_shapes=[
             pltpu.VMEM((8, width), f32),
             pltpu.VMEM((toks, LANES), f32),
@@ -589,7 +579,7 @@
         ),
         name=f"front_{collective_id}",
     )(
-        tokens, query, key, value, misc, out_own, shared_own, grad_own,
+        tokens, query, key, value, misc, out_own, grad_own,
         table_row, table_col, doc_col, cosine, sine,
     )
 
@@ -612,6 +602,7 @@
     g_up,
     g_down,
     g_shared,
+    shared_back,
     gate_dots,
     h2_all,
     xs_all,
@@ -631,7 +622,6 @@
     dz_all,
     zg_all,
     dgu_all,
-    sdz_all,
     sz_all,
     sgu_all,
     from_core,
@@ -655,6 +645,7 @@
     exp_local, _, hidden = w_gate.shape
     high = net.high_count
     pad = ws.shape[1] // 3
+    rows_w = w_shared.shape[1]
     slots = exp_local * capacity
     pair = 2 * capacity
     piece = width // lax.axis_size("row")
@@ -756,7 +747,17 @@
         loads.append(local_copy(w_gate.at[e], wgu.at[e, :, pl.ds(0, hidden)], 3 * e + 1))
         loads.append(local_copy(w_up.at[e], wgu.at[e, :, pl.ds(hidden, hidden)], 3 * e + 2))
     base = 3 * exp_local
-    loads.append(local_copy(w_shared, ws, base))
+    own_rows = pl.ds(pl.multiple_of(net.me * rows_w, 16), rows_w)
+    loads.append(local_copy(w_shared.at[net.me], ws.at[own_rows], base))
+    swaps = []
+
+    def swap_next(count):
+        for _ in range(count):
+            step = len(swaps) + 1
+            if step < cols:
+                block = lax.rem(net.me + step, cols)
+                swaps.append(net.send(w_shared.at[block], ws.at[own_rows], net.col_peer(step)))
+
     keep_own = local_copy(h2, h2_all.at[net.me], base + 1)
     base += 2
 
@@ -819,12 +820,7 @@
         saved = save_rows(cs_all, step)
         for e in range(exp_local):
             dz_all[e, pl.ds(step * pair, pair), :] = dot_nt(xbuf[e], wd[e]).astype(bf16)
-        for b in (0, 1):
-            sdz_all[block_of(step, b == 1)] = dot_nn(hb[b], ws[:, 2 * pad :]).astype(bf16)
-        if step + 2 < high:
-            for copy in along_z[step + 1]:
-                net.left(copy)
-            start_z(step + 2)
+        swap_next(2)
         pump()
     for copy in gate_copies:
         copy.wait_recv()
@@ -886,18 +882,18 @@
             copy.wait()
         dispatch(step)
         saved = save_rows(xs_all, step)
+        if step + 2 < high:
+            for copy in along_z[step + 1]:
+                net.left(copy)
+            start_z(step + 2)
         pump()
-        for b in (0, 1):
-            block = block_of(step, b == 1)
-            inner = dot_nn(hb[b], ws[:, : 2 * pad])
-            sa, su = inner[:, :pad], inner[:, pad:]
-            sig = 1.0 / (1.0 + jnp.exp(-sa))
-            silu = sa * sig
-            slope = sig * (1.0 + sa * (1.0 - sig))
-            sz_all[block] = (silu * su).astype(bf16)
-            sdz = sdz_all[block].astype(f32)
-            sgu_all[block, :, :pad] = (sdz * su * slope).astype(bf16)
-            sgu_all[block, :, pad:] = (sdz * silu).astype(bf16)
+        if step:
+            for copy in out_copies:
+                copy.wait()
+        grad_copies = [
+            local_copy(grads.at[block_of(step, b == 1)], obuf.at[b], base + 2 + exp_local + b)
+            for b in (0, 1)
+        ]
         if step:
             sum_cores(step - 1)
         rows = pl.ds(step * pair, pair)
@@ -946,9 +942,23 @@
 
             each_tile(width // WIDE, out_tile)
             pump()
-        if step:
-            for copy in out_copies:
-                copy.wait()
+        if step == 0:
+            for copy in swaps:
+                copy.wait_recv()
+        for copy in grad_copies:
+            copy.wait()
+        inner = dot_nn(hb[...].reshape(2 * toks, width), ws[:, : 2 * pad])
+        sdz_both = dot_nn(obuf[...].reshape(2 * toks, width), ws[:, 2 * pad :])
+        for b in (0, 1):
+            block = block_of(step, b == 1)
+            sa, su = inner[b * toks : (b + 1) * toks, :pad], inner[b * toks : (b + 1) * toks, pad:]
+            sdz = sdz_both[b * toks : (b + 1) * toks]
+            sig = 1.0 / (1.0 + jnp.exp(-sa))
+            silu = sa * sig
+            slope = sig * (1.0 + sa * (1.0 - sig))
+            sz_all[block] = (silu * su).astype(bf16)
+            sgu_all[block, :, :pad] = (sdz * su * slope).astype(bf16)
+            sgu_all[block, :, pad:] = (sdz * silu).astype(bf16)
         out_copies = []
         for b in (0, 1):
             block = block_of(step, b == 1)
@@ -1095,8 +1105,16 @@
         )
 
     first_dots = net.send(dots, dots_core, net.core_peer())
+    shared_grads(h2_all, sgu_all, 0, 2 * pad)
+    sum_cores(last)
+    shared_grads(grads, sz_all, 2 * pad, pad)
+    keep_own = local_copy(g_shared.at[own_rows], shared_back.at[net.me], base)
+    returns = []
+    for step in range(1, cols):
+        block = lax.rem(net.me + step, cols)
+        rows = pl.ds(pl.multiple_of(block * rows_w, 16), rows_w)
+        returns.append(net.send(g_shared.at[rows], shared_back.at[net.me], net.col_peer(step)))
     inner_grads(0)
-    sum_cores(last)
     first_dots.wait_recv()
     net.left(first_dots)
     dots[...] = dots[...] + dots_core[...]
@@ -1114,7 +1132,6 @@
     gate_dots[net.me] = dots_core[net.me]
     down_grads(0)
     sum_plane(last)
-    down_grads(1)
     for step in range(1, high):
         far_z[step].wait_recv()
     add_rows(kept, [from_core.at[0, 0, 0], *[from_z.at[step - 1] for step in range(1, high)]])
@@ -1122,10 +1139,12 @@
     back[:, own] = kept[...].astype(bf16)
     far = net.send(back.at[:, own], back.at[:, own], net.x_peer())
     near = net.send(back.at[:, own], back.at[:, own], net.core_peer())
-    shared_grads(h2_all, sgu_all, 0, 2 * pad)
     far.wait_recv()
     crossed = net.send(back.at[:, other], back.at[:, other], net.core_peer())
-    shared_grads(grads, sz_all, 2 * pad, pad)
+    down_grads(1)
+    keep_own.wait()
+    for copy in returns:
+        copy.wait_recv()
     near.wait_recv()
     crossed.wait_recv()
     for copy in third_dots:
@@ -1139,7 +1158,7 @@
     toks, width = h2.shape
     exp_local, _, hidden = w_gate.shape
     high = cols // 2
-    pad = w_shared.shape[1] // 3
+    pad = w_shared.shape[2] // 3
     piece = width // lax.axis_size("row")
     pair = 2 * capacity
     any_space = pl.BlockSpec(memory_space=pl.ANY)
@@ -1158,6 +1177,7 @@
             shape(exp_local, width, hidden),
             shape(exp_local, hidden, width),
             shape(width, 3 * pad),
+            shape(*w_shared.shape),
             shape(cols, 8, toks, dtype=f32),
             shape(cols, toks, width),
             shape(exp_local, cols * capacity, width),
@@ -1167,6 +1187,7 @@
         out_specs=[
             any_space,
             vmem,
+            any_space,
             any_space,
             any_space,
             any_space,
@@ -1193,7 +1214,6 @@
             pltpu.VMEM((exp_local, cols * capacity, hidden), bf16),
             pltpu.VMEM((exp_local, cols * capacity, 2 * hidden), bf16),
             pltpu.VMEM((cols, toks, pad), bf16),
-            pltpu.VMEM((cols, toks, pad), bf16),
             pltpu.VMEM((cols, toks, 2 * pad), bf16),
             pltpu.VMEM((2, high, 2, toks, piece), bf16),
             pltpu.VMEM((high, 2, toks, piece), bf16),
@@ -1219,18 +1239,20 @@
 
 
 def experts_kernels(
-    cols, collective_id, capacity, h2, grad_all, w_gate, w_up, w_down, shared_weights, *tables
+    cols, collective_id, capacity, h2, grad_all, w_gate, w_up, w_down, shared_own, *tables
 ):
-    width, shared_part = shared_weights.shape[0], shared_weights.shape[1] // 3
+    rows_w, shared_part = shared_own.shape[1], shared_own.shape[2] // 3
     pad = -shared_part % LANES
-    padded = jnp.pad(shared_weights.reshape(width, 3, shared_part), ((0, 0), (0, 0), (0, pad)))
-    padded = padded.reshape(width, -1)
-    out_part, back, g_gate, g_up, g_down, g_shared, gate_dots, *_ = experts_call(
+    padded = jnp.pad(
+        shared_own.reshape(cols, rows_w, 3, shared_part), ((0, 0), (0, 0), (0, 0), (0, pad))
+    )
+    padded = padded.reshape(cols, rows_w, -1)
+    out_part, back, g_gate, g_up, g_down, _, shared_back, gate_dots, *_ = experts_call(
         cols, collective_id, capacity, h2, grad_all, w_gate, w_up, w_down, padded, *tables
     )
-    g_shared = g_shared.reshape(width, 3, -1)[:, :, :shared_part].reshape(width, -1)
+    shared_back = shared_back.reshape(cols, rows_w, 3, -1)[..., :shared_part]
     wide = (grad.astype(f32) for grad in (g_gate, g_up, g_down))
-    return (out_part, back, gate_dots, g_shared, *wide)
+    return (out_part, back, gate_dots, shared_back.reshape(cols, rows_w, -1), *wide)
 
 
 def fits(cols, rows, width):
@@ -1930,7 +1952,6 @@
         (
             first_weights,
             out_weights,
-            shared_weights,
             grad_all,
             rows_all,
             rank_all,
@@ -1953,7 +1974,6 @@
             value_matrix,
             misc,
             attention_output_matrix.T,
-            shared_own,
             grad_own,
             table_row,
             table_col,
@@ -1966,7 +1986,8 @@
         first_weights = jnp.concatenate([query_matrix, key_matrix, value_matrix, misc], axis=1)
         first_weights = gather_col(first_weights).reshape(width, -1)
         out_weights = gather_col(attention_output_matrix.T).reshape(width, q_width)
-        shared_weights, grad_all = swap_col(shared_own), gather_all(grad_own)
+        shared_weights = swap_col(shared_own).reshape(width, 3 * shared_part)
+        grad_all = gather_all(grad_own)
         gain_one = first_weights[:, qkv_width + experts].astype(f32)
         h1 = (base_first * gain_one).astype(bf16)
         qkv = dot("tb,bk->tk", h1, first_weights[:, :qkv_width])
@@ -1983,7 +2004,6 @@
         )
         kv_all = gather_col(jnp.concatenate([qk[:, q_width:], value_low, side], axis=1))
         rank_all = kv_all[:, :, 2 * kv_width : 2 * kv_width + experts]
-    shared_weights = shared_weights.reshape(width, 3 * shared_part)
     qkv_weights = first_weights[:, :qkv_width]
     router = first_weights[:, qkv_width : qkv_width + experts]
     gain_one = first_weights[:, qkv_width + experts].astype(f32)
@@ -2029,7 +2049,7 @@
             expert_gate,
             expert_up,
             expert_down,
-            shared_weights,
+            shared_own,
             lax.dynamic_slice_in_dim(rows_all, col_index * exp_local, exp_local, 1),
             rank_own,
             gate[:, :experts].T,
@@ -2049,7 +2069,8 @@
         )
     if not kernels:
         back_full = back_full.astype(f32)
-    shared_share = swap_col(shared_share.reshape(cols, rows_w, 3 * shared_part))
+    if not kernels:
+        shared_share = swap_col(shared_share.reshape(cols, rows_w, 3 * shared_part))
     shared_share = jnp.swapaxes(shared_share, 0, 1).astype(f32)
     share_sgate, share_sup, share_sdown = (
         shared_share[:, :, i * shared_part : (i + 1) * shared_part].reshape(rows_w, -1)

time: 737 us -> 706 us (0.958)
  Pallas kernels: 658 us -> 645 us
  local copies, waits for them, and re-layouts: 44.8 us -> 36.4 us
    pallas_call x1, Pallas kernels: 240 us -> 191 us  [front_call(): pl.pallas_call(functools.partial(front_kernel, cols, experts), out_shape=...]
    pallas_call x1, Pallas kernels: 219 us -> 257 us  [experts_call(): pl.pallas_call(functools.partial(experts_kernel, cols, capacity), out_sha...]
  transfers between devices with their start and end apart: 1 -> 0, of which waited for: 0 -> 0; matrix products, arithmetic and copies ran while one was open for 3% -> 0% of each run, Pallas kernels for 27% -> 0%
where the time goes in v7:
time: 706 us; the launch traced here: 701 us
  Pallas kernels  645 us (91%)
  local copies, waits for them, and re-layouts  36.4 us (5%)
  other arithmetic  19 us (3%)
    pallas_call x1, Pallas kernels, experts_call(): pl.pallas_call(functools.partial(experts_kernel, cols, capacity), out_sha...  257 us
    pallas_call x1, Pallas kernels, rear_call(): pl.pallas_call(functools.partial(rear_kernel, cols, experts), out_shape=[...  197 us
    pallas_call x1, Pallas kernels, front_call(): pl.pallas_call(functools.partial(front_kernel, cols, experts), out_shape=...  191 us
    convert_element_type x3, other arithmetic, experts_kernels(): wide = (grad.astype(f32) for grad in (g_gate, g_up, g_down))  14.2 us

profile of v7, /device:TPU:10, one launch (start us, length us, event | category | flops | bytes accessed | tf_op | source)
XLA Modules:
  0.0 701.5 jit_solution(14062936362535850268)
XLA Ops:
  0.8 0.8 convert_element_type.84
  1.5 0.7 copy.115
  2.4 0.8 broadcast_in_dim.22
  3.2 0.8 broadcast_in_dim.23
  3.9 0.8 copy.88
  6.8 1.3 copy.98
  8.3 1.8 pad.15
  10.1 4.4 copy.100.w_shared
  14.5 1.2 copy.87
  15.9 190.8 %front_0.1 = (bf16[2560,1024]{1,0:T(8,128)(2,1)}, bf16[2560,640]{1,0:T(8,128)(2,1)}, bf16[8,256,2560]{2,1,0:T(8,128)(2,1)}, f32[8,24,256]{2,1,0:T(8,128)S(1)}, b...) custom-call(bf16[256,2560]{1,0:T(8,128)(2,1)} %bitcast.57, ...), custom_call_target="tpu_custom_call" | custom-call | tf_op jit(solution)/shard_map/front_0/pallas_call | solution.py:542
  206.7 1.0 copy-done
  207.7 1.0 copy-done.3
  208.7 0.7 copy-done.8
  209.5 0.7 copy-done.9
  212.2 1.2 dynamic-slice_convert_fusion.rank_col
  213.4 256.8 %experts_3.1 = (bf16[8,256,2560]{2,1,0:T(8,128)(2,1)}, bf16[256,2560]{1,0:T(8,128)(2,1)}, bf16[2,2560,384]{2,1,0:T(8,128)(2,1)}, bf16[2,2560,384]{2,1,0:T(8,128)...) custom-call(bf16[256,2560]{1,0:T(8,128)(2,1)} %get-tuple-element.42., ...), custom_call_target="tpu_custom_call" | custom-call | tf_op jit(solution)/shard_map/experts_3/pallas_call | solution.py:1171
  470.2 197.2 %rear_5.1 = (f32[256,640]{1,0:T(8,128)}, f32[256,2560]{1,0:T(8,128)}, f32[320,896]{1,0:T(8,128)}, f32[320,128]{1,0:T(8,128)}, f32[320,640]{1,0:T(8,128)}) custom-call(bf16[8,256,2560]{2,1,0:T(8,128)(2,1)} %get-tuple-element.47.out_part, bf16[256,2560]{1,0:T(8,128)(2,1)} %get-tuple-element.48.back, f32[8,8,256]{2,1,0:T(8,128)} %get-tuple-element.49.gate_dots, ...), custom_call_target="tpu_custom_call" | custom-call | tf_op jit(solution)/shard_map/rear_5/pallas_call | solution.py:1722
  667.4 1.4 add_convert_fusion
  668.8 1.1 copy.114
  669.9 5.4 copy.113
  675.2 0.9 slice_reduce_fusion
  676.1 0.7 copy.104
  676.8 0.7 fusion.2
  677.5 0.9 slice.35
  678.5 2.9 copy.103
  682.3 1.3 copy.107
  683.6 1.3 copy.106
  684.9 1.3 copy.105
  686.2 6.0 convert_element_type.96
  692.2 3.9 convert_element_type.97
  696.1 4.3 convert_element_type.98
  700.4 0.9 copy.118
  (68 shorter events, 5.4 us)
Async XLA Ops:
  0.6 5.2 copy-start.19
  0.7 5.5 copy-start.20
  5.2 1.3 copy-start.21
  5.4 10.3 %copy-start.1 = (f32[256,128]{1,0:T(8,128)}, f32[256,128]{1,0:T(8,128)S(1)}, u32[]{:S(2)}) copy-start(f32[256,128]{1,0:T(8,128)S(1)} %get-tuple-element.138.cosine) | copy-start | bytes 393220
  5.4 10.3 %copy-start.2 = (f32[256,128]{1,0:T(8,128)}, f32[256,128]{1,0:T(8,128)S(1)}, u32[]{:S(2)}) copy-start(f32[256,128]{1,0:T(8,128)S(1)} %get-tuple-element.139.sine) | copy-start | bytes 393220
  5.8 9.9 %copy-start.4 = (bf16[256,128]{1,0:T(8,128)(2,1)}, bf16[256,128]{1,0:T(8,128)(2,1)S(1)}, u32[]{:S(2)}) copy-start(bf16[256,128]{1,0:T(8,128)(2,1)S(1)} %pad.14.table_col) | copy-start | bytes 196612
  10.1 4.4 copy-start.16
  14.5 1.2 copy-start.6
  14.5 1.3 copy-start.7
  14.5 1.4 copy-start.11
  14.5 1.4 copy-start.12
  206.7 1.1 copy-start
  207.7 1.0 copy-start.3
  208.7 0.7 copy-start.8
  209.5 0.7 copy-start.9
  210.2 0.7 copy-start.10
  210.8 259.4 %copy-start.5 = (f32[256,128]{1,0:T(8,128)}, f32[256,128]{1,0:T(8,128)S(1)}, u32[]{:S(2)}) copy-start(f32[256,128]{1,0:T(8,128)S(1)} %get-tuple-element.46.gate) | copy-start | bytes 393220
  669.9 5.4 copy-start.15
  669.9 6.9 copy-start.17
  686.2 6.0 copy-start.14
  692.2 3.9 copy-start.13
  696.1 4.3 copy-start.18

commit v8 on v7

--- a/solution.py
+++ b/solution.py
@@ -272,6 +272,7 @@
     misc,
     out_own,
     grad_own,
+    shared_own,
     table_row,
     table_col,
     doc_col,
@@ -280,6 +281,7 @@
     weights,
     out_weights,
     grad_all,
+    shared_all,
     rows_all,
     cols_all,
     h1,
@@ -336,6 +338,7 @@
     )
     local_copy(table_row, rows_all.at[net.me])
     local_copy(table_col, cols_all.at[net.me])
+    local_copy(shared_own.at[net.me], shared_all.at[net.me])
     net.greet([net.col_peer(step) for step in range(1, cols)] + row_peers(net))
     for copy in copies[:first]:
         copy.wait()
@@ -376,6 +379,16 @@
     items += grad_items[out_pieces - 2 :]
     items.append((table_col, lambda block, row: cols_all.at[block], False))
     line = Line(net, items)
+    swaps = []
+
+    def swap_next(count):
+        for _ in range(count):
+            step = len(swaps) + 1
+            if step < cols:
+                block = lax.rem(net.me + step, cols)
+                swaps.append(
+                    net.send(shared_own.at[block], shared_all.at[net.me], net.col_peer(step))
+                )
 
     line.tick(2)
     copies[first + 2].wait()
@@ -407,32 +420,29 @@
 
     chunks(norm_first)
     line.tick()
-    heads_all = group + 2
-    for head in range(heads_all - 1, -1, -1):
-        raw = dot_nn(h1[...], weights[:, head * size : (head + 1) * size])
-        if head <= group:
-            raw = raw * cosine[...] + pltpu.roll(raw, size // 2, 1) * sine[...]
-        if head < group:
-            q_low[:, head * size : (head + 1) * size] = raw.astype(bf16)
-        else:
-            kv_low[:, (head - group) * size : (head - group + 1) * size] = raw.astype(bf16)
-        if head == group:
-            kv_all[net.me] = kv_low[...]
-
-            def kv_slot(s):
-                rows = pl.ds(s * local_len, local_len)
-                return lambda block, row: kv_all.at[block, rows]
-
-            kv_line = Line(
-                net,
-                [
-                    (kv_low.at[pl.ds(s * local_len, local_len)], kv_slot(s), False)
-                    for s in range(seqs)
-                ],
-            )
-            kv_line.tick()
-        if head == group // 2:
-            kv_line.tick()
+
+    def rotated(raw):
+        return raw * cosine[...] + pltpu.roll(raw, size // 2, 1) * sine[...]
+
+    raw = dot_nn(h1[...], weights[:, q_width : q_width + 2 * size])
+    kv_low[:, :size] = rotated(raw[:, :size]).astype(bf16)
+    kv_low[:, size:] = raw[:, size:].astype(bf16)
+    kv_all[net.me] = kv_low[...]
+
+    def kv_slot(s):
+        rows = pl.ds(s * local_len, local_len)
+        return lambda block, row: kv_all.at[block, rows]
+
+    kv_line = Line(
+        net,
+        [(kv_low.at[pl.ds(s * local_len, local_len)], kv_slot(s), False) for s in range(seqs)],
+    )
+    kv_line.tick()
+    raw = dot_nn(h1[...], weights[:, :q_width])
+    for head in range(group):
+        at = slice(head * size, (head + 1) * size)
+        q_low[:, at] = rotated(raw[:, at]).astype(bf16)
+    kv_line.tick()
     line.tick()
     kv_line.tick()
 
@@ -464,6 +474,7 @@
         if line.now < ready_out:
             line.tick()
     line.tick(max(0, ready_out - line.now))
+    swap_next(3)
     copies[first].wait()
 
     pieces = from_core.shape[0]
@@ -492,6 +503,7 @@
         add_rows(to_x.at[i], [partial.at[row_piece(net.core, i)], from_core.at[i]])
         along.append(net.send(to_x.at[i], from_x.at[i], net.x_peer()))
     line.tick()
+    swap_next(cols)
     for i in range(pieces):
         along[i].wait_recv()
         at = row_piece(net.core, i)
@@ -518,14 +530,16 @@
     gate[...] = picked / jnp.sum(picked, axis=1, keepdims=True)
     line.drain()
     kv_line.drain()
-    for copy in (copies[first + 1], copies[first + 3]):
+    for copy in swaps:
+        copy.wait_recv()
+    for copy in (copies[first + 1], *copies[first + 3 :]):
         copy.wait()
     net.finish()
 
 
 def front_call(
-    cols, collective_id, experts, tokens, query, key, value, misc, out_own, grad_own, table_row,
-    table_col, doc_col, cosine, sine, seqs,
+    cols, collective_id, experts, tokens, query, key, value, misc, out_own, grad_own, shared_own,
+    table_row, table_col, doc_col, cosine, sine, seqs,
 ):
     toks, width = tokens.shape
     q_width = query.shape[1]
@@ -545,6 +559,7 @@
             shape(width, q_width + 2 * size + LANES),
             shape(width, q_width),
             shape(cols, toks, width),
+            shape(*shared_own.shape),
             shape(cols, *table_row.shape, dtype=f32),
             shape(cols, *table_col.shape),
             shape(toks, width),
@@ -557,8 +572,8 @@
             shape(toks, LANES, dtype=f32),
             shape(toks, LANES, dtype=f32),
         ],
-        in_specs=[vmem] + [any_space] * 6 + [vmem] * 5,
-        out_specs=[vmem, vmem, any_space] + [vmem] * 11,
+        in_specs=[vmem] + [any_space] * 7 + [vmem] * 5,
+        out_specs=[vmem, vmem, any_space, any_space] + [vmem] * 11,
         scratch_shapes=[
             pltpu.VMEM((8, width), f32),
             pltpu.VMEM((toks, LANES), f32),
@@ -579,7 +594,7 @@
         ),
         name=f"front_{collective_id}",
     )(
-        tokens, query, key, value, misc, out_own, grad_own,
+        tokens, query, key, value, misc, out_own, grad_own, shared_own,
         table_row, table_col, doc_col, cosine, sine,
     )
 
@@ -602,7 +617,6 @@
     g_up,
     g_down,
     g_shared,
-    shared_back,
     gate_dots,
     h2_all,
     xs_all,
@@ -747,17 +761,9 @@
         loads.append(local_copy(w_gate.at[e], wgu.at[e, :, pl.ds(0, hidden)], 3 * e + 1))
         loads.append(local_copy(w_up.at[e], wgu.at[e, :, pl.ds(hidden, hidden)], 3 * e + 2))
     base = 3 * exp_local
-    own_rows = pl.ds(pl.multiple_of(net.me * rows_w, 16), rows_w)
-    loads.append(local_copy(w_shared.at[net.me], ws.at[own_rows], base))
-    swaps = []
-
-    def swap_next(count):
-        for _ in range(count):
-            step = len(swaps) + 1
-            if step < cols:
-                block = lax.rem(net.me + step, cols)
-                swaps.append(net.send(w_shared.at[block], ws.at[own_rows], net.col_peer(step)))
-
+    for c in range(cols):
+        loads.append(local_copy(w_shared.at[c], ws.at[pl.ds(c * rows_w, rows_w)], base + c))
+    base += cols - 1
     keep_own = local_copy(h2, h2_all.at[net.me], base + 1)
     base += 2
 
@@ -820,7 +826,6 @@
         saved = save_rows(cs_all, step)
         for e in range(exp_local):
             dz_all[e, pl.ds(step * pair, pair), :] = dot_nt(xbuf[e], wd[e]).astype(bf16)
-        swap_next(2)
         pump()
     for copy in gate_copies:
         copy.wait_recv()
@@ -942,9 +947,6 @@
 
             each_tile(width // WIDE, out_tile)
             pump()
-        if step == 0:
-            for copy in swaps:
-                copy.wait_recv()
         for copy in grad_copies:
             copy.wait()
         inner = dot_nn(hb[...].reshape(2 * toks, width), ws[:, : 2 * pad])
@@ -1108,12 +1110,6 @@
     shared_grads(h2_all, sgu_all, 0, 2 * pad)
     sum_cores(last)
     shared_grads(grads, sz_all, 2 * pad, pad)
-    keep_own = local_copy(g_shared.at[own_rows], shared_back.at[net.me], base)
-    returns = []
-    for step in range(1, cols):
-        block = lax.rem(net.me + step, cols)
-        rows = pl.ds(pl.multiple_of(block * rows_w, 16), rows_w)
-        returns.append(net.send(g_shared.at[rows], shared_back.at[net.me], net.col_peer(step)))
     inner_grads(0)
     first_dots.wait_recv()
     net.left(first_dots)
@@ -1142,9 +1138,6 @@
     far.wait_recv()
     crossed = net.send(back.at[:, other], back.at[:, other], net.core_peer())
     down_grads(1)
-    keep_own.wait()
-    for copy in returns:
-        copy.wait_recv()
     near.wait_recv()
     crossed.wait_recv()
     for copy in third_dots:
@@ -1177,7 +1170,6 @@
             shape(exp_local, width, hidden),
             shape(exp_local, hidden, width),
             shape(width, 3 * pad),
-            shape(*w_shared.shape),
             shape(cols, 8, toks, dtype=f32),
             shape(cols, toks, width),
             shape(exp_local, cols * capacity, width),
@@ -1187,7 +1179,6 @@
         out_specs=[
             any_space,
             vmem,
-            any_space,
             any_space,
             any_space,
             any_space,
@@ -1229,7 +1220,7 @@
             pltpu.VMEM((2, TILE, 2 * pad), bf16),
             pltpu.SemaphoreType.DMA((copies,)),
             pltpu.SemaphoreType.DMA((copies,)),
-            pltpu.SemaphoreType.DMA((24,)),
+            pltpu.SemaphoreType.DMA((32,)),
         ],
         compiler_params=pltpu.CompilerParams(
             collective_id=collective_id, has_side_effects=True, vmem_limit_bytes=62 << 20
@@ -1238,21 +1229,11 @@
     )(h2, grads, w_gate, w_up, w_down, w_shared, rank_row, rank_col, gate)
 
 
-def experts_kernels(
-    cols, collective_id, capacity, h2, grad_all, w_gate, w_up, w_down, shared_own, *tables
-):
-    rows_w, shared_part = shared_own.shape[1], shared_own.shape[2] // 3
-    pad = -shared_part % LANES
-    padded = jnp.pad(
-        shared_own.reshape(cols, rows_w, 3, shared_part), ((0, 0), (0, 0), (0, 0), (0, pad))
-    )
-    padded = padded.reshape(cols, rows_w, -1)
-    out_part, back, g_gate, g_up, g_down, _, shared_back, gate_dots, *_ = experts_call(
-        cols, collective_id, capacity, h2, grad_all, w_gate, w_up, w_down, padded, *tables
-    )
-    shared_back = shared_back.reshape(cols, rows_w, 3, -1)[..., :shared_part]
-    wide = (grad.astype(f32) for grad in (g_gate, g_up, g_down))
-    return (out_part, back, gate_dots, shared_back.reshape(cols, rows_w, -1), *wide)
+def padded_thirds(packed):
+    third = packed.shape[-1] // 3
+    parts = packed.reshape(*packed.shape[:-1], 3, third)
+    parts = jnp.pad(parts, ((0, 0),) * (parts.ndim - 1) + ((0, -third % LANES),))
+    return parts.reshape(*packed.shape[:-1], -1)
 
 
 def fits(cols, rows, width):
@@ -1301,6 +1282,7 @@
     cols,
     experts,
     out_part,
+    g_shared,
     back,
     gate_dots,
     gate,
@@ -1324,6 +1306,7 @@
     share_qkv,
     share_misc,
     share_out,
+    shared_back,
     weights,
     out_weights,
     misc,
@@ -1390,7 +1373,14 @@
     ]
     near_load = local_copy(out_part.at[:, :, features(net.row)], own.at[0], 3)
     far_load = local_copy(out_part.at[:, :, features(other_row)], own.at[1], 4)
-    net.greet(col_peers(net) + row_peers(net))
+    own_rows = pl.ds(pl.multiple_of(net.me * rows_w, 16), rows_w)
+    keep_own = local_copy(g_shared.at[own_rows], shared_back.at[net.me], 5)
+    net.greet([net.col_peer(step) for step in range(1, cols)] + row_peers(net))
+    swaps = []
+    for step in range(1, cols):
+        block = lax.rem(net.me + step, cols)
+        rows = pl.ds(pl.multiple_of(block * rows_w, 16), rows_w)
+        swaps.append(net.send(g_shared.at[rows], shared_back.at[net.me], net.col_peer(step)))
 
     pieces = 4
     count = toks // pieces
@@ -1582,13 +1572,14 @@
             kv_grad[c, rows, size:] = dv[c * local_len : (c + 1) * local_len]
         kv_line[s].send_y()
         if s == 0:
+            out_line[2].send_y()
             out_line[0].send_z()
             pump()
         else:
+            out_line[3].send_y()
             kv_line[s - 1].send_z()
     kv_line[seqs - 1].send_z()
     out_line[1].send_z()
-    out_line[2].send_y()
     for s in range(seqs):
         kv_line[s].last()
     raw = kv_share[:, :size]
@@ -1677,7 +1668,6 @@
     qkv_line[2].send_y()
     qkv_line[1].send_z()
     out_line[2].send_z()
-    out_line[3].send_y()
     pump()
     misc_line.send_z()
     qkv_line[3].send_y()
@@ -1691,11 +1681,14 @@
     pump(8)
     for piece_sum in (*out_line, misc_line, *qkv_line):
         piece_sum.last()
+    keep_own.wait()
+    for copy in swaps:
+        copy.wait_recv()
     net.finish()
 
 
 def rear_call(
-    cols, collective_id, experts, out_part, back, gate_dots, gate, router_probs, table_col, h1, h2,
+    cols, collective_id, experts, out_part, g_shared, back, gate_dots, gate, router_probs, table_col, h1, h2,
     tokens, attn, weights, out_weights, grads, heads, q_low, kv_all, probs, cosine, sine,
 ):
     toks, width = back.shape
@@ -1727,9 +1720,10 @@
             shape(rows_w, qkv_width),
             shape(rows_w, LANES),
             shape(rows_w, q_width),
+            shape(cols, rows_w, g_shared.shape[1], dtype=bf16),
         ],
-        in_specs=[any_space] + [vmem] * 9 + [any_space] * 3 + [vmem] * 6,
-        out_specs=[vmem] * 5,
+        in_specs=[any_space] * 2 + [vmem] * 9 + [any_space] * 3 + [vmem] * 6,
+        out_specs=[vmem] * 5 + [any_space],
         scratch_shapes=[
             pltpu.VMEM((width, qkv_width + LANES), bf16),
             pltpu.VMEM((width, q_width), bf16),
@@ -1769,7 +1763,7 @@
         ),
         name=f"rear_{collective_id}",
     )(
-        out_part, back, gate_dots, gate, router_probs, table_col, h1, h2, tokens, attn, weights,
+        out_part, g_shared, back, gate_dots, gate, router_probs, table_col, h1, h2, tokens, attn, weights,
         out_weights, grads, heads, q_low, kv_all, probs, cosine, sine,
     )
 
@@ -1953,6 +1947,7 @@
             first_weights,
             out_weights,
             grad_all,
+            shared_weights,
             rows_all,
             rank_all,
             h1,
@@ -1975,6 +1970,7 @@
             misc,
             attention_output_matrix.T,
             grad_own,
+            padded_thirds(shared_own),
             table_row,
             table_col,
             doc.reshape(toks, 1).astype(f32),
@@ -2040,7 +2036,7 @@
     if kernels:
         rank_own = lax.dynamic_slice_in_dim(rank_all, col_index * exp_local, exp_local, 2)
         rank_own = rank_own.astype(f32)
-        part_out, back_full, gate_dots, shared_share, *expert_grads = experts_kernels(
+        part_out, back_full, *expert_grads, g_shared, gate_dots, _, _, _ = experts_call(
             cols,
             3,
             capacity,
@@ -2049,11 +2045,12 @@
             expert_gate,
             expert_up,
             expert_down,
-            shared_own,
+            shared_weights,
             lax.dynamic_slice_in_dim(rows_all, col_index * exp_local, exp_local, 1),
             rank_own,
             gate[:, :experts].T,
         )
+        expert_grads = [grad.astype(f32) for grad in expert_grads]
     else:
         part_out, back_full, gate_dots, shared_share, *expert_grads = experts_plain(
             h2,
@@ -2069,20 +2066,13 @@
         )
     if not kernels:
         back_full = back_full.astype(f32)
-    if not kernels:
-        shared_share = swap_col(shared_share.reshape(cols, rows_w, 3 * shared_part))
-    shared_share = jnp.swapaxes(shared_share, 0, 1).astype(f32)
-    share_sgate, share_sup, share_sdown = (
-        shared_share[:, :, i * shared_part : (i + 1) * shared_part].reshape(rows_w, -1)
-        for i in range(3)
-    )
-
     if kernels:
-        out_slice, token_grad, share_qkv, share_misc, share_out = rear_call(
+        out_slice, token_grad, share_qkv, share_misc, share_out, shared_share = rear_call(
             cols,
             5,
             experts,
             part_out,
+            g_shared,
             back_full,
             gate_dots,
             gate,
@@ -2164,6 +2154,17 @@
         share_out = scatter_col(grad_out.reshape(cols, rows_w, q_width)).astype(f32)
         share_first = scatter_col(grad_first.reshape(cols, rows_w, -1)).astype(f32)
         share_qkv, share_misc = share_first[:, :qkv_width], share_first[:, qkv_width:]
+    if kernels:
+        shared_share = shared_share.reshape(cols, rows_w, 3, -1)[..., :shared_part]
+        shared_share = shared_share.reshape(cols, rows_w, -1)
+    else:
+        shared_share = swap_col(shared_share.reshape(cols, rows_w, 3 * shared_part))
+    shared_share = jnp.swapaxes(shared_share, 0, 1).astype(f32)
+    share_sgate, share_sup, share_sdown = (
+        shared_share[:, :, i * shared_part : (i + 1) * shared_part].reshape(rows_w, -1)
+        for i in range(3)
+    )
+
     middle_slice = lax.dynamic_slice_in_dim(middle, row_index * row_width, row_width, 1)
     block_out = (middle_slice + out_slice).astype(bf16)
 

time: 706 us -> 716 us (1.014)
    pallas_call x1, Pallas kernels: 257 us -> 236 us  [experts_call(): pl.pallas_call(functools.partial(experts_kernel, cols, capacity), out_sha...]
    pallas_call x1, Pallas kernels: 197 us -> 215 us  [rear_call(): pl.pallas_call(functools.partial(rear_kernel, cols, experts), out_shape=[...]
    pallas_call x1, Pallas kernels: 191 us -> 199 us  [front_call(): pl.pallas_call(functools.partial(front_kernel, cols, experts), out_shape=...]
    unnamed x54 -> x52, local copies, waits for them, and re-layouts: 13.4 us -> 15.1 us
where the time goes in v8:
time: 716 us; the launch traced here: 708 us
  Pallas kernels  649 us (91%)
  local copies, waits for them, and re-layouts  38.2 us (5%)
  other arithmetic  20 us (3%)
    pallas_call x1, Pallas kernels, experts_call(): pl.pallas_call(functools.partial(experts_kernel, cols, capacity), out_sha...  236 us
    pallas_call x1, Pallas kernels, rear_call(): pl.pallas_call(functools.partial(rear_kernel, cols, experts), out_shape=[...  215 us
    pallas_call x1, Pallas kernels, front_call(): pl.pallas_call(functools.partial(front_kernel, cols, experts), out_shape=...  199 us
    unnamed x52, local copies, waits for them, and re-layouts  15.1 us

profile of v8, /device:TPU:10, one launch (start us, length us, event | category | flops | bytes accessed | tf_op | source)
XLA Modules:
  0.0 708.4 jit_solution(11821921583682172213)
XLA Ops:
  0.8 0.8 convert_element_type.84
  2.4 0.8 broadcast_in_dim.22
  3.2 0.8 broadcast_in_dim.23
  3.9 0.8 copy.88
  6.5 1.3 copy.93
  7.8 2.1 copy.94
  9.9 1.3 pad_maximum_fusion
  11.2 1.8 pad.13
  12.9 4.4 copy.98.shared_own
  17.3 1.2 copy.87
  18.7 198.6 %front_0.1 = (bf16[2560,1024]{1,0:T(8,128)(2,1)}, bf16[2560,640]{1,0:T(8,128)(2,1)}, bf16[8,256,2560]{2,1,0:T(8,128)(2,1)}, bf16[8,320,384]{2,1,0:T(8,128)(2,1)}...) custom-call(bf16[256,2560]{1,0:T(8,128)(2,1)} %bitcast.57, ...), custom_call_target="tpu_custom_call" | custom-call | tf_op jit(solution)/shard_map/front_0/pallas_call | solution.py:556
  217.4 1.0 copy-done
  218.4 1.0 copy-done.3
  219.4 0.7 copy-done.8
  220.1 0.7 copy-done.9
  222.9 1.2 dynamic-slice_convert_fusion.rank_col
  224.0 235.8 %experts_3.1 = (bf16[8,256,2560]{2,1,0:T(8,128)(2,1)}, bf16[256,2560]{1,0:T(8,128)(2,1)}, bf16[2,2560,384]{2,1,0:T(8,128)(2,1)}, bf16[2,2560,384]{2,1,0:T(8,128)...) custom-call(bf16[256,2560]{1,0:T(8,128)(2,1)} %get-tuple-element.44., ...), custom_call_target="tpu_custom_call" | custom-call | tf_op jit(solution)/shard_map/experts_3/pallas_call | solution.py:1164
  459.8 214.5 %rear_5.1 = (f32[256,640]{1,0:T(8,128)}, f32[256,2560]{1,0:T(8,128)}, f32[320,896]{1,0:T(8,128)}, f32[320,128]{1,0:T(8,128)}, f32[320,640]{1,0:T(8,128)}, /*index=5*/bf16[8,320,384]{2,1,0:T(8,128)(2,1)}) custom-call(bf16[8,256,2560]{2,1,0:T(8,128)(2,1)} %get-tuple-element.50.out_part, bf16[2560,384]{1,0:T(8,128)(2,1)} %get-tuple-element.51.g_shared, ...), custom_call_target="tpu_custom_call" | custom-call | tf_op jit(solution)/shard_map/rear_5/pallas_call | solution.py:1715
  674.3 1.4 add_convert_fusion
  675.7 1.1 copy.114
  676.8 5.4 copy.113
  682.2 0.9 slice_reduce_fusion
  683.7 0.7 fusion.2
  684.5 0.9 slice.35
  685.4 2.9 copy.103
  689.2 1.3 copy.107
  690.5 1.3 copy.106
  691.8 1.3 copy.105
  693.1 6.0 convert_element_type.96
  699.1 3.9 convert_element_type.97
  703.0 4.3 convert_element_type.98
  707.3 0.9 copy.118
  (66 shorter events, 6.3 us)
Async XLA Ops:
  0.6 5.2 copy-start.19
  0.7 5.5 copy-start.20
  5.4 13.1 %copy-start.1 = (f32[256,128]{1,0:T(8,128)}, f32[256,128]{1,0:T(8,128)S(1)}, u32[]{:S(2)}) copy-start(f32[256,128]{1,0:T(8,128)S(1)} %get-tuple-element.142.cosine) | copy-start | bytes 393220
  5.4 13.1 %copy-start.2 = (f32[256,128]{1,0:T(8,128)}, f32[256,128]{1,0:T(8,128)S(1)}, u32[]{:S(2)}) copy-start(f32[256,128]{1,0:T(8,128)S(1)} %get-tuple-element.143.sine) | copy-start | bytes 393220
  5.8 12.7 %copy-start.4 = (bf16[256,128]{1,0:T(8,128)(2,1)}, bf16[256,128]{1,0:T(8,128)(2,1)S(1)}, u32[]{:S(2)}) copy-start(bf16[256,128]{1,0:T(8,128)(2,1)S(1)} %pad.15.table_col) | copy-start | bytes 196612
  12.9 4.4 copy-start.16
  17.3 1.2 copy-start.6
  17.3 1.3 copy-start.7
  17.3 1.4 copy-start.11
  17.3 1.4 copy-start.12
  217.4 1.1 copy-start
  218.4 1.0 copy-start.3
  219.4 0.7 copy-start.8
  220.1 0.7 copy-start.9
  220.8 0.7 copy-start.10
  221.5 238.3 %copy-start.5 = (f32[256,128]{1,0:T(8,128)}, f32[256,128]{1,0:T(8,128)S(1)}, u32[]{:S(2)}) copy-start(f32[256,128]{1,0:T(8,128)S(1)} %get-tuple-element.49.gate) | copy-start | bytes 393220
  676.8 5.4 copy-start.15
  676.8 6.9 copy-start.17
  693.1 6.0 copy-start.14
  699.1 3.9 copy-start.13
  703.0 4.3 copy-start.18

commit v9 on v8

--- a/solution.py
+++ b/solution.py
@@ -617,6 +617,7 @@
     g_up,
     g_down,
     g_shared,
+    shared_back,
     gate_dots,
     h2_all,
     xs_all,
@@ -636,6 +637,7 @@
     dz_all,
     zg_all,
     dgu_all,
+    sdz_all,
     sz_all,
     sgu_all,
     from_core,
@@ -826,6 +828,12 @@
         saved = save_rows(cs_all, step)
         for e in range(exp_local):
             dz_all[e, pl.ds(step * pair, pair), :] = dot_nt(xbuf[e], wd[e]).astype(bf16)
+        for b in (0, 1):
+            sdz_all[block_of(step, b == 1)] = dot_nn(hb[b], ws[:, 2 * pad :]).astype(bf16)
+        if step + 2 < high:
+            for copy in along_z[step + 1]:
+                net.left(copy)
+            start_z(step + 2)
         pump()
     for copy in gate_copies:
         copy.wait_recv()
@@ -887,18 +895,18 @@
             copy.wait()
         dispatch(step)
         saved = save_rows(xs_all, step)
-        if step + 2 < high:
-            for copy in along_z[step + 1]:
-                net.left(copy)
-            start_z(step + 2)
         pump()
-        if step:
-            for copy in out_copies:
-                copy.wait()
-        grad_copies = [
-            local_copy(grads.at[block_of(step, b == 1)], obuf.at[b], base + 2 + exp_local + b)
-            for b in (0, 1)
-        ]
+        for b in (0, 1):
+            block = block_of(step, b == 1)
+            inner = dot_nn(hb[b], ws[:, : 2 * pad])
+            sa, su = inner[:, :pad], inner[:, pad:]
+            sig = 1.0 / (1.0 + jnp.exp(-sa))
+            silu = sa * sig
+            slope = sig * (1.0 + sa * (1.0 - sig))
+            sz_all[block] = (silu * su).astype(bf16)
+            sdz = sdz_all[block].astype(f32)
+            sgu_all[block, :, :pad] = (sdz * su * slope).astype(bf16)
+            sgu_all[block, :, pad:] = (sdz * silu).astype(bf16)
         if step:
             sum_cores(step - 1)
         rows = pl.ds(step * pair, pair)
@@ -947,20 +955,9 @@
 
             each_tile(width // WIDE, out_tile)
             pump()
-        for copy in grad_copies:
-            copy.wait()
-        inner = dot_nn(hb[...].reshape(2 * toks, width), ws[:, : 2 * pad])
-        sdz_both = dot_nn(obuf[...].reshape(2 * toks, width), ws[:, 2 * pad :])
-        for b in (0, 1):
-            block = block_of(step, b == 1)
-            sa, su = inner[b * toks : (b + 1) * toks, :pad], inner[b * toks : (b + 1) * toks, pad:]
-            sdz = sdz_both[b * toks : (b + 1) * toks]
-            sig = 1.0 / (1.0 + jnp.exp(-sa))
-            silu = sa * sig
-            slope = sig * (1.0 + sa * (1.0 - sig))
-            sz_all[block] = (silu * su).astype(bf16)
-            sgu_all[block, :, :pad] = (sdz * su * slope).astype(bf16)
-            sgu_all[block, :, pad:] = (sdz * silu).astype(bf16)
+        if step:
+            for copy in out_copies:
+                copy.wait()
         out_copies = []
         for b in (0, 1):
             block = block_of(step, b == 1)
@@ -1109,13 +1106,19 @@
     first_dots = net.send(dots, dots_core, net.core_peer())
     shared_grads(h2_all, sgu_all, 0, 2 * pad)
     sum_cores(last)
-    shared_grads(grads, sz_all, 2 * pad, pad)
-    inner_grads(0)
     first_dots.wait_recv()
     net.left(first_dots)
     dots[...] = dots[...] + dots_core[...]
     second_dots = net.send(dots, dots_x, net.x_peer())
-    inner_grads(1)
+    shared_grads(grads, sz_all, 2 * pad, pad)
+    own_rows = pl.ds(pl.multiple_of(net.me * rows_w, 16), rows_w)
+    keep_own = local_copy(g_shared.at[own_rows], shared_back.at[net.me], base)
+    returns = []
+    for step in range(1, cols):
+        block = lax.rem(net.me + step, cols)
+        rows = pl.ds(pl.multiple_of(block * rows_w, 16), rows_w)
+        returns.append(net.send(g_shared.at[rows], shared_back.at[net.me], net.col_peer(step)))
+    inner_grads(0)
     sum_chips(last)
     second_dots.wait_recv()
     dots_core[...] = dots[...] + dots_x[...]
@@ -1126,8 +1129,9 @@
             net.send(dots_core.at[block], gate_dots.at[net.me], net.col_peer(step))
         )
     gate_dots[net.me] = dots_core[net.me]
+    inner_grads(1)
+    sum_plane(last)
     down_grads(0)
-    sum_plane(last)
     for step in range(1, high):
         far_z[step].wait_recv()
     add_rows(kept, [from_core.at[0, 0, 0], *[from_z.at[step - 1] for step in range(1, high)]])
@@ -1135,9 +1139,12 @@
     back[:, own] = kept[...].astype(bf16)
     far = net.send(back.at[:, own], back.at[:, own], net.x_peer())
     near = net.send(back.at[:, own], back.at[:, own], net.core_peer())
+    down_grads(1)
     far.wait_recv()
     crossed = net.send(back.at[:, other], back.at[:, other], net.core_peer())
-    down_grads(1)
+    keep_own.wait()
+    for copy in returns:
+        copy.wait_recv()
     near.wait_recv()
     crossed.wait_recv()
     for copy in third_dots:
@@ -1170,6 +1177,7 @@
             shape(exp_local, width, hidden),
             shape(exp_local, hidden, width),
             shape(width, 3 * pad),
+            shape(*w_shared.shape),
             shape(cols, 8, toks, dtype=f32),
             shape(cols, toks, width),
             shape(exp_local, cols * capacity, width),
@@ -1179,6 +1187,7 @@
         out_specs=[
             any_space,
             vmem,
+            any_space,
             any_space,
             any_space,
             any_space,
@@ -1205,6 +1214,7 @@
             pltpu.VMEM((exp_local, cols * capacity, hidden), bf16),
             pltpu.VMEM((exp_local, cols * capacity, 2 * hidden), bf16),
             pltpu.VMEM((cols, toks, pad), bf16),
+            pltpu.VMEM((cols, toks, pad), bf16),
             pltpu.VMEM((cols, toks, 2 * pad), bf16),
             pltpu.VMEM((2, high, 2, toks, piece), bf16),
             pltpu.VMEM((high, 2, toks, piece), bf16),
@@ -1282,7 +1292,6 @@
     cols,
     experts,
     out_part,
-    g_shared,
     back,
     gate_dots,
     gate,
@@ -1306,7 +1315,6 @@
     share_qkv,
     share_misc,
     share_out,
-    shared_back,
     weights,
     out_weights,
     misc,
@@ -1373,14 +1381,7 @@
     ]
     near_load = local_copy(out_part.at[:, :, features(net.row)], own.at[0], 3)
     far_load = local_copy(out_part.at[:, :, features(other_row)], own.at[1], 4)
-    own_rows = pl.ds(pl.multiple_of(net.me * rows_w, 16), rows_w)
-    keep_own = local_copy(g_shared.at[own_rows], shared_back.at[net.me], 5)
-    net.greet([net.col_peer(step) for step in range(1, cols)] + row_peers(net))
-    swaps = []
-    for step in range(1, cols):
-        block = lax.rem(net.me + step, cols)
-        rows = pl.ds(pl.multiple_of(block * rows_w, 16), rows_w)
-        swaps.append(net.send(g_shared.at[rows], shared_back.at[net.me], net.col_peer(step)))
+    net.greet(col_peers(net) + row_peers(net))
 
     pieces = 4
     count = toks // pieces
@@ -1572,14 +1573,13 @@
             kv_grad[c, rows, size:] = dv[c * local_len : (c + 1) * local_len]
         kv_line[s].send_y()
         if s == 0:
-            out_line[2].send_y()
             out_line[0].send_z()
             pump()
         else:
-            out_line[3].send_y()
             kv_line[s - 1].send_z()
     kv_line[seqs - 1].send_z()
     out_line[1].send_z()
+    out_line[2].send_y()
     for s in range(seqs):
         kv_line[s].last()
     raw = kv_share[:, :size]
@@ -1668,6 +1668,7 @@
     qkv_line[2].send_y()
     qkv_line[1].send_z()
     out_line[2].send_z()
+    out_line[3].send_y()
     pump()
     misc_line.send_z()
     qkv_line[3].send_y()
@@ -1681,14 +1682,11 @@
     pump(8)
     for piece_sum in (*out_line, misc_line, *qkv_line):
         piece_sum.last()
-    keep_own.wait()
-    for copy in swaps:
-        copy.wait_recv()
     net.finish()
 
 
 def rear_call(
-    cols, collective_id, experts, out_part, g_shared, back, gate_dots, gate, router_probs, table_col, h1, h2,
+    cols, collective_id, experts, out_part, back, gate_dots, gate, router_probs, table_col, h1, h2,
     tokens, attn, weights, out_weights, grads, heads, q_low, kv_all, probs, cosine, sine,
 ):
     toks, width = back.shape
@@ -1720,10 +1718,9 @@
             shape(rows_w, qkv_width),
             shape(rows_w, LANES),
             shape(rows_w, q_width),
-            shape(cols, rows_w, g_shared.shape[1], dtype=bf16),
         ],
-        in_specs=[any_space] * 2 + [vmem] * 9 + [any_space] * 3 + [vmem] * 6,
-        out_specs=[vmem] * 5 + [any_space],
+        in_specs=[any_space] + [vmem] * 9 + [any_space] * 3 + [vmem] * 6,
+        out_specs=[vmem] * 5,
         scratch_shapes=[
             pltpu.VMEM((width, qkv_width + LANES), bf16),
             pltpu.VMEM((width, q_width), bf16),
@@ -1763,7 +1760,7 @@
         ),
         name=f"rear_{collective_id}",
     )(
-        out_part, g_shared, back, gate_dots, gate, router_probs, table_col, h1, h2, tokens, attn, weights,
+        out_part, back, gate_dots, gate, router_probs, table_col, h1, h2, tokens, attn, weights,
         out_weights, grads, heads, q_low, kv_all, probs, cosine, sine,
     )
 
@@ -2036,7 +2033,7 @@
     if kernels:
         rank_own = lax.dynamic_slice_in_dim(rank_all, col_index * exp_local, exp_local, 2)
         rank_own = rank_own.astype(f32)
-        part_out, back_full, *expert_grads, g_shared, gate_dots, _, _, _ = experts_call(
+        part_out, back_full, *expert_grads, _, shared_share, gate_dots, _, _, _ = experts_call(
             cols,
             3,
             capacity,
@@ -2067,12 +2064,22 @@
     if not kernels:
         back_full = back_full.astype(f32)
     if kernels:
-        out_slice, token_grad, share_qkv, share_misc, share_out, shared_share = rear_call(
+        shared_share = shared_share.reshape(cols, rows_w, 3, -1)[..., :shared_part]
+        shared_share = shared_share.reshape(cols, rows_w, -1)
+    else:
+        shared_share = swap_col(shared_share.reshape(cols, rows_w, 3 * shared_part))
+    shared_share = jnp.swapaxes(shared_share, 0, 1).astype(f32)
+    share_sgate, share_sup, share_sdown = (
+        shared_share[:, :, i * shared_part : (i + 1) * shared_part].reshape(rows_w, -1)
+        for i in range(3)
+    )
+
+    if kernels:
+        out_slice, token_grad, share_qkv, share_misc, share_out = rear_call(
             cols,
             5,
             experts,
             part_out,
-            g_shared,
             back_full,
             gate_dots,
             gate,
@@ -2154,17 +2161,6 @@
         share_out = scatter_col(grad_out.reshape(cols, rows_w, q_width)).astype(f32)
         share_first = scatter_col(grad_first.reshape(cols, rows_w, -1)).astype(f32)
         share_qkv, share_misc = share_first[:, :qkv_width], share_first[:, qkv_width:]
-    if kernels:
-        shared_share = shared_share.reshape(cols, rows_w, 3, -1)[..., :shared_part]
-        shared_share = shared_share.reshape(cols, rows_w, -1)
-    else:
-        shared_share = swap_col(shared_share.reshape(cols, rows_w, 3 * shared_part))
-    shared_share = jnp.swapaxes(shared_share, 0, 1).astype(f32)
-    share_sgate, share_sup, share_sdown = (
-        shared_share[:, :, i * shared_part : (i + 1) * shared_part].reshape(rows_w, -1)
-        for i in range(3)
-    )
-
     middle_slice = lax.dynamic_slice_in_dim(middle, row_index * row_width, row_width, 1)
     block_out = (middle_slice + out_slice).astype(bf16)
 

time: 716 us -> 699 us (0.976)
  Pallas kernels: 649 us -> 631 us
    pallas_call x1, Pallas kernels: 215 us -> 194 us  [rear_call(): pl.pallas_call(functools.partial(rear_kernel, cols, experts), out_shape=[...]
where the time goes in v9:
time: 699 us; the launch traced here: 691 us
  Pallas kernels  631 us (90%)
  local copies, waits for them, and re-layouts  38.2 us (5%)
  other arithmetic  20 us (3%)
    pallas_call x1, Pallas kernels, experts_call(): pl.pallas_call(functools.partial(experts_kernel, cols, capacity), out_sha...  239 us
    pallas_call x1, Pallas kernels, front_call(): pl.pallas_call(functools.partial(front_kernel, cols, experts), out_shape=...  199 us
    pallas_call x1, Pallas kernels, rear_call(): pl.pallas_call(functools.partial(rear_kernel, cols, experts), out_shape=[...  194 us
    unnamed x52, local copies, waits for them, and re-layouts  15.1 us
    convert_element_type x3, other arithmetic, on_device(): expert_grads = [grad.astype(f32) for grad in expert_grads]  14.2 us

profile of v9, /device:TPU:10, one launch (start us, length us, event | category | flops | bytes accessed | tf_op | source)
XLA Modules:
  0.0 690.9 jit_solution(2362905376558187235)
XLA Ops:
  0.8 0.8 convert_element_type.84
  2.4 0.8 broadcast_in_dim.22
  3.2 0.8 broadcast_in_dim.23
  3.9 0.8 copy.88
  6.5 1.3 copy.93
  7.8 2.1 copy.94
  9.9 1.3 pad_maximum_fusion
  11.2 1.8 pad.13
  12.9 4.4 copy.98.shared_own
  17.3 1.2 copy.87
  18.7 198.6 %front_0.1 = (bf16[2560,1024]{1,0:T(8,128)(2,1)}, bf16[2560,640]{1,0:T(8,128)(2,1)}, bf16[8,256,2560]{2,1,0:T(8,128)(2,1)}, bf16[8,320,384]{2,1,0:T(8,128)(2,1)}...) custom-call(bf16[256,2560]{1,0:T(8,128)(2,1)} %bitcast.57, ...), custom_call_target="tpu_custom_call" | custom-call | tf_op jit(solution)/shard_map/front_0/pallas_call | solution.py:556
  217.3 1.0 copy-done
  218.4 1.0 copy-done.3
  219.3 0.7 copy-done.8
  220.1 0.7 copy-done.9
  222.8 1.2 dynamic-slice_convert_fusion.rank_col
  224.0 238.6 %experts_3.1 = (bf16[8,256,2560]{2,1,0:T(8,128)(2,1)}, bf16[256,2560]{1,0:T(8,128)(2,1)}, bf16[2,2560,384]{2,1,0:T(8,128)(2,1)}, bf16[2,2560,384]{2,1,0:T(8,128)...) custom-call(bf16[256,2560]{1,0:T(8,128)(2,1)} %get-tuple-element.43., ...), custom_call_target="tpu_custom_call" | custom-call | tf_op jit(solution)/shard_map/experts_3/pallas_call | solution.py:1171
  462.6 194.2 %rear_5.1 = (f32[256,640]{1,0:T(8,128)}, f32[256,2560]{1,0:T(8,128)}, f32[320,896]{1,0:T(8,128)}, f32[320,128]{1,0:T(8,128)}, f32[320,640]{1,0:T(8,128)}) custom-call(bf16[8,256,2560]{2,1,0:T(8,128)(2,1)} %get-tuple-element.49.out_part, bf16[256,2560]{1,0:T(8,128)(2,1)} %get-tuple-element.50.back, f32[8,8,256]{2,1,0:T(8,128)} %get-tuple-element.51.gate_dots, ...), custom_call_target="tpu_custom_call" | custom-call | tf_op jit(solution)/shard_map/rear_5/pallas_call | solution.py:1713
  656.9 1.4 add_convert_fusion
  658.3 1.1 copy.114
  659.3 5.4 copy.113
  664.7 0.9 slice_reduce_fusion
  666.3 0.7 fusion.2
  667.0 0.9 slice.35
  668.0 2.9 copy.103
  671.7 1.3 copy.107
  673.0 1.3 copy.106
  674.3 1.3 copy.105
  675.6 6.0 convert_element_type.96
  681.6 3.9 convert_element_type.97
  685.6 4.3 convert_element_type.98
  689.9 0.9 copy.118
  (66 shorter events, 6.3 us)
Async XLA Ops:
  0.6 5.2 copy-start.19
  0.7 5.5 copy-start.20
  5.4 13.1 %copy-start.1 = (f32[256,128]{1,0:T(8,128)}, f32[256,128]{1,0:T(8,128)S(1)}, u32[]{:S(2)}) copy-start(f32[256,128]{1,0:T(8,128)S(1)} %get-tuple-element.140.cosine) | copy-start | bytes 393220
  5.4 13.1 %copy-start.2 = (f32[256,128]{1,0:T(8,128)}, f32[256,128]{1,0:T(8,128)S(1)}, u32[]{:S(2)}) copy-start(f32[256,128]{1,0:T(8,128)S(1)} %get-tuple-element.141.sine) | copy-start | bytes 393220
  5.8 12.7 %copy-start.4 = (bf16[256,128]{1,0:T(8,128)(2,1)}, bf16[256,128]{1,0:T(8,128)(2,1)S(1)}, u32[]{:S(2)}) copy-start(bf16[256,128]{1,0:T(8,128)(2,1)S(1)} %pad.15.table_col) | copy-start | bytes 196612
  12.9 4.4 copy-start.16
  17.3 1.2 copy-start.6
  17.3 1.3 copy-start.7
  17.3 1.4 copy-start.11
  17.3 1.4 copy-start.12
  217.3 1.1 copy-start
  218.4 1.0 copy-start.3
  219.3 0.7 copy-start.8
  220.1 0.7 copy-start.9
  220.8 0.7 copy-start.10
  221.4 241.2 %copy-start.5 = (f32[256,128]{1,0:T(8,128)}, f32[256,128]{1,0:T(8,128)S(1)}, u32[]{:S(2)}) copy-start(f32[256,128]{1,0:T(8,128)S(1)} %get-tuple-element.48.gate) | copy-start | bytes 393220
  659.3 5.4 copy-start.15
  659.3 6.9 %copy-start.17 = (f32[320,896]{1,0:T(8,128)S(1)}, f32[320,896]{1,0:T(8,128)}, u32[]{:S(2)}) copy-start(f32[320,896]{1,0:T(8,128)} %get-tuple-element.63) | copy-start | bytes 3440644
  675.6 6.0 copy-start.14
  681.6 3.9 copy-start.13
  685.6 4.3 copy-start.18
